TPU v7x, 32 devices: a whole 2x2x4 slice. The times are simulated.
32 devices in a mesh: row: 4 (over y, x), col: 8 (over z, core).
Axes of the slice: x: 2, y: 2, z: 4, core: 2. Of those that a mesh axis runs over, the one named last changes fastest.
Arguments:
- panel: bfloat16 [15, 8, 512, 512], P(None, 'row', 'col'), may hold values from -0.109375 to 0.109375
- diag_inverse: float32 [6, 8, 512, 512], P(None, 'row', 'col'), as said below
- parents: int32 [5, 8], replicated, may hold values from 0 to 7, as said below
- supernode_sizes: int32 [6, 8], replicated, may hold values from 128 to 512
Outputs:
- cross: float32 [15, 8, 512, 512], P(None, 'row', 'col')
- marginal: float32 [6, 8, 512, 512], P(None, 'row', 'col')
Inputs may be any that keep to these rules, and one draw needn't show every extreme that they name: `parents`: the parent of a supernode g of level d + 1 is a supernode of level d whose index divided by 2 equals g divided by 2, or that minus 1 modulo 8 / 2. `diag_inverse`: every block is symmetric and positive definite.
All inputs are finite; a program needn't handle non-finite values.
Results may differ from a plain program's by a relative error of at most 0.0023.
Values may be sent and summed in bfloat16 or wider, within the bound.
No kernel may reach another device: no remote copies, remote signals or barrier semaphores. Data moves between devices by JAX's collectives and lax.ppermute only.
A program may use at most 128 MiB of HBM per device.

v0:
```python
import jax
import jax.numpy as jnp
from jax import lax
from jax.sharding import PartitionSpec as P


def from_behind(x, axis, by):
    size = lax.axis_size(axis)
    return lax.ppermute(x, axis, [(i, (i + by) % size) for i in range(size)])


def turn_over(cross):
    swapped = lax.all_to_all(cross, "col", split_axis=3, concat_axis=2, tiled=True)
    return jnp.swapaxes(swapped, 2, 3)


def shards(panel, diag_inverse, parents, supernode_sizes):
    levels = diag_inverse.shape[0]
    per_row = diag_inverse.shape[1]
    row_count = diag_inverse.shape[2]
    width = diag_inverse.shape[3]
    my_row = lax.axis_index("row")
    my_col = lax.axis_index("col")
    my_nodes = my_row * per_row + jnp.arange(per_row, dtype=jnp.int32)
    my_lines = my_col * row_count + jnp.arange(row_count, dtype=jnp.int32)
    columns = jnp.arange(width, dtype=jnp.int32)
    on_diag = (my_lines[:, None] == columns[None, :]).astype(jnp.float32)
    ancestry_ids = jnp.zeros((0, parents.shape[1]), jnp.int32)
    crosses = []
    diagonals = []
    chain = None
    for level in range(levels):
        own_sizes = supernode_sizes[level][my_nodes]
        live_cols = (columns[None, :] < own_sizes[:, None]).astype(jnp.float32)
        live_lines = (my_lines[None, :] < own_sizes[:, None]).astype(jnp.float32)
        diag_base = (
            diag_inverse[level] * live_lines[:, :, None] * live_cols[:, None, :]
            + on_diag[None] * (1.0 - live_lines)[:, :, None]
        )
        if level == 0:
            diagonal = diag_base
        else:
            parent_ids = parents[level - 1]
            ancestry_ids = jnp.concatenate(
                [ancestry_ids[:, parent_ids], parent_ids[None, :]], axis=0
            )
            my_parents = parent_ids[my_nodes]
            pick_slot = jnp.where(
                my_parents // per_row == my_row,
                my_parents % per_row,
                per_row + my_parents % per_row,
            )
            passed = from_behind(chain, "row", 1)
            ancestry = jnp.take(jnp.concatenate([chain, passed], axis=0), pick_slot, axis=0)
            upper_sizes = supernode_sizes[
                jnp.arange(level, dtype=jnp.int32)[:, None], ancestry_ids[:, my_nodes]
            ]
            live_upper = (my_lines[None, None, :] < upper_sizes[:, :, None]).astype(jnp.float32)
            start = level * (level - 1) // 2
            keep = (live_upper[:, :, :, None] * live_cols[None, :, None, :]).astype(jnp.bfloat16)
            lower = jnp.transpose(panel[start : start + level] * keep, (1, 0, 2, 3))
            whole = lax.all_gather(lower, "col", axis=2, tiled=True).astype(jnp.float32)
            cross = -jnp.einsum(
                "nlmik,nmkj->nlij", ancestry, whole, precision=lax.Precision.HIGHEST
            )
            turned = turn_over(cross)
            diagonal = diag_base - jnp.einsum(
                "nlik,nlkj->nij", turned, whole, precision=lax.Precision.HIGHEST
            )
            crosses.append(jnp.transpose(cross, (1, 0, 2, 3)))
        diagonals.append(diagonal)
        if level < levels - 1:
            if level == 0:
                chain = diagonal[:, None, None]
            else:
                upper = jnp.concatenate([ancestry, cross[:, :, None]], axis=2)
                bottom = jnp.concatenate([turned[:, None], diagonal[:, None, None]], axis=2)
                chain = jnp.concatenate([upper, bottom], axis=1)
    return (jnp.concatenate(crosses, axis=0), jnp.stack(diagonals))


def solution(mesh):
    in_specs = (P(None, "row", "col", None), P(None, "row", "col", None), P(), P())
    out_specs = (P(None, "row", "col", None), P(None, "row", "col", None))
    return jax.shard_map(shards, mesh=mesh, in_specs=in_specs, out_specs=out_specs, check_vma=False)
```

profile of v0, /device:TPU:0, one launch (start us, length us, event | category | flops | bytes accessed | tf_op | source)
XLA Modules:
  0.0 696.2 jit_solution(12440427458597847939)
XLA Ops:
  24.7 3.0 collective-permute-start
  32.2 2.7 collective-permute-done
  35.6 7.3 %all-gather.15.cloned.1.call-done = bf16[1,2,512,512]{3,2,1,0:T(8,128)(2,1)} async-done(((bf16[1,2,64,512]{3,2,1,0:T(8,128)(2,1)}), bf16[1,2,512,512]{3,2,1,0:T(8,128)(2,1)}) %all-gather.15.cloned.1.call-update) | async-done | bytes 1048592 | tf_op jit(solution)/shard_map/all_gather | solution.py:62
  42.9 2.7 bitcast_dynamic-update-slice_fusion.4
  47.1 3.4 all-to-all-start
  52.4 14.0 %all-to-all-done = f32[8,1,8192]{2,1,0:T(1,128)S(1)} async-done(((f32[8,1,8192]{2,1,0:T(1,128)}), f32[8,1,8192]{2,1,0:T(1,128)S(1)}, u32[]{:S(2)}, u32[]{:S(2)}) %all-to-all-start) | async-done | bytes 262176 | tf_op jit(solution)/shard_map/all_to_all | solution.py:13
  74.8 20.6 %collective-permute-done.1 = f32[2,2,2,64,512]{4,3,0,2,1:T(8,128)} collective-permute-done((f32[2,2,2,64,512]{4,3,0,2,1:T(8,128)S(1)}, f32[2,2,2,64,512]{4,3,0,2,1:T(8,128)}, u32[]{:S(2)}, u32[]{:S(2)}) %collective-permute-start.1) | collective-permute-done | bytes 1048608 | tf_op jit(solution)/shard_map/ppermute | solution.py:9
  98.4 3.4 bitcast_dynamic-update-slice_fusion.3
  103.7 23.4 %all_to_all.90 = f32[8,1,16384]{2,1,0:T(1,128)S(1)} all-to-all(f32[8,1,16384]{2,1,0:T(1,128)S(1)} %reshape.1601), channel_id=1, replica_groups=mesh['row'=4,'col'=8] {'col'}, dimensions={0} | all-to-all | bytes 1048576 | tf_op jit(solution)/shard_map/all_to_all | solution.py:13
  132.8 3.5 bitcast_dynamic-update-slice_fusion.7
  146.1 46.3 %collective-permute-done.2 = f32[2,3,3,64,512]{4,3,2,1,0:T(8,128)} collective-permute-done((f32[2,3,3,64,512]{4,3,2,1,0:T(8,128)}, f32[2,3,3,64,512]{4,3,2,1,0:T(8,128)}, u32[]{:S(2)}, u32[]{:S(2)}) %collective-permute-start.2) | collective-permute-done | bytes 2359328 | tf_op jit(solution)/shard_map/ppermute | solution.py:9
  192.4 3.8 pad_maximum_fusion.2
  196.1 4.4 gather_fusion.12
  202.7 4.8 bitcast_dynamic-update-slice_fusion.2
  209.5 3.6 reshape.1603
  213.2 25.7 %all_to_all.91 = f32[8,1,24576]{2,1,0:T(1,128)} all-to-all(f32[8,1,24576]{2,1,0:T(1,128)} %reshape.1603), channel_id=1, replica_groups=mesh['row'=4,'col'=8] {'col'}, dimensions={0} | all-to-all | bytes 1572864 | tf_op jit(solution)/shard_map/all_to_all | solution.py:13
  238.9 4.5 reduce.8
  243.4 3.4 reshape.1604
  246.8 3.5 copy.167
  250.3 2.6 all_to_all.76
  252.9 4.6 bitcast_dynamic-update-slice_fusion.6
  257.5 2.6 maximum_maximum_fusion.1
  266.1 87.3 %collective-permute-done.3 = f32[2,4,4,64,512]{4,3,2,1,0:T(8,128)} collective-permute-done((f32[2,4,4,64,512]{4,3,2,1,0:T(8,128)}, f32[2,4,4,64,512]{4,3,2,1,0:T(8,128)}, u32[]{:S(2)}, u32[]{:S(2)}) %collective-permute-start.3) | collective-permute-done | bytes 4194336 | tf_op jit(solution)/shard_map/ppermute | solution.py:9
  353.4 5.7 pad_maximum_fusion.1
  359.1 6.2 gather_fusion.18
  365.3 5.1 broadcast_select_fusion
  370.4 7.8 %bitcast_dynamic-update-slice_fusion.1 = (f32[15,2,64,512]{3,2,0,1:T(8,128)}, f32[2,4,64,512]{3,2,1,0:T(8,128)S(1)}) fusion(f32[15,2,64,512]{3,2,0,1:T(8,128)} %get-tuple-element.46, f32[2,4,4,64,512]{4,3,2,1,0:T(8,128)} %broadcast_select_fusion, bf16[2,4,512,512]{3,2,1,0:T(8,128)(2,1)} %all-gather.11.cloned.1.call-done), kind=kOutput, calls=%fused_computation.79 | convolution fusion | flops 6442713088 | bytes 10485760 | tf_op jit(solution)/shard_map/nlmik,nmkj->nlij/dot_general | solution.py:63
  380.0 4.0 reshape.1605
  384.0 3.7 all-to-all-start.3
  392.1 37.8 %all-to-all-done.3 = f32[8,1,32768]{2,1,0:T(1,128)S(1)} async-done(((f32[8,1,32768]{2,1,0:T(1,128)}), f32[8,1,32768]{2,1,0:T(1,128)S(1)}, u32[]{:S(2)}, u32[]{:S(2)}) %all-to-all-start.3) | async-done | bytes 1048608 | tf_op jit(solution)/shard_map/all_to_all | solution.py:13
  429.9 3.1 reduce.9
  433.0 2.7 reshape.1606
  435.7 4.1 copy.166
  441.8 5.4 bitcast_dynamic-update-slice_fusion.5
  447.2 3.2 maximum_maximum_fusion
  451.5 140.3 %collective-permute-done.4 = f32[2,5,5,64,512]{4,3,2,1,0:T(8,128)} collective-permute-done((f32[2,5,5,64,512]{4,3,2,1,0:T(8,128)}, f32[2,5,5,64,512]{4,3,2,1,0:T(8,128)}, u32[]{:S(2)}, u32[]{:S(2)}) %collective-permute-start.4) | collective-permute-done | bytes 6553632 | tf_op jit(solution)/shard_map/ppermute | solution.py:9
  591.8 9.6 %pad_maximum_fusion = f32[4,5,5,64,512]{4,3,2,1,0:T(8,128)} fusion(f32[2,5,5,64,512]{4,3,2,1,0:T(8,128)} %collective-permute-done.4, f32[2,1,1,64,512]{4,3,2,1,0:T(8,128)S(1)} %bitcast.460, f32[2,1,4,64,512]{4,3,2,1,0:T(8,128)S(1)} %bitcast.431, f32[2,4,1,64,512]{4,3,2,1,0:T(8,128)S(1)} %bitcast.429, f32[2,4,4,64,512]{4,3,2,1,0:T(8,128)} %broadcast_select_fusion), kind=kLoop, calls=%fused_computation.30 | loop fusion | flops 13107200 | bytes 26214400 | tf_op jit(solution)/shard_map/concatenate | solution.py:54
  601.4 8.4 %gather_fusion.24 = f32[2,5,5,64,512]{4,3,2,1,0:T(8,128)} fusion(f32[4,5,5,64,512]{4,3,2,1,0:T(8,128)} %pad_maximum_fusion, s32[1024]{0:T(1024)S(1)} %pad_clamp_fusion.1), kind=kCustom, calls=%fused_computation.25 | custom fusion | bytes 13107208 | tf_op jit(solution)/shard_map/jit(_take)/gather | solution.py:54
  609.7 10.0 %bitcast_dynamic-update-slice_fusion = (f32[15,2,64,512]{3,2,0,1:T(8,128)}, f32[2,5,64,512]{3,2,1,0:T(8,128)S(1)}) fusion(f32[15,2,64,512]{3,2,0,1:T(8,128)} %get-tuple-element.48, bf16[2,5,512,512]{3,2,1,0:T(8,128)(2,1)} %all-gather.13.cloned.1.call-done, f32[2,5,5,64,512]{4,3,2,1,0:T(8,128)} %gather_fusion.24, pred[2]{0:T(512)(128)(4,1)S(1)} %compare_and_fusion), kind=kOutput, calls=%fused_computation.58 | convolution fusion | flops 10068295680 | bytes 14417922 | tf_op jit(solution)/shard_map/nlmik,nmkj->nlij/dot_general | solution.py:63
  619.8 2.5 copy.129
  622.3 4.9 reshape.1607
  627.2 6.9 all-to-all-start.4
  634.1 4.7 copy.131
  638.8 27.5 %all-to-all-done.4 = f32[8,1,40960]{2,1,0:T(1,128)S(1)} async-done(((f32[8,1,40960]{2,1,0:T(1,128)}), f32[8,1,40960]{2,1,0:T(1,128)S(1)}, u32[]{:S(2)}, u32[]{:S(2)}) %all-to-all-start.4) | async-done | bytes 1310752 | tf_op jit(solution)/shard_map/all_to_all | solution.py:13
  666.3 5.2 reduce.10
  671.6 4.7 reshape.1608
  676.2 4.8 copy.165
  683.1 6.0 fusion.50
  (213 shorter events, 75.7 us)
Async XLA Ops:
  7.2 10.8 %copy-start.28 = (s32[5,8]{1,0:T(8,128)S(1)}, s32[5,8]{1,0:T(8,128)}, u32[]{:S(2)}) copy-start(s32[5,8]{1,0:T(8,128)} %param.6) | copy-start | bytes 484
  7.2 12.8 %copy-start = (s32[6,8]{1,0:T(8,128)S(1)}, s32[6,8]{1,0:T(8,128)}, u32[]{:S(2)}) copy-start(s32[6,8]{1,0:T(8,128)} %param.7) | copy-start | bytes 580
  7.2 35.7 %all-gather.15.cloned.1.call-start = ((), (), s32[]{:S(2)}) async-start(), calls=%async_computation.9 | async-start | bytes 1179648 | tf_op jit(solution)/shard_map/all_gather | solution.py:62
  7.3 21.2 %copy-start.15 = (s32[1024]{0:T(1024)}, s32[1024]{0:T(1024)S(1)}, u32[]{:S(2)}) copy-start(s32[1024]{0:T(1024)S(1)} %pad_clamp_fusion.9) | copy-start | bytes 12292
  14.2 9.4 %copy-start.26 = (s32[2]{0:T(128)}, s32[2]{0:T(128)S(1)}, u32[]{:S(2)}) copy-start(s32[2]{0:T(128)S(1)} %gather_fusion.22) | copy-start | bytes 28
  14.8 13.4 %copy-start.24 = (s32[2]{0:T(128)}, s32[2]{0:T(128)S(1)}, u32[]{:S(2)}) copy-start(s32[2]{0:T(128)S(1)} %gather_fusion.28) | copy-start | bytes 28
  15.5 16.7 %copy-start.16 = (s32[64]{0:T(128)}, s32[64]{0:T(128)S(1)}, u32[]{:S(2)}) copy-start(s32[64]{0:T(128)S(1)} %iota_add_fusion) | copy-start | bytes 772
  15.6 0.7 copy-start.13
  17.9 80.5 %all-gather.7.cloned.1.call-start = ((), (), s32[]{:S(2)}) async-start(), calls=%async_computation.5 | async-start | bytes 2359296 | tf_op jit(solution)/shard_map/all_gather | solution.py:62
  20.9 2.7 copy-start.10
  22.8 180.0 %all-gather.9.cloned.1.call-start = ((), (), s32[]{:S(2)}) async-start(), calls=%async_computation.6 | async-start | bytes 3538944 | tf_op jit(solution)/shard_map/all_gather | solution.py:62
  24.7 10.3 %collective-permute-start = (f32[2,1,1,64,512]{4,3,0,2,1:T(8,128)S(1)}, f32[2,1,1,64,512]{4,3,0,2,1:T(8,128)S(1)}, u32[]{:S(2)}, u32[]{:S(2)}) collective-permute-start(f32[2,1,1,64,512]{4,3,0,2,1:T(8,128)S(1)} %fusion.81), channel_id=1, source_target_pairs={{0,8},{8,16},{16,24},{24,0},{1,9},{9,17},{17,25},{25,1},{2,10},{10... | collective-permute-start | bytes 786440 | tf_op jit(solution)/shard_map/ppermute | solution.py:9
  28.4 17.1 %copy-start.4 = (s32[3,8]{0,1:T(8,128)}, s32[3,8]{0,1:T(8,128)S(1)}, u32[]{:S(2)}) copy-start(s32[3,8]{0,1:T(8,128)S(1)} %pad_add_fusion) | copy-start | bytes 292
  30.1 17.0 %copy-start.8 = (f32[2,512]{1,0:T(2,128)}, f32[2,512]{1,0:T(2,128)S(1)}, u32[]{:S(2)}) copy-start(f32[2,512]{1,0:T(2,128)S(1)} %compare_convert_fusion.3) | copy-start | bytes 12292
  45.6 23.5 %copy-start.3 = (bf16[1,2,512,512]{3,2,1,0:T(8,128)(2,1)S(1)}, bf16[1,2,512,512]{3,2,1,0:T(8,128)(2,1)}, u32[]{:S(2)}) copy-start(bf16[1,2,512,512]{3,2,1,0:T(8,128)(2,1)} %all-gather.15.cloned.1.call-done) | copy-start | bytes 3145732
  45.6 23.5 %copy-start.14 = (f32[2,512]{1,0:T(2,128)S(1)}, f32[2,512]{1,0:T(2,128)}, u32[]{:S(2)}) copy-start(f32[2,512]{1,0:T(2,128)} %copy-done.13) | copy-start | bytes 12292
  45.6 23.5 %copy-start.29 = (f32[2,64]{1,0:T(2,128)S(1)}, f32[2,64]{1,0:T(2,128)}, u32[]{:S(2)}) copy-start(f32[2,64]{1,0:T(2,128)} %get-tuple-element.40) | copy-start | bytes 1540
  45.6 23.5 %copy-start.30 = (f32[2,64]{1,0:T(2,128)S(1)}, f32[2,64]{1,0:T(2,128)}, u32[]{:S(2)}) copy-start(f32[2,64]{1,0:T(2,128)} %get-tuple-element.31) | copy-start | bytes 1540
  47.1 19.3 %all-to-all-start = ((f32[8,1,8192]{2,1,0:T(1,128)}), f32[8,1,8192]{2,1,0:T(1,128)S(1)}, u32[]{:S(2)}, u32[]{:S(2)}) async-start(f32[8,1,8192]{2,1,0:T(1,128)} %reshape.1599), calls=%async_computation | async-start | bytes 524288 | tf_op jit(solution)/shard_map/all_to_all | solution.py:13
  50.5 319.9 %all-gather.11.cloned.1.call-start = ((), (), s32[]{:S(2)}) async-start(), calls=%async_computation.7 | async-start | bytes 4718592 | tf_op jit(solution)/shard_map/all_gather | solution.py:62
  71.5 23.9 %collective-permute-start.1 = (f32[2,2,2,64,512]{4,3,0,2,1:T(8,128)S(1)}, f32[2,2,2,64,512]{4,3,0,2,1:T(8,128)}, u32[]{:S(2)}, u32[]{:S(2)}) collective-permute-start(f32[2,2,2,64,512]{4,3,0,2,1:T(8,128)S(1)} %maximum_maximum_fusion.3), channel_id=1, source_target_pairs={{0,8},{8,16},{16,24},{24,0},{1,9},{9,17},{17,25},{25,1},{2,10},{10... | collective-permute-start | bytes 3145736 | tf_op jit(solution)/shard_map/ppermute | solution.py:9
  136.3 3.2 copy-start.32
  136.3 3.2 copy-start.33
  136.3 3.8 copy-start.5
  136.3 4.4 copy-start.31
  136.3 6.2 copy-start.27
  136.3 6.3 copy-start.17
  138.0 54.3 %collective-permute-start.2 = (f32[2,3,3,64,512]{4,3,2,1,0:T(8,128)}, f32[2,3,3,64,512]{4,3,2,1,0:T(8,128)}, u32[]{:S(2)}, u32[]{:S(2)}) collective-permute-start(f32[2,3,3,64,512]{4,3,2,1,0:T(8,128)} %maximum_maximum_fusion.2), channel_id=1, source_target_pairs={{0,8},{8,16},{16,24},{24,0},{1,9},{9,17},{17,25},{25,1},{2,10},{10... | collective-permute-start | bytes 7077896 | tf_op jit(solution)/shard_map/ppermute | solution.py:9
  140.8 55.3 %copy-start.6 = (s32[4,8]{0,1:T(8,128)}, s32[4,8]{0,1:T(8,128)S(1)}, u32[]{:S(2)}) copy-start(s32[4,8]{0,1:T(8,128)S(1)} %pad_add_fusion.1) | copy-start | bytes 388
  142.6 0.6 copy-start.11
  246.8 6.1 copy-start.9
  252.9 4.6 copy-start.2
  257.5 4.7 copy-start.7
  260.1 93.3 %collective-permute-start.3 = (f32[2,4,4,64,512]{4,3,2,1,0:T(8,128)}, f32[2,4,4,64,512]{4,3,2,1,0:T(8,128)}, u32[]{:S(2)}, u32[]{:S(2)}) collective-permute-start(f32[2,4,4,64,512]{4,3,2,1,0:T(8,128)} %maximum_maximum_fusion.1), channel_id=1, source_target_pairs={{0,8},{8,16},{16,24},{24,0},{1,9},{9,17},{17,25},{25,1},{2,10},{10... | collective-permute-start | bytes 12582920 | tf_op jit(solution)/shard_map/ppermute | solution.py:9
  359.1 6.2 copy-start.34
  380.0 8.0 %copy-start.23 = (s32[8,4]{1,0:T(8,128)S(1)}, s32[8,4]{1,0:T(8,128)}, u32[]{:S(2)}) copy-start(s32[8,4]{1,0:T(8,128)} %gather_fusion.25) | copy-start | bytes 388
  384.0 5.8 copy-start.25
  384.0 5.8 copy-start.18
  384.0 45.9 %all-to-all-start.3 = ((f32[8,1,32768]{2,1,0:T(1,128)}), f32[8,1,32768]{2,1,0:T(1,128)S(1)}, u32[]{:S(2)}, u32[]{:S(2)}) async-start(f32[8,1,32768]{2,1,0:T(1,128)} %reshape.1605), calls=%async_computation.3 | async-start | bytes 2097152 | tf_op jit(solution)/shard_map/all_to_all | solution.py:13
  387.7 222.0 %all-gather.13.cloned.1.call-start = ((), (), s32[]{:S(2)}) async-start(), calls=%async_computation.8 | async-start | bytes 5898240 | tf_op jit(solution)/shard_map/all_gather | solution.py:62
  435.7 6.1 copy-start.12
  435.7 6.1 copy-start.20
  435.7 6.1 copy-start.22
  441.8 5.4 copy-start.1
  450.4 141.4 %collective-permute-start.4 = (f32[2,5,5,64,512]{4,3,2,1,0:T(8,128)}, f32[2,5,5,64,512]{4,3,2,1,0:T(8,128)}, u32[]{:S(2)}, u32[]{:S(2)}) collective-permute-start(f32[2,5,5,64,512]{4,3,2,1,0:T(8,128)} %maximum_maximum_fusion), channel_id=1, source_target_pairs={{0,8},{8,16},{16,24},{24,0},{1,9},{9,17},{17,25},{25,1},{2,10},{10... | collective-permute-start | bytes 19660808 | tf_op jit(solution)/shard_map/ppermute | solution.py:9
  627.2 39.1 %all-to-all-start.4 = ((f32[8,1,40960]{2,1,0:T(1,128)}), f32[8,1,40960]{2,1,0:T(1,128)S(1)}, u32[]{:S(2)}, u32[]{:S(2)}) async-start(f32[8,1,40960]{2,1,0:T(1,128)} %reshape.1607), calls=%async_computation.4 | async-start | bytes 2621440 | tf_op jit(solution)/shard_map/all_to_all | solution.py:13
  681.0 2.1 copy-start.19
  681.0 2.1 copy-start.21
Sparse Core Ops, SparseCore 0:
  18.0 24.8 all-gather.14
  44.5 34.1 all-gather.6
  80.3 39.2 all-gather.8
  145.4 45.0 all-gather.10
  392.3 65.9 all-gather.12
where the time goes:
time: 704 us; the launch traced here: 696 us
  waiting for transfers between devices  384 us (55%)
  local copies, waits for them, and re-layouts  105 us (15%)
  other arithmetic  71.2 us (10%)
  matrix products  50.7 us (7%)
  blocking collectives  49.1 us (7%)
  starting transfers between devices  21.4 us (3%)
  between operations  14.8 us (2%)
    ppermute x5, waiting for transfers between devices, from_behind(): return lax.ppermute(x, axis, [(i, (i + by) % size) for i in range(size)])  297 us
    all_to_all x3, waiting for transfers between devices, turn_over(): lax.all_to_all(cross, 'col', split_axis=3, concat_axis=2, tiled=True)  79.3 us
    all_to_all x2, blocking collectives, turn_over(): lax.all_to_all(cross, 'col', split_axis=3, concat_axis=2, tiled=True)  49.1 us
    unnamed x84, local copies, waits for them, and re-layouts  33.1 us
    dot_general x5, matrix products, shards(): jnp.einsum('nlmik,nmkj->nlij', ancestry, whole, precision=lax.Precision.H...  28.8 us
    all_to_all x11, local copies, waits for them, and re-layouts, turn_over(): lax.all_to_all(cross, 'col', split_axis=3, concat_axis=2, tiled=True)  23 us
    dot_general x5, matrix products, shards(): jnp.einsum('nlik,nlkj->nij', turned, whole, precision=lax.Precision.HIGHEST)  21.9 us
    concatenate x5, other arithmetic, shards(): jnp.concatenate([chain, passed], axis=0)  20.5 us
  transfers between devices with their start and end apart: 13, of which 9 were waited for; matrix products, arithmetic and copies ran while one was open for 22% of the time, Pallas kernels for 0%

commit v1 on v0

v1 whole, which is shorter than its diff:
```python
import functools

import jax
import jax.numpy as jnp
from jax import lax
from jax.experimental import pallas as pl
from jax.experimental.pallas import tpu as pltpu
from jax.sharding import PartitionSpec as P

F32 = jnp.float32
BF16 = jnp.bfloat16
F16 = jnp.float16
TOP = 2.0**14
TAIL = 8
VMEM = pl.BlockSpec(memory_space=pltpu.VMEM)
SMEM = pl.BlockSpec(memory_space=pltpu.SMEM)
ANY = pl.BlockSpec(memory_space=pl.ANY)


def factors(peak):
    rows = lax.broadcasted_iota(jnp.int32, (TAIL, peak.shape[1]), 0)
    rest = jnp.maximum(peak, 2.0**-100)
    table = jnp.ones((TAIL, peak.shape[1]), F32)
    whole = jnp.ones_like(rest)
    for i in range(TAIL):
        one = jnp.clip(rest, 2.0**-14, TOP).astype(BF16).astype(F32)
        rest = rest / one
        table = jnp.where(rows == i, jnp.broadcast_to(one, table.shape), table)
        whole = whole * one
    return table, whole


def product(table):
    whole = table[0:1]
    for i in range(1, TAIL):
        whole = whole * table[i : i + 1]
    return whole * (1.0 / TOP)


def peak_of(x):
    down = jnp.max(jnp.abs(x), axis=0, keepdims=True)
    return jnp.broadcast_to(jnp.max(down, axis=1, keepdims=True), down.shape)


def chain_of(parents, level, node):
    found = [None] * level
    for up in range(level - 1, -1, -1):
        node = parents[up, node]
        found[up] = node
    return found


def live_lanes(shape, size):
    return lax.broadcasted_iota(jnp.int32, shape, len(shape) - 1) < size


def base_kernel(npr, rows, width, place, sizes, diag, marginal, message):
    row, col = place[0], place[1]
    for n in range(npr):
        value = diag_base(diag[n], sizes[0, row * npr + n], col * rows, rows, width)
        marginal[n] = value
        table, whole = factors(peak_of(value))
        message[n, :rows] = value * (TOP / whole)
        message[n, rows:] = table


def diag_base(block, size, first, rows, width):
    lines = lax.broadcasted_iota(jnp.int32, (rows, width), 0) + first
    lanes = lax.broadcasted_iota(jnp.int32, (rows, width), 1)
    kept = jnp.where((lines < size) & (lanes < size), block, 0.0)
    return kept + jnp.where((lines == lanes) & (lines >= size), 1.0, 0.0)


def cross_kernel(level, last, spans, n_row, npr, rows, width, *refs):
    place, parents, sizes, panel = refs[:4]
    at = 4
    sources = []
    for up in range(level):
        parts = []
        for _ in range(1 if up == 0 else 2):
            parts.append(refs[at : at + spans[up]])
            at += spans[up]
        sources.append(parts)
    n_out = 2 if last else 3
    outs = refs[at : at + n_out]
    scratch = refs[at + n_out :]
    cross, turn = outs[0], outs[1]
    passed = None if last else outs[2]
    lower, split, panel_sem, block_sem = scratch[:4]
    holders = scratch[4:]
    row = place[0]
    n_col = panel.shape[0]
    high = level * rows

    chains = [chain_of(parents, level, row * npr + n) for n in range(npr)]

    def panel_copy(n, m):
        return pltpu.make_async_copy(panel.at[:, m, n], lower.at[n, m], panel_sem.at[n, m])

    def holder(up, part):
        return holders[0] if up == 0 else holders[1 + 2 * (up - 1) + part]

    for n in range(npr):
        for up in range(level):
            node = chains[n][up]
            back = lax.rem(row - lax.div(node, npr) + n_row, n_row)
            slot = lax.rem(node, npr)
            for part, choices in enumerate(sources[up]):
                for i, source in enumerate(choices):

                    @pl.when(back == i)
                    def _():
                        pltpu.make_async_copy(
                            source.at[slot], holder(up, part).at[n], block_sem.at[n, up, part]
                        ).start()
        for m in range(level):
            panel_copy(n, m).start()

    for n in range(npr):
        for up in range(level):
            size = sizes[up, chains[n][up]]
            for part, choices in enumerate(sources[up]):
                held = holder(up, part)
                pltpu.make_async_copy(choices[0].at[0], held.at[n], block_sem.at[n, up, part]).wait()
                count = (held.shape[1] - TAIL) // rows
                whole = product(held[n, count * rows :])
                for b in range(count):
                    value = held[n, b * rows : (b + 1) * rows] * whole
                    if up > 0 and part == 0:
                        l, m = b, up
                        value = jnp.where(live_lanes(value.shape, size), value, 0.0)
                    else:
                        l, m = up, b
                        value = jnp.where(
                            live_lanes(value.shape, sizes[m, chains[n][m]]), value, 0.0
                        )
                    top = value.astype(BF16)
                    split[n, m, l * rows : (l + 1) * rows] = top
                    split[n, m, high + l * rows : high + (l + 1) * rows] = (
                        value - top.astype(F32)
                    ).astype(BF16)

    results = []
    for n in range(npr):
        total = None
        for m in range(level):
            panel_copy(n, m).wait()
            block = lower[n, m].reshape(width, width)
            term = jnp.dot(split[n, m], block, preferred_element_type=F32)
            total = term if total is None else total + term
        value = -(total[:high] + total[high:])
        value = jnp.where(live_lanes(value.shape, sizes[level, row * npr + n]), value, 0.0)
        for l in range(level):
            cross[l, n] = value[l * rows : (l + 1) * rows]
        table, whole = factors(peak_of(value))
        value = value * (TOP / whole)
        if not last:
            passed[n, :high] = value
            passed[n, high:] = table
        results.append((value, table))
    for c in range(n_col):
        piece = slice(c * rows, (c + 1) * rows)
        turn[c, :high] = jnp.concatenate([v[:, piece] for v, _ in results], axis=1)
        turn[c, high:] = jnp.concatenate([t[:, piece] for _, t in results], axis=1)


def marginal_kernel(level, last, n_row, npr, rows, width, *refs):
    place, sizes, panel, turned, diag = refs[:5]
    n_out = 1 if last else 2
    outs = refs[5 : 5 + n_out]
    lower, panel_sem = refs[5 + n_out :]
    marginal = outs[0]
    message = None if last else outs[1]
    row, col = place[0], place[1]
    n_col = panel.shape[0]
    high = level * rows

    def panel_copy(n, m):
        return pltpu.make_async_copy(panel.at[:, m, n], lower.at[n, m], panel_sem.at[n, m])

    for m in range(level):
        for n in range(npr):
            panel_copy(n, m).start()

    scales = jnp.concatenate(
        [jnp.broadcast_to(product(turned[c, high:]), (rows, npr * rows)) for c in range(n_col)], axis=0
    )
    totals = [None] * npr
    sides = [[] for _ in range(npr)]
    for l in range(level):
        upright = turned[:, l * rows : (l + 1) * rows].reshape(width, npr * rows) * scales
        flat = upright.T
        top = flat.astype(BF16)
        low = (flat - top.astype(F32)).astype(BF16)
        for n in range(npr):
            mine = slice(n * rows, (n + 1) * rows)
            panel_copy(n, l).wait()
            block = lower[n, l].reshape(width, width)
            pair = jnp.concatenate([top[mine], low[mine]], axis=0)
            term = jnp.dot(pair, block, preferred_element_type=F32)
            term = term[:rows] + term[rows:]
            totals[n] = term if totals[n] is None else totals[n] + term
            sides[n].append(flat[mine])
    for n in range(npr):
        size = sizes[level, row * npr + n]
        value = diag_base(diag[n], size, col * rows, rows, width)
        value = value - jnp.where(live_lanes(value.shape, size), totals[n], 0.0)
        marginal[n] = value
        if not last:
            peak = peak_of(value)
            for side in sides[n]:
                peak = jnp.maximum(peak, peak_of(side))
            table, whole = factors(peak)
            scale = TOP / whole
            for l in range(level):
                message[n, l * rows : (l + 1) * rows] = sides[n][l] * scale
            message[n, high : high + rows] = value * scale
            message[n, high + rows :] = table


def params(limit=60 * 2**20):
    return pltpu.CompilerParams(vmem_limit_bytes=limit)


def shards(panel, diag_inverse, parents, supernode_sizes):
    levels, npr, rows, width = diag_inverse.shape
    n_row = lax.axis_size("row")
    n_col = lax.axis_size("col")
    place = jnp.stack([lax.axis_index("row"), lax.axis_index("col")]).astype(jnp.int32)

    def shape(*dims, dtype=F32):
        return jax.ShapeDtypeStruct(dims, dtype)

    def reach(level):
        return min(levels - 1 - level, n_row - 1)

    def spread(message, level):
        found = [message]
        half = message.astype(F16)
        for back in range(1, reach(level) + 1):
            route = [(i, (i + back) % n_row) for i in range(n_row)]
            found.append(lax.ppermute(half, "row", route).astype(F32))
        return found

    whole_panel = []
    for level in range(1, levels):
        start = level * (level - 1) // 2
        whole_panel.append(lax.all_gather(panel[start : start + level], "col", axis=0))

    base, message = pl.pallas_call(
        functools.partial(base_kernel, npr, rows, width),
        out_shape=(shape(npr, rows, width), shape(npr, rows + TAIL, width)),
        in_specs=[SMEM, SMEM, VMEM],
        out_specs=(VMEM, VMEM),
        compiler_params=params(),
        name="base",
    )(place, supernode_sizes, diag_inverse[0])
    crosses = []
    diagonals = [base]
    table = [[spread(message, 0)]]
    for level in range(1, levels):
        last = level == levels - 1
        high = level * rows
        whole = whole_panel[level - 1]
        spans = [min(level - up, n_row - 1) + 1 for up in range(level)]
        sources = [a for up in range(level) for part in table[up] for a in part[: spans[up]]]
        out_shape = [shape(level, npr, rows, width), shape(n_col, high + TAIL, npr * rows)]
        if not last:
            out_shape.append(shape(npr, high + TAIL, width))
        scratch = [
            pltpu.VMEM((npr, level, n_col, rows, width), BF16),
            pltpu.VMEM((npr, level, 2 * high, width), BF16),
            pltpu.SemaphoreType.DMA((npr, level)),
            pltpu.SemaphoreType.DMA((npr, level, 2)),
            pltpu.VMEM((npr, rows + TAIL, width), F32),
        ]
        for up in range(1, level):
            scratch.append(pltpu.VMEM((npr, up * rows + TAIL, width), F32))
            scratch.append(pltpu.VMEM((npr, (up + 1) * rows + TAIL, width), F32))
        made = pl.pallas_call(
            functools.partial(cross_kernel, level, last, spans, n_row, npr, rows, width),
            out_shape=tuple(out_shape),
            in_specs=[SMEM, SMEM, SMEM] + [ANY] * (1 + len(sources)),
            out_specs=(VMEM,) * len(out_shape),
            scratch_shapes=scratch,
            compiler_params=params(),
            name=f"cross{level}",
        )(place, parents, supernode_sizes, whole, *sources)
        crosses.append(made[0])
        ahead = None if last else spread(made[2], level)
        turned = lax.all_to_all(made[1].astype(F16), "col", 0, 0, tiled=True).astype(F32)
        out_shape = [shape(npr, rows, width)]
        if not last:
            out_shape.append(shape(npr, high + rows + TAIL, width))
        done = pl.pallas_call(
            functools.partial(marginal_kernel, level, last, n_row, npr, rows, width),
            out_shape=tuple(out_shape),
            in_specs=[SMEM, SMEM, ANY, VMEM, VMEM],
            out_specs=(VMEM,) * len(out_shape),
            scratch_shapes=[
                pltpu.VMEM((npr, level, n_col, rows, width), BF16),
                pltpu.SemaphoreType.DMA((npr, level)),
            ],
            compiler_params=params(),
            name=f"marginal{level}",
        )(place, supernode_sizes, whole, turned, diag_inverse[level])
        diagonals.append(done[0])
        if not last:
            table.append([ahead, spread(done[1], level)])
    return (jnp.concatenate(crosses, axis=0), jnp.stack(diagonals))


def solution(mesh):
    in_specs = (P(None, "row", "col", None), P(None, "row", "col", None), P(), P())
    out_specs = (P(None, "row", "col", None), P(None, "row", "col", None))
    return jax.shard_map(shards, mesh=mesh, in_specs=in_specs, out_specs=out_specs, check_vma=False)
```

time: 704 us -> 361 us (0.51)
  waiting for transfers between devices: 384 us -> 139 us
  local copies, waits for them, and re-layouts: 105 us -> 18.3 us
  Pallas kernels: 0 us -> 61.5 us
  matrix products: 50.7 us -> 0 us
  other arithmetic: 71.2 us -> 39.1 us
  starting transfers between devices: 21.4 us -> 32.6 us
    ppermute x5 -> x21, waiting for transfers between devices: 297 us -> 104 us  [spread(): found.append(lax.ppermute(half, 'row', route).astype(F32))]
    pallas_call x0 -> x11, Pallas kernels: none -> 61.5 us  [the longest x5 37.1 us: shards(): pl.pallas_call(functools.partial(cross_kernel, level, last, spans, n_row,...]
    all_to_all x3 -> x2, waiting for transfers between devices: 79.3 us -> 27.7 us  [shards(): lax.all_to_all(made[1].astype(F16), 'col', 0, 0, tiled=True).astype(F32)]
    dot_general x10 -> x0, matrix products: 50.7 us -> none  [the longest x5 28.8 us: shards(): jnp.einsum('nlmik,nmkj->nlij', ancestry, whole, precision=lax.Precision.H...]
    gather x38 -> x0, local copies, waits for them, and re-layouts: 38.6 us -> none  [the longest x5 20.3 us: shards(): jnp.take(jnp.concatenate([chain, passed], axis=0), pick_slot, axis=0)]
    convert_element_type x12 -> x40, other arithmetic: 1.46 us -> 38.5 us  [the longest x21 19.6 us: spread(): found.append(lax.ppermute(half, 'row', route).astype(F32))]
    concatenate x18 -> x0, other arithmetic: 28.4 us -> none  [the longest x5 20.5 us: shards(): jnp.concatenate([chain, passed], axis=0)]
    unnamed x84 -> x41, local copies, waits for them, and re-layouts: 33.1 us -> 7.23 us
  transfers between devices with their start and end apart: 13 -> 28, of which waited for: 9 -> 12; matrix products, arithmetic and copies ran while one was open for 22% -> 14% of each run, Pallas kernels for 0% -> 13%
where the time goes in v1:
time: 361 us; the launch traced here: 360 us
  waiting for transfers between devices  139 us (39%)
  Pallas kernels  61.5 us (17%)
  blocking collectives  55.2 us (15%)
  other arithmetic  39.1 us (11%)
  starting transfers between devices  32.6 us (9%)
  local copies, waits for them, and re-layouts  18.3 us (5%)
  between operations  14.1 us (4%)
    ppermute x21, waiting for transfers between devices, spread(): found.append(lax.ppermute(half, 'row', route).astype(F32))  104 us
    all_to_all x3, blocking collectives, shards(): lax.all_to_all(made[1].astype(F16), 'col', 0, 0, tiled=True).astype(F32)  55.2 us
    pallas_call x5, Pallas kernels, shards(): pl.pallas_call(functools.partial(cross_kernel, level, last, spans, n_row,...  37.1 us
    all_to_all x2, waiting for transfers between devices, shards(): lax.all_to_all(made[1].astype(F16), 'col', 0, 0, tiled=True).astype(F32)  27.7 us
    ppermute x21, starting transfers between devices, spread(): found.append(lax.ppermute(half, 'row', route).astype(F32))  25.2 us
    pallas_call x5, Pallas kernels, shards(): pl.pallas_call(functools.partial(marginal_kernel, level, last, n_row, npr...  22.5 us
    convert_element_type x21, other arithmetic, spread(): found.append(lax.ppermute(half, 'row', route).astype(F32))  19.6 us
    convert_element_type x5, other arithmetic, shards(): made[1].astype(F16)  7.72 us
  transfers between devices with their start and end apart: 28, of which 12 were waited for; matrix products, arithmetic and copies ran while one was open for 14% of the time, Pallas kernels for 13%

profile of v1, /device:TPU:0, one launch (start us, length us, event | category | flops | bytes accessed | tf_op | source)
XLA Modules:
  0.0 359.7 jit_solution(8641871150450322499)
XLA Ops:
  7.2 1.7 slice.33
  9.0 1.7 slice.35
  10.8 1.8 slice.37
  16.3 1.9 base.1
  19.2 3.0 collective-permute-start
  22.2 4.8 %collective-permute-done = f16[2,72,512]{2,1,0:T(8,128)(2,1)S(1)} collective-permute-done((f16[2,72,512]{2,1,0:T(8,128)(2,1)S(1)}, f16[2,72,512]{2,1,0:T(8,128)(2,1)S(1)}, u32[]{:S(2)}, u32[]{:S(2)}) %collective-permute-start) | collective-permute-done | bytes 147488 | tf_op jit(solution)/shard_map/ppermute | solution.py:242
  27.8 6.6 %all-gather.11.cloned.1.call-done = bf16[8,2,64,512]{3,2,1,0:T(8,128)(2,1)} async-done(((bf16[1,2,64,512]{3,2,1,0:T(8,128)(2,1)}), bf16[8,2,64,512]{3,2,1,0:T(8,128)(2,1)}) %all-gather.11.cloned.1.call-update) | async-done | bytes 1048592 | tf_op jit(solution)/shard_map/all_gather | solution.py:248
  34.4 3.9 %cross1.1 = (f32[1,2,64,512]{3,2,1,0:T(8,128)}, f32[8,72,128]{2,1,0:T(8,128)}, f32[2,72,512]{2,1,0:T(8,128)}) custom-call(s32[2]{0:T(128)} %pad_add_fusion.place.refs_0_, s32[5,8]{1,0:T(8,128)} %refs_1_.18, s32[6,8]{1,0:T(8,128)} %refs_1_.19, bf16[8,1,2,64,512]{4,3,2,1,0:T(8,128)(2,1)} %bitcast.39, f32[2,72,512]{2,1,0:T(8,128)} %get-tuple-element.26.refs_4_, ...), custom_call_target="tpu_custom_call" | custom-call | tf_op jit(solution)/shard_map/cross1/pallas_call | solution.py:280
  39.4 14.1 %all_to_all.25 = f16[8,72,128]{2,1,0:T(8,128)(2,1)S(1)} all-to-all(f16[8,72,128]{2,1,0:T(8,128)(2,1)S(1)} %convert_element_type.125), channel_id=1, replica_groups=mesh['row'=4,'col'=8] {'col'}, dimensions={0} | all-to-all | bytes 294912 | tf_op jit(solution)/shard_map/all_to_all | solution.py:291
  54.2 3.6 marginal1.1
  58.9 1.6 collective-permute-start.3
  60.5 1.5 collective-permute-start.1
  62.5 11.1 %collective-permute-done.1 = f16[2,72,512]{2,1,0:T(8,128)(2,1)S(1)} collective-permute-done((f16[2,72,512]{2,1,0:T(8,128)(2,1)S(1)}, f16[2,72,512]{2,1,0:T(8,128)(2,1)S(1)}, u32[]{:S(2)}, u32[]{:S(2)}) %collective-permute-start.1) | collective-permute-done | bytes 147488 | tf_op jit(solution)/shard_map/ppermute | solution.py:242
  76.0 5.3 %cross2.1 = (f32[2,2,64,512]{3,2,1,0:T(8,128)}, f32[8,136,128]{2,1,0:T(8,128)}, f32[2,136,512]{2,1,0:T(8,128)}) custom-call(s32[2]{0:T(128)} %pad_add_fusion.place.refs_0_, s32[5,8]{1,0:T(8,128)} %refs_1_.18, s32[6,8]{1,0:T(8,128)} %refs_1_.19, bf16[8,2,2,64,512]{4,3,2,1,0:T(8,128)(2,1)} %bitcast.37, f32[2,72,512]{2,1,0:T(8,128)} %get-tuple-element.26.refs_4_, ...), custom_call_target="tpu_custom_call" | custom-call | tf_op jit(solution)/shard_map/cross2/pallas_call | solution.py:280
  82.3 22.3 %all_to_all.26 = f16[8,136,128]{2,1,0:T(8,128)(2,1)S(1)} all-to-all(f16[8,136,128]{2,1,0:T(8,128)(2,1)S(1)} %convert_element_type.134), channel_id=1, replica_groups=mesh['row'=4,'col'=8] {'col'}, dimensions={0} | all-to-all | bytes 557056 | tf_op jit(solution)/shard_map/all_to_all | solution.py:291
  105.5 4.2 %marginal2.1 = (f32[2,64,512]{2,1,0:T(8,128)}, f32[2,200,512]{2,1,0:T(8,128)}) custom-call(s32[2]{0:T(128)} %pad_add_fusion.place.refs_0_, s32[6,8]{1,0:T(8,128)} %refs_1_.19, bf16[8,2,2,64,512]{4,3,2,1,0:T(8,128)(2,1)} %bitcast.38, f32[8,136,128]{2,1,0:T(8,128)} %convert_element_type.135.refs_3_, f32[2,64,512]{2,1,0:T(8,128)} %get-tuple-element.52.refs_4_), custom_call_target="tpu_custom_call" | custom-call | tf_op jit(solution)/shard_map/marginal2/pallas_call | solution.py:295
  111.0 1.4 collective-permute-start.6
  112.4 2.1 collective-permute-start.7
  116.1 16.3 %collective-permute-done.4 = f16[2,72,512]{2,1,0:T(8,128)(2,1)S(1)} collective-permute-done((f16[2,72,512]{2,1,0:T(8,128)(2,1)S(1)}, f16[2,72,512]{2,1,0:T(8,128)(2,1)S(1)}, u32[]{:S(2)}, u32[]{:S(2)}) %collective-permute-start.4) | collective-permute-done | bytes 147488 | tf_op jit(solution)/shard_map/ppermute | solution.py:242
  133.1 4.5 %collective-permute-done.5 = f16[2,72,512]{2,1,0:T(8,128)(2,1)S(1)} collective-permute-done((f16[2,72,512]{2,1,0:T(8,128)(2,1)S(1)}, f16[2,72,512]{2,1,0:T(8,128)(2,1)S(1)}, u32[]{:S(2)}, u32[]{:S(2)}) %collective-permute-start.5) | collective-permute-done | bytes 147488 | tf_op jit(solution)/shard_map/ppermute | solution.py:242
  141.1 7.2 %cross3.1 = (f32[3,2,64,512]{3,2,1,0:T(8,128)}, f32[8,200,128]{2,1,0:T(8,128)}, f32[2,200,512]{2,1,0:T(8,128)}) custom-call(s32[2]{0:T(128)} %pad_add_fusion.place.refs_0_, s32[5,8]{1,0:T(8,128)} %refs_1_.18, s32[6,8]{1,0:T(8,128)} %refs_1_.19, bf16[8,3,2,64,512]{4,3,2,1,0:T(8,128)(2,1)} %bitcast.35, f32[2,72,512]{2,1,0:T(8,128)} %get-tuple-element.26.refs_4_, ...), custom_call_target="tpu_custom_call" | custom-call | tf_op jit(solution)/shard_map/cross3/pallas_call | solution.py:280
  149.5 18.8 %all_to_all.27 = f16[8,200,128]{2,1,0:T(8,128)(2,1)S(1)} all-to-all(f16[8,200,128]{2,1,0:T(8,128)(2,1)S(1)} %convert_element_type.144), channel_id=1, replica_groups=mesh['row'=4,'col'=8] {'col'}, dimensions={0} | all-to-all | bytes 819200 | tf_op jit(solution)/shard_map/all_to_all | solution.py:291
  169.2 4.6 %marginal3.1 = (f32[2,64,512]{2,1,0:T(8,128)}, f32[2,264,512]{2,1,0:T(8,128)}) custom-call(s32[2]{0:T(128)} %pad_add_fusion.place.refs_0_, s32[6,8]{1,0:T(8,128)} %refs_1_.19, bf16[8,3,2,64,512]{4,3,2,1,0:T(8,128)(2,1)} %bitcast.36, f32[8,200,128]{2,1,0:T(8,128)} %convert_element_type.145.refs_3_, f32[2,64,512]{2,1,0:T(8,128)} %get-tuple-element.51.refs_4_), custom_call_target="tpu_custom_call" | custom-call | tf_op jit(solution)/shard_map/marginal3/pallas_call | solution.py:295
  173.8 1.4 convert_element_type.146
  175.2 1.5 collective-permute-start.14
  176.7 1.5 collective-permute-start.9
  178.2 1.5 collective-permute-start.12
  179.8 2.9 collective-permute-start.10
  182.7 11.8 %collective-permute-done.9 = f16[2,72,512]{2,1,0:T(8,128)(2,1)S(1)} collective-permute-done((f16[2,72,512]{2,1,0:T(8,128)(2,1)S(1)}, f16[2,72,512]{2,1,0:T(8,128)(2,1)S(1)}, u32[]{:S(2)}, u32[]{:S(2)}) %collective-permute-start.9) | collective-permute-done | bytes 147488 | tf_op jit(solution)/shard_map/ppermute | solution.py:242
  195.9 12.4 %collective-permute-done.10 = f16[2,136,512]{2,1,0:T(8,128)(2,1)S(1)} collective-permute-done((f16[2,136,512]{2,1,0:T(8,128)(2,1)S(1)}, f16[2,136,512]{2,1,0:T(8,128)(2,1)S(1)}, u32[]{:S(2)}, u32[]{:S(2)}) %collective-permute-start.10) | collective-permute-done | bytes 278560 | tf_op jit(solution)/shard_map/ppermute | solution.py:242
  209.2 4.6 %collective-permute-done.11 = f16[2,136,512]{2,1,0:T(8,128)(2,1)S(1)} collective-permute-done((f16[2,136,512]{2,1,0:T(8,128)(2,1)S(1)}, f16[2,136,512]{2,1,0:T(8,128)(2,1)S(1)}, u32[]{:S(2)}, u32[]{:S(2)}) %collective-permute-start.11) | collective-permute-done | bytes 278560 | tf_op jit(solution)/shard_map/ppermute | solution.py:242
  218.0 9.4 %cross4.1 = (f32[4,2,64,512]{3,2,1,0:T(8,128)}, f32[8,264,128]{2,1,0:T(8,128)}, f32[2,264,512]{2,1,0:T(8,128)}) custom-call(s32[2]{0:T(128)} %pad_add_fusion.place.refs_0_, s32[5,8]{1,0:T(8,128)} %refs_1_.18, s32[6,8]{1,0:T(8,128)} %refs_1_.19, bf16[8,4,2,64,512]{4,3,2,1,0:T(8,128)(2,1)} %bitcast.33, f32[2,72,512]{2,1,0:T(8,128)} %get-tuple-element.26.refs_4_, ...), custom_call_target="tpu_custom_call" | custom-call | tf_op jit(solution)/shard_map/cross4/pallas_call | solution.py:280
  227.3 2.1 convert_element_type.154
  229.4 3.5 all-to-all-start.3
  233.1 15.6 %all-to-all-done.3 = f16[8,264,128]{2,1,0:T(8,128)(2,1)S(1)} async-done(((f16[8,264,128]{2,1,0:T(8,128)(2,1)}), f16[8,264,128]{2,1,0:T(8,128)(2,1)S(1)}, u32[]{:S(2)}, u32[]{:S(2)}) %all-to-all-start.3) | async-done | bytes 540704 | tf_op jit(solution)/shard_map/all_to_all | solution.py:291
  249.7 5.2 %marginal4.1 = (f32[2,64,512]{2,1,0:T(8,128)}, f32[2,328,512]{2,1,0:T(8,128)}) custom-call(s32[2]{0:T(128)} %pad_add_fusion.place.refs_0_, s32[6,8]{1,0:T(8,128)} %refs_1_.19, bf16[8,4,2,64,512]{4,3,2,1,0:T(8,128)(2,1)} %bitcast.34, f32[8,264,128]{2,1,0:T(8,128)} %convert_element_type.155.refs_3_, f32[2,64,512]{2,1,0:T(8,128)} %get-tuple-element.55.refs_4_), custom_call_target="tpu_custom_call" | custom-call | tf_op jit(solution)/shard_map/marginal4/pallas_call | solution.py:295
  254.9 1.6 convert_element_type.156
  256.5 2.9 collective-permute-start.16
  259.4 1.6 collective-permute-start.17
  265.1 19.3 %collective-permute-done.16 = f16[2,200,512]{2,1,0:T(8,128)(2,1)S(1)} collective-permute-done((f16[2,200,512]{2,1,0:T(8,128)(2,1)S(1)}, f16[2,200,512]{2,1,0:T(8,128)(2,1)S(1)}, u32[]{:S(2)}, u32[]{:S(2)}) %collective-permute-start.16) | collective-permute-done | bytes 409632 | tf_op jit(solution)/shard_map/ppermute | solution.py:242
  286.4 19.6 %collective-permute-done.18 = f16[2,264,512]{2,1,0:T(8,128)(2,1)S(1)} collective-permute-done((f16[2,264,512]{2,1,0:T(8,128)(2,1)S(1)}, f16[2,264,512]{2,1,0:T(8,128)(2,1)S(1)}, u32[]{:S(2)}, u32[]{:S(2)}) %collective-permute-start.18) | collective-permute-done | bytes 540704 | tf_op jit(solution)/shard_map/ppermute | solution.py:242
  308.3 1.3 convert_element_type.157.refs_33_
  309.5 11.4 %cross5.1 = (f32[5,2,64,512]{3,2,1,0:T(8,128)}, f32[8,328,128]{2,1,0:T(8,128)}) custom-call(s32[2]{0:T(128)} %pad_add_fusion.place.refs_0_, s32[5,8]{1,0:T(8,128)} %refs_1_.18, s32[6,8]{1,0:T(8,128)} %refs_1_.19, bf16[8,5,2,64,512]{4,3,2,1,0:T(8,128)(2,1)} %bitcast.31, f32[2,72,512]{2,1,0:T(8,128)} %get-tuple-element.26.refs_4_, ...), custom_call_target="tpu_custom_call" | custom-call | tf_op jit(solution)/shard_map/cross5/pallas_call | solution.py:280
  321.0 2.3 convert_element_type.158
  323.3 3.7 %all-to-all-start.4 = ((f16[8,328,128]{2,1,0:T(8,128)(2,1)}), f16[8,328,128]{2,1,0:T(8,128)(2,1)S(1)}, u32[]{:S(2)}, u32[]{:S(2)}) async-start(f16[8,328,128]{2,1,0:T(8,128)(2,1)} %convert_element_type.158), calls=%async_computation.4 | async-start | bytes 1343488 | tf_op jit(solution)/shard_map/all_to_all | solution.py:291
  333.2 12.2 %all-to-all-done.4 = f16[8,328,128]{2,1,0:T(8,128)(2,1)S(1)} async-done(((f16[8,328,128]{2,1,0:T(8,128)(2,1)}), f16[8,328,128]{2,1,0:T(8,128)(2,1)S(1)}, u32[]{:S(2)}, u32[]{:S(2)}) %all-to-all-start.4) | async-done | bytes 671776 | tf_op jit(solution)/shard_map/all_to_all | solution.py:291
  346.6 4.9 %marginal5.1 = f32[2,64,512]{2,1,0:T(8,128)} custom-call(s32[2]{0:T(128)} %pad_add_fusion.place.refs_0_, s32[6,8]{1,0:T(8,128)} %refs_1_.19, bf16[8,5,2,64,512]{4,3,2,1,0:T(8,128)(2,1)} %bitcast.32, f32[8,328,128]{2,1,0:T(8,128)} %convert_element_type.159.refs_3_, f32[2,64,512]{2,1,0:T(8,128)} %get-tuple-element.50.refs_4_), custom_call_target="tpu_custom_call" | custom-call | tf_op jit(solution)/shard_map/marginal5/pallas_call | solution.py:295
  351.5 1.7 bitcast_dynamic-update-slice_fusion
  (117 shorter events, 45.9 us)
Async XLA Ops:
  7.2 5.5 %copy-start.4 = (bf16[15,2,64,512]{3,2,1,0:T(8,128)(2,1)S(1)}, bf16[15,2,64,512]{3,2,1,0:T(8,128)(2,1)}, u32[]{:S(2)}) copy-start(bf16[15,2,64,512]{3,2,1,0:T(8,128)(2,1)} %param.4) | copy-start | bytes 5898244
  7.2 27.3 %all-gather.11.cloned.1.call-start = ((), (), s32[]{:S(2)}) async-start(), calls=%async_computation.5 | async-start | bytes 1179648 | tf_op jit(solution)/shard_map/all_gather | solution.py:248
  8.9 67.0 %all-gather.13.cloned.1.call-start = ((), (), s32[]{:S(2)}) async-start(), calls=%async_computation.6 | async-start | bytes 2359296 | tf_op jit(solution)/shard_map/all_gather | solution.py:248
  10.7 130.4 %all-gather.15.cloned.1.call-start = ((), (), s32[]{:S(2)}) async-start(), calls=%async_computation.7 | async-start | bytes 3538944 | tf_op jit(solution)/shard_map/all_gather | solution.py:248
  12.6 2.6 copy-start.5
  12.6 205.4 %all-gather.17.cloned.1.call-start = ((), (), s32[]{:S(2)}) async-start(), calls=%async_computation.8 | async-start | bytes 4718592 | tf_op jit(solution)/shard_map/all_gather | solution.py:248
  13.5 296.0 %all-gather.19.cloned.1.call-start = ((), (), s32[]{:S(2)}) async-start(), calls=%async_computation.9 | async-start | bytes 5898240 | tf_op jit(solution)/shard_map/all_gather | solution.py:248
  19.2 7.8 %collective-permute-start = (f16[2,72,512]{2,1,0:T(8,128)(2,1)S(1)}, f16[2,72,512]{2,1,0:T(8,128)(2,1)S(1)}, u32[]{:S(2)}, u32[]{:S(2)}) collective-permute-start(f16[2,72,512]{2,1,0:T(8,128)(2,1)S(1)} %convert_element_type.120), channel_id=1, source_target_pairs={{0,8},{8,16},{16,24},{24,0},{1,9},{9,17},{17,25},{25,1},{2,10},{10... | collective-permute-start | bytes 442376 | tf_op jit(solution)/shard_map/ppermute | solution.py:242
  39.3 22.6 %copy-start.1 = (f32[2,72,512]{2,1,0:T(8,128)S(1)}, f32[2,72,512]{2,1,0:T(8,128)}, u32[]{:S(2)}) copy-start(f32[2,72,512]{2,1,0:T(8,128)} %get-tuple-element.28.refs_7_.refs_8_) | copy-start | bytes 884740
  58.9 16.2 %collective-permute-start.3 = (f16[2,136,512]{2,1,0:T(8,128)(2,1)S(1)}, f16[2,136,512]{2,1,0:T(8,128)(2,1)S(1)}, u32[]{:S(2)}, u32[]{:S(2)}) collective-permute-start(f16[2,136,512]{2,1,0:T(8,128)(2,1)S(1)} %convert_element_type.127), channel_id=1, source_target_pairs={{0,8},{8,16},{16,24},{24,0},{1,9},{9,17},{17,25},{25,1},{2,10},{10... | collective-permute-start | bytes 835592 | tf_op jit(solution)/shard_map/ppermute | solution.py:242
  60.5 13.1 %collective-permute-start.1 = (f16[2,72,512]{2,1,0:T(8,128)(2,1)S(1)}, f16[2,72,512]{2,1,0:T(8,128)(2,1)S(1)}, u32[]{:S(2)}, u32[]{:S(2)}) collective-permute-start(f16[2,72,512]{2,1,0:T(8,128)(2,1)S(1)} %convert_element_type.120), channel_id=1, source_target_pairs={{0,16},{8,24},{16,0},{24,8},{1,17},{9,25},{17,1},{25,9},{2,18},{10... | collective-permute-start | bytes 442376 | tf_op jit(solution)/shard_map/ppermute | solution.py:242
  62.0 12.4 %collective-permute-start.2 = (f16[2,72,512]{2,1,0:T(8,128)(2,1)S(1)}, f16[2,72,512]{2,1,0:T(8,128)(2,1)S(1)}, u32[]{:S(2)}, u32[]{:S(2)}) collective-permute-start(f16[2,72,512]{2,1,0:T(8,128)(2,1)S(1)} %convert_element_type.123), channel_id=1, source_target_pairs={{0,8},{8,16},{16,24},{24,0},{1,9},{9,17},{17,25},{25,1},{2,10},{10... | collective-permute-start | bytes 442376 | tf_op jit(solution)/shard_map/ppermute | solution.py:242
  105.5 6.9 %copy-start = (f32[2,136,512]{2,1,0:T(8,128)S(1)}, f32[2,136,512]{2,1,0:T(8,128)}, u32[]{:S(2)}) copy-start(f32[2,136,512]{2,1,0:T(8,128)} %get-tuple-element.32.refs_14_.refs_16_) | copy-start | bytes 1671172
  110.9 29.2 %collective-permute-start.8 = (f16[2,200,512]{2,1,0:T(8,128)(2,1)S(1)}, f16[2,200,512]{2,1,0:T(8,128)(2,1)S(1)}, u32[]{:S(2)}, u32[]{:S(2)}) collective-permute-start(f16[2,200,512]{2,1,0:T(8,128)(2,1)S(1)} %convert_element_type.136), channel_id=1, source_target_pairs={{0,8},{8,16},{16,24},{24,0},{1,9},{9,17},{17,25},{25,1},{2,10},{10... | collective-permute-start | bytes 1228808 | tf_op jit(solution)/shard_map/ppermute | solution.py:242
  111.0 27.4 %collective-permute-start.6 = (f16[2,136,512]{2,1,0:T(8,128)(2,1)S(1)}, f16[2,136,512]{2,1,0:T(8,128)(2,1)S(1)}, u32[]{:S(2)}, u32[]{:S(2)}) collective-permute-start(f16[2,136,512]{2,1,0:T(8,128)(2,1)S(1)} %convert_element_type.127), channel_id=1, source_target_pairs={{0,16},{8,24},{16,0},{24,8},{1,17},{9,25},{17,1},{25,9},{2,18},{10... | collective-permute-start | bytes 835592 | tf_op jit(solution)/shard_map/ppermute | solution.py:242
  112.4 26.8 %collective-permute-start.7 = (f16[2,136,512]{2,1,0:T(8,128)(2,1)S(1)}, f16[2,136,512]{2,1,0:T(8,128)(2,1)S(1)}, u32[]{:S(2)}, u32[]{:S(2)}) collective-permute-start(f16[2,136,512]{2,1,0:T(8,128)(2,1)S(1)} %convert_element_type.132), channel_id=1, source_target_pairs={{0,8},{8,16},{16,24},{24,0},{1,9},{9,17},{17,25},{25,1},{2,10},{10... | collective-permute-start | bytes 835592 | tf_op jit(solution)/shard_map/ppermute | solution.py:242
  114.5 17.8 %collective-permute-start.4 = (f16[2,72,512]{2,1,0:T(8,128)(2,1)S(1)}, f16[2,72,512]{2,1,0:T(8,128)(2,1)S(1)}, u32[]{:S(2)}, u32[]{:S(2)}) collective-permute-start(f16[2,72,512]{2,1,0:T(8,128)(2,1)S(1)} %convert_element_type.120), channel_id=1, source_target_pairs={{0,24},{8,0},{16,8},{24,16},{1,25},{9,1},{17,9},{25,17},{2,26},{10... | collective-permute-start | bytes 442376 | tf_op jit(solution)/shard_map/ppermute | solution.py:242
  115.4 22.2 %collective-permute-start.5 = (f16[2,72,512]{2,1,0:T(8,128)(2,1)S(1)}, f16[2,72,512]{2,1,0:T(8,128)(2,1)S(1)}, u32[]{:S(2)}, u32[]{:S(2)}) collective-permute-start(f16[2,72,512]{2,1,0:T(8,128)(2,1)S(1)} %convert_element_type.123), channel_id=1, source_target_pairs={{0,16},{8,24},{16,0},{24,8},{1,17},{9,25},{17,1},{25,9},{2,18},{10... | collective-permute-start | bytes 442376 | tf_op jit(solution)/shard_map/ppermute | solution.py:242
  173.8 5.9 %copy-start.2 = (f32[2,200,512]{2,1,0:T(8,128)S(1)}, f32[2,200,512]{2,1,0:T(8,128)}, u32[]{:S(2)}) copy-start(f32[2,200,512]{2,1,0:T(8,128)} %get-tuple-element.36.refs_22_.refs_24_) | copy-start | bytes 2457604
  175.2 41.6 %collective-permute-start.14 = (f16[2,264,512]{2,1,0:T(8,128)(2,1)S(1)}, f16[2,264,512]{2,1,0:T(8,128)(2,1)S(1)}, u32[]{:S(2)}, u32[]{:S(2)}) collective-permute-start(f16[2,264,512]{2,1,0:T(8,128)(2,1)S(1)} %convert_element_type.146), channel_id=1, source_target_pairs={{0,8},{8,16},{16,24},{24,0},{1,9},{9,17},{17,25},{25,1},{2,10},{10... | collective-permute-start | bytes 1622024 | tf_op jit(solution)/shard_map/ppermute | solution.py:242
  176.7 17.9 %collective-permute-start.9 = (f16[2,72,512]{2,1,0:T(8,128)(2,1)S(1)}, f16[2,72,512]{2,1,0:T(8,128)(2,1)S(1)}, u32[]{:S(2)}, u32[]{:S(2)}) collective-permute-start(f16[2,72,512]{2,1,0:T(8,128)(2,1)S(1)} %convert_element_type.123), channel_id=1, source_target_pairs={{0,24},{8,0},{16,8},{24,16},{1,25},{9,1},{17,9},{25,17},{2,26},{10... | collective-permute-start | bytes 442376 | tf_op jit(solution)/shard_map/ppermute | solution.py:242
  178.2 36.5 %collective-permute-start.12 = (f16[2,200,512]{2,1,0:T(8,128)(2,1)S(1)}, f16[2,200,512]{2,1,0:T(8,128)(2,1)S(1)}, u32[]{:S(2)}, u32[]{:S(2)}) collective-permute-start(f16[2,200,512]{2,1,0:T(8,128)(2,1)S(1)} %convert_element_type.136), channel_id=1, source_target_pairs={{0,16},{8,24},{16,0},{24,8},{1,17},{9,25},{17,1},{25,9},{2,18},{10... | collective-permute-start | bytes 1228808 | tf_op jit(solution)/shard_map/ppermute | solution.py:242
  179.8 36.0 %collective-permute-start.13 = (f16[2,200,512]{2,1,0:T(8,128)(2,1)S(1)}, f16[2,200,512]{2,1,0:T(8,128)(2,1)S(1)}, u32[]{:S(2)}, u32[]{:S(2)}) collective-permute-start(f16[2,200,512]{2,1,0:T(8,128)(2,1)S(1)} %convert_element_type.142), channel_id=1, source_target_pairs={{0,8},{8,16},{16,24},{24,0},{1,9},{9,17},{17,25},{25,1},{2,10},{10... | collective-permute-start | bytes 1228808 | tf_op jit(solution)/shard_map/ppermute | solution.py:242
  179.8 28.5 %collective-permute-start.10 = (f16[2,136,512]{2,1,0:T(8,128)(2,1)S(1)}, f16[2,136,512]{2,1,0:T(8,128)(2,1)S(1)}, u32[]{:S(2)}, u32[]{:S(2)}) collective-permute-start(f16[2,136,512]{2,1,0:T(8,128)(2,1)S(1)} %convert_element_type.127), channel_id=1, source_target_pairs={{0,24},{8,0},{16,8},{24,16},{1,25},{9,1},{17,9},{25,17},{2,26},{10... | collective-permute-start | bytes 835592 | tf_op jit(solution)/shard_map/ppermute | solution.py:242
  194.6 19.3 %collective-permute-start.11 = (f16[2,136,512]{2,1,0:T(8,128)(2,1)S(1)}, f16[2,136,512]{2,1,0:T(8,128)(2,1)S(1)}, u32[]{:S(2)}, u32[]{:S(2)}) collective-permute-start(f16[2,136,512]{2,1,0:T(8,128)(2,1)S(1)} %convert_element_type.132), channel_id=1, source_target_pairs={{0,16},{8,24},{16,0},{24,8},{1,17},{9,25},{17,1},{25,9},{2,18},{10... | collective-permute-start | bytes 835592 | tf_op jit(solution)/shard_map/ppermute | solution.py:242
  229.4 19.2 %all-to-all-start.3 = ((f16[8,264,128]{2,1,0:T(8,128)(2,1)}), f16[8,264,128]{2,1,0:T(8,128)(2,1)S(1)}, u32[]{:S(2)}, u32[]{:S(2)}) async-start(f16[8,264,128]{2,1,0:T(8,128)(2,1)} %convert_element_type.154), calls=%async_computation.3 | async-start | bytes 1081344 | tf_op jit(solution)/shard_map/all_to_all | solution.py:291
  233.0 28.6 %collective-permute-start.15 = (f16[2,136,512]{2,1,0:T(8,128)(2,1)S(1)}, f16[2,136,512]{2,1,0:T(8,128)(2,1)S(1)}, u32[]{:S(2)}, u32[]{:S(2)}) collective-permute-start(f16[2,136,512]{2,1,0:T(8,128)(2,1)S(1)} %convert_element_type.132), channel_id=1, source_target_pairs={{0,24},{8,0},{16,8},{24,16},{1,25},{9,1},{17,9},{25,17},{2,26},{10... | collective-permute-start | bytes 835592 | tf_op jit(solution)/shard_map/ppermute | solution.py:242
  254.9 6.6 %copy-start.3 = (f32[2,264,512]{2,1,0:T(8,128)S(1)}, f32[2,264,512]{2,1,0:T(8,128)}, u32[]{:S(2)}) copy-start(f32[2,264,512]{2,1,0:T(8,128)} %get-tuple-element.40.refs_30_) | copy-start | bytes 3244036
  254.9 7.1 %copy-start.11 = (f32[2,64,512]{2,1,0:T(8,128)S(1)}, f32[2,64,512]{2,1,0:T(8,128)}, u32[]{:S(2)}) copy-start(f32[2,64,512]{2,1,0:T(8,128)} %get-tuple-element.44) | copy-start | bytes 786436
  256.4 6.3 %copy-start.12 = (f32[1,2,64,512]{3,2,1,0:T(8,128)S(1)}, f32[1,2,64,512]{3,2,1,0:T(8,128)}, u32[]{:S(2)}) copy-start(f32[1,2,64,512]{3,2,1,0:T(8,128)} %get-tuple-element.27) | copy-start | bytes 786436
  256.4 7.0 %copy-start.13 = (f32[2,64,512]{2,1,0:T(8,128)S(1)}, f32[2,64,512]{2,1,0:T(8,128)}, u32[]{:S(2)}) copy-start(f32[2,64,512]{2,1,0:T(8,128)} %get-tuple-element.45) | copy-start | bytes 786436
  256.5 51.8 %collective-permute-start.20 = (f16[2,328,512]{2,1,0:T(8,128)(2,1)S(1)}, f16[2,328,512]{2,1,0:T(8,128)(2,1)S(1)}, u32[]{:S(2)}, u32[]{:S(2)}) collective-permute-start(f16[2,328,512]{2,1,0:T(8,128)(2,1)S(1)} %convert_element_type.156), channel_id=1, source_target_pairs={{0,8},{8,16},{16,24},{24,0},{1,9},{9,17},{17,25},{25,1},{2,10},{10... | collective-permute-start | bytes 2015240 | tf_op jit(solution)/shard_map/ppermute | solution.py:242
  256.5 27.9 %collective-permute-start.16 = (f16[2,200,512]{2,1,0:T(8,128)(2,1)S(1)}, f16[2,200,512]{2,1,0:T(8,128)(2,1)S(1)}, u32[]{:S(2)}, u32[]{:S(2)}) collective-permute-start(f16[2,200,512]{2,1,0:T(8,128)(2,1)S(1)} %convert_element_type.136), channel_id=1, source_target_pairs={{0,24},{8,0},{16,8},{24,16},{1,25},{9,1},{17,9},{25,17},{2,26},{10... | collective-permute-start | bytes 1228808 | tf_op jit(solution)/shard_map/ppermute | solution.py:242
  259.4 26.0 %collective-permute-start.17 = (f16[2,200,512]{2,1,0:T(8,128)(2,1)S(1)}, f16[2,200,512]{2,1,0:T(8,128)(2,1)S(1)}, u32[]{:S(2)}, u32[]{:S(2)}) collective-permute-start(f16[2,200,512]{2,1,0:T(8,128)(2,1)S(1)} %convert_element_type.142), channel_id=1, source_target_pairs={{0,16},{8,24},{16,0},{24,8},{1,17},{9,25},{17,1},{25,9},{2,18},{10... | collective-permute-start | bytes 1228808 | tf_op jit(solution)/shard_map/ppermute | solution.py:242
  261.0 44.9 %collective-permute-start.18 = (f16[2,264,512]{2,1,0:T(8,128)(2,1)S(1)}, f16[2,264,512]{2,1,0:T(8,128)(2,1)S(1)}, u32[]{:S(2)}, u32[]{:S(2)}) collective-permute-start(f16[2,264,512]{2,1,0:T(8,128)(2,1)S(1)} %convert_element_type.146), channel_id=1, source_target_pairs={{0,16},{8,24},{16,0},{24,8},{1,17},{9,25},{17,1},{25,9},{2,18},{10... | collective-permute-start | bytes 1622024 | tf_op jit(solution)/shard_map/ppermute | solution.py:242
  261.6 45.5 %collective-permute-start.19 = (f16[2,264,512]{2,1,0:T(8,128)(2,1)S(1)}, f16[2,264,512]{2,1,0:T(8,128)(2,1)S(1)}, u32[]{:S(2)}, u32[]{:S(2)}) collective-permute-start(f16[2,264,512]{2,1,0:T(8,128)(2,1)S(1)} %convert_element_type.152), channel_id=1, source_target_pairs={{0,8},{8,16},{16,24},{24,0},{1,9},{9,17},{17,25},{25,1},{2,10},{10... | collective-permute-start | bytes 1622024 | tf_op jit(solution)/shard_map/ppermute | solution.py:242
  321.0 6.0 %copy-start.9 = (f32[2,2,64,512]{3,2,1,0:T(8,128)S(1)}, f32[2,2,64,512]{3,2,1,0:T(8,128)}, u32[]{:S(2)}) copy-start(f32[2,2,64,512]{3,2,1,0:T(8,128)} %get-tuple-element.31) | copy-start | bytes 1572868
  323.3 4.5 %copy-start.10 = (f32[2,64,512]{2,1,0:T(8,128)S(1)}, f32[2,64,512]{2,1,0:T(8,128)}, u32[]{:S(2)}) copy-start(f32[2,64,512]{2,1,0:T(8,128)} %get-tuple-element.46) | copy-start | bytes 786436
  323.3 5.3 %copy-start.8 = (f32[3,2,64,512]{3,2,1,0:T(8,128)S(1)}, f32[3,2,64,512]{3,2,1,0:T(8,128)}, u32[]{:S(2)}) copy-start(f32[3,2,64,512]{3,2,1,0:T(8,128)} %get-tuple-element.35) | copy-start | bytes 2359300
  323.3 22.1 %all-to-all-start.4 = ((f16[8,328,128]{2,1,0:T(8,128)(2,1)}), f16[8,328,128]{2,1,0:T(8,128)(2,1)S(1)}, u32[]{:S(2)}, u32[]{:S(2)}) async-start(f16[8,328,128]{2,1,0:T(8,128)(2,1)} %convert_element_type.158), calls=%async_computation.4 | async-start | bytes 1343488 | tf_op jit(solution)/shard_map/all_to_all | solution.py:291
  327.0 2.5 copy-start.14
  327.8 2.4 copy-start.7
  329.5 1.8 copy-start.15
  329.5 2.5 copy-start.6
Sparse Core Ops, SparseCore 0:
  9.6 24.7 all-gather.10
  36.0 32.1 all-gather.12
  69.8 43.1 all-gather.14
  115.1 48.9 all-gather.16
  165.6 60.4 all-gather.18

commit v2 on v1

--- a/solution.py
+++ b/solution.py
@@ -167,8 +167,9 @@
 def marginal_kernel(level, last, n_row, npr, rows, width, *refs):
     place, sizes, panel, turned, diag = refs[:5]
     n_out = 1 if last else 2
-    outs = refs[5 : 5 + n_out]
-    lower, panel_sem = refs[5 + n_out :]
+    at = 5
+    outs = refs[at : at + n_out]
+    lower, panel_sem = refs[at + n_out :]
     marginal = outs[0]
     message = None if last else outs[1]
     row, col = place[0], place[1]
@@ -234,12 +235,18 @@
     def reach(level):
         return min(levels - 1 - level, n_row - 1)
 
-    def spread(message, level):
+    due = [[] for _ in range(levels)]
+
+    def spread(message, level, at_once):
         found = [message]
         half = message.astype(F16)
         for back in range(1, reach(level) + 1):
             route = [(i, (i + back) % n_row) for i in range(n_row)]
-            found.append(lax.ppermute(half, "row", route).astype(F32))
+            got = lax.ppermute(half, "row", route)
+            when = level + back - 1
+            if at_once or back > 1:
+                due[min(when, levels - 1)].append(got)
+            found.append(got.astype(F32))
         return found
 
     whole_panel = []
@@ -257,7 +264,7 @@
     )(place, supernode_sizes, diag_inverse[0])
     crosses = []
     diagonals = [base]
-    table = [[spread(message, 0)]]
+    table = [[spread(message, 0, False)]]
     for level in range(1, levels):
         last = level == levels - 1
         high = level * rows
@@ -287,8 +294,10 @@
             name=f"cross{level}",
         )(place, parents, supernode_sizes, whole, *sources)
         crosses.append(made[0])
-        ahead = None if last else spread(made[2], level)
+        ahead = None if last else spread(made[2], level, True)
         turned = lax.all_to_all(made[1].astype(F16), "col", 0, 0, tiled=True).astype(F32)
+        for got in [] if last else due[level]:
+            turned = jnp.where(got[0, -1, 0] > 0, turned, 0.0)
         out_shape = [shape(npr, rows, width)]
         if not last:
             out_shape.append(shape(npr, high + rows + TAIL, width))
@@ -306,7 +315,7 @@
         )(place, supernode_sizes, whole, turned, diag_inverse[level])
         diagonals.append(done[0])
         if not last:
-            table.append([ahead, spread(done[1], level)])
+            table.append([ahead, spread(done[1], level, False)])
     return (jnp.concatenate(crosses, axis=0), jnp.stack(diagonals))
 
 

time: 361 us -> 326 us (0.903)
  blocking collectives: 55.2 us -> 0 us
  waiting for transfers between devices: 139 us -> 121 us
  starting transfers between devices: 32.6 us -> 47.4 us
  between operations: 14.1 us -> 24.7 us
  local copies, waits for them, and re-layouts: 18.3 us -> 26.6 us
  other arithmetic: 39.1 us -> 42.8 us
    all_to_all x3 -> x0, blocking collectives: 55.2 us -> none  [shards(): lax.all_to_all(made[1].astype(F16), 'col', 0, 0, tiled=True).astype(F32)]
    all_to_all x2 -> x5, waiting for transfers between devices: 27.7 us -> 12.4 us  [shards(): lax.all_to_all(made[1].astype(F16), 'col', 0, 0, tiled=True).astype(F32)]
    all_to_all x2 -> x5, starting transfers between devices: 7.21 us -> 20.3 us  [shards(): lax.all_to_all(made[1].astype(F16), 'col', 0, 0, tiled=True).astype(F32)]
    slice x0 -> x16, local copies, waits for them, and re-layouts: none -> 8.33 us  [shards(): turned = jnp.where(got[0, -1, 0] > 0, turned, 0.0)]
    select_n x0 -> x4, other arithmetic: none -> 3.91 us  [shards(): turned = jnp.where(got[0, -1, 0] > 0, turned, 0.0)]
    unnamed x41 -> x53, local copies, waits for them, and re-layouts: 7.23 us -> 7.25 us
  transfers between devices with their start and end apart: 28 -> 31, of which waited for: 12 -> 15; matrix products, arithmetic and copies ran while one was open for 14% -> 19% of each run, Pallas kernels for 13% -> 14%
where the time goes in v2:
time: 326 us; the launch traced here: 324 us
  waiting for transfers between devices  121 us (37%)
  Pallas kernels  61.7 us (19%)
  starting transfers between devices  47.4 us (15%)
  other arithmetic  42.8 us (13%)
  local copies, waits for them, and re-layouts  26.6 us (8%)
  between operations  24.7 us (8%)
    ppermute x21, waiting for transfers between devices, spread(): got = lax.ppermute(half, 'row', route)  102 us
    pallas_call x5, Pallas kernels, shards(): pl.pallas_call(functools.partial(cross_kernel, level, last, spans, n_row,...  37.4 us
    ppermute x21, starting transfers between devices, spread(): got = lax.ppermute(half, 'row', route)  26.9 us
    pallas_call x5, Pallas kernels, shards(): pl.pallas_call(functools.partial(marginal_kernel, level, last, n_row, npr...  22.4 us
    all_to_all x5, starting transfers between devices, shards(): lax.all_to_all(made[1].astype(F16), 'col', 0, 0, tiled=True).astype(F32)  20.3 us
    convert_element_type x21, other arithmetic, spread(): found.append(got.astype(F32))  19.7 us
    all_to_all x5, waiting for transfers between devices, shards(): lax.all_to_all(made[1].astype(F16), 'col', 0, 0, tiled=True).astype(F32)  12.4 us
    convert_element_type x5, other arithmetic, shards(): made[1].astype(F16)  10.1 us
  transfers between devices with their start and end apart: 31, of which 15 were waited for; matrix products, arithmetic and copies ran while one was open for 19% of the time, Pallas kernels for 14%

profile of v2, /device:TPU:0, one launch (start us, length us, event | category | flops | bytes accessed | tf_op | source)
XLA Modules:
  0.0 324.4 jit_solution(13248989286651640724)
XLA Ops:
  7.2 1.7 slice.81
  9.0 1.7 slice.83
  10.7 1.8 slice.87
  16.3 1.9 base.1
  19.2 3.0 collective-permute-start
  22.2 4.8 %collective-permute-done = f16[2,72,512]{2,1,0:T(8,128)(2,1)S(1)} collective-permute-done((f16[2,72,512]{2,1,0:T(8,128)(2,1)S(1)}, f16[2,72,512]{2,1,0:T(8,128)(2,1)S(1)}, u32[]{:S(2)}, u32[]{:S(2)}) %collective-permute-start) | collective-permute-done | bytes 147488 | tf_op jit(solution)/shard_map/ppermute | solution.py:245
  27.7 6.7 %all-gather.11.cloned.1.call-done = bf16[8,2,64,512]{3,2,1,0:T(8,128)(2,1)} async-done(((bf16[1,2,64,512]{3,2,1,0:T(8,128)(2,1)}), bf16[8,2,64,512]{3,2,1,0:T(8,128)(2,1)}) %all-gather.11.cloned.1.call-update) | async-done | bytes 1048592 | tf_op jit(solution)/shard_map/all_gather | solution.py:255
  34.4 3.9 %cross1.1 = (f32[1,2,64,512]{3,2,1,0:T(8,128)}, f32[8,72,128]{2,1,0:T(8,128)}, f32[2,72,512]{2,1,0:T(8,128)}) custom-call(s32[2]{0:T(128)} %pad_add_fusion.place.refs_0_, s32[5,8]{1,0:T(8,128)} %refs_1_.18, s32[6,8]{1,0:T(8,128)} %refs_1_.19, bf16[8,1,2,64,512]{4,3,2,1,0:T(8,128)(2,1)} %bitcast.55, f32[2,72,512]{2,1,0:T(8,128)} %get-tuple-element.26.refs_4_, ...), custom_call_target="tpu_custom_call" | custom-call | tf_op jit(solution)/shard_map/cross1/pallas_call | solution.py:287
  38.4 1.6 convert_element_type.125
  40.0 3.4 %all-to-all-start = ((f16[8,72,128]{2,1,0:T(8,128)(2,1)}), f16[8,72,128]{2,1,0:T(8,128)(2,1)S(1)}, u32[]{:S(2)}, u32[]{:S(2)}) async-start(f16[8,72,128]{2,1,0:T(8,128)(2,1)} %convert_element_type.125), calls=%async_computation | async-start | bytes 294912 | tf_op jit(solution)/shard_map/all_to_all | solution.py:298
  43.4 1.5 collective-permute-start.1
  47.4 4.3 %collective-permute-done.1 = f16[2,72,512]{2,1,0:T(8,128)(2,1)S(1)} collective-permute-done((f16[2,72,512]{2,1,0:T(8,128)(2,1)S(1)}, f16[2,72,512]{2,1,0:T(8,128)(2,1)S(1)}, u32[]{:S(2)}, u32[]{:S(2)}) %collective-permute-start.1) | collective-permute-done | bytes 147488 | tf_op jit(solution)/shard_map/ppermute | solution.py:245
  54.9 3.6 %marginal1.1 = (f32[2,64,512]{2,1,0:T(8,128)}, f32[2,136,512]{2,1,0:T(8,128)}) custom-call(s32[2]{0:T(128)} %pad_add_fusion.place.refs_0_, s32[6,8]{1,0:T(8,128)} %refs_1_.19, bf16[8,1,2,64,512]{4,3,2,1,0:T(8,128)(2,1)} %bitcast.56, f32[8,72,128]{2,1,0:T(8,128)} %select_select_fusion.3.refs_3_, f32[2,64,512]{2,1,0:T(8,128)} %get-tuple-element.53.refs_4_), custom_call_target="tpu_custom_call" | custom-call | tf_op jit(solution)/shard_map/marginal1/pallas_call | solution.py:304
  62.7 6.5 %collective-permute-done.3 = f16[2,136,512]{2,1,0:T(8,128)(2,1)S(1)} collective-permute-done((f16[2,136,512]{2,1,0:T(8,128)(2,1)S(1)}, f16[2,136,512]{2,1,0:T(8,128)(2,1)S(1)}, u32[]{:S(2)}, u32[]{:S(2)}) %collective-permute-start.3) | collective-permute-done | bytes 278560 | tf_op jit(solution)/shard_map/ppermute | solution.py:245
  70.1 5.3 %cross2.1 = (f32[2,2,64,512]{3,2,1,0:T(8,128)}, f32[8,136,128]{2,1,0:T(8,128)}, f32[2,136,512]{2,1,0:T(8,128)}) custom-call(s32[2]{0:T(128)} %pad_add_fusion.place.refs_0_, s32[5,8]{1,0:T(8,128)} %refs_1_.18, s32[6,8]{1,0:T(8,128)} %refs_1_.19, bf16[8,2,2,64,512]{4,3,2,1,0:T(8,128)(2,1)} %bitcast.53, f32[2,72,512]{2,1,0:T(8,128)} %get-tuple-element.26.refs_4_, ...), custom_call_target="tpu_custom_call" | custom-call | tf_op jit(solution)/shard_map/cross2/pallas_call | solution.py:287
  75.4 1.9 convert_element_type.134
  77.3 3.5 %all-to-all-start.1 = ((f16[8,136,128]{2,1,0:T(8,128)(2,1)}), f16[8,136,128]{2,1,0:T(8,128)(2,1)S(1)}, u32[]{:S(2)}, u32[]{:S(2)}) async-start(f16[8,136,128]{2,1,0:T(8,128)(2,1)} %convert_element_type.134), calls=%async_computation.1 | async-start | bytes 557056 | tf_op jit(solution)/shard_map/all_to_all | solution.py:298
  80.8 3.0 collective-permute-start.6
  83.9 2.9 collective-permute-start.4
  86.8 8.8 %collective-permute-done.4 = f16[2,72,512]{2,1,0:T(8,128)(2,1)S(1)} collective-permute-done((f16[2,72,512]{2,1,0:T(8,128)(2,1)S(1)}, f16[2,72,512]{2,1,0:T(8,128)(2,1)S(1)}, u32[]{:S(2)}, u32[]{:S(2)}) %collective-permute-start.4) | collective-permute-done | bytes 147488 | tf_op jit(solution)/shard_map/ppermute | solution.py:245
  96.8 3.4 %collective-permute-done.5 = f16[2,72,512]{2,1,0:T(8,128)(2,1)S(1)} collective-permute-done((f16[2,72,512]{2,1,0:T(8,128)(2,1)S(1)}, f16[2,72,512]{2,1,0:T(8,128)(2,1)S(1)}, u32[]{:S(2)}, u32[]{:S(2)}) %collective-permute-start.5) | collective-permute-done | bytes 147488 | tf_op jit(solution)/shard_map/ppermute | solution.py:245
  104.7 4.1 %marginal2.1 = (f32[2,64,512]{2,1,0:T(8,128)}, f32[2,200,512]{2,1,0:T(8,128)}) custom-call(s32[2]{0:T(128)} %pad_add_fusion.place.refs_0_, s32[6,8]{1,0:T(8,128)} %refs_1_.19, bf16[8,2,2,64,512]{4,3,2,1,0:T(8,128)(2,1)} %bitcast.54, f32[8,136,128]{2,1,0:T(8,128)} %select_select_fusion.2.refs_3_, f32[2,64,512]{2,1,0:T(8,128)} %get-tuple-element.52.refs_4_), custom_call_target="tpu_custom_call" | custom-call | tf_op jit(solution)/shard_map/marginal2/pallas_call | solution.py:304
  113.3 9.1 %collective-permute-done.8 = f16[2,200,512]{2,1,0:T(8,128)(2,1)S(1)} collective-permute-done((f16[2,200,512]{2,1,0:T(8,128)(2,1)S(1)}, f16[2,200,512]{2,1,0:T(8,128)(2,1)S(1)}, u32[]{:S(2)}, u32[]{:S(2)}) %collective-permute-start.8) | collective-permute-done | bytes 409632 | tf_op jit(solution)/shard_map/ppermute | solution.py:245
  123.4 7.1 %cross3.1 = (f32[3,2,64,512]{3,2,1,0:T(8,128)}, f32[8,200,128]{2,1,0:T(8,128)}, f32[2,200,512]{2,1,0:T(8,128)}) custom-call(s32[2]{0:T(128)} %pad_add_fusion.place.refs_0_, s32[5,8]{1,0:T(8,128)} %refs_1_.18, s32[6,8]{1,0:T(8,128)} %refs_1_.19, bf16[8,3,2,64,512]{4,3,2,1,0:T(8,128)(2,1)} %bitcast.51, f32[2,72,512]{2,1,0:T(8,128)} %get-tuple-element.26.refs_4_, ...), custom_call_target="tpu_custom_call" | custom-call | tf_op jit(solution)/shard_map/cross3/pallas_call | solution.py:287
  130.5 2.0 convert_element_type.144
  132.5 4.5 %all-to-all-start.2 = ((f16[8,200,128]{2,1,0:T(8,128)(2,1)}), f16[8,200,128]{2,1,0:T(8,128)(2,1)S(1)}, u32[]{:S(2)}, u32[]{:S(2)}) async-start(f16[8,200,128]{2,1,0:T(8,128)(2,1)} %convert_element_type.144), calls=%async_computation.2 | async-start | bytes 819200 | tf_op jit(solution)/shard_map/all_to_all | solution.py:298
  138.5 2.9 collective-permute-start.10
  142.1 17.3 %collective-permute-done.9 = f16[2,72,512]{2,1,0:T(8,128)(2,1)S(1)} collective-permute-done((f16[2,72,512]{2,1,0:T(8,128)(2,1)}, f16[2,72,512]{2,1,0:T(8,128)(2,1)S(1)}, u32[]{:S(2)}, u32[]{:S(2)}) %collective-permute-start.9) | collective-permute-done | bytes 147488 | tf_op jit(solution)/shard_map/ppermute | solution.py:245
  161.7 1.9 collective-permute-done.11
  168.2 4.6 %marginal3.1 = (f32[2,64,512]{2,1,0:T(8,128)}, f32[2,264,512]{2,1,0:T(8,128)}) custom-call(s32[2]{0:T(128)} %pad_add_fusion.place.refs_0_, s32[6,8]{1,0:T(8,128)} %refs_1_.19, bf16[8,3,2,64,512]{4,3,2,1,0:T(8,128)(2,1)} %bitcast.52, f32[8,200,128]{2,1,0:T(8,128)} %select_select_fusion.1.refs_3_, f32[2,64,512]{2,1,0:T(8,128)} %get-tuple-element.51.refs_4_), custom_call_target="tpu_custom_call" | custom-call | tf_op jit(solution)/shard_map/marginal3/pallas_call | solution.py:304
  179.1 10.3 %collective-permute-done.14 = f16[2,264,512]{2,1,0:T(8,128)(2,1)S(1)} collective-permute-done((f16[2,264,512]{2,1,0:T(8,128)(2,1)S(1)}, f16[2,264,512]{2,1,0:T(8,128)(2,1)S(1)}, u32[]{:S(2)}, u32[]{:S(2)}) %collective-permute-start.14) | collective-permute-done | bytes 540704 | tf_op jit(solution)/shard_map/ppermute | solution.py:245
  190.5 9.4 %cross4.1 = (f32[4,2,64,512]{3,2,1,0:T(8,128)}, f32[8,264,128]{2,1,0:T(8,128)}, f32[2,264,512]{2,1,0:T(8,128)}) custom-call(s32[2]{0:T(128)} %pad_add_fusion.place.refs_0_, s32[5,8]{1,0:T(8,128)} %refs_1_.18, s32[6,8]{1,0:T(8,128)} %refs_1_.19, bf16[8,4,2,64,512]{4,3,2,1,0:T(8,128)(2,1)} %bitcast.49, f32[2,72,512]{2,1,0:T(8,128)} %get-tuple-element.26.refs_4_, ...), custom_call_target="tpu_custom_call" | custom-call | tf_op jit(solution)/shard_map/cross4/pallas_call | solution.py:287
  199.9 2.2 convert_element_type.154
  202.1 4.4 %all-to-all-start.3 = ((f16[8,264,128]{2,1,0:T(8,128)(2,1)}), f16[8,264,128]{2,1,0:T(8,128)(2,1)S(1)}, u32[]{:S(2)}, u32[]{:S(2)}) async-start(f16[8,264,128]{2,1,0:T(8,128)(2,1)} %convert_element_type.154), calls=%async_computation.3 | async-start | bytes 1081344 | tf_op jit(solution)/shard_map/all_to_all | solution.py:298
  206.5 1.6 collective-permute-start.18
  208.3 2.9 collective-permute-start.16
  211.8 25.5 %collective-permute-done.15 = f16[2,136,512]{2,1,0:T(8,128)(2,1)S(1)} collective-permute-done((f16[2,136,512]{2,1,0:T(8,128)(2,1)S(1)}, f16[2,136,512]{2,1,0:T(8,128)(2,1)S(1)}, u32[]{:S(2)}, u32[]{:S(2)}) %collective-permute-start.15) | collective-permute-done | bytes 278560 | tf_op jit(solution)/shard_map/ppermute | solution.py:245
  239.7 1.8 collective-permute-done.17
  246.4 5.2 %marginal4.1 = (f32[2,64,512]{2,1,0:T(8,128)}, f32[2,328,512]{2,1,0:T(8,128)}) custom-call(s32[2]{0:T(128)} %pad_add_fusion.place.refs_0_, s32[6,8]{1,0:T(8,128)} %refs_1_.19, bf16[8,4,2,64,512]{4,3,2,1,0:T(8,128)(2,1)} %bitcast.50, f32[8,264,128]{2,1,0:T(8,128)} %select_select_fusion.refs_3_, f32[2,64,512]{2,1,0:T(8,128)} %get-tuple-element.55.refs_4_), custom_call_target="tpu_custom_call" | custom-call | tf_op jit(solution)/shard_map/marginal4/pallas_call | solution.py:304
  251.6 1.5 convert_element_type.156
  253.1 2.9 collective-permute-start.20
  263.5 8.2 %collective-permute-done.20 = f16[2,328,512]{2,1,0:T(8,128)(2,1)S(1)} collective-permute-done((f16[2,328,512]{2,1,0:T(8,128)(2,1)S(1)}, f16[2,328,512]{2,1,0:T(8,128)(2,1)S(1)}, u32[]{:S(2)}, u32[]{:S(2)}) %collective-permute-start.20) | collective-permute-done | bytes 671776 | tf_op jit(solution)/shard_map/ppermute | solution.py:245
  273.0 11.7 %cross5.1 = (f32[5,2,64,512]{3,2,1,0:T(8,128)}, f32[8,328,128]{2,1,0:T(8,128)}) custom-call(s32[2]{0:T(128)} %pad_add_fusion.place.refs_0_, s32[5,8]{1,0:T(8,128)} %refs_1_.18, s32[6,8]{1,0:T(8,128)} %refs_1_.19, bf16[8,5,2,64,512]{4,3,2,1,0:T(8,128)(2,1)} %bitcast.47, f32[2,72,512]{2,1,0:T(8,128)} %get-tuple-element.26.refs_4_, ...), custom_call_target="tpu_custom_call" | custom-call | tf_op jit(solution)/shard_map/cross5/pallas_call | solution.py:287
  284.7 2.3 convert_element_type.158
  287.0 4.5 %all-to-all-start.4 = ((f16[8,328,128]{2,1,0:T(8,128)(2,1)}), f16[8,328,128]{2,1,0:T(8,128)(2,1)S(1)}, u32[]{:S(2)}, u32[]{:S(2)}) async-start(f16[8,328,128]{2,1,0:T(8,128)(2,1)} %convert_element_type.158), calls=%async_computation.4 | async-start | bytes 1343488 | tf_op jit(solution)/shard_map/all_to_all | solution.py:298
  297.8 12.3 %all-to-all-done.4 = f16[8,328,128]{2,1,0:T(8,128)(2,1)S(1)} async-done(((f16[8,328,128]{2,1,0:T(8,128)(2,1)}), f16[8,328,128]{2,1,0:T(8,128)(2,1)S(1)}, u32[]{:S(2)}, u32[]{:S(2)}) %all-to-all-start.4) | async-done | bytes 671776 | tf_op jit(solution)/shard_map/all_to_all | solution.py:298
  311.2 4.9 %marginal5.1 = f32[2,64,512]{2,1,0:T(8,128)} custom-call(s32[2]{0:T(128)} %pad_add_fusion.place.refs_0_, s32[6,8]{1,0:T(8,128)} %refs_1_.19, bf16[8,5,2,64,512]{4,3,2,1,0:T(8,128)(2,1)} %bitcast.48, f32[8,328,128]{2,1,0:T(8,128)} %convert_element_type.159.refs_3_, f32[2,64,512]{2,1,0:T(8,128)} %get-tuple-element.50.refs_4_), custom_call_target="tpu_custom_call" | custom-call | tf_op jit(solution)/shard_map/marginal5/pallas_call | solution.py:304
  316.2 1.7 bitcast_dynamic-update-slice_fusion
  (148 shorter events, 57.5 us)
Async XLA Ops:
  7.2 5.4 %copy-start.3 = (bf16[15,2,64,512]{3,2,1,0:T(8,128)(2,1)S(1)}, bf16[15,2,64,512]{3,2,1,0:T(8,128)(2,1)}, u32[]{:S(2)}) copy-start(bf16[15,2,64,512]{3,2,1,0:T(8,128)(2,1)} %param.4) | copy-start | bytes 5898244
  7.2 27.3 %all-gather.11.cloned.1.call-start = ((), (), s32[]{:S(2)}) async-start(), calls=%async_computation.5 | async-start | bytes 1179648 | tf_op jit(solution)/shard_map/all_gather | solution.py:255
  8.9 61.1 %all-gather.13.cloned.1.call-start = ((), (), s32[]{:S(2)}) async-start(), calls=%async_computation.6 | async-start | bytes 2359296 | tf_op jit(solution)/shard_map/all_gather | solution.py:255
  10.7 112.7 %all-gather.15.cloned.1.call-start = ((), (), s32[]{:S(2)}) async-start(), calls=%async_computation.7 | async-start | bytes 3538944 | tf_op jit(solution)/shard_map/all_gather | solution.py:255
  12.5 178.0 %all-gather.17.cloned.1.call-start = ((), (), s32[]{:S(2)}) async-start(), calls=%async_computation.8 | async-start | bytes 4718592 | tf_op jit(solution)/shard_map/all_gather | solution.py:255
  13.5 259.5 %all-gather.19.cloned.1.call-start = ((), (), s32[]{:S(2)}) async-start(), calls=%async_computation.9 | async-start | bytes 5898240 | tf_op jit(solution)/shard_map/all_gather | solution.py:255
  19.2 7.8 %collective-permute-start = (f16[2,72,512]{2,1,0:T(8,128)(2,1)S(1)}, f16[2,72,512]{2,1,0:T(8,128)(2,1)S(1)}, u32[]{:S(2)}, u32[]{:S(2)}) collective-permute-start(f16[2,72,512]{2,1,0:T(8,128)(2,1)S(1)} %convert_element_type.120), channel_id=1, source_target_pairs={{0,8},{8,16},{16,24},{24,0},{1,9},{9,17},{17,25},{25,1},{2,10},{10... | collective-permute-start | bytes 442376 | tf_op jit(solution)/shard_map/ppermute | solution.py:245
  40.0 14.2 %all-to-all-start = ((f16[8,72,128]{2,1,0:T(8,128)(2,1)}), f16[8,72,128]{2,1,0:T(8,128)(2,1)S(1)}, u32[]{:S(2)}, u32[]{:S(2)}) async-start(f16[8,72,128]{2,1,0:T(8,128)(2,1)} %convert_element_type.125), calls=%async_computation | async-start | bytes 294912 | tf_op jit(solution)/shard_map/all_to_all | solution.py:298
  43.4 8.3 %collective-permute-start.1 = (f16[2,72,512]{2,1,0:T(8,128)(2,1)S(1)}, f16[2,72,512]{2,1,0:T(8,128)(2,1)S(1)}, u32[]{:S(2)}, u32[]{:S(2)}) collective-permute-start(f16[2,72,512]{2,1,0:T(8,128)(2,1)S(1)} %convert_element_type.120), channel_id=1, source_target_pairs={{0,16},{8,24},{16,0},{24,8},{1,17},{9,25},{17,1},{25,9},{2,18},{10... | collective-permute-start | bytes 442376 | tf_op jit(solution)/shard_map/ppermute | solution.py:245
  45.9 40.9 %copy-start.21 = (f16[2,72,512]{2,1,0:T(8,128)(2,1)}, f16[2,72,512]{2,1,0:T(8,128)(2,1)S(1)}, u32[]{:S(2)}) copy-start(f16[2,72,512]{2,1,0:T(8,128)(2,1)S(1)} %convert_element_type.123) | copy-start | bytes 442372
  45.9 7.0 %collective-permute-start.2 = (f16[2,72,512]{2,1,0:T(8,128)(2,1)S(1)}, f16[2,72,512]{2,1,0:T(8,128)(2,1)S(1)}, u32[]{:S(2)}, u32[]{:S(2)}) collective-permute-start(f16[2,72,512]{2,1,0:T(8,128)(2,1)S(1)} %convert_element_type.123), channel_id=1, source_target_pairs={{0,8},{8,16},{16,24},{24,0},{1,9},{9,17},{17,25},{25,1},{2,10},{10... | collective-permute-start | bytes 442376 | tf_op jit(solution)/shard_map/ppermute | solution.py:245
  59.6 9.5 %collective-permute-start.3 = (f16[2,136,512]{2,1,0:T(8,128)(2,1)S(1)}, f16[2,136,512]{2,1,0:T(8,128)(2,1)S(1)}, u32[]{:S(2)}, u32[]{:S(2)}) collective-permute-start(f16[2,136,512]{2,1,0:T(8,128)(2,1)S(1)} %convert_element_type.127), channel_id=1, source_target_pairs={{0,8},{8,16},{16,24},{24,0},{1,9},{9,17},{17,25},{25,1},{2,10},{10... | collective-permute-start | bytes 835592 | tf_op jit(solution)/shard_map/ppermute | solution.py:245
  75.4 8.4 %copy-start = (f32[2,136,512]{2,1,0:T(8,128)S(1)}, f32[2,136,512]{2,1,0:T(8,128)}, u32[]{:S(2)}) copy-start(f32[2,136,512]{2,1,0:T(8,128)} %get-tuple-element.32.refs_14_.refs_16_) | copy-start | bytes 1671172
  77.3 26.5 %all-to-all-start.1 = ((f16[8,136,128]{2,1,0:T(8,128)(2,1)}), f16[8,136,128]{2,1,0:T(8,128)(2,1)S(1)}, u32[]{:S(2)}, u32[]{:S(2)}) async-start(f16[8,136,128]{2,1,0:T(8,128)(2,1)} %convert_element_type.134), calls=%async_computation.1 | async-start | bytes 557056 | tf_op jit(solution)/shard_map/all_to_all | solution.py:298
  80.8 20.6 %collective-permute-start.6 = (f16[2,136,512]{2,1,0:T(8,128)(2,1)S(1)}, f16[2,136,512]{2,1,0:T(8,128)(2,1)S(1)}, u32[]{:S(2)}, u32[]{:S(2)}) collective-permute-start(f16[2,136,512]{2,1,0:T(8,128)(2,1)S(1)} %convert_element_type.127), channel_id=1, source_target_pairs={{0,16},{8,24},{16,0},{24,8},{1,17},{9,25},{17,1},{25,9},{2,18},{10... | collective-permute-start | bytes 835592 | tf_op jit(solution)/shard_map/ppermute | solution.py:245
  83.8 57.6 %copy-start.11 = (f16[2,136,512]{2,1,0:T(8,128)(2,1)}, f16[2,136,512]{2,1,0:T(8,128)(2,1)S(1)}, u32[]{:S(2)}) copy-start(f16[2,136,512]{2,1,0:T(8,128)(2,1)S(1)} %convert_element_type.132) | copy-start | bytes 835588
  83.8 18.8 %collective-permute-start.7 = (f16[2,136,512]{2,1,0:T(8,128)(2,1)S(1)}, f16[2,136,512]{2,1,0:T(8,128)(2,1)S(1)}, u32[]{:S(2)}, u32[]{:S(2)}) collective-permute-start(f16[2,136,512]{2,1,0:T(8,128)(2,1)S(1)} %convert_element_type.132), channel_id=1, source_target_pairs={{0,8},{8,16},{16,24},{24,0},{1,9},{9,17},{17,25},{25,1},{2,10},{10... | collective-permute-start | bytes 835592 | tf_op jit(solution)/shard_map/ppermute | solution.py:245
  83.9 11.7 %collective-permute-start.4 = (f16[2,72,512]{2,1,0:T(8,128)(2,1)S(1)}, f16[2,72,512]{2,1,0:T(8,128)(2,1)S(1)}, u32[]{:S(2)}, u32[]{:S(2)}) collective-permute-start(f16[2,72,512]{2,1,0:T(8,128)(2,1)S(1)} %convert_element_type.120), channel_id=1, source_target_pairs={{0,24},{8,0},{16,8},{24,16},{1,25},{9,1},{17,9},{25,17},{2,26},{10... | collective-permute-start | bytes 442376 | tf_op jit(solution)/shard_map/ppermute | solution.py:245
  86.8 13.4 %collective-permute-start.5 = (f16[2,72,512]{2,1,0:T(8,128)(2,1)S(1)}, f16[2,72,512]{2,1,0:T(8,128)(2,1)S(1)}, u32[]{:S(2)}, u32[]{:S(2)}) collective-permute-start(f16[2,72,512]{2,1,0:T(8,128)(2,1)S(1)} %convert_element_type.123), channel_id=1, source_target_pairs={{0,16},{8,24},{16,0},{24,8},{1,17},{9,25},{17,1},{25,9},{2,18},{10... | collective-permute-start | bytes 442376 | tf_op jit(solution)/shard_map/ppermute | solution.py:245
  110.0 12.4 %collective-permute-start.8 = (f16[2,200,512]{2,1,0:T(8,128)(2,1)S(1)}, f16[2,200,512]{2,1,0:T(8,128)(2,1)S(1)}, u32[]{:S(2)}, u32[]{:S(2)}) collective-permute-start(f16[2,200,512]{2,1,0:T(8,128)(2,1)S(1)} %convert_element_type.136), channel_id=1, source_target_pairs={{0,8},{8,16},{16,24},{24,0},{1,9},{9,17},{17,25},{25,1},{2,10},{10... | collective-permute-start | bytes 1228808 | tf_op jit(solution)/shard_map/ppermute | solution.py:245
  130.5 7.9 %copy-start.1 = (f32[2,200,512]{2,1,0:T(8,128)S(1)}, f32[2,200,512]{2,1,0:T(8,128)}, u32[]{:S(2)}) copy-start(f32[2,200,512]{2,1,0:T(8,128)} %get-tuple-element.36.refs_22_.refs_24_) | copy-start | bytes 2457604
  132.5 34.6 %all-to-all-start.2 = ((f16[8,200,128]{2,1,0:T(8,128)(2,1)}), f16[8,200,128]{2,1,0:T(8,128)(2,1)S(1)}, u32[]{:S(2)}, u32[]{:S(2)}) async-start(f16[8,200,128]{2,1,0:T(8,128)(2,1)} %convert_element_type.144), calls=%async_computation.2 | async-start | bytes 819200 | tf_op jit(solution)/shard_map/all_to_all | solution.py:298
  137.0 27.8 %collective-permute-start.12 = (f16[2,200,512]{2,1,0:T(8,128)(2,1)S(1)}, f16[2,200,512]{2,1,0:T(8,128)(2,1)S(1)}, u32[]{:S(2)}, u32[]{:S(2)}) collective-permute-start(f16[2,200,512]{2,1,0:T(8,128)(2,1)S(1)} %convert_element_type.136), channel_id=1, source_target_pairs={{0,16},{8,24},{16,0},{24,8},{1,17},{9,25},{17,1},{25,9},{2,18},{10... | collective-permute-start | bytes 1228808 | tf_op jit(solution)/shard_map/ppermute | solution.py:245
  138.4 27.5 %collective-permute-start.13 = (f16[2,200,512]{2,1,0:T(8,128)(2,1)S(1)}, f16[2,200,512]{2,1,0:T(8,128)(2,1)S(1)}, u32[]{:S(2)}, u32[]{:S(2)}) collective-permute-start(f16[2,200,512]{2,1,0:T(8,128)(2,1)S(1)} %convert_element_type.142), channel_id=1, source_target_pairs={{0,8},{8,16},{16,24},{24,0},{1,9},{9,17},{17,25},{25,1},{2,10},{10... | collective-permute-start | bytes 1228808 | tf_op jit(solution)/shard_map/ppermute | solution.py:245
  138.5 22.0 %collective-permute-start.10 = (f16[2,136,512]{2,1,0:T(8,128)(2,1)S(1)}, f16[2,136,512]{2,1,0:T(8,128)(2,1)S(1)}, u32[]{:S(2)}, u32[]{:S(2)}) collective-permute-start(f16[2,136,512]{2,1,0:T(8,128)(2,1)S(1)} %convert_element_type.127), channel_id=1, source_target_pairs={{0,24},{8,0},{16,8},{24,16},{1,25},{9,1},{17,9},{25,17},{2,26},{10... | collective-permute-start | bytes 835592 | tf_op jit(solution)/shard_map/ppermute | solution.py:245
  141.4 22.2 %collective-permute-start.11 = (f16[2,136,512]{2,1,0:T(8,128)(2,1)S(1)}, f16[2,136,512]{2,1,0:T(8,128)(2,1)S(1)}, u32[]{:S(2)}, u32[]{:S(2)}) collective-permute-start(f16[2,136,512]{2,1,0:T(8,128)(2,1)S(1)} %convert_element_type.132), channel_id=1, source_target_pairs={{0,16},{8,24},{16,0},{24,8},{1,17},{9,25},{17,1},{25,9},{2,18},{10... | collective-permute-start | bytes 835592 | tf_op jit(solution)/shard_map/ppermute | solution.py:245
  142.1 17.3 %collective-permute-start.9 = (f16[2,72,512]{2,1,0:T(8,128)(2,1)}, f16[2,72,512]{2,1,0:T(8,128)(2,1)S(1)}, u32[]{:S(2)}, u32[]{:S(2)}) collective-permute-start(f16[2,72,512]{2,1,0:T(8,128)(2,1)} %copy-done.21), channel_id=1, source_target_pairs={{0,24},{8,0},{16,8},{24,16},{1,25},{9,1},{17,9},{25,17},{2,26},{10... | collective-permute-start | bytes 442376 | tf_op jit(solution)/shard_map/ppermute | solution.py:245
  174.2 15.1 %collective-permute-start.14 = (f16[2,264,512]{2,1,0:T(8,128)(2,1)S(1)}, f16[2,264,512]{2,1,0:T(8,128)(2,1)S(1)}, u32[]{:S(2)}, u32[]{:S(2)}) collective-permute-start(f16[2,264,512]{2,1,0:T(8,128)(2,1)S(1)} %convert_element_type.146), channel_id=1, source_target_pairs={{0,8},{8,16},{16,24},{24,0},{1,9},{9,17},{17,25},{25,1},{2,10},{10... | collective-permute-start | bytes 1622024 | tf_op jit(solution)/shard_map/ppermute | solution.py:245
  199.9 8.2 %copy-start.2 = (f32[2,264,512]{2,1,0:T(8,128)S(1)}, f32[2,264,512]{2,1,0:T(8,128)}, u32[]{:S(2)}) copy-start(f32[2,264,512]{2,1,0:T(8,128)} %get-tuple-element.40.refs_30_) | copy-start | bytes 3244036
  202.1 43.0 %all-to-all-start.3 = ((f16[8,264,128]{2,1,0:T(8,128)(2,1)}), f16[8,264,128]{2,1,0:T(8,128)(2,1)S(1)}, u32[]{:S(2)}, u32[]{:S(2)}) async-start(f16[8,264,128]{2,1,0:T(8,128)(2,1)} %convert_element_type.154), calls=%async_computation.3 | async-start | bytes 1081344 | tf_op jit(solution)/shard_map/all_to_all | solution.py:298
  206.5 5.2 %copy-start.12 = (f16[2,136,512]{2,1,0:T(8,128)(2,1)S(1)}, f16[2,136,512]{2,1,0:T(8,128)(2,1)}, u32[]{:S(2)}) copy-start(f16[2,136,512]{2,1,0:T(8,128)(2,1)} %copy-done.11) | copy-start | bytes 835588
  206.5 36.3 %collective-permute-start.18 = (f16[2,264,512]{2,1,0:T(8,128)(2,1)S(1)}, f16[2,264,512]{2,1,0:T(8,128)(2,1)S(1)}, u32[]{:S(2)}, u32[]{:S(2)}) collective-permute-start(f16[2,264,512]{2,1,0:T(8,128)(2,1)S(1)} %convert_element_type.146), channel_id=1, source_target_pairs={{0,16},{8,24},{16,0},{24,8},{1,17},{9,25},{17,1},{25,9},{2,18},{10... | collective-permute-start | bytes 1622024 | tf_op jit(solution)/shard_map/ppermute | solution.py:245
  208.2 35.8 %collective-permute-start.19 = (f16[2,264,512]{2,1,0:T(8,128)(2,1)S(1)}, f16[2,264,512]{2,1,0:T(8,128)(2,1)S(1)}, u32[]{:S(2)}, u32[]{:S(2)}) collective-permute-start(f16[2,264,512]{2,1,0:T(8,128)(2,1)S(1)} %convert_element_type.152), channel_id=1, source_target_pairs={{0,8},{8,16},{16,24},{24,0},{1,9},{9,17},{17,25},{25,1},{2,10},{10... | collective-permute-start | bytes 1622024 | tf_op jit(solution)/shard_map/ppermute | solution.py:245
  208.3 30.3 %collective-permute-start.16 = (f16[2,200,512]{2,1,0:T(8,128)(2,1)S(1)}, f16[2,200,512]{2,1,0:T(8,128)(2,1)S(1)}, u32[]{:S(2)}, u32[]{:S(2)}) collective-permute-start(f16[2,200,512]{2,1,0:T(8,128)(2,1)S(1)} %convert_element_type.136), channel_id=1, source_target_pairs={{0,24},{8,0},{16,8},{24,16},{1,25},{9,1},{17,9},{25,17},{2,26},{10... | collective-permute-start | bytes 1228808 | tf_op jit(solution)/shard_map/ppermute | solution.py:245
  211.2 30.4 %collective-permute-start.17 = (f16[2,200,512]{2,1,0:T(8,128)(2,1)S(1)}, f16[2,200,512]{2,1,0:T(8,128)(2,1)S(1)}, u32[]{:S(2)}, u32[]{:S(2)}) collective-permute-start(f16[2,200,512]{2,1,0:T(8,128)(2,1)S(1)} %convert_element_type.142), channel_id=1, source_target_pairs={{0,16},{8,24},{16,0},{24,8},{1,17},{9,25},{17,1},{25,9},{2,18},{10... | collective-permute-start | bytes 1228808 | tf_op jit(solution)/shard_map/ppermute | solution.py:245
  211.7 25.6 %collective-permute-start.15 = (f16[2,136,512]{2,1,0:T(8,128)(2,1)S(1)}, f16[2,136,512]{2,1,0:T(8,128)(2,1)S(1)}, u32[]{:S(2)}, u32[]{:S(2)}) collective-permute-start(f16[2,136,512]{2,1,0:T(8,128)(2,1)S(1)} %copy-done.12), channel_id=1, source_target_pairs={{0,24},{8,0},{16,8},{24,16},{1,25},{9,1},{17,9},{25,17},{2,26},{10... | collective-permute-start | bytes 835592 | tf_op jit(solution)/shard_map/ppermute | solution.py:245
  237.4 7.2 %copy-start.13 = (f16[2,136,512]{2,1,0:T(8,128)(2,1)}, f16[2,136,512]{2,1,0:T(8,128)(2,1)S(1)}, u32[]{:S(2)}) copy-start(f16[2,136,512]{2,1,0:T(8,128)(2,1)S(1)} %collective-permute-done.15) | copy-start | bytes 835588
  241.6 2.9 copy-start.9
  251.6 4.5 %copy-start.15 = (f32[2,64,512]{2,1,0:T(8,128)S(1)}, f32[2,64,512]{2,1,0:T(8,128)}, u32[]{:S(2)}) copy-start(f32[2,64,512]{2,1,0:T(8,128)} %get-tuple-element.44) | copy-start | bytes 786436
  251.6 5.2 %copy-start.16 = (f32[1,2,64,512]{3,2,1,0:T(8,128)S(1)}, f32[1,2,64,512]{3,2,1,0:T(8,128)}, u32[]{:S(2)}) copy-start(f32[1,2,64,512]{3,2,1,0:T(8,128)} %get-tuple-element.27) | copy-start | bytes 786436
  251.6 5.9 %copy-start.17 = (f32[2,64,512]{2,1,0:T(8,128)S(1)}, f32[2,64,512]{2,1,0:T(8,128)}, u32[]{:S(2)}) copy-start(f32[2,64,512]{2,1,0:T(8,128)} %get-tuple-element.45) | copy-start | bytes 786436
  251.6 6.6 %copy-start.14 = (f16[2,136,512]{2,1,0:T(8,128)(2,1)S(1)}, f16[2,136,512]{2,1,0:T(8,128)(2,1)}, u32[]{:S(2)}) copy-start(f16[2,136,512]{2,1,0:T(8,128)(2,1)} %copy-done.13) | copy-start | bytes 835588
  253.1 18.6 %collective-permute-start.20 = (f16[2,328,512]{2,1,0:T(8,128)(2,1)S(1)}, f16[2,328,512]{2,1,0:T(8,128)(2,1)S(1)}, u32[]{:S(2)}, u32[]{:S(2)}) collective-permute-start(f16[2,328,512]{2,1,0:T(8,128)(2,1)S(1)} %convert_element_type.156), channel_id=1, source_target_pairs={{0,8},{8,16},{16,24},{24,0},{1,9},{9,17},{17,25},{25,1},{2,10},{10... | collective-permute-start | bytes 2015240 | tf_op jit(solution)/shard_map/ppermute | solution.py:245
  256.8 3.4 %copy-start.10 = (f16[2,200,512]{2,1,0:T(8,128)(2,1)S(1)}, f16[2,200,512]{2,1,0:T(8,128)(2,1)}, u32[]{:S(2)}) copy-start(f16[2,200,512]{2,1,0:T(8,128)(2,1)} %copy-done.9) | copy-start | bytes 1228804
  284.7 6.9 %copy-start.8 = (f32[2,2,64,512]{3,2,1,0:T(8,128)S(1)}, f32[2,2,64,512]{3,2,1,0:T(8,128)}, u32[]{:S(2)}) copy-start(f32[2,2,64,512]{3,2,1,0:T(8,128)} %get-tuple-element.31) | copy-start | bytes 1572868
  287.0 5.4 %copy-start.18 = (f32[2,64,512]{2,1,0:T(8,128)S(1)}, f32[2,64,512]{2,1,0:T(8,128)}, u32[]{:S(2)}) copy-start(f32[2,64,512]{2,1,0:T(8,128)} %get-tuple-element.46) | copy-start | bytes 786436
  287.0 6.1 %copy-start.7 = (f32[3,2,64,512]{3,2,1,0:T(8,128)S(1)}, f32[3,2,64,512]{3,2,1,0:T(8,128)}, u32[]{:S(2)}) copy-start(f32[3,2,64,512]{3,2,1,0:T(8,128)} %get-tuple-element.35) | copy-start | bytes 2359300
  287.0 23.1 %all-to-all-start.4 = ((f16[8,328,128]{2,1,0:T(8,128)(2,1)}), f16[8,328,128]{2,1,0:T(8,128)(2,1)S(1)}, u32[]{:S(2)}, u32[]{:S(2)}) async-start(f16[8,328,128]{2,1,0:T(8,128)(2,1)} %convert_element_type.158), calls=%async_computation.4 | async-start | bytes 1343488 | tf_op jit(solution)/shard_map/all_to_all | solution.py:298
  (5 other events, 11.8 us)
Sparse Core Ops, SparseCore 0:
  9.6 24.7 all-gather.10
  36.0 32.4 all-gather.12
  70.2 43.1 all-gather.14
  115.3 54.5 all-gather.16
  171.4 66.2 all-gather.18

commit v3 on v1

--- a/solution.py
+++ b/solution.py
@@ -71,87 +71,154 @@
     return kept + jnp.where((lines == lanes) & (lines >= size), 1.0, 0.0)
 
 
-def cross_kernel(level, last, spans, n_row, npr, rows, width, *refs):
+def split_block(value, size, split, top_rows, low_rows):
+    value = jnp.where(live_lanes(value.shape, size), value, 0.0)
+    top = value.astype(BF16)
+    split[top_rows] = top
+    split[low_rows] = (value - top.astype(F32)).astype(BF16)
+
+
+def upper_kernel(level, off, spans, n_row, npr, rows, width, *refs):
     place, parents, sizes, panel = refs[:4]
     at = 4
     sources = []
     for up in range(level):
         parts = []
-        for _ in range(1 if up == 0 else 2):
+        for part in range(2):
+            if (up, part) == (0, 0) or (up, part) == (level - 1, 1):
+                parts.append(())
+                continue
             parts.append(refs[at : at + spans[up]])
             at += spans[up]
         sources.append(parts)
-    n_out = 2 if last else 3
-    outs = refs[at : at + n_out]
-    scratch = refs[at + n_out :]
-    cross, turn = outs[0], outs[1]
-    passed = None if last else outs[2]
-    lower, split, panel_sem, block_sem = scratch[:4]
-    holders = scratch[4:]
+    out = refs[at]
+    lower, split, panel_sem, block_sem = refs[at + 1 : at + 5]
+    holders = iter(refs[at + 5 :])
     row = place[0]
-    n_col = panel.shape[0]
-    high = level * rows
-
+    high = (level - 1) * rows
+    held = {
+        (up, part): next(holders)
+        for up in range(level)
+        for part in range(2)
+        if sources[up][part]
+    }
     chains = [chain_of(parents, level, row * npr + n) for n in range(npr)]
 
     def panel_copy(n, m):
-        return pltpu.make_async_copy(panel.at[:, m, n], lower.at[n, m], panel_sem.at[n, m])
-
-    def holder(up, part):
-        return holders[0] if up == 0 else holders[1 + 2 * (up - 1) + part]
+        return pltpu.make_async_copy(panel.at[:, off + m, n], lower.at[n, m], panel_sem.at[n, m])
 
     for n in range(npr):
         for up in range(level):
             node = chains[n][up]
             back = lax.rem(row - lax.div(node, npr) + n_row, n_row)
             slot = lax.rem(node, npr)
-            for part, choices in enumerate(sources[up]):
-                for i, source in enumerate(choices):
+            for part in range(2):
+                for i, source in enumerate(sources[up][part]):
 
                     @pl.when(back == i)
                     def _():
                         pltpu.make_async_copy(
-                            source.at[slot], holder(up, part).at[n], block_sem.at[n, up, part]
+                            source.at[slot], held[up, part].at[n], block_sem.at[n, up, part]
                         ).start()
         for m in range(level):
             panel_copy(n, m).start()
 
     for n in range(npr):
+        live = [sizes[up, chains[n][up]] for up in range(level)]
+        total = None
         for up in range(level):
-            size = sizes[up, chains[n][up]]
-            for part, choices in enumerate(sources[up]):
-                held = holder(up, part)
-                pltpu.make_async_copy(choices[0].at[0], held.at[n], block_sem.at[n, up, part]).wait()
-                count = (held.shape[1] - TAIL) // rows
-                whole = product(held[n, count * rows :])
+            for part in range(2):
+                if not sources[up][part]:
+                    continue
+                block = held[up, part]
+                pltpu.make_async_copy(
+                    sources[up][part][0].at[0], block.at[n], block_sem.at[n, up, part]
+                ).wait()
+                count = (block.shape[1] - TAIL) // rows
+                whole = product(block[n, count * rows :])
                 for b in range(count):
-                    value = held[n, b * rows : (b + 1) * rows] * whole
-                    if up > 0 and part == 0:
-                        l, m = b, up
-                        value = jnp.where(live_lanes(value.shape, size), value, 0.0)
-                    else:
-                        l, m = up, b
-                        value = jnp.where(
-                            live_lanes(value.shape, sizes[m, chains[n][m]]), value, 0.0
-                        )
-                    top = value.astype(BF16)
-                    split[n, m, l * rows : (l + 1) * rows] = top
-                    split[n, m, high + l * rows : high + (l + 1) * rows] = (
-                        value - top.astype(F32)
-                    ).astype(BF16)
-
-    results = []
-    for n in range(npr):
-        total = None
+                    value = block[n, b * rows : (b + 1) * rows] * whole
+                    l, m = (b, up) if up > 0 and part == 0 else (up, b)
+                    split_block(
+                        value,
+                        live[m],
+                        split,
+                        (n, m, slice(l * rows, (l + 1) * rows)),
+                        (n, m, slice(high + l * rows, high + (l + 1) * rows)),
+                    )
         for m in range(level):
             panel_copy(n, m).wait()
             block = lower[n, m].reshape(width, width)
             term = jnp.dot(split[n, m], block, preferred_element_type=F32)
             total = term if total is None else total + term
         value = -(total[:high] + total[high:])
+        out[n] = jnp.where(live_lanes(value.shape, sizes[level, row * npr + n]), value, 0.0)
+
+
+def cross_kernel(level, last, off, n_source, n_wait, n_row, npr, rows, width, *refs):
+    place, parents, sizes, panel = refs[:4]
+    sources = refs[4 : 4 + n_source]
+    at = 4 + n_source
+    upper = None
+    if level > 1:
+        upper = refs[at]
+        at += 1
+    at += n_wait
+    n_out = 2 if last else 3
+    outs = refs[at : at + n_out]
+    lower, split, held, panel_sem, block_sem = refs[at + n_out :]
+    cross, turn = outs[0], outs[1]
+    passed = None if last else outs[2]
+    row = place[0]
+    n_col = panel.shape[0]
+    high = level * rows
+    chains = [chain_of(parents, level, row * npr + n) for n in range(npr)]
+
+    def panel_copy(n, m):
+        return pltpu.make_async_copy(panel.at[:, off + m, n], lower.at[n, m], panel_sem.at[n, m])
+
+    for n in range(npr):
+        node = chains[n][level - 1]
+        back = lax.rem(row - lax.div(node, npr) + n_row, n_row)
+        for i, source in enumerate(sources):
+
+            @pl.when(back == i)
+            def _():
+                pltpu.make_async_copy(
+                    source.at[lax.rem(node, npr)], held.at[n], block_sem.at[n]
+                ).start()
+
+    for m in range(level):
+        for n in range(npr):
+            panel_copy(n, m).start()
+
+    for n in range(npr):
+        pltpu.make_async_copy(sources[0].at[0], held.at[n], block_sem.at[n]).wait()
+        whole = product(held[n, high:])
+        for m in range(level):
+            split_block(
+                held[n, m * rows : (m + 1) * rows] * whole,
+                sizes[m, chains[n][m]],
+                split,
+                (n, m, slice(0, rows)),
+                (n, m, slice(rows, 2 * rows)),
+            )
+    totals = [None] * npr
+    for m in range(level):
+        for n in range(npr):
+            panel_copy(n, m).wait()
+            block = lower[n, m].reshape(width, width)
+            term = jnp.dot(split[n, m], block, preferred_element_type=F32)
+            totals[n] = term if totals[n] is None else totals[n] + term
+    results = []
+    for n in range(npr):
+        value = -(totals[n][:rows] + totals[n][rows:])
         value = jnp.where(live_lanes(value.shape, sizes[level, row * npr + n]), value, 0.0)
-        for l in range(level):
-            cross[l, n] = value[l * rows : (l + 1) * rows]
+        cross[level - 1, n] = value
+        if level > 1:
+            value = jnp.concatenate([upper[n], value], axis=0)
+            for l in range(level - 1):
+                cross[l, n] = value[l * rows : (l + 1) * rows]
         table, whole = factors(peak_of(value))
         value = value * (TOP / whole)
         if not last:
@@ -164,11 +231,12 @@
         turn[c, high:] = jnp.concatenate([t[:, piece] for _, t in results], axis=1)
 
 
-def marginal_kernel(level, last, n_row, npr, rows, width, *refs):
+def marginal_kernel(level, last, off, n_wait, n_row, npr, rows, width, *refs):
     place, sizes, panel, turned, diag = refs[:5]
     n_out = 1 if last else 2
-    outs = refs[5 : 5 + n_out]
-    lower, panel_sem = refs[5 + n_out :]
+    at = 5 + n_wait
+    outs = refs[at : at + n_out]
+    lower, panel_sem = refs[at + n_out :]
     marginal = outs[0]
     message = None if last else outs[1]
     row, col = place[0], place[1]
@@ -176,7 +244,7 @@
     high = level * rows
 
     def panel_copy(n, m):
-        return pltpu.make_async_copy(panel.at[:, m, n], lower.at[n, m], panel_sem.at[n, m])
+        return pltpu.make_async_copy(panel.at[:, off + m, n], lower.at[n, m], panel_sem.at[n, m])
 
     for m in range(level):
         for n in range(npr):
@@ -234,18 +302,32 @@
     def reach(level):
         return min(levels - 1 - level, n_row - 1)
 
-    def spread(message, level):
+    due = [[] for _ in range(levels)]
+
+    def spread(message, level, rows_only):
         found = [message]
         half = message.astype(F16)
         for back in range(1, reach(level) + 1):
             route = [(i, (i + back) % n_row) for i in range(n_row)]
             found.append(lax.ppermute(half, "row", route).astype(F32))
+            if rows_only:
+                due[level if back < 3 or level < 2 else level + back - 2].append(found[-1])
+            elif back > 1:
+                due[level if level == 0 else level + 1 if level == 1 else level + back - 1].append(found[-1])
         return found
 
-    whole_panel = []
-    for level in range(1, levels):
-        start = level * (level - 1) // 2
-        whole_panel.append(lax.all_gather(panel[start : start + level], "col", axis=0))
+    def gathered(first, count):
+        return lax.all_gather(panel[first : first + count], "col", axis=0)
+
+    whole_panel = [None] * levels
+    ones = [lax.all_gather(panel[0:1, n : n + 1], "col", axis=0) for n in range(npr)]
+    whole_panel[1] = (jnp.concatenate(ones, axis=2), 0)
+    groups = [(2, 3), (4,), (5,)] if levels == 6 else [(level,) for level in range(2, levels)]
+    for group in groups:
+        first = group[0] * (group[0] - 1) // 2
+        both = gathered(first, sum(group))
+        for level in group:
+            whole_panel[level] = (both, level * (level - 1) // 2 - first)
 
     base, message = pl.pallas_call(
         functools.partial(base_kernel, npr, rows, width),
@@ -257,56 +339,81 @@
     )(place, supernode_sizes, diag_inverse[0])
     crosses = []
     diagonals = [base]
-    table = [[spread(message, 0)]]
+    table = [[(), spread(message, 0, False)]]
     for level in range(1, levels):
         last = level == levels - 1
         high = level * rows
-        whole = whole_panel[level - 1]
-        spans = [min(level - up, n_row - 1) + 1 for up in range(level)]
-        sources = [a for up in range(level) for part in table[up] for a in part[: spans[up]]]
+        whole, off = whole_panel[level]
+        panel_scratch = [pltpu.VMEM((npr, level, n_col, rows, width), BF16)]
+        upper = []
+        if level > 1:
+            spans = [min(level - up, n_row - 1) + 1 for up in range(level)]
+            sources = []
+            held = []
+            for up in range(level):
+                for part in range(2):
+                    if (up, part) == (0, 0) or (up, part) == (level - 1, 1):
+                        continue
+                    sources.extend(table[up][part][: spans[up]])
+                    held.append(pltpu.VMEM(table[up][part][0].shape, F32))
+            upper = [
+                pl.pallas_call(
+                    functools.partial(upper_kernel, level, off, spans, n_row, npr, rows, width),
+                    out_shape=shape(npr, high - rows, width),
+                    in_specs=[SMEM, SMEM, SMEM] + [ANY] * (1 + len(sources)),
+                    out_specs=VMEM,
+                    scratch_shapes=panel_scratch
+                    + [
+                        pltpu.VMEM((npr, level, 2 * (high - rows), width), BF16),
+                        pltpu.SemaphoreType.DMA((npr, level)),
+                        pltpu.SemaphoreType.DMA((npr, level, 2)),
+                    ]
+                    + held,
+                    compiler_params=params(),
+                    name=f"upper{level}",
+                )(place, parents, supernode_sizes, whole, *sources)
+            ]
+        newest = table[level - 1][1][: min(1, n_row - 1) + 1]
+        waits = due[0] if level == 1 else []
         out_shape = [shape(level, npr, rows, width), shape(n_col, high + TAIL, npr * rows)]
         if not last:
             out_shape.append(shape(npr, high + TAIL, width))
-        scratch = [
-            pltpu.VMEM((npr, level, n_col, rows, width), BF16),
-            pltpu.VMEM((npr, level, 2 * high, width), BF16),
-            pltpu.SemaphoreType.DMA((npr, level)),
-            pltpu.SemaphoreType.DMA((npr, level, 2)),
-            pltpu.VMEM((npr, rows + TAIL, width), F32),
-        ]
-        for up in range(1, level):
-            scratch.append(pltpu.VMEM((npr, up * rows + TAIL, width), F32))
-            scratch.append(pltpu.VMEM((npr, (up + 1) * rows + TAIL, width), F32))
         made = pl.pallas_call(
-            functools.partial(cross_kernel, level, last, spans, n_row, npr, rows, width),
+            functools.partial(
+                cross_kernel, level, last, off, len(newest), len(waits), n_row, npr, rows, width
+            ),
             out_shape=tuple(out_shape),
-            in_specs=[SMEM, SMEM, SMEM] + [ANY] * (1 + len(sources)),
+            in_specs=[SMEM, SMEM, SMEM] + [ANY] * (1 + len(newest)) + [VMEM] * len(upper) + [ANY] * len(waits),
             out_specs=(VMEM,) * len(out_shape),
-            scratch_shapes=scratch,
+            scratch_shapes=panel_scratch
+            + [
+                pltpu.VMEM((npr, level, 2 * rows, width), BF16),
+                pltpu.VMEM((npr, high + TAIL, width), F32),
+                pltpu.SemaphoreType.DMA((npr, level)),
+                pltpu.SemaphoreType.DMA((npr,)),
+            ],
             compiler_params=params(),
             name=f"cross{level}",
-        )(place, parents, supernode_sizes, whole, *sources)
+        )(place, parents, supernode_sizes, whole, *newest, *upper, *waits)
         crosses.append(made[0])
-        ahead = None if last else spread(made[2], level)
+        ahead = () if last else spread(made[2], level, True)
         turned = lax.all_to_all(made[1].astype(F16), "col", 0, 0, tiled=True).astype(F32)
+        waits = [] if last else due[level]
         out_shape = [shape(npr, rows, width)]
         if not last:
             out_shape.append(shape(npr, high + rows + TAIL, width))
         done = pl.pallas_call(
-            functools.partial(marginal_kernel, level, last, n_row, npr, rows, width),
+            functools.partial(marginal_kernel, level, last, off, len(waits), n_row, npr, rows, width),
             out_shape=tuple(out_shape),
-            in_specs=[SMEM, SMEM, ANY, VMEM, VMEM],
+            in_specs=[SMEM, SMEM, ANY, VMEM, VMEM] + [ANY] * len(waits),
             out_specs=(VMEM,) * len(out_shape),
-            scratch_shapes=[
-                pltpu.VMEM((npr, level, n_col, rows, width), BF16),
-                pltpu.SemaphoreType.DMA((npr, level)),
-            ],
+            scratch_shapes=panel_scratch + [pltpu.SemaphoreType.DMA((npr, level))],
             compiler_params=params(),
             name=f"marginal{level}",
-        )(place, supernode_sizes, whole, turned, diag_inverse[level])
+        )(place, supernode_sizes, whole, turned, diag_inverse[level], *waits)
         diagonals.append(done[0])
         if not last:
-            table.append([ahead, spread(done[1], level)])
+            table.append([ahead, spread(done[1], level, False)])
     return (jnp.concatenate(crosses, axis=0), jnp.stack(diagonals))
 
 

time: 361 us -> 339 us (0.939)
  waiting for transfers between devices: 139 us -> 105 us
  blocking collectives: 55.2 us -> 35 us
  Pallas kernels: 61.5 us -> 76.3 us
  starting transfers between devices: 32.6 us -> 46.3 us
  other arithmetic: 39.1 us -> 43.4 us
    all_to_all x3 -> x0, blocking collectives: 55.2 us -> none  [shards(): lax.all_to_all(made[1].astype(F16), 'col', 0, 0, tiled=True).astype(F32)]
    all_gather x0 -> x2, blocking collectives: none -> 35 us  [shards(): lax.all_gather(panel[0:1, n:n + 1], 'col', axis=0)]
    all_to_all x2 -> x5, waiting for transfers between devices: 27.7 us -> 12.3 us  [shards(): lax.all_to_all(made[1].astype(F16), 'col', 0, 0, tiled=True).astype(F32)]
    all_to_all x2 -> x5, starting transfers between devices: 7.21 us -> 22.3 us  [shards(): lax.all_to_all(made[1].astype(F16), 'col', 0, 0, tiled=True).astype(F32)]
    pallas_call x10 -> x14, Pallas kernels: 59.6 us -> 74.3 us  [the longest x5 28.2 us: shards(): pl.pallas_call(functools.partial(cross_kernel, level, last, off, len(newe...]
    ppermute x21, waiting for transfers between devices: 104 us -> 92.5 us  [spread(): found.append(lax.ppermute(half, 'row', route).astype(F32))]
    all_gather x5 -> x3, waiting for transfers between devices: 6.65 us -> 0.02 us  [gathered(): return lax.all_gather(panel[first:first + count], 'col', axis=0)]
    unnamed x41 -> x37, local copies, waits for them, and re-layouts: 7.23 us -> 7.21 us
  transfers between devices with their start and end apart: 28 -> 29, of which waited for: 12 -> 15; matrix products, arithmetic and copies ran while one was open for 14% -> 15% of each run, Pallas kernels for 13% -> 19%
where the time goes in v3:
time: 339 us; the launch traced here: 337 us
  waiting for transfers between devices  105 us (31%)
  Pallas kernels  76.3 us (23%)
  starting transfers between devices  46.3 us (14%)
  other arithmetic  43.4 us (13%)
  blocking collectives  35 us (10%)
  local copies, waits for them, and re-layouts  16.6 us (5%)
  between operations  14.1 us (4%)
    ppermute x21, waiting for transfers between devices, spread(): found.append(lax.ppermute(half, 'row', route).astype(F32))  92.5 us
    all_gather x2, blocking collectives, shards(): lax.all_gather(panel[0:1, n:n + 1], 'col', axis=0)  35 us
    pallas_call x5, Pallas kernels, shards(): pl.pallas_call(functools.partial(cross_kernel, level, last, off, len(newe...  28.2 us
    ppermute x21, starting transfers between devices, spread(): found.append(lax.ppermute(half, 'row', route).astype(F32))  23.9 us
    pallas_call x4, Pallas kernels, shards(): pl.pallas_call(functools.partial(upper_kernel, level, off, spans, n_row,...  23.4 us
    pallas_call x5, Pallas kernels, shards(): pl.pallas_call(functools.partial(marginal_kernel, level, last, off, len(w...  22.7 us
    all_to_all x5, starting transfers between devices, shards(): lax.all_to_all(made[1].astype(F16), 'col', 0, 0, tiled=True).astype(F32)  22.3 us
    convert_element_type x21, other arithmetic, spread(): found.append(lax.ppermute(half, 'row', route).astype(F32))  19.5 us
  transfers between devices with their start and end apart: 29, of which 15 were waited for; matrix products, arithmetic and copies ran while one was open for 15% of the time, Pallas kernels for 19%

profile of v3, /device:TPU:0, one launch (start us, length us, event | category | flops | bytes accessed | tf_op | source)
XLA Modules:
  0.0 337.0 jit_solution(15317479468963572383)
XLA Ops:
  7.2 2.5 fusion
  9.7 2.0 slice.39
  14.3 1.9 base.1
  17.2 3.0 collective-permute-start
  20.2 1.5 collective-permute-start.1
  24.0 17.5 %all-gather = bf16[8,1,64,512]{3,2,1,0:T(8,128)(2,1)S(1)} all-gather(bf16[1,1,64,512]{3,2,1,0:T(8,128)(2,1)S(1)} %get-tuple-element.52), channel_id=2, replica_groups=mesh['row'=4,'col'=8] {'col'}, dimensions={0}, use_global_device_ids=true | all-gather | bytes 589824 | tf_op jit(solution)/shard_map/all_gather | solution.py:323
  41.5 17.5 %all-gather.1 = bf16[8,1,64,512]{3,2,1,0:T(8,128)(2,1)S(1)} all-gather(bf16[1,1,64,512]{3,2,1,0:T(8,128)(2,1)S(1)} %get-tuple-element.53), channel_id=3, replica_groups=mesh['row'=4,'col'=8] {'col'}, dimensions={0}, use_global_device_ids=true | all-gather | bytes 589824 | tf_op jit(solution)/shard_map/all_gather | solution.py:323
  62.3 3.7 %cross1.1 = (f32[1,2,64,512]{3,2,1,0:T(8,128)}, f32[8,72,128]{2,1,0:T(8,128)}, f32[2,72,512]{2,1,0:T(8,128)}) custom-call(s32[2]{0:T(128)} %pad_add_fusion.place.refs_0_, s32[5,8]{1,0:T(8,128)} %refs_1_.26, s32[6,8]{1,0:T(8,128)} %refs_1_.27, bf16[8,1,2,64,512]{4,3,2,1,0:T(8,128)(2,1)} %pad_maximum_fusion.refs_3_.refs_2_, ...), custom_call_target="tpu_custom_call" | custom-call | tf_op jit(solution)/shard_map/cross1/pallas_call | solution.py:381
  66.0 1.6 convert_element_type.124
  67.6 4.7 %all-to-all-start = ((f16[8,72,128]{2,1,0:T(8,128)(2,1)}), f16[8,72,128]{2,1,0:T(8,128)(2,1)S(1)}, u32[]{:S(2)}, u32[]{:S(2)}) async-start(f16[8,72,128]{2,1,0:T(8,128)(2,1)} %convert_element_type.124), calls=%async_computation | async-start | bytes 294912 | tf_op jit(solution)/shard_map/all_to_all | solution.py:400
  74.2 2.3 collective-permute-start.5
  76.5 4.5 %collective-permute-done.3 = f16[2,72,512]{2,1,0:T(8,128)(2,1)S(1)} collective-permute-done((f16[2,72,512]{2,1,0:T(8,128)(2,1)S(1)}, f16[2,72,512]{2,1,0:T(8,128)(2,1)S(1)}, u32[]{:S(2)}, u32[]{:S(2)}) %collective-permute-start.3) | collective-permute-done | bytes 147488 | tf_op jit(solution)/shard_map/ppermute | solution.py:312
  85.1 3.7 %marginal1.1 = (f32[2,64,512]{2,1,0:T(8,128)}, f32[2,136,512]{2,1,0:T(8,128)}) custom-call(s32[2]{0:T(128)} %pad_add_fusion.place.refs_0_, s32[6,8]{1,0:T(8,128)} %refs_1_.27, bf16[8,1,2,64,512]{4,3,2,1,0:T(8,128)(2,1)} %pad_maximum_fusion.refs_3_.refs_2_, f32[8,72,128]{2,1,0:T(8,128)} %convert_element_type.125.refs_3_, ...), custom_call_target="tpu_custom_call" | custom-call | tf_op jit(solution)/shard_map/marginal1/pallas_call | solution.py:405
  91.3 7.5 %collective-permute-done.6 = f16[2,136,512]{2,1,0:T(8,128)(2,1)S(1)} collective-permute-done((f16[2,136,512]{2,1,0:T(8,128)(2,1)S(1)}, f16[2,136,512]{2,1,0:T(8,128)(2,1)S(1)}, u32[]{:S(2)}, u32[]{:S(2)}) %collective-permute-start.6) | collective-permute-done | bytes 278560 | tf_op jit(solution)/shard_map/ppermute | solution.py:312
  99.7 3.7 %upper2.1.refs_6_ = f32[2,64,512]{2,1,0:T(8,128)} custom-call(s32[2]{0:T(128)} %pad_add_fusion.place.refs_0_, s32[5,8]{1,0:T(8,128)} %refs_1_.26, s32[6,8]{1,0:T(8,128)} %refs_1_.27, bf16[8,5,2,64,512]{4,3,2,1,0:T(8,128)(2,1)} %bitcast.31, f32[2,72,512]{2,1,0:T(8,128)} %get-tuple-element.26.refs_4_, f32[2,72,512]{2,1,0:T(8,128)} %convert_element_type.121.refs_5_, ...), custom_call_target="tpu_custom_call" | custom-call | tf_op jit(solution)/shard_map/upper2/pallas_call | solution.py:360
  103.3 4.6 %cross2.1 = (f32[2,2,64,512]{3,2,1,0:T(8,128)}, f32[8,136,128]{2,1,0:T(8,128)}, f32[2,136,512]{2,1,0:T(8,128)}) custom-call(s32[2]{0:T(128)} %pad_add_fusion.place.refs_0_, s32[5,8]{1,0:T(8,128)} %refs_1_.26, s32[6,8]{1,0:T(8,128)} %refs_1_.27, bf16[8,5,2,64,512]{4,3,2,1,0:T(8,128)(2,1)} %bitcast.32, ...), custom_call_target="tpu_custom_call" | custom-call | tf_op jit(solution)/shard_map/cross2/pallas_call | solution.py:381
  108.0 1.9 convert_element_type.132
  109.9 4.6 %all-to-all-start.1 = ((f16[8,136,128]{2,1,0:T(8,128)(2,1)}), f16[8,136,128]{2,1,0:T(8,128)(2,1)S(1)}, u32[]{:S(2)}, u32[]{:S(2)}) async-start(f16[8,136,128]{2,1,0:T(8,128)(2,1)} %convert_element_type.132), calls=%async_computation.1 | async-start | bytes 557056 | tf_op jit(solution)/shard_map/all_to_all | solution.py:400
  118.6 5.3 %collective-permute-done.7 = f16[2,136,512]{2,1,0:T(8,128)(2,1)S(1)} collective-permute-done((f16[2,136,512]{2,1,0:T(8,128)(2,1)S(1)}, f16[2,136,512]{2,1,0:T(8,128)(2,1)S(1)}, u32[]{:S(2)}, u32[]{:S(2)}) %collective-permute-start.7) | collective-permute-done | bytes 278560 | tf_op jit(solution)/shard_map/ppermute | solution.py:312
  125.7 5.0 %collective-permute-done.9 = f16[2,136,512]{2,1,0:T(8,128)(2,1)S(1)} collective-permute-done((f16[2,136,512]{2,1,0:T(8,128)(2,1)S(1)}, f16[2,136,512]{2,1,0:T(8,128)(2,1)S(1)}, u32[]{:S(2)}, u32[]{:S(2)}) %collective-permute-start.9) | collective-permute-done | bytes 278560 | tf_op jit(solution)/shard_map/ppermute | solution.py:312
  131.6 3.8 %collective-permute-done.10 = f16[2,136,512]{2,1,0:T(8,128)(2,1)S(1)} collective-permute-done((f16[2,136,512]{2,1,0:T(8,128)(2,1)S(1)}, f16[2,136,512]{2,1,0:T(8,128)(2,1)S(1)}, u32[]{:S(2)}, u32[]{:S(2)}) %collective-permute-start.10) | collective-permute-done | bytes 278560 | tf_op jit(solution)/shard_map/ppermute | solution.py:312
  137.2 4.2 %marginal2.1 = (f32[2,64,512]{2,1,0:T(8,128)}, f32[2,200,512]{2,1,0:T(8,128)}) custom-call(s32[2]{0:T(128)} %pad_add_fusion.place.refs_0_, s32[6,8]{1,0:T(8,128)} %refs_1_.27, bf16[8,5,2,64,512]{4,3,2,1,0:T(8,128)(2,1)} %bitcast.33, f32[8,136,128]{2,1,0:T(8,128)} %convert_element_type.133.refs_3_, f32[2,64,512]{2,1,0:T(8,128)} %get-tuple-element.56.refs_4_, ...), custom_call_target="tpu_custom_call" | custom-call | tf_op jit(solution)/shard_map/marginal2/pallas_call | solution.py:405
  143.0 4.9 %upper3.1.refs_6_ = f32[2,128,512]{2,1,0:T(8,128)} custom-call(s32[2]{0:T(128)} %pad_add_fusion.place.refs_0_, s32[5,8]{1,0:T(8,128)} %refs_1_.26, s32[6,8]{1,0:T(8,128)} %refs_1_.27, bf16[8,5,2,64,512]{4,3,2,1,0:T(8,128)(2,1)} %bitcast.34, f32[2,72,512]{2,1,0:T(8,128)} %get-tuple-element.26.refs_4_, f32[2,72,512]{2,1,0:T(8,128)} %convert_element_type.121.refs_5_, ...), custom_call_target="tpu_custom_call" | custom-call | tf_op jit(solution)/shard_map/upper3/pallas_call | solution.py:360
  147.8 6.9 %collective-permute-done.11 = f16[2,200,512]{2,1,0:T(8,128)(2,1)S(1)} collective-permute-done((f16[2,200,512]{2,1,0:T(8,128)(2,1)S(1)}, f16[2,200,512]{2,1,0:T(8,128)(2,1)S(1)}, u32[]{:S(2)}, u32[]{:S(2)}) %collective-permute-start.11) | collective-permute-done | bytes 409632 | tf_op jit(solution)/shard_map/ppermute | solution.py:312
  155.7 5.7 %cross3.1 = (f32[3,2,64,512]{3,2,1,0:T(8,128)}, f32[8,200,128]{2,1,0:T(8,128)}, f32[2,200,512]{2,1,0:T(8,128)}) custom-call(s32[2]{0:T(128)} %pad_add_fusion.place.refs_0_, s32[5,8]{1,0:T(8,128)} %refs_1_.26, s32[6,8]{1,0:T(8,128)} %refs_1_.27, bf16[8,5,2,64,512]{4,3,2,1,0:T(8,128)(2,1)} %bitcast.35, ...), custom_call_target="tpu_custom_call" | custom-call | tf_op jit(solution)/shard_map/cross3/pallas_call | solution.py:381
  161.5 2.0 convert_element_type.141
  163.5 4.3 %all-to-all-start.2 = ((f16[8,200,128]{2,1,0:T(8,128)(2,1)}), f16[8,200,128]{2,1,0:T(8,128)(2,1)S(1)}, u32[]{:S(2)}, u32[]{:S(2)}) async-start(f16[8,200,128]{2,1,0:T(8,128)(2,1)} %convert_element_type.141), calls=%async_computation.2 | async-start | bytes 819200 | tf_op jit(solution)/shard_map/all_to_all | solution.py:400
  170.0 2.8 collective-permute-start.12
  172.8 14.1 %collective-permute-done.12 = f16[2,136,512]{2,1,0:T(8,128)(2,1)S(1)} collective-permute-done((f16[2,136,512]{2,1,0:T(8,128)(2,1)S(1)}, f16[2,136,512]{2,1,0:T(8,128)(2,1)S(1)}, u32[]{:S(2)}, u32[]{:S(2)}) %collective-permute-start.12) | collective-permute-done | bytes 278560 | tf_op jit(solution)/shard_map/ppermute | solution.py:312
  190.8 6.4 %collective-permute-done.15 = f16[2,200,512]{2,1,0:T(8,128)(2,1)S(1)} collective-permute-done((f16[2,200,512]{2,1,0:T(8,128)(2,1)S(1)}, f16[2,200,512]{2,1,0:T(8,128)(2,1)S(1)}, u32[]{:S(2)}, u32[]{:S(2)}) %collective-permute-start.15) | collective-permute-done | bytes 409632 | tf_op jit(solution)/shard_map/ppermute | solution.py:312
  199.2 4.7 %marginal3.1 = (f32[2,64,512]{2,1,0:T(8,128)}, f32[2,264,512]{2,1,0:T(8,128)}) custom-call(s32[2]{0:T(128)} %pad_add_fusion.place.refs_0_, s32[6,8]{1,0:T(8,128)} %refs_1_.27, bf16[8,5,2,64,512]{4,3,2,1,0:T(8,128)(2,1)} %bitcast.36, f32[8,200,128]{2,1,0:T(8,128)} %convert_element_type.142.refs_3_, f32[2,64,512]{2,1,0:T(8,128)} %get-tuple-element.55.refs_4_, ...), custom_call_target="tpu_custom_call" | custom-call | tf_op jit(solution)/shard_map/marginal3/pallas_call | solution.py:405
  205.3 6.6 %upper4.1.refs_6_ = f32[2,192,512]{2,1,0:T(8,128)} custom-call(s32[2]{0:T(128)} %pad_add_fusion.place.refs_0_, s32[5,8]{1,0:T(8,128)} %refs_1_.26, s32[6,8]{1,0:T(8,128)} %refs_1_.27, bf16[8,4,2,64,512]{4,3,2,1,0:T(8,128)(2,1)} %bitcast.40, f32[2,72,512]{2,1,0:T(8,128)} %get-tuple-element.26.refs_4_, f32[2,72,512]{2,1,0:T(8,128)} %convert_element_type.121.refs_5_, ...), custom_call_target="tpu_custom_call" | custom-call | tf_op jit(solution)/shard_map/upper4/pallas_call | solution.py:360
  211.9 8.2 %collective-permute-done.16 = f16[2,264,512]{2,1,0:T(8,128)(2,1)S(1)} collective-permute-done((f16[2,264,512]{2,1,0:T(8,128)(2,1)S(1)}, f16[2,264,512]{2,1,0:T(8,128)(2,1)S(1)}, u32[]{:S(2)}, u32[]{:S(2)}) %collective-permute-start.16) | collective-permute-done | bytes 540704 | tf_op jit(solution)/shard_map/ppermute | solution.py:312
  221.2 6.8 %cross4.1 = (f32[4,2,64,512]{3,2,1,0:T(8,128)}, f32[8,264,128]{2,1,0:T(8,128)}, f32[2,264,512]{2,1,0:T(8,128)}) custom-call(s32[2]{0:T(128)} %pad_add_fusion.place.refs_0_, s32[5,8]{1,0:T(8,128)} %refs_1_.26, s32[6,8]{1,0:T(8,128)} %refs_1_.27, bf16[8,4,2,64,512]{4,3,2,1,0:T(8,128)(2,1)} %bitcast.41, f32[2,264,512]{2,1,0:T(8,128)} %get-tuple-element.38.refs_4_.refs_27_, ...), custom_call_target="tpu_custom_call" | custom-call | tf_op jit(solution)/shard_map/cross4/pallas_call | solution.py:381
  228.0 2.2 convert_element_type.150
  230.2 4.3 %all-to-all-start.3 = ((f16[8,264,128]{2,1,0:T(8,128)(2,1)}), f16[8,264,128]{2,1,0:T(8,128)(2,1)S(1)}, u32[]{:S(2)}, u32[]{:S(2)}) async-start(f16[8,264,128]{2,1,0:T(8,128)(2,1)} %convert_element_type.150), calls=%async_computation.3 | async-start | bytes 1081344 | tf_op jit(solution)/shard_map/all_to_all | solution.py:400
  235.4 2.9 collective-permute-start.17
  238.3 21.1 %collective-permute-done.17 = f16[2,200,512]{2,1,0:T(8,128)(2,1)S(1)} collective-permute-done((f16[2,200,512]{2,1,0:T(8,128)(2,1)S(1)}, f16[2,200,512]{2,1,0:T(8,128)(2,1)S(1)}, u32[]{:S(2)}, u32[]{:S(2)}) %collective-permute-start.17) | collective-permute-done | bytes 409632 | tf_op jit(solution)/shard_map/ppermute | solution.py:312
  264.2 5.2 %marginal4.1 = (f32[2,64,512]{2,1,0:T(8,128)}, f32[2,328,512]{2,1,0:T(8,128)}) custom-call(s32[2]{0:T(128)} %pad_add_fusion.place.refs_0_, s32[6,8]{1,0:T(8,128)} %refs_1_.27, bf16[8,4,2,64,512]{4,3,2,1,0:T(8,128)(2,1)} %bitcast.42, f32[8,264,128]{2,1,0:T(8,128)} %convert_element_type.151.refs_3_, f32[2,64,512]{2,1,0:T(8,128)} %get-tuple-element.59.refs_4_, ...), custom_call_target="tpu_custom_call" | custom-call | tf_op jit(solution)/shard_map/marginal4/pallas_call | solution.py:405
  269.4 1.5 convert_element_type.156
  273.4 8.3 %upper5.1.refs_6_ = f32[2,256,512]{2,1,0:T(8,128)} custom-call(s32[2]{0:T(128)} %pad_add_fusion.place.refs_0_, s32[5,8]{1,0:T(8,128)} %refs_1_.26, s32[6,8]{1,0:T(8,128)} %refs_1_.27, bf16[8,5,2,64,512]{4,3,2,1,0:T(8,128)(2,1)} %bitcast.37, f32[2,72,512]{2,1,0:T(8,128)} %get-tuple-element.26.refs_4_, f32[2,72,512]{2,1,0:T(8,128)} %convert_element_type.121.refs_5_, ...), custom_call_target="tpu_custom_call" | custom-call | tf_op jit(solution)/shard_map/upper5/pallas_call | solution.py:360
  281.7 7.2 %collective-permute-done.20 = f16[2,328,512]{2,1,0:T(8,128)(2,1)S(1)} collective-permute-done((f16[2,328,512]{2,1,0:T(8,128)(2,1)S(1)}, f16[2,328,512]{2,1,0:T(8,128)(2,1)S(1)}, u32[]{:S(2)}, u32[]{:S(2)}) %collective-permute-start.20) | collective-permute-done | bytes 671776 | tf_op jit(solution)/shard_map/ppermute | solution.py:312
  290.1 7.3 %cross5.1 = (f32[5,2,64,512]{3,2,1,0:T(8,128)}, f32[8,328,128]{2,1,0:T(8,128)}) custom-call(s32[2]{0:T(128)} %pad_add_fusion.place.refs_0_, s32[5,8]{1,0:T(8,128)} %refs_1_.26, s32[6,8]{1,0:T(8,128)} %refs_1_.27, bf16[8,5,2,64,512]{4,3,2,1,0:T(8,128)(2,1)} %bitcast.38, f32[2,328,512]{2,1,0:T(8,128)} %get-tuple-element.42.refs_4_, ...), custom_call_target="tpu_custom_call" | custom-call | tf_op jit(solution)/shard_map/cross5/pallas_call | solution.py:381
  297.4 2.3 convert_element_type.158
  299.7 4.5 %all-to-all-start.4 = ((f16[8,328,128]{2,1,0:T(8,128)(2,1)}), f16[8,328,128]{2,1,0:T(8,128)(2,1)S(1)}, u32[]{:S(2)}, u32[]{:S(2)}) async-start(f16[8,328,128]{2,1,0:T(8,128)(2,1)} %convert_element_type.158), calls=%async_computation.4 | async-start | bytes 1343488 | tf_op jit(solution)/shard_map/all_to_all | solution.py:400
  310.4 12.3 %all-to-all-done.4 = f16[8,328,128]{2,1,0:T(8,128)(2,1)S(1)} async-done(((f16[8,328,128]{2,1,0:T(8,128)(2,1)}), f16[8,328,128]{2,1,0:T(8,128)(2,1)S(1)}, u32[]{:S(2)}, u32[]{:S(2)}) %all-to-all-start.4) | async-done | bytes 671776 | tf_op jit(solution)/shard_map/all_to_all | solution.py:400
  323.9 4.9 %marginal5.1 = f32[2,64,512]{2,1,0:T(8,128)} custom-call(s32[2]{0:T(128)} %pad_add_fusion.place.refs_0_, s32[6,8]{1,0:T(8,128)} %refs_1_.27, bf16[8,5,2,64,512]{4,3,2,1,0:T(8,128)(2,1)} %bitcast.39, f32[8,328,128]{2,1,0:T(8,128)} %convert_element_type.159.refs_3_, f32[2,64,512]{2,1,0:T(8,128)} %get-tuple-element.54.refs_4_), custom_call_target="tpu_custom_call" | custom-call | tf_op jit(solution)/shard_map/marginal5/pallas_call | solution.py:405
  328.8 1.7 bitcast_dynamic-update-slice_fusion
  (115 shorter events, 57.0 us)
Async XLA Ops:
  7.2 92.5 %all-gather.9.cloned.1.call-start = ((), (), s32[]{:S(2)}) async-start(), calls=%async_computation.5 | async-start | bytes 5898240 | tf_op jit(solution)/shard_map/all_gather | solution.py:320
  9.7 3.4 %copy-start.3 = (f32[6,2,64,512]{3,2,1,0:T(8,128)S(1)}, f32[6,2,64,512]{3,2,1,0:T(8,128)}, u32[]{:S(2)}) copy-start(f32[6,2,64,512]{3,2,1,0:T(8,128)} %param.5) | copy-start | bytes 4718596
  9.7 195.6 %all-gather.11.cloned.1.call-start = ((), (), s32[]{:S(2)}) async-start(), calls=%async_computation.6 | async-start | bytes 4718592 | tf_op jit(solution)/shard_map/all_gather | solution.py:320
  11.8 261.6 %all-gather.13.cloned.1.call-start = ((), (), s32[]{:S(2)}) async-start(), calls=%async_computation.7 | async-start | bytes 5898240 | tf_op jit(solution)/shard_map/all_gather | solution.py:320
  17.2 42.9 %collective-permute-start = (f16[2,72,512]{2,1,0:T(8,128)(2,1)S(1)}, f16[2,72,512]{2,1,0:T(8,128)(2,1)S(1)}, u32[]{:S(2)}, u32[]{:S(2)}) collective-permute-start(f16[2,72,512]{2,1,0:T(8,128)(2,1)S(1)} %convert_element_type.120), channel_id=1, source_target_pairs={{0,8},{8,16},{16,24},{24,0},{1,9},{9,17},{17,25},{25,1},{2,10},{10... | collective-permute-start | bytes 442376 | tf_op jit(solution)/shard_map/ppermute | solution.py:312
  20.2 40.6 %collective-permute-start.1 = (f16[2,72,512]{2,1,0:T(8,128)(2,1)S(1)}, f16[2,72,512]{2,1,0:T(8,128)(2,1)S(1)}, u32[]{:S(2)}, u32[]{:S(2)}) collective-permute-start(f16[2,72,512]{2,1,0:T(8,128)(2,1)S(1)} %convert_element_type.120), channel_id=1, source_target_pairs={{0,16},{8,24},{16,0},{24,8},{1,17},{9,25},{17,1},{25,9},{2,18},{10... | collective-permute-start | bytes 442376 | tf_op jit(solution)/shard_map/ppermute | solution.py:312
  21.7 39.8 %collective-permute-start.2 = (f16[2,72,512]{2,1,0:T(8,128)(2,1)S(1)}, f16[2,72,512]{2,1,0:T(8,128)(2,1)S(1)}, u32[]{:S(2)}, u32[]{:S(2)}) collective-permute-start(f16[2,72,512]{2,1,0:T(8,128)(2,1)S(1)} %convert_element_type.120), channel_id=1, source_target_pairs={{0,24},{8,0},{16,8},{24,16},{1,25},{9,1},{17,9},{25,17},{2,26},{10... | collective-permute-start | bytes 442376 | tf_op jit(solution)/shard_map/ppermute | solution.py:312
  67.6 16.7 %all-to-all-start = ((f16[8,72,128]{2,1,0:T(8,128)(2,1)}), f16[8,72,128]{2,1,0:T(8,128)(2,1)S(1)}, u32[]{:S(2)}, u32[]{:S(2)}) async-start(f16[8,72,128]{2,1,0:T(8,128)(2,1)} %convert_element_type.124), calls=%async_computation | async-start | bytes 294912 | tf_op jit(solution)/shard_map/all_to_all | solution.py:400
  73.3 7.6 %collective-permute-start.3 = (f16[2,72,512]{2,1,0:T(8,128)(2,1)S(1)}, f16[2,72,512]{2,1,0:T(8,128)(2,1)S(1)}, u32[]{:S(2)}, u32[]{:S(2)}) collective-permute-start(f16[2,72,512]{2,1,0:T(8,128)(2,1)S(1)} %convert_element_type.126), channel_id=1, source_target_pairs={{0,8},{8,16},{16,24},{24,0},{1,9},{9,17},{17,25},{25,1},{2,10},{10... | collective-permute-start | bytes 442376 | tf_op jit(solution)/shard_map/ppermute | solution.py:312
  73.7 9.2 %collective-permute-start.4 = (f16[2,72,512]{2,1,0:T(8,128)(2,1)S(1)}, f16[2,72,512]{2,1,0:T(8,128)(2,1)S(1)}, u32[]{:S(2)}, u32[]{:S(2)}) collective-permute-start(f16[2,72,512]{2,1,0:T(8,128)(2,1)S(1)} %convert_element_type.126), channel_id=1, source_target_pairs={{0,16},{8,24},{16,0},{24,8},{1,17},{9,25},{17,1},{25,9},{2,18},{10... | collective-permute-start | bytes 442376 | tf_op jit(solution)/shard_map/ppermute | solution.py:312
  74.2 9.4 %collective-permute-start.5 = (f16[2,72,512]{2,1,0:T(8,128)(2,1)S(1)}, f16[2,72,512]{2,1,0:T(8,128)(2,1)S(1)}, u32[]{:S(2)}, u32[]{:S(2)}) collective-permute-start(f16[2,72,512]{2,1,0:T(8,128)(2,1)S(1)} %convert_element_type.126), channel_id=1, source_target_pairs={{0,24},{8,0},{16,8},{24,16},{1,25},{9,1},{17,9},{25,17},{2,26},{10... | collective-permute-start | bytes 442376 | tf_op jit(solution)/shard_map/ppermute | solution.py:312
  89.8 8.9 %collective-permute-start.6 = (f16[2,136,512]{2,1,0:T(8,128)(2,1)S(1)}, f16[2,136,512]{2,1,0:T(8,128)(2,1)S(1)}, u32[]{:S(2)}, u32[]{:S(2)}) collective-permute-start(f16[2,136,512]{2,1,0:T(8,128)(2,1)S(1)} %convert_element_type.130), channel_id=1, source_target_pairs={{0,8},{8,16},{16,24},{24,0},{1,9},{9,17},{17,25},{25,1},{2,10},{10... | collective-permute-start | bytes 835592 | tf_op jit(solution)/shard_map/ppermute | solution.py:312
  108.0 8.0 %copy-start = (f32[2,136,512]{2,1,0:T(8,128)S(1)}, f32[2,136,512]{2,1,0:T(8,128)}, u32[]{:S(2)}) copy-start(f32[2,136,512]{2,1,0:T(8,128)} %get-tuple-element.33.refs_14_.refs_16_) | copy-start | bytes 1671172
  109.9 26.5 %all-to-all-start.1 = ((f16[8,136,128]{2,1,0:T(8,128)(2,1)}), f16[8,136,128]{2,1,0:T(8,128)(2,1)S(1)}, u32[]{:S(2)}, u32[]{:S(2)}) async-start(f16[8,136,128]{2,1,0:T(8,128)(2,1)} %convert_element_type.132), calls=%async_computation.1 | async-start | bytes 557056 | tf_op jit(solution)/shard_map/all_to_all | solution.py:400
  114.4 9.5 %collective-permute-start.7 = (f16[2,136,512]{2,1,0:T(8,128)(2,1)S(1)}, f16[2,136,512]{2,1,0:T(8,128)(2,1)S(1)}, u32[]{:S(2)}, u32[]{:S(2)}) collective-permute-start(f16[2,136,512]{2,1,0:T(8,128)(2,1)S(1)} %convert_element_type.130), channel_id=1, source_target_pairs={{0,16},{8,24},{16,0},{24,8},{1,17},{9,25},{17,1},{25,9},{2,18},{10... | collective-permute-start | bytes 835592 | tf_op jit(solution)/shard_map/ppermute | solution.py:312
  115.1 9.7 %collective-permute-start.8 = (f16[2,136,512]{2,1,0:T(8,128)(2,1)S(1)}, f16[2,136,512]{2,1,0:T(8,128)(2,1)S(1)}, u32[]{:S(2)}, u32[]{:S(2)}) collective-permute-start(f16[2,136,512]{2,1,0:T(8,128)(2,1)S(1)} %convert_element_type.130), channel_id=1, source_target_pairs={{0,24},{8,0},{16,8},{24,16},{1,25},{9,1},{17,9},{25,17},{2,26},{10... | collective-permute-start | bytes 835592 | tf_op jit(solution)/shard_map/ppermute | solution.py:312
  116.0 14.7 %collective-permute-start.9 = (f16[2,136,512]{2,1,0:T(8,128)(2,1)S(1)}, f16[2,136,512]{2,1,0:T(8,128)(2,1)S(1)}, u32[]{:S(2)}, u32[]{:S(2)}) collective-permute-start(f16[2,136,512]{2,1,0:T(8,128)(2,1)S(1)} %convert_element_type.136), channel_id=1, source_target_pairs={{0,8},{8,16},{16,24},{24,0},{1,9},{9,17},{17,25},{25,1},{2,10},{10... | collective-permute-start | bytes 835592 | tf_op jit(solution)/shard_map/ppermute | solution.py:312
  117.3 18.2 %collective-permute-start.10 = (f16[2,136,512]{2,1,0:T(8,128)(2,1)S(1)}, f16[2,136,512]{2,1,0:T(8,128)(2,1)S(1)}, u32[]{:S(2)}, u32[]{:S(2)}) collective-permute-start(f16[2,136,512]{2,1,0:T(8,128)(2,1)S(1)} %convert_element_type.136), channel_id=1, source_target_pairs={{0,16},{8,24},{16,0},{24,8},{1,17},{9,25},{17,1},{25,9},{2,18},{10... | collective-permute-start | bytes 835592 | tf_op jit(solution)/shard_map/ppermute | solution.py:312
  142.7 12.0 %collective-permute-start.11 = (f16[2,200,512]{2,1,0:T(8,128)(2,1)S(1)}, f16[2,200,512]{2,1,0:T(8,128)(2,1)S(1)}, u32[]{:S(2)}, u32[]{:S(2)}) collective-permute-start(f16[2,200,512]{2,1,0:T(8,128)(2,1)S(1)} %convert_element_type.139), channel_id=1, source_target_pairs={{0,8},{8,16},{16,24},{24,0},{1,9},{9,17},{17,25},{25,1},{2,10},{10... | collective-permute-start | bytes 1228808 | tf_op jit(solution)/shard_map/ppermute | solution.py:312
  161.5 6.9 %copy-start.1 = (f32[2,200,512]{2,1,0:T(8,128)S(1)}, f32[2,200,512]{2,1,0:T(8,128)}, u32[]{:S(2)}) copy-start(f32[2,200,512]{2,1,0:T(8,128)} %get-tuple-element.37.refs_22_.refs_24_) | copy-start | bytes 2457604
  163.5 34.7 %all-to-all-start.2 = ((f16[8,200,128]{2,1,0:T(8,128)(2,1)}), f16[8,200,128]{2,1,0:T(8,128)(2,1)S(1)}, u32[]{:S(2)}, u32[]{:S(2)}) async-start(f16[8,200,128]{2,1,0:T(8,128)(2,1)} %convert_element_type.141), calls=%async_computation.2 | async-start | bytes 819200 | tf_op jit(solution)/shard_map/all_to_all | solution.py:400
  167.8 21.0 %collective-permute-start.13 = (f16[2,200,512]{2,1,0:T(8,128)(2,1)S(1)}, f16[2,200,512]{2,1,0:T(8,128)(2,1)S(1)}, u32[]{:S(2)}, u32[]{:S(2)}) collective-permute-start(f16[2,200,512]{2,1,0:T(8,128)(2,1)S(1)} %convert_element_type.139), channel_id=1, source_target_pairs={{0,16},{8,24},{16,0},{24,8},{1,17},{9,25},{17,1},{25,9},{2,18},{10... | collective-permute-start | bytes 1228808 | tf_op jit(solution)/shard_map/ppermute | solution.py:312
  168.5 21.3 %collective-permute-start.14 = (f16[2,200,512]{2,1,0:T(8,128)(2,1)S(1)}, f16[2,200,512]{2,1,0:T(8,128)(2,1)S(1)}, u32[]{:S(2)}, u32[]{:S(2)}) collective-permute-start(f16[2,200,512]{2,1,0:T(8,128)(2,1)S(1)} %convert_element_type.145), channel_id=1, source_target_pairs={{0,8},{8,16},{16,24},{24,0},{1,9},{9,17},{17,25},{25,1},{2,10},{10... | collective-permute-start | bytes 1228808 | tf_op jit(solution)/shard_map/ppermute | solution.py:312
  169.0 28.2 %collective-permute-start.15 = (f16[2,200,512]{2,1,0:T(8,128)(2,1)S(1)}, f16[2,200,512]{2,1,0:T(8,128)(2,1)S(1)}, u32[]{:S(2)}, u32[]{:S(2)}) collective-permute-start(f16[2,200,512]{2,1,0:T(8,128)(2,1)S(1)} %convert_element_type.145), channel_id=1, source_target_pairs={{0,16},{8,24},{16,0},{24,8},{1,17},{9,25},{17,1},{25,9},{2,18},{10... | collective-permute-start | bytes 1228808 | tf_op jit(solution)/shard_map/ppermute | solution.py:312
  170.0 17.0 %collective-permute-start.12 = (f16[2,136,512]{2,1,0:T(8,128)(2,1)S(1)}, f16[2,136,512]{2,1,0:T(8,128)(2,1)S(1)}, u32[]{:S(2)}, u32[]{:S(2)}) collective-permute-start(f16[2,136,512]{2,1,0:T(8,128)(2,1)S(1)} %convert_element_type.136), channel_id=1, source_target_pairs={{0,24},{8,0},{16,8},{24,16},{1,25},{9,1},{17,9},{25,17},{2,26},{10... | collective-permute-start | bytes 835592 | tf_op jit(solution)/shard_map/ppermute | solution.py:312
  205.2 14.9 %collective-permute-start.16 = (f16[2,264,512]{2,1,0:T(8,128)(2,1)S(1)}, f16[2,264,512]{2,1,0:T(8,128)(2,1)S(1)}, u32[]{:S(2)}, u32[]{:S(2)}) collective-permute-start(f16[2,264,512]{2,1,0:T(8,128)(2,1)S(1)} %convert_element_type.148), channel_id=1, source_target_pairs={{0,8},{8,16},{16,24},{24,0},{1,9},{9,17},{17,25},{25,1},{2,10},{10... | collective-permute-start | bytes 1622024 | tf_op jit(solution)/shard_map/ppermute | solution.py:312
  228.0 7.2 %copy-start.2 = (f32[2,264,512]{2,1,0:T(8,128)S(1)}, f32[2,264,512]{2,1,0:T(8,128)}, u32[]{:S(2)}) copy-start(f32[2,264,512]{2,1,0:T(8,128)} %get-tuple-element.41.refs_30_) | copy-start | bytes 3244036
  230.2 32.9 %all-to-all-start.3 = ((f16[8,264,128]{2,1,0:T(8,128)(2,1)}), f16[8,264,128]{2,1,0:T(8,128)(2,1)S(1)}, u32[]{:S(2)}, u32[]{:S(2)}) async-start(f16[8,264,128]{2,1,0:T(8,128)(2,1)} %convert_element_type.150), calls=%async_computation.3 | async-start | bytes 1081344 | tf_op jit(solution)/shard_map/all_to_all | solution.py:400
  234.6 26.3 %collective-permute-start.18 = (f16[2,264,512]{2,1,0:T(8,128)(2,1)S(1)}, f16[2,264,512]{2,1,0:T(8,128)(2,1)S(1)}, u32[]{:S(2)}, u32[]{:S(2)}) collective-permute-start(f16[2,264,512]{2,1,0:T(8,128)(2,1)S(1)} %convert_element_type.148), channel_id=1, source_target_pairs={{0,16},{8,24},{16,0},{24,8},{1,17},{9,25},{17,1},{25,9},{2,18},{10... | collective-permute-start | bytes 1622024 | tf_op jit(solution)/shard_map/ppermute | solution.py:312
  235.3 26.7 %collective-permute-start.19 = (f16[2,264,512]{2,1,0:T(8,128)(2,1)S(1)}, f16[2,264,512]{2,1,0:T(8,128)(2,1)S(1)}, u32[]{:S(2)}, u32[]{:S(2)}) collective-permute-start(f16[2,264,512]{2,1,0:T(8,128)(2,1)S(1)} %convert_element_type.154), channel_id=1, source_target_pairs={{0,8},{8,16},{16,24},{24,0},{1,9},{9,17},{17,25},{25,1},{2,10},{10... | collective-permute-start | bytes 1622024 | tf_op jit(solution)/shard_map/ppermute | solution.py:312
  235.4 24.0 %collective-permute-start.17 = (f16[2,200,512]{2,1,0:T(8,128)(2,1)S(1)}, f16[2,200,512]{2,1,0:T(8,128)(2,1)S(1)}, u32[]{:S(2)}, u32[]{:S(2)}) collective-permute-start(f16[2,200,512]{2,1,0:T(8,128)(2,1)S(1)} %convert_element_type.139), channel_id=1, source_target_pairs={{0,24},{8,0},{16,8},{24,16},{1,25},{9,1},{17,9},{25,17},{2,26},{10... | collective-permute-start | bytes 1228808 | tf_op jit(solution)/shard_map/ppermute | solution.py:312
  269.4 1.8 copy-start.8
  269.4 2.6 copy-start.9
  269.4 3.3 copy-start.10
  270.9 17.9 %collective-permute-start.20 = (f16[2,328,512]{2,1,0:T(8,128)(2,1)S(1)}, f16[2,328,512]{2,1,0:T(8,128)(2,1)S(1)}, u32[]{:S(2)}, u32[]{:S(2)}) collective-permute-start(f16[2,328,512]{2,1,0:T(8,128)(2,1)S(1)} %convert_element_type.156), channel_id=1, source_target_pairs={{0,8},{8,16},{16,24},{24,0},{1,9},{9,17},{17,25},{25,1},{2,10},{10... | collective-permute-start | bytes 2015240 | tf_op jit(solution)/shard_map/ppermute | solution.py:312
  297.4 6.8 %copy-start.7 = (f32[2,2,64,512]{3,2,1,0:T(8,128)S(1)}, f32[2,2,64,512]{3,2,1,0:T(8,128)}, u32[]{:S(2)}) copy-start(f32[2,2,64,512]{3,2,1,0:T(8,128)} %get-tuple-element.31) | copy-start | bytes 1572868
  299.7 5.3 %copy-start.11 = (f32[2,64,512]{2,1,0:T(8,128)S(1)}, f32[2,64,512]{2,1,0:T(8,128)}, u32[]{:S(2)}) copy-start(f32[2,64,512]{2,1,0:T(8,128)} %get-tuple-element.46) | copy-start | bytes 786436
  299.7 6.1 %copy-start.6 = (f32[3,2,64,512]{3,2,1,0:T(8,128)S(1)}, f32[3,2,64,512]{3,2,1,0:T(8,128)}, u32[]{:S(2)}) copy-start(f32[3,2,64,512]{3,2,1,0:T(8,128)} %get-tuple-element.35) | copy-start | bytes 2359300
  299.7 23.0 %all-to-all-start.4 = ((f16[8,328,128]{2,1,0:T(8,128)(2,1)}), f16[8,328,128]{2,1,0:T(8,128)(2,1)S(1)}, u32[]{:S(2)}, u32[]{:S(2)}) async-start(f16[8,328,128]{2,1,0:T(8,128)(2,1)} %convert_element_type.158), calls=%async_computation.4 | async-start | bytes 1343488 | tf_op jit(solution)/shard_map/all_to_all | solution.py:400
  304.2 2.5 copy-start.12
  305.0 2.4 copy-start.5
  306.7 1.8 copy-start.13
  306.7 2.5 copy-start.4
Sparse Core Ops, SparseCore 0:
  10.2 67.0 all-gather.8
  78.9 53.4 all-gather.10
  134.0 63.3 all-gather.12

commit v4 on v3

--- a/solution.py
+++ b/solution.py
@@ -320,10 +320,7 @@
         return lax.all_gather(panel[first : first + count], "col", axis=0)
 
     whole_panel = [None] * levels
-    ones = [lax.all_gather(panel[0:1, n : n + 1], "col", axis=0) for n in range(npr)]
-    whole_panel[1] = (jnp.concatenate(ones, axis=2), 0)
-    groups = [(2, 3), (4,), (5,)] if levels == 6 else [(level,) for level in range(2, levels)]
-    for group in groups:
+    for group in [(level,) for level in range(1, levels)]:
         first = group[0] * (group[0] - 1) // 2
         both = gathered(first, sum(group))
         for level in group:
@@ -398,7 +395,7 @@
         crosses.append(made[0])
         ahead = () if last else spread(made[2], level, True)
         turned = lax.all_to_all(made[1].astype(F16), "col", 0, 0, tiled=True).astype(F32)
-        waits = [] if last else due[level]
+        waits = [] if last else due[level] + ([whole_panel[level + 1][0]] if level > 1 else [])
         out_shape = [shape(npr, rows, width)]
         if not last:
             out_shape.append(shape(npr, high + rows + TAIL, width))

time: 339 us -> 316 us (0.932)
  blocking collectives: 35 us -> 0 us
  waiting for transfers between devices: 105 us -> 119 us
    all_gather x2 -> x0, blocking collectives: 35 us -> none  [shards(): lax.all_gather(panel[0:1, n:n + 1], 'col', axis=0)]
    ppermute x21, waiting for transfers between devices: 92.5 us -> 102 us  [spread(): found.append(lax.ppermute(half, 'row', route).astype(F32))]
    all_gather x3 -> x5, waiting for transfers between devices: 0.02 us -> 4.63 us  [gathered(): return lax.all_gather(panel[first:first + count], 'col', axis=0)]
    slice x2 -> x5, local copies, waits for them, and re-layouts: 4.45 us -> 6.95 us  [gathered(): return lax.all_gather(panel[first:first + count], 'col', axis=0)]
    unnamed x37 -> x39, local copies, waits for them, and re-layouts: 7.21 us -> 7.22 us
  transfers between devices with their start and end apart: 29 -> 31, of which waited for: 15 -> 18; matrix products, arithmetic and copies ran while one was open for 15% -> 16% of each run, Pallas kernels for 19% -> 19%
where the time goes in v4:
time: 316 us; the launch traced here: 315 us
  waiting for transfers between devices  119 us (38%)
  Pallas kernels  76.8 us (24%)
  starting transfers between devices  43.8 us (14%)
  other arithmetic  42.5 us (13%)
  local copies, waits for them, and re-layouts  18.2 us (6%)
  between operations  14.1 us (4%)
    ppermute x21, waiting for transfers between devices, spread(): found.append(lax.ppermute(half, 'row', route).astype(F32))  102 us
    pallas_call x5, Pallas kernels, shards(): pl.pallas_call(functools.partial(cross_kernel, level, last, off, len(newe...  28.4 us
    ppermute x21, starting transfers between devices, spread(): found.append(lax.ppermute(half, 'row', route).astype(F32))  24.2 us
    pallas_call x4, Pallas kernels, shards(): pl.pallas_call(functools.partial(upper_kernel, level, off, spans, n_row,...  23.6 us
    pallas_call x5, Pallas kernels, shards(): pl.pallas_call(functools.partial(marginal_kernel, level, last, off, len(w...  22.9 us
    convert_element_type x21, other arithmetic, spread(): found.append(lax.ppermute(half, 'row', route).astype(F32))  19.7 us
    all_to_all x5, starting transfers between devices, shards(): lax.all_to_all(made[1].astype(F16), 'col', 0, 0, tiled=True).astype(F32)  19.5 us
    all_to_all x5, waiting for transfers between devices, shards(): lax.all_to_all(made[1].astype(F16), 'col', 0, 0, tiled=True).astype(F32)  12.3 us
  transfers between devices with their start and end apart: 31, of which 18 were waited for; matrix products, arithmetic and copies ran while one was open for 16% of the time, Pallas kernels for 19%

profile of v4, /device:TPU:0, one launch (start us, length us, event | category | flops | bytes accessed | tf_op | source)
XLA Modules:
  0.0 314.6 jit_solution(17915875091683392832)
XLA Ops:
  7.2 1.7 slice.33
  9.0 1.7 slice.35
  10.7 1.8 slice.37
  16.3 1.9 base.1
  19.2 3.9 %collective-permute-start.2 = (f16[2,72,512]{2,1,0:T(8,128)(2,1)S(1)}, f16[2,72,512]{2,1,0:T(8,128)(2,1)S(1)}, u32[]{:S(2)}, u32[]{:S(2)}) collective-permute-start(f16[2,72,512]{2,1,0:T(8,128)(2,1)S(1)} %convert_element_type.120), channel_id=1, source_target_pairs={{0,24},{8,0},{16,8},{24,16},{1,25},{9,1},{17,9},{25,17},{2,26},{10... | collective-permute-start | bytes 442376 | tf_op jit(solution)/shard_map/ppermute | solution.py:312
  24.3 3.2 %collective-permute-done.2 = f16[2,72,512]{2,1,0:T(8,128)(2,1)S(1)} collective-permute-done((f16[2,72,512]{2,1,0:T(8,128)(2,1)S(1)}, f16[2,72,512]{2,1,0:T(8,128)(2,1)S(1)}, u32[]{:S(2)}, u32[]{:S(2)}) %collective-permute-start.2) | collective-permute-done | bytes 147488 | tf_op jit(solution)/shard_map/ppermute | solution.py:312
  28.2 3.5 %collective-permute-done.1 = f16[2,72,512]{2,1,0:T(8,128)(2,1)S(1)} collective-permute-done((f16[2,72,512]{2,1,0:T(8,128)(2,1)S(1)}, f16[2,72,512]{2,1,0:T(8,128)(2,1)S(1)}, u32[]{:S(2)}, u32[]{:S(2)}) %collective-permute-start.1) | collective-permute-done | bytes 147488 | tf_op jit(solution)/shard_map/ppermute | solution.py:312
  34.4 3.7 %cross1.1 = (f32[1,2,64,512]{3,2,1,0:T(8,128)}, f32[8,72,128]{2,1,0:T(8,128)}, f32[2,72,512]{2,1,0:T(8,128)}) custom-call(s32[2]{0:T(128)} %pad_add_fusion.place.refs_0_, s32[5,8]{1,0:T(8,128)} %refs_1_.26, s32[6,8]{1,0:T(8,128)} %refs_1_.27, bf16[8,1,2,64,512]{4,3,2,1,0:T(8,128)(2,1)} %bitcast.46, f32[2,72,512]{2,1,0:T(8,128)} %get-tuple-element.26.refs_4_, ...), custom_call_target="tpu_custom_call" | custom-call | tf_op jit(solution)/shard_map/cross1/pallas_call | solution.py:378
  39.8 3.6 %all-to-all-start = ((f16[8,72,128]{2,1,0:T(8,128)(2,1)}), f16[8,72,128]{2,1,0:T(8,128)(2,1)S(1)}, u32[]{:S(2)}, u32[]{:S(2)}) async-start(f16[8,72,128]{2,1,0:T(8,128)(2,1)} %convert_element_type.124), calls=%async_computation | async-start | bytes 294912 | tf_op jit(solution)/shard_map/all_to_all | solution.py:397
  44.4 2.2 collective-permute-start.5
  47.7 3.1 collective-permute-done.5
  51.5 4.1 %collective-permute-done.4 = f16[2,72,512]{2,1,0:T(8,128)(2,1)S(1)} collective-permute-done((f16[2,72,512]{2,1,0:T(8,128)(2,1)S(1)}, f16[2,72,512]{2,1,0:T(8,128)(2,1)S(1)}, u32[]{:S(2)}, u32[]{:S(2)}) %collective-permute-start.4) | collective-permute-done | bytes 147488 | tf_op jit(solution)/shard_map/ppermute | solution.py:312
  57.9 3.6 %marginal1.1 = (f32[2,64,512]{2,1,0:T(8,128)}, f32[2,136,512]{2,1,0:T(8,128)}) custom-call(s32[2]{0:T(128)} %pad_add_fusion.place.refs_0_, s32[6,8]{1,0:T(8,128)} %refs_1_.27, bf16[8,1,2,64,512]{4,3,2,1,0:T(8,128)(2,1)} %bitcast.47, f32[8,72,128]{2,1,0:T(8,128)} %convert_element_type.125.refs_3_, f32[2,64,512]{2,1,0:T(8,128)} %get-tuple-element.53.refs_4_, ...), custom_call_target="tpu_custom_call" | custom-call | tf_op jit(solution)/shard_map/marginal1/pallas_call | solution.py:402
  62.7 8.9 %collective-permute-done.6 = f16[2,136,512]{2,1,0:T(8,128)(2,1)S(1)} collective-permute-done((f16[2,136,512]{2,1,0:T(8,128)(2,1)S(1)}, f16[2,136,512]{2,1,0:T(8,128)(2,1)S(1)}, u32[]{:S(2)}, u32[]{:S(2)}) %collective-permute-start.6) | collective-permute-done | bytes 278560 | tf_op jit(solution)/shard_map/ppermute | solution.py:312
  72.5 3.6 %upper2.1.refs_6_ = f32[2,64,512]{2,1,0:T(8,128)} custom-call(s32[2]{0:T(128)} %pad_add_fusion.place.refs_0_, s32[5,8]{1,0:T(8,128)} %refs_1_.26, s32[6,8]{1,0:T(8,128)} %refs_1_.27, bf16[8,2,2,64,512]{4,3,2,1,0:T(8,128)(2,1)} %bitcast.43, f32[2,72,512]{2,1,0:T(8,128)} %get-tuple-element.26.refs_4_, f32[2,72,512]{2,1,0:T(8,128)} %convert_element_type.121.refs_5_, ...), custom_call_target="tpu_custom_call" | custom-call | tf_op jit(solution)/shard_map/upper2/pallas_call | solution.py:357
  76.1 4.9 %cross2.1 = (f32[2,2,64,512]{3,2,1,0:T(8,128)}, f32[8,136,128]{2,1,0:T(8,128)}, f32[2,136,512]{2,1,0:T(8,128)}) custom-call(s32[2]{0:T(128)} %pad_add_fusion.place.refs_0_, s32[5,8]{1,0:T(8,128)} %refs_1_.26, s32[6,8]{1,0:T(8,128)} %refs_1_.27, bf16[8,2,2,64,512]{4,3,2,1,0:T(8,128)(2,1)} %bitcast.44, ...), custom_call_target="tpu_custom_call" | custom-call | tf_op jit(solution)/shard_map/cross2/pallas_call | solution.py:378
  81.0 1.8 convert_element_type.132
  82.9 3.5 %all-to-all-start.1 = ((f16[8,136,128]{2,1,0:T(8,128)(2,1)}), f16[8,136,128]{2,1,0:T(8,128)(2,1)S(1)}, u32[]{:S(2)}, u32[]{:S(2)}) async-start(f16[8,136,128]{2,1,0:T(8,128)(2,1)} %convert_element_type.132), calls=%async_computation.1 | async-start | bytes 557056 | tf_op jit(solution)/shard_map/all_to_all | solution.py:397
  90.5 5.3 %collective-permute-done.8 = f16[2,136,512]{2,1,0:T(8,128)(2,1)S(1)} collective-permute-done((f16[2,136,512]{2,1,0:T(8,128)(2,1)S(1)}, f16[2,136,512]{2,1,0:T(8,128)(2,1)S(1)}, u32[]{:S(2)}, u32[]{:S(2)}) %collective-permute-start.8) | collective-permute-done | bytes 278560 | tf_op jit(solution)/shard_map/ppermute | solution.py:312
  96.7 5.9 %collective-permute-done.7 = f16[2,136,512]{2,1,0:T(8,128)(2,1)S(1)} collective-permute-done((f16[2,136,512]{2,1,0:T(8,128)(2,1)S(1)}, f16[2,136,512]{2,1,0:T(8,128)(2,1)S(1)}, u32[]{:S(2)}, u32[]{:S(2)}) %collective-permute-start.7) | collective-permute-done | bytes 278560 | tf_op jit(solution)/shard_map/ppermute | solution.py:312
  103.5 4.4 %collective-permute-done.10 = f16[2,136,512]{2,1,0:T(8,128)(2,1)S(1)} collective-permute-done((f16[2,136,512]{2,1,0:T(8,128)(2,1)S(1)}, f16[2,136,512]{2,1,0:T(8,128)(2,1)S(1)}, u32[]{:S(2)}, u32[]{:S(2)}) %collective-permute-start.10) | collective-permute-done | bytes 278560 | tf_op jit(solution)/shard_map/ppermute | solution.py:312
  110.5 3.3 %all-gather.15.cloned.1.call-done = bf16[24,2,64,512]{3,2,1,0:T(8,128)(2,1)} async-done(((bf16[3,2,64,512]{3,2,1,0:T(8,128)(2,1)}), bf16[24,2,64,512]{3,2,1,0:T(8,128)(2,1)}) %all-gather.15.cloned.1.call-update) | async-done | bytes 3145744 | tf_op jit(solution)/shard_map/all_gather | solution.py:320
  113.9 4.1 %marginal2.1 = (f32[2,64,512]{2,1,0:T(8,128)}, f32[2,200,512]{2,1,0:T(8,128)}) custom-call(s32[2]{0:T(128)} %pad_add_fusion.place.refs_0_, s32[6,8]{1,0:T(8,128)} %refs_1_.27, bf16[8,2,2,64,512]{4,3,2,1,0:T(8,128)(2,1)} %bitcast.45, f32[8,136,128]{2,1,0:T(8,128)} %convert_element_type.133.refs_3_, f32[2,64,512]{2,1,0:T(8,128)} %get-tuple-element.52.refs_4_, ...), custom_call_target="tpu_custom_call" | custom-call | tf_op jit(solution)/shard_map/marginal2/pallas_call | solution.py:402
  120.7 5.2 %upper3.1.refs_6_ = f32[2,128,512]{2,1,0:T(8,128)} custom-call(s32[2]{0:T(128)} %pad_add_fusion.place.refs_0_, s32[5,8]{1,0:T(8,128)} %refs_1_.26, s32[6,8]{1,0:T(8,128)} %refs_1_.27, bf16[8,3,2,64,512]{4,3,2,1,0:T(8,128)(2,1)} %bitcast.40, f32[2,72,512]{2,1,0:T(8,128)} %get-tuple-element.26.refs_4_, f32[2,72,512]{2,1,0:T(8,128)} %convert_element_type.121.refs_5_, ...), custom_call_target="tpu_custom_call" | custom-call | tf_op jit(solution)/shard_map/upper3/pallas_call | solution.py:357
  126.0 5.8 %collective-permute-done.11 = f16[2,200,512]{2,1,0:T(8,128)(2,1)S(1)} collective-permute-done((f16[2,200,512]{2,1,0:T(8,128)(2,1)S(1)}, f16[2,200,512]{2,1,0:T(8,128)(2,1)S(1)}, u32[]{:S(2)}, u32[]{:S(2)}) %collective-permute-start.11) | collective-permute-done | bytes 409632 | tf_op jit(solution)/shard_map/ppermute | solution.py:312
  132.8 5.7 %cross3.1 = (f32[3,2,64,512]{3,2,1,0:T(8,128)}, f32[8,200,128]{2,1,0:T(8,128)}, f32[2,200,512]{2,1,0:T(8,128)}) custom-call(s32[2]{0:T(128)} %pad_add_fusion.place.refs_0_, s32[5,8]{1,0:T(8,128)} %refs_1_.26, s32[6,8]{1,0:T(8,128)} %refs_1_.27, bf16[8,3,2,64,512]{4,3,2,1,0:T(8,128)(2,1)} %bitcast.41, ...), custom_call_target="tpu_custom_call" | custom-call | tf_op jit(solution)/shard_map/cross3/pallas_call | solution.py:378
  138.5 2.0 convert_element_type.141
  140.5 3.5 %all-to-all-start.2 = ((f16[8,200,128]{2,1,0:T(8,128)(2,1)}), f16[8,200,128]{2,1,0:T(8,128)(2,1)S(1)}, u32[]{:S(2)}, u32[]{:S(2)}) async-start(f16[8,200,128]{2,1,0:T(8,128)(2,1)} %convert_element_type.141), calls=%async_computation.2 | async-start | bytes 819200 | tf_op jit(solution)/shard_map/all_to_all | solution.py:397
  146.8 2.3 collective-permute-start.12
  149.1 15.2 %collective-permute-done.12 = f16[2,136,512]{2,1,0:T(8,128)(2,1)S(1)} collective-permute-done((f16[2,136,512]{2,1,0:T(8,128)(2,1)S(1)}, f16[2,136,512]{2,1,0:T(8,128)(2,1)S(1)}, u32[]{:S(2)}, u32[]{:S(2)}) %collective-permute-start.12) | collective-permute-done | bytes 278560 | tf_op jit(solution)/shard_map/ppermute | solution.py:312
  166.2 7.1 %collective-permute-done.15 = f16[2,200,512]{2,1,0:T(8,128)(2,1)S(1)} collective-permute-done((f16[2,200,512]{2,1,0:T(8,128)(2,1)S(1)}, f16[2,200,512]{2,1,0:T(8,128)(2,1)S(1)}, u32[]{:S(2)}, u32[]{:S(2)}) %collective-permute-start.15) | collective-permute-done | bytes 409632 | tf_op jit(solution)/shard_map/ppermute | solution.py:312
  176.3 5.1 %marginal3.1 = (f32[2,64,512]{2,1,0:T(8,128)}, f32[2,264,512]{2,1,0:T(8,128)}) custom-call(s32[2]{0:T(128)} %pad_add_fusion.place.refs_0_, s32[6,8]{1,0:T(8,128)} %refs_1_.27, bf16[8,3,2,64,512]{4,3,2,1,0:T(8,128)(2,1)} %bitcast.42, f32[8,200,128]{2,1,0:T(8,128)} %convert_element_type.142.refs_3_, f32[2,64,512]{2,1,0:T(8,128)} %get-tuple-element.51.refs_4_, ...), custom_call_target="tpu_custom_call" | custom-call | tf_op jit(solution)/shard_map/marginal3/pallas_call | solution.py:402
  182.9 6.5 %upper4.1.refs_6_ = f32[2,192,512]{2,1,0:T(8,128)} custom-call(s32[2]{0:T(128)} %pad_add_fusion.place.refs_0_, s32[5,8]{1,0:T(8,128)} %refs_1_.26, s32[6,8]{1,0:T(8,128)} %refs_1_.27, bf16[8,4,2,64,512]{4,3,2,1,0:T(8,128)(2,1)} %bitcast.36, f32[2,72,512]{2,1,0:T(8,128)} %get-tuple-element.26.refs_4_, f32[2,72,512]{2,1,0:T(8,128)} %convert_element_type.121.refs_5_, ...), custom_call_target="tpu_custom_call" | custom-call | tf_op jit(solution)/shard_map/upper4/pallas_call | solution.py:357
  189.5 7.9 %collective-permute-done.16 = f16[2,264,512]{2,1,0:T(8,128)(2,1)S(1)} collective-permute-done((f16[2,264,512]{2,1,0:T(8,128)(2,1)S(1)}, f16[2,264,512]{2,1,0:T(8,128)(2,1)S(1)}, u32[]{:S(2)}, u32[]{:S(2)}) %collective-permute-start.16) | collective-permute-done | bytes 540704 | tf_op jit(solution)/shard_map/ppermute | solution.py:312
  198.5 6.9 %cross4.1 = (f32[4,2,64,512]{3,2,1,0:T(8,128)}, f32[8,264,128]{2,1,0:T(8,128)}, f32[2,264,512]{2,1,0:T(8,128)}) custom-call(s32[2]{0:T(128)} %pad_add_fusion.place.refs_0_, s32[5,8]{1,0:T(8,128)} %refs_1_.26, s32[6,8]{1,0:T(8,128)} %refs_1_.27, bf16[8,4,2,64,512]{4,3,2,1,0:T(8,128)(2,1)} %bitcast.37, f32[2,264,512]{2,1,0:T(8,128)} %get-tuple-element.38.refs_4_.refs_27_, ...), custom_call_target="tpu_custom_call" | custom-call | tf_op jit(solution)/shard_map/cross4/pallas_call | solution.py:378
  205.4 2.2 convert_element_type.150
  207.6 4.5 %all-to-all-start.3 = ((f16[8,264,128]{2,1,0:T(8,128)(2,1)}), f16[8,264,128]{2,1,0:T(8,128)(2,1)S(1)}, u32[]{:S(2)}, u32[]{:S(2)}) async-start(f16[8,264,128]{2,1,0:T(8,128)(2,1)} %convert_element_type.150), calls=%async_computation.3 | async-start | bytes 1081344 | tf_op jit(solution)/shard_map/all_to_all | solution.py:397
  213.8 2.9 collective-permute-start.17
  216.7 20.2 %collective-permute-done.17 = f16[2,200,512]{2,1,0:T(8,128)(2,1)S(1)} collective-permute-done((f16[2,200,512]{2,1,0:T(8,128)(2,1)S(1)}, f16[2,200,512]{2,1,0:T(8,128)(2,1)S(1)}, u32[]{:S(2)}, u32[]{:S(2)}) %collective-permute-start.17) | collective-permute-done | bytes 409632 | tf_op jit(solution)/shard_map/ppermute | solution.py:312
  241.7 5.2 %marginal4.1 = (f32[2,64,512]{2,1,0:T(8,128)}, f32[2,328,512]{2,1,0:T(8,128)}) custom-call(s32[2]{0:T(128)} %pad_add_fusion.place.refs_0_, s32[6,8]{1,0:T(8,128)} %refs_1_.27, bf16[8,4,2,64,512]{4,3,2,1,0:T(8,128)(2,1)} %bitcast.38, f32[8,264,128]{2,1,0:T(8,128)} %convert_element_type.151.refs_3_, f32[2,64,512]{2,1,0:T(8,128)} %get-tuple-element.55.refs_4_, ...), custom_call_target="tpu_custom_call" | custom-call | tf_op jit(solution)/shard_map/marginal4/pallas_call | solution.py:402
  250.9 8.2 %upper5.1.refs_6_ = f32[2,256,512]{2,1,0:T(8,128)} custom-call(s32[2]{0:T(128)} %pad_add_fusion.place.refs_0_, s32[5,8]{1,0:T(8,128)} %refs_1_.26, s32[6,8]{1,0:T(8,128)} %refs_1_.27, bf16[8,5,2,64,512]{4,3,2,1,0:T(8,128)(2,1)} %bitcast.32, f32[2,72,512]{2,1,0:T(8,128)} %get-tuple-element.26.refs_4_, f32[2,72,512]{2,1,0:T(8,128)} %convert_element_type.121.refs_5_, ...), custom_call_target="tpu_custom_call" | custom-call | tf_op jit(solution)/shard_map/upper5/pallas_call | solution.py:357
  259.1 7.2 %collective-permute-done.20 = f16[2,328,512]{2,1,0:T(8,128)(2,1)S(1)} collective-permute-done((f16[2,328,512]{2,1,0:T(8,128)(2,1)S(1)}, f16[2,328,512]{2,1,0:T(8,128)(2,1)S(1)}, u32[]{:S(2)}, u32[]{:S(2)}) %collective-permute-start.20) | collective-permute-done | bytes 671776 | tf_op jit(solution)/shard_map/ppermute | solution.py:312
  267.7 7.3 %cross5.1 = (f32[5,2,64,512]{3,2,1,0:T(8,128)}, f32[8,328,128]{2,1,0:T(8,128)}) custom-call(s32[2]{0:T(128)} %pad_add_fusion.place.refs_0_, s32[5,8]{1,0:T(8,128)} %refs_1_.26, s32[6,8]{1,0:T(8,128)} %refs_1_.27, bf16[8,5,2,64,512]{4,3,2,1,0:T(8,128)(2,1)} %bitcast.33, f32[2,328,512]{2,1,0:T(8,128)} %get-tuple-element.42.refs_4_, ...), custom_call_target="tpu_custom_call" | custom-call | tf_op jit(solution)/shard_map/cross5/pallas_call | solution.py:378
  275.0 2.4 convert_element_type.158
  277.3 4.5 %all-to-all-start.4 = ((f16[8,328,128]{2,1,0:T(8,128)(2,1)}), f16[8,328,128]{2,1,0:T(8,128)(2,1)S(1)}, u32[]{:S(2)}, u32[]{:S(2)}) async-start(f16[8,328,128]{2,1,0:T(8,128)(2,1)} %convert_element_type.158), calls=%async_computation.4 | async-start | bytes 1343488 | tf_op jit(solution)/shard_map/all_to_all | solution.py:397
  288.1 12.3 %all-to-all-done.4 = f16[8,328,128]{2,1,0:T(8,128)(2,1)S(1)} async-done(((f16[8,328,128]{2,1,0:T(8,128)(2,1)}), f16[8,328,128]{2,1,0:T(8,128)(2,1)S(1)}, u32[]{:S(2)}, u32[]{:S(2)}) %all-to-all-start.4) | async-done | bytes 671776 | tf_op jit(solution)/shard_map/all_to_all | solution.py:397
  301.5 4.9 %marginal5.1 = f32[2,64,512]{2,1,0:T(8,128)} custom-call(s32[2]{0:T(128)} %pad_add_fusion.place.refs_0_, s32[6,8]{1,0:T(8,128)} %refs_1_.27, bf16[8,5,2,64,512]{4,3,2,1,0:T(8,128)(2,1)} %bitcast.34, f32[8,328,128]{2,1,0:T(8,128)} %convert_element_type.159.refs_3_, f32[2,64,512]{2,1,0:T(8,128)} %get-tuple-element.50.refs_4_), custom_call_target="tpu_custom_call" | custom-call | tf_op jit(solution)/shard_map/marginal5/pallas_call | solution.py:402
  306.4 1.7 bitcast_dynamic-update-slice_fusion
  (122 shorter events, 60.2 us)
Async XLA Ops:
  7.2 5.4 %copy-start.3 = (bf16[15,2,64,512]{3,2,1,0:T(8,128)(2,1)S(1)}, bf16[15,2,64,512]{3,2,1,0:T(8,128)(2,1)}, u32[]{:S(2)}) copy-start(bf16[15,2,64,512]{3,2,1,0:T(8,128)(2,1)} %param.4) | copy-start | bytes 5898244
  7.2 27.3 %all-gather.11.cloned.1.call-start = ((), (), s32[]{:S(2)}) async-start(), calls=%async_computation.5 | async-start | bytes 1179648 | tf_op jit(solution)/shard_map/all_gather | solution.py:320
  8.9 63.5 %all-gather.13.cloned.1.call-start = ((), (), s32[]{:S(2)}) async-start(), calls=%async_computation.6 | async-start | bytes 2359296 | tf_op jit(solution)/shard_map/all_gather | solution.py:320
  10.7 103.2 %all-gather.15.cloned.1.call-start = ((), (), s32[]{:S(2)}) async-start(), calls=%async_computation.7 | async-start | bytes 3538944 | tf_op jit(solution)/shard_map/all_gather | solution.py:320
  12.5 2.6 copy-start.4
  12.6 163.7 %all-gather.17.cloned.1.call-start = ((), (), s32[]{:S(2)}) async-start(), calls=%async_computation.8 | async-start | bytes 4718592 | tf_op jit(solution)/shard_map/all_gather | solution.py:320
  13.5 228.1 %all-gather.19.cloned.1.call-start = ((), (), s32[]{:S(2)}) async-start(), calls=%async_computation.9 | async-start | bytes 5898240 | tf_op jit(solution)/shard_map/all_gather | solution.py:320
  19.2 8.2 %collective-permute-start.2 = (f16[2,72,512]{2,1,0:T(8,128)(2,1)S(1)}, f16[2,72,512]{2,1,0:T(8,128)(2,1)S(1)}, u32[]{:S(2)}, u32[]{:S(2)}) collective-permute-start(f16[2,72,512]{2,1,0:T(8,128)(2,1)S(1)} %convert_element_type.120), channel_id=1, source_target_pairs={{0,24},{8,0},{16,8},{24,16},{1,25},{9,1},{17,9},{25,17},{2,26},{10... | collective-permute-start | bytes 442376 | tf_op jit(solution)/shard_map/ppermute | solution.py:312
  23.2 8.5 %collective-permute-start.1 = (f16[2,72,512]{2,1,0:T(8,128)(2,1)S(1)}, f16[2,72,512]{2,1,0:T(8,128)(2,1)S(1)}, u32[]{:S(2)}, u32[]{:S(2)}) collective-permute-start(f16[2,72,512]{2,1,0:T(8,128)(2,1)S(1)} %convert_element_type.120), channel_id=1, source_target_pairs={{0,16},{8,24},{16,0},{24,8},{1,17},{9,25},{17,1},{25,9},{2,18},{10... | collective-permute-start | bytes 442376 | tf_op jit(solution)/shard_map/ppermute | solution.py:312
  23.7 8.7 %collective-permute-start = (f16[2,72,512]{2,1,0:T(8,128)(2,1)S(1)}, f16[2,72,512]{2,1,0:T(8,128)(2,1)S(1)}, u32[]{:S(2)}, u32[]{:S(2)}) collective-permute-start(f16[2,72,512]{2,1,0:T(8,128)(2,1)S(1)} %convert_element_type.120), channel_id=1, source_target_pairs={{0,8},{8,16},{16,24},{24,0},{1,9},{9,17},{17,25},{25,1},{2,10},{10... | collective-permute-start | bytes 442376 | tf_op jit(solution)/shard_map/ppermute | solution.py:312
  39.8 17.4 %all-to-all-start = ((f16[8,72,128]{2,1,0:T(8,128)(2,1)}), f16[8,72,128]{2,1,0:T(8,128)(2,1)S(1)}, u32[]{:S(2)}, u32[]{:S(2)}) async-start(f16[8,72,128]{2,1,0:T(8,128)(2,1)} %convert_element_type.124), calls=%async_computation | async-start | bytes 294912 | tf_op jit(solution)/shard_map/all_to_all | solution.py:397
  44.4 6.4 %collective-permute-start.5 = (f16[2,72,512]{2,1,0:T(8,128)(2,1)S(1)}, f16[2,72,512]{2,1,0:T(8,128)(2,1)S(1)}, u32[]{:S(2)}, u32[]{:S(2)}) collective-permute-start(f16[2,72,512]{2,1,0:T(8,128)(2,1)S(1)} %convert_element_type.126), channel_id=1, source_target_pairs={{0,24},{8,0},{16,8},{24,16},{1,25},{9,1},{17,9},{25,17},{2,26},{10... | collective-permute-start | bytes 442376 | tf_op jit(solution)/shard_map/ppermute | solution.py:312
  46.6 9.1 %collective-permute-start.4 = (f16[2,72,512]{2,1,0:T(8,128)(2,1)S(1)}, f16[2,72,512]{2,1,0:T(8,128)(2,1)S(1)}, u32[]{:S(2)}, u32[]{:S(2)}) collective-permute-start(f16[2,72,512]{2,1,0:T(8,128)(2,1)S(1)} %convert_element_type.126), channel_id=1, source_target_pairs={{0,16},{8,24},{16,0},{24,8},{1,17},{9,25},{17,1},{25,9},{2,18},{10... | collective-permute-start | bytes 442376 | tf_op jit(solution)/shard_map/ppermute | solution.py:312
  47.1 9.3 %collective-permute-start.3 = (f16[2,72,512]{2,1,0:T(8,128)(2,1)S(1)}, f16[2,72,512]{2,1,0:T(8,128)(2,1)S(1)}, u32[]{:S(2)}, u32[]{:S(2)}) collective-permute-start(f16[2,72,512]{2,1,0:T(8,128)(2,1)S(1)} %convert_element_type.126), channel_id=1, source_target_pairs={{0,8},{8,16},{16,24},{24,0},{1,9},{9,17},{17,25},{25,1},{2,10},{10... | collective-permute-start | bytes 442376 | tf_op jit(solution)/shard_map/ppermute | solution.py:312
  62.6 9.0 %collective-permute-start.6 = (f16[2,136,512]{2,1,0:T(8,128)(2,1)S(1)}, f16[2,136,512]{2,1,0:T(8,128)(2,1)S(1)}, u32[]{:S(2)}, u32[]{:S(2)}) collective-permute-start(f16[2,136,512]{2,1,0:T(8,128)(2,1)S(1)} %convert_element_type.130), channel_id=1, source_target_pairs={{0,8},{8,16},{16,24},{24,0},{1,9},{9,17},{17,25},{25,1},{2,10},{10... | collective-permute-start | bytes 835592 | tf_op jit(solution)/shard_map/ppermute | solution.py:312
  81.0 7.1 %copy-start = (f32[2,136,512]{2,1,0:T(8,128)S(1)}, f32[2,136,512]{2,1,0:T(8,128)}, u32[]{:S(2)}) copy-start(f32[2,136,512]{2,1,0:T(8,128)} %get-tuple-element.33.refs_14_.refs_16_) | copy-start | bytes 1671172
  82.9 26.8 %all-to-all-start.1 = ((f16[8,136,128]{2,1,0:T(8,128)(2,1)}), f16[8,136,128]{2,1,0:T(8,128)(2,1)S(1)}, u32[]{:S(2)}, u32[]{:S(2)}) async-start(f16[8,136,128]{2,1,0:T(8,128)(2,1)} %convert_element_type.132), calls=%async_computation.1 | async-start | bytes 557056 | tf_op jit(solution)/shard_map/all_to_all | solution.py:397
  86.4 9.5 %collective-permute-start.8 = (f16[2,136,512]{2,1,0:T(8,128)(2,1)S(1)}, f16[2,136,512]{2,1,0:T(8,128)(2,1)S(1)}, u32[]{:S(2)}, u32[]{:S(2)}) collective-permute-start(f16[2,136,512]{2,1,0:T(8,128)(2,1)S(1)} %convert_element_type.130), channel_id=1, source_target_pairs={{0,24},{8,0},{16,8},{24,16},{1,25},{9,1},{17,9},{25,17},{2,26},{10... | collective-permute-start | bytes 835592 | tf_op jit(solution)/shard_map/ppermute | solution.py:312
  87.2 15.5 %collective-permute-start.7 = (f16[2,136,512]{2,1,0:T(8,128)(2,1)S(1)}, f16[2,136,512]{2,1,0:T(8,128)(2,1)S(1)}, u32[]{:S(2)}, u32[]{:S(2)}) collective-permute-start(f16[2,136,512]{2,1,0:T(8,128)(2,1)S(1)} %convert_element_type.130), channel_id=1, source_target_pairs={{0,16},{8,24},{16,0},{24,8},{1,17},{9,25},{17,1},{25,9},{2,18},{10... | collective-permute-start | bytes 835592 | tf_op jit(solution)/shard_map/ppermute | solution.py:312
  88.2 19.7 %collective-permute-start.10 = (f16[2,136,512]{2,1,0:T(8,128)(2,1)S(1)}, f16[2,136,512]{2,1,0:T(8,128)(2,1)S(1)}, u32[]{:S(2)}, u32[]{:S(2)}) collective-permute-start(f16[2,136,512]{2,1,0:T(8,128)(2,1)S(1)} %convert_element_type.136), channel_id=1, source_target_pairs={{0,16},{8,24},{16,0},{24,8},{1,17},{9,25},{17,1},{25,9},{2,18},{10... | collective-permute-start | bytes 835592 | tf_op jit(solution)/shard_map/ppermute | solution.py:312
  89.3 19.5 %collective-permute-start.9 = (f16[2,136,512]{2,1,0:T(8,128)(2,1)S(1)}, f16[2,136,512]{2,1,0:T(8,128)(2,1)S(1)}, u32[]{:S(2)}, u32[]{:S(2)}) collective-permute-start(f16[2,136,512]{2,1,0:T(8,128)(2,1)S(1)} %convert_element_type.136), channel_id=1, source_target_pairs={{0,8},{8,16},{16,24},{24,0},{1,9},{9,17},{17,25},{25,1},{2,10},{10... | collective-permute-start | bytes 835592 | tf_op jit(solution)/shard_map/ppermute | solution.py:312
  119.2 12.5 %collective-permute-start.11 = (f16[2,200,512]{2,1,0:T(8,128)(2,1)S(1)}, f16[2,200,512]{2,1,0:T(8,128)(2,1)S(1)}, u32[]{:S(2)}, u32[]{:S(2)}) collective-permute-start(f16[2,200,512]{2,1,0:T(8,128)(2,1)S(1)} %convert_element_type.139), channel_id=1, source_target_pairs={{0,8},{8,16},{16,24},{24,0},{1,9},{9,17},{17,25},{25,1},{2,10},{10... | collective-permute-start | bytes 1228808 | tf_op jit(solution)/shard_map/ppermute | solution.py:312
  138.5 7.1 %copy-start.1 = (f32[2,200,512]{2,1,0:T(8,128)S(1)}, f32[2,200,512]{2,1,0:T(8,128)}, u32[]{:S(2)}) copy-start(f32[2,200,512]{2,1,0:T(8,128)} %get-tuple-element.37.refs_22_.refs_24_) | copy-start | bytes 2457604
  140.5 34.8 %all-to-all-start.2 = ((f16[8,200,128]{2,1,0:T(8,128)(2,1)}), f16[8,200,128]{2,1,0:T(8,128)(2,1)S(1)}, u32[]{:S(2)}, u32[]{:S(2)}) async-start(f16[8,200,128]{2,1,0:T(8,128)(2,1)} %convert_element_type.141), calls=%async_computation.2 | async-start | bytes 819200 | tf_op jit(solution)/shard_map/all_to_all | solution.py:397
  144.0 21.2 %collective-permute-start.13 = (f16[2,200,512]{2,1,0:T(8,128)(2,1)S(1)}, f16[2,200,512]{2,1,0:T(8,128)(2,1)S(1)}, u32[]{:S(2)}, u32[]{:S(2)}) collective-permute-start(f16[2,200,512]{2,1,0:T(8,128)(2,1)S(1)} %convert_element_type.139), channel_id=1, source_target_pairs={{0,16},{8,24},{16,0},{24,8},{1,17},{9,25},{17,1},{25,9},{2,18},{10... | collective-permute-start | bytes 1228808 | tf_op jit(solution)/shard_map/ppermute | solution.py:312
  145.6 27.7 %collective-permute-start.15 = (f16[2,200,512]{2,1,0:T(8,128)(2,1)S(1)}, f16[2,200,512]{2,1,0:T(8,128)(2,1)S(1)}, u32[]{:S(2)}, u32[]{:S(2)}) collective-permute-start(f16[2,200,512]{2,1,0:T(8,128)(2,1)S(1)} %convert_element_type.145), channel_id=1, source_target_pairs={{0,16},{8,24},{16,0},{24,8},{1,17},{9,25},{17,1},{25,9},{2,18},{10... | collective-permute-start | bytes 1228808 | tf_op jit(solution)/shard_map/ppermute | solution.py:312
  146.2 28.1 %collective-permute-start.14 = (f16[2,200,512]{2,1,0:T(8,128)(2,1)S(1)}, f16[2,200,512]{2,1,0:T(8,128)(2,1)S(1)}, u32[]{:S(2)}, u32[]{:S(2)}) collective-permute-start(f16[2,200,512]{2,1,0:T(8,128)(2,1)S(1)} %convert_element_type.145), channel_id=1, source_target_pairs={{0,8},{8,16},{16,24},{24,0},{1,9},{9,17},{17,25},{25,1},{2,10},{10... | collective-permute-start | bytes 1228808 | tf_op jit(solution)/shard_map/ppermute | solution.py:312
  146.8 17.5 %collective-permute-start.12 = (f16[2,136,512]{2,1,0:T(8,128)(2,1)S(1)}, f16[2,136,512]{2,1,0:T(8,128)(2,1)S(1)}, u32[]{:S(2)}, u32[]{:S(2)}) collective-permute-start(f16[2,136,512]{2,1,0:T(8,128)(2,1)S(1)} %convert_element_type.136), channel_id=1, source_target_pairs={{0,24},{8,0},{16,8},{24,16},{1,25},{9,1},{17,9},{25,17},{2,26},{10... | collective-permute-start | bytes 835592 | tf_op jit(solution)/shard_map/ppermute | solution.py:312
  182.7 14.7 %collective-permute-start.16 = (f16[2,264,512]{2,1,0:T(8,128)(2,1)S(1)}, f16[2,264,512]{2,1,0:T(8,128)(2,1)S(1)}, u32[]{:S(2)}, u32[]{:S(2)}) collective-permute-start(f16[2,264,512]{2,1,0:T(8,128)(2,1)S(1)} %convert_element_type.148), channel_id=1, source_target_pairs={{0,8},{8,16},{16,24},{24,0},{1,9},{9,17},{17,25},{25,1},{2,10},{10... | collective-permute-start | bytes 1622024 | tf_op jit(solution)/shard_map/ppermute | solution.py:312
  205.4 8.2 %copy-start.2 = (f32[2,264,512]{2,1,0:T(8,128)S(1)}, f32[2,264,512]{2,1,0:T(8,128)}, u32[]{:S(2)}) copy-start(f32[2,264,512]{2,1,0:T(8,128)} %get-tuple-element.41.refs_30_) | copy-start | bytes 3244036
  207.6 33.0 %all-to-all-start.3 = ((f16[8,264,128]{2,1,0:T(8,128)(2,1)}), f16[8,264,128]{2,1,0:T(8,128)(2,1)S(1)}, u32[]{:S(2)}, u32[]{:S(2)}) async-start(f16[8,264,128]{2,1,0:T(8,128)(2,1)} %convert_element_type.150), calls=%async_computation.3 | async-start | bytes 1081344 | tf_op jit(solution)/shard_map/all_to_all | solution.py:397
  212.1 26.3 %collective-permute-start.18 = (f16[2,264,512]{2,1,0:T(8,128)(2,1)S(1)}, f16[2,264,512]{2,1,0:T(8,128)(2,1)S(1)}, u32[]{:S(2)}, u32[]{:S(2)}) collective-permute-start(f16[2,264,512]{2,1,0:T(8,128)(2,1)S(1)} %convert_element_type.148), channel_id=1, source_target_pairs={{0,16},{8,24},{16,0},{24,8},{1,17},{9,25},{17,1},{25,9},{2,18},{10... | collective-permute-start | bytes 1622024 | tf_op jit(solution)/shard_map/ppermute | solution.py:312
  213.7 25.8 %collective-permute-start.19 = (f16[2,264,512]{2,1,0:T(8,128)(2,1)S(1)}, f16[2,264,512]{2,1,0:T(8,128)(2,1)S(1)}, u32[]{:S(2)}, u32[]{:S(2)}) collective-permute-start(f16[2,264,512]{2,1,0:T(8,128)(2,1)S(1)} %convert_element_type.154), channel_id=1, source_target_pairs={{0,8},{8,16},{16,24},{24,0},{1,9},{9,17},{17,25},{25,1},{2,10},{10... | collective-permute-start | bytes 1622024 | tf_op jit(solution)/shard_map/ppermute | solution.py:312
  213.8 23.2 %collective-permute-start.17 = (f16[2,200,512]{2,1,0:T(8,128)(2,1)S(1)}, f16[2,200,512]{2,1,0:T(8,128)(2,1)S(1)}, u32[]{:S(2)}, u32[]{:S(2)}) collective-permute-start(f16[2,200,512]{2,1,0:T(8,128)(2,1)S(1)} %convert_element_type.139), channel_id=1, source_target_pairs={{0,24},{8,0},{16,8},{24,16},{1,25},{9,1},{17,9},{25,17},{2,26},{10... | collective-permute-start | bytes 1228808 | tf_op jit(solution)/shard_map/ppermute | solution.py:312
  246.9 1.8 copy-start.9
  246.9 2.6 copy-start.10
  246.9 3.3 %copy-start.11 = (f32[2,64,512]{2,1,0:T(8,128)S(1)}, f32[2,64,512]{2,1,0:T(8,128)}, u32[]{:S(2)}) copy-start(f32[2,64,512]{2,1,0:T(8,128)} %get-tuple-element.45) | copy-start | bytes 786436
  248.4 17.9 %collective-permute-start.20 = (f16[2,328,512]{2,1,0:T(8,128)(2,1)S(1)}, f16[2,328,512]{2,1,0:T(8,128)(2,1)S(1)}, u32[]{:S(2)}, u32[]{:S(2)}) collective-permute-start(f16[2,328,512]{2,1,0:T(8,128)(2,1)S(1)} %convert_element_type.156), channel_id=1, source_target_pairs={{0,8},{8,16},{16,24},{24,0},{1,9},{9,17},{17,25},{25,1},{2,10},{10... | collective-permute-start | bytes 2015240 | tf_op jit(solution)/shard_map/ppermute | solution.py:312
  275.0 6.8 %copy-start.8 = (f32[2,2,64,512]{3,2,1,0:T(8,128)S(1)}, f32[2,2,64,512]{3,2,1,0:T(8,128)}, u32[]{:S(2)}) copy-start(f32[2,2,64,512]{3,2,1,0:T(8,128)} %get-tuple-element.31) | copy-start | bytes 1572868
  277.3 5.3 %copy-start.12 = (f32[2,64,512]{2,1,0:T(8,128)S(1)}, f32[2,64,512]{2,1,0:T(8,128)}, u32[]{:S(2)}) copy-start(f32[2,64,512]{2,1,0:T(8,128)} %get-tuple-element.46) | copy-start | bytes 786436
  277.3 6.1 %copy-start.7 = (f32[3,2,64,512]{3,2,1,0:T(8,128)S(1)}, f32[3,2,64,512]{3,2,1,0:T(8,128)}, u32[]{:S(2)}) copy-start(f32[3,2,64,512]{3,2,1,0:T(8,128)} %get-tuple-element.35) | copy-start | bytes 2359300
  277.3 23.0 %all-to-all-start.4 = ((f16[8,328,128]{2,1,0:T(8,128)(2,1)}), f16[8,328,128]{2,1,0:T(8,128)(2,1)S(1)}, u32[]{:S(2)}, u32[]{:S(2)}) async-start(f16[8,328,128]{2,1,0:T(8,128)(2,1)} %convert_element_type.158), calls=%async_computation.4 | async-start | bytes 1343488 | tf_op jit(solution)/shard_map/all_to_all | solution.py:397
  281.8 2.5 copy-start.13
  282.7 2.4 copy-start.6
  284.4 1.8 copy-start.14
  284.4 2.5 copy-start.5
Sparse Core Ops, SparseCore 0:
  9.6 24.7 all-gather.10
  36.0 32.4 all-gather.12
  70.7 43.1 all-gather.14
  115.3 54.5 all-gather.16
  171.5 65.3 all-gather.18

commit v5 on v4

v5 whole, which is shorter than its diff:
```python
import functools

import jax
import jax.numpy as jnp
from jax import lax
from jax.experimental import pallas as pl
from jax.experimental.pallas import tpu as pltpu
from jax.sharding import PartitionSpec as P

F32 = jnp.float32
BF16 = jnp.bfloat16
F16 = jnp.float16
TOP = 2.0**14
TAIL = 8
VMEM = pl.BlockSpec(memory_space=pltpu.VMEM)
SMEM = pl.BlockSpec(memory_space=pltpu.SMEM)
ANY = pl.BlockSpec(memory_space=pl.ANY)


def factors(peak):
    rows = lax.broadcasted_iota(jnp.int32, (TAIL, peak.shape[1]), 0)
    rest = jnp.maximum(peak, 2.0**-100)
    table = jnp.ones((TAIL, peak.shape[1]), F32)
    whole = jnp.ones_like(rest)
    for i in range(TAIL):
        one = jnp.clip(rest, 2.0**-14, TOP).astype(BF16).astype(F32)
        rest = rest / one
        table = jnp.where(rows == i, jnp.broadcast_to(one, table.shape), table)
        whole = whole * one
    return table, whole


def product(table):
    whole = table[0:1]
    for i in range(1, TAIL):
        whole = whole * table[i : i + 1]
    return whole * (1.0 / TOP)


def peak_of(x):
    down = jnp.max(jnp.abs(x), axis=0, keepdims=True)
    return jnp.broadcast_to(jnp.max(down, axis=1, keepdims=True), down.shape)


def chain_of(parents, level, node):
    found = [None] * level
    for up in range(level - 1, -1, -1):
        node = parents[up, node]
        found[up] = node
    return found


def live_lanes(shape, size):
    return lax.broadcasted_iota(jnp.int32, shape, len(shape) - 1) < size


def base_kernel(npr, rows, width, place, sizes, whole_diag, out, message, marginal, diag, out_sem):
    row, col = place[0], place[1]
    bring = pltpu.make_async_copy(whole_diag.at[0], diag, out_sem)
    bring.start()
    bring.wait()
    for n in range(npr):
        value = diag_base(diag[n], sizes[0, row * npr + n], col * rows, rows, width)
        marginal[n] = value
        table, whole = factors(peak_of(value))
        message[n, :rows] = value * (TOP / whole)
        message[n, rows:] = table
    keep = pltpu.make_async_copy(marginal, out.at[0], out_sem)
    keep.start()
    keep.wait()


def diag_base(block, size, first, rows, width):
    lines = lax.broadcasted_iota(jnp.int32, (rows, width), 0) + first
    lanes = lax.broadcasted_iota(jnp.int32, (rows, width), 1)
    kept = jnp.where((lines < size) & (lanes < size), block, 0.0)
    return kept + jnp.where((lines == lanes) & (lines >= size), 1.0, 0.0)


def pack(turn, values, rows):
    high = values[0].shape[0]
    parts = []
    for value in values:
        table, whole = factors(peak_of(value))
        parts.append((value * (TOP / whole), table))
    for c in range(turn.shape[0]):
        piece = slice(c * rows, (c + 1) * rows)
        turn[c, :high] = jnp.concatenate([v[:, piece] for v, _ in parts], axis=1)
        turn[c, high:] = jnp.concatenate([t[:, piece] for _, t in parts], axis=1)


def panel_moves(panel, off, lower, sem, col, n_col):
    def start(n, m):
        if len(panel) == 1:
            pltpu.make_async_copy(panel[0].at[:, off + m, n], lower.at[n, m], sem.at[n, m]).start()
            return
        z, core = lax.div(col, 2), lax.rem(col, 2)
        for i, piece in enumerate(panel):
            owner = lax.rem(z - i // 2 + n_col // 2, n_col // 2) * 2 + (core if i % 2 == 0 else 1 - core)
            pltpu.make_async_copy(piece.at[m, n], lower.at[n, m, owner], sem.at[n, m]).start()

    def wait(n, m):
        pltpu.make_async_copy(lower.at[n, m], lower.at[n, m], sem.at[n, m]).wait()

    return start, wait


def split_block(value, size, split, top_rows, low_rows):
    value = jnp.where(live_lanes(value.shape, size), value, 0.0)
    top = value.astype(BF16)
    split[top_rows] = top
    split[low_rows] = (value - top.astype(F32)).astype(BF16)


def upper_kernel(level, n_panel, off, n_wait, spans, n_row, npr, rows, width, *refs):
    place, parents, sizes = refs[:3]
    panel = refs[3 : 3 + n_panel]
    at = 3 + n_panel
    sources = []
    for up in range(level):
        parts = []
        for part in range(2):
            if (up, part) == (0, 0) or (up, part) == (level - 1, 1):
                parts.append(())
                continue
            parts.append(refs[at : at + spans[up]])
            at += spans[up]
        sources.append(parts)
    at += n_wait
    out, turn = refs[at : at + 2]
    lower, split, panel_sem, block_sem = refs[at + 2 : at + 6]
    holders = iter(refs[at + 6 :])
    row = place[0]
    high = (level - 1) * rows
    held = {
        (up, part): next(holders)
        for up in range(level)
        for part in range(2)
        if sources[up][part]
    }
    chains = [chain_of(parents, level, row * npr + n) for n in range(npr)]

    start, wait = panel_moves(panel, off, lower, panel_sem, place[1], lower.shape[2])

    for n in range(npr):
        for up in range(level):
            node = chains[n][up]
            back = lax.rem(row - lax.div(node, npr) + n_row, n_row)
            slot = lax.rem(node, npr)
            for part in range(2):
                for i, source in enumerate(sources[up][part]):

                    @pl.when(back == i)
                    def _():
                        pltpu.make_async_copy(
                            source.at[slot], held[up, part].at[n], block_sem.at[n, up, part]
                        ).start()
        for m in range(level):
            start(n, m)

    values = []
    for n in range(npr):
        live = [sizes[up, chains[n][up]] for up in range(level)]
        total = None
        for up in range(level):
            for part in range(2):
                if not sources[up][part]:
                    continue
                block = held[up, part]
                pltpu.make_async_copy(
                    sources[up][part][0].at[0], block.at[n], block_sem.at[n, up, part]
                ).wait()
                count = (block.shape[1] - TAIL) // rows
                whole = product(block[n, count * rows :])
                for b in range(count):
                    value = block[n, b * rows : (b + 1) * rows] * whole
                    l, m = (b, up) if up > 0 and part == 0 else (up, b)
                    split_block(
                        value,
                        live[m],
                        split,
                        (n, m, slice(l * rows, (l + 1) * rows)),
                        (n, m, slice(high + l * rows, high + (l + 1) * rows)),
                    )
        for m in range(level):
            wait(n, m)
            block = lower[n, m].reshape(width, width)
            term = jnp.dot(split[n, m], block, preferred_element_type=F32)
            total = term if total is None else total + term
        value = -(total[:high] + total[high:])
        values.append(jnp.where(live_lanes(value.shape, sizes[level, row * npr + n]), value, 0.0))
        out[n] = values[n]
    pack(turn, values, rows)


def cross_kernel(level, last, n_panel, off, n_source, n_wait, n_row, npr, rows, width, *refs):
    place, parents, sizes = refs[:3]
    panel = refs[3 : 3 + n_panel]
    sources = refs[3 + n_panel : 3 + n_panel + n_source]
    at = 3 + n_panel + n_source
    upper = None
    if level > 1:
        upper = refs[at]
        at += 1
    at += n_wait
    n_out = 2 if last else 3
    outs = refs[at : at + n_out]
    lower, split, held, panel_sem, block_sem, cross, out_sem = refs[at + n_out :]
    out, turn = outs[0], outs[1]
    passed = None if last else outs[2]
    row = place[0]
    high = level * rows
    chains = [chain_of(parents, level, row * npr + n) for n in range(npr)]

    start, wait = panel_moves(panel, off, lower, panel_sem, place[1], lower.shape[2])

    for n in range(npr):
        node = chains[n][level - 1]
        back = lax.rem(row - lax.div(node, npr) + n_row, n_row)
        for i, source in enumerate(sources):

            @pl.when(back == i)
            def _():
                pltpu.make_async_copy(
                    source.at[lax.rem(node, npr)], held.at[n], block_sem.at[n]
                ).start()

    for m in range(level):
        for n in range(npr):
            start(n, m)

    for n in range(npr):
        pltpu.make_async_copy(sources[0].at[0], held.at[n], block_sem.at[n]).wait()
        whole = product(held[n, high:])
        for m in range(level):
            split_block(
                held[n, m * rows : (m + 1) * rows] * whole,
                sizes[m, chains[n][m]],
                split,
                (n, m, slice(0, rows)),
                (n, m, slice(rows, 2 * rows)),
            )
    totals = [None] * npr
    for m in range(level):
        for n in range(npr):
            wait(n, m)
            block = lower[n, m].reshape(width, width)
            term = jnp.dot(split[n, m], block, preferred_element_type=F32)
            totals[n] = term if totals[n] is None else totals[n] + term
    values = []
    for n in range(npr):
        value = -(totals[n][:rows] + totals[n][rows:])
        values.append(jnp.where(live_lanes(value.shape, sizes[level, row * npr + n]), value, 0.0))
    for n in range(npr):
        cross[level - 1, n] = values[n]
        for l in range(level - 1):
            cross[l, n] = upper[n, l * rows : (l + 1) * rows]
    first = level * (level - 1) // 2
    keep = pltpu.make_async_copy(cross, out.at[first : first + level], out_sem)
    keep.start()
    pack(turn, values, rows)
    for n in range(npr):
        value = values[n]
        if level > 1:
            value = jnp.concatenate([upper[n], value], axis=0)
        if not last:
            table, whole = factors(peak_of(value))
            passed[n, :high] = value * (TOP / whole)
            passed[n, high:] = table
    keep.wait()


def marginal_kernel(level, last, n_panel, off, n_wait, n_row, npr, rows, width, *refs):
    place, sizes, diag = refs[:3]
    n_turned = min(level, 2)
    turned = refs[3 : 3 + n_turned]
    panel = refs[3 + n_turned : 3 + n_turned + n_panel]
    n_out = 1 if last else 2
    at = 3 + n_turned + n_panel + n_wait
    outs = refs[at : at + n_out]
    lower, panel_sem, marginal, out_sem = refs[at + n_out :]
    message = None if last else outs[1]
    row, col = place[0], place[1]
    n_col = lower.shape[2]
    high = level * rows

    start, wait = panel_moves(panel, off, lower, panel_sem, place[1], lower.shape[2])

    for m in range(level):
        for n in range(npr):
            start(n, m)

    def scales_of(part):
        lines = part.shape[1] - TAIL
        return jnp.concatenate(
            [jnp.broadcast_to(product(part[c, lines:]), (rows, npr * rows)) for c in range(n_col)], axis=0
        )

    scales = [scales_of(part) for part in turned]
    totals = [None] * npr
    sides = [[] for _ in range(npr)]
    for l in range(level):
        i, at_row = (n_turned - 1, 0) if l == level - 1 else (0, l * rows)
        upright = turned[i][:, at_row : at_row + rows].reshape(width, npr * rows) * scales[i]
        flat = upright.T
        top = flat.astype(BF16)
        low = (flat - top.astype(F32)).astype(BF16)
        for n in range(npr):
            mine = slice(n * rows, (n + 1) * rows)
            wait(n, l)
            block = lower[n, l].reshape(width, width)
            pair = jnp.concatenate([top[mine], low[mine]], axis=0)
            term = jnp.dot(pair, block, preferred_element_type=F32)
            term = term[:rows] + term[rows:]
            totals[n] = term if totals[n] is None else totals[n] + term
            sides[n].append(flat[mine])
    for n in range(npr):
        size = sizes[level, row * npr + n]
        value = diag_base(diag[n], size, col * rows, rows, width)
        value = value - jnp.where(live_lanes(value.shape, size), totals[n], 0.0)
        marginal[n] = value
        if n == npr - 1:
            keep = pltpu.make_async_copy(marginal, outs[0].at[level], out_sem)
            keep.start()
        if not last:
            peak = peak_of(value)
            for side in sides[n]:
                peak = jnp.maximum(peak, peak_of(side))
            table, whole = factors(peak)
            scale = TOP / whole
            for l in range(level):
                message[n, l * rows : (l + 1) * rows] = sides[n][l] * scale
            message[n, high : high + rows] = value * scale
            message[n, high + rows :] = table
    keep.wait()


def gate_kernel(count, *refs):
    refs[count][...] = jnp.ones((1, 1, 1), F32)


def timing(rows_only, level, back):
    if level == 0 or (back == 1 and not rows_only):
        return ("due", level + 1) if back > 1 else ("free", -1)
    if rows_only:
        if back == 1:
            return "due", level
        return "due", (level if back < 3 or level < 2 else level + back - 2)
    return "due", (level + 1 if level == 1 else level + back - 1)


def params(limit=60 * 2**20):
    return pltpu.CompilerParams(vmem_limit_bytes=limit)


def shards(panel, diag_inverse, parents, supernode_sizes):
    levels, npr, rows, width = diag_inverse.shape
    n_row = lax.axis_size("row")
    n_col = lax.axis_size("col")
    place = jnp.stack([lax.axis_index("row"), lax.axis_index("col")]).astype(jnp.int32)

    def shape(*dims, dtype=F32):
        return jax.ShapeDtypeStruct(dims, dtype)

    def reach(level):
        return min(levels - 1 - level, n_row - 1)

    def gate(name, arrays):
        return pl.pallas_call(
            functools.partial(gate_kernel, len(arrays)),
            out_shape=shape(1, 1, 1),
            in_specs=[ANY] * len(arrays),
            out_specs=VMEM,
            name=name,
        )(*arrays)

    due = [[] for _ in range(levels)]
    gates = [[] for _ in range(levels)]

    def spread(message, level, rows_only):
        found = [message]
        half = message
        if rows_only and gates[level]:
            half = jnp.where(gate(f"gate{level}", gates[level]) > 0, message, 0.0)
        half = half.astype(F16)
        for back in range(1, reach(level) + 1):
            route = [(i, (i + back) % n_row) for i in range(n_row)]
            found.append(lax.ppermute(half, "row", route).astype(F32))
            where, when = timing(rows_only, level, back)
            {"due": due, "gate": gates, "free": due + [[]]}[where][when].append(found[-1])
        return found

    def turn_over(message):
        return lax.all_to_all(message.astype(F16), "col", 0, 0, tiled=True).astype(F32)

    def gathered(first, count, there):
        mine = jnp.where(there.astype(BF16).reshape(1, 1, 1, 1) > 0, panel[first : first + count], 0)
        return lax.all_gather(mine, "col", axis=0)

    def pieces(mine):
        swap = [(i, i ^ 1) for i in range(n_col)]
        found = []
        for back in range(n_col // 2):
            got = mine
            if back:
                got = lax.ppermute(mine, "col", [(i, (i + 2 * back) % n_col) for i in range(n_col)])
            found += [got, lax.ppermute(got, "col", swap)]
        return found

    whole_panel = [None] * levels
    whole_panel[1] = (pieces(panel[0:1]), 0)
    diagonals, message = pl.pallas_call(
        functools.partial(base_kernel, npr, rows, width),
        out_shape=(shape(levels, npr, rows, width), shape(npr, rows + TAIL, width)),
        in_specs=[SMEM, SMEM, ANY],
        out_specs=(ANY, VMEM),
        scratch_shapes=[
            pltpu.VMEM((npr, rows, width), F32),
            pltpu.VMEM((npr, rows, width), F32),
            pltpu.SemaphoreType.DMA(()),
        ],
        compiler_params=params(),
        name="base",
    )(place, supernode_sizes, diag_inverse)
    crosses = None
    table = [[(), spread(message, 0, False)]]

    def gather_level(level, there):
        first = level * (level - 1) // 2
        whole_panel[level] = ([gathered(first, level, there)], 0)

    there = gate("first", whole_panel[1][0][::2] + [message])
    for deeper in range(2, levels):
        gather_level(deeper, there)
    for level in range(1, levels):
        last = level == levels - 1
        high = level * rows
        whole, off = whole_panel[level]
        panel_scratch = [pltpu.VMEM((npr, level, n_col, rows, width), BF16)]
        upper = []
        turned = []
        if level > 1:
            spans = [min(level - up, n_row - 1) + 1 for up in range(level)]
            sources = []
            held = []
            for up in range(level):
                for part in range(2):
                    if (up, part) == (0, 0) or (up, part) == (level - 1, 1):
                        continue
                    sources.extend(table[up][part][: spans[up]])
                    held.append(pltpu.VMEM(table[up][part][0].shape, F32))
            upper = list(
                pl.pallas_call(
                    functools.partial(upper_kernel, level, len(whole), off, 1, spans, n_row, npr, rows, width),
                    out_shape=(
                        shape(npr, high - rows, width),
                        shape(n_col, high - rows + TAIL, npr * rows),
                    ),
                    in_specs=[SMEM, SMEM, SMEM] + [ANY] * (len(whole) + len(sources) + 1),
                    out_specs=(VMEM, VMEM),
                    scratch_shapes=panel_scratch
                    + [
                        pltpu.VMEM((npr, level, 2 * (high - rows), width), BF16),
                        pltpu.SemaphoreType.DMA((npr, level)),
                        pltpu.SemaphoreType.DMA((npr, level, 2)),
                    ]
                    + held,
                    compiler_params=params(),
                    name=f"upper{level}",
                )(place, parents, supernode_sizes, *whole, *sources, table[level - 1][1][0])
            )
            turned.append(turn_over(upper.pop()))
        newest = table[level - 1][1][: min(1, n_row - 1) + 1]
        waits = due[0] if level == 1 else []
        out_shape = [shape(panel.shape[0], npr, rows, width), shape(n_col, rows + TAIL, npr * rows)]
        if not last:
            out_shape.append(shape(npr, high + TAIL, width))
        before = [] if crosses is None else [crosses]
        n_given = 3 + len(whole) + len(newest) + len(upper) + len(waits)
        made = pl.pallas_call(
            functools.partial(
                cross_kernel, level, last, len(whole), off, len(newest), len(waits) + len(before), n_row, npr, rows, width
            ),
            out_shape=tuple(out_shape),
            in_specs=[SMEM, SMEM, SMEM] + [ANY] * (len(whole) + len(newest)) + [VMEM] * len(upper) + [ANY] * (len(waits) + len(before)),
            out_specs=(ANY,) + (VMEM,) * (len(out_shape) - 1),
            scratch_shapes=panel_scratch
            + [
                pltpu.VMEM((npr, level, 2 * rows, width), BF16),
                pltpu.VMEM((npr, high + TAIL, width), F32),
                pltpu.SemaphoreType.DMA((npr, level)),
                pltpu.SemaphoreType.DMA((npr,)),
                pltpu.VMEM((level, npr, rows, width), F32),
                pltpu.SemaphoreType.DMA(()),
            ],
            input_output_aliases={n_given: 0} if before else {},
            compiler_params=params(),
            cost_estimate=pl.CostEstimate(flops=4 * 10**10, bytes_accessed=2**20, transcendentals=0) if last else None,
            name=f"cross{level}",
        )(place, parents, supernode_sizes, *whole, *newest, *upper, *waits, *before)
        crosses = made[0]
        ahead = () if last else spread(made[2], level, True)
        newer = made[1]
        if last and turned:
            newer = jnp.where(gate(f"turn{level}", turned) > 0, newer, 0.0)
        turned.append(turn_over(newer))
        waits = [] if last else due[level] + whole_panel[level + 1][0]
        out_shape = [shape(levels, npr, rows, width)]
        if not last:
            out_shape.append(shape(npr, high + rows + TAIL, width))
        done = pl.pallas_call(
            functools.partial(marginal_kernel, level, last, len(whole), off, len(waits) + 1, n_row, npr, rows, width),
            out_shape=tuple(out_shape),
            in_specs=[SMEM, SMEM, VMEM] + [VMEM] * len(turned) + [ANY] * (len(whole) + len(waits) + 1),
            out_specs=(ANY,) + (VMEM,) * (len(out_shape) - 1),
            scratch_shapes=panel_scratch
            + [
                pltpu.SemaphoreType.DMA((npr, level)),
                pltpu.VMEM((npr, rows, width), F32),
                pltpu.SemaphoreType.DMA(()),
            ],
            input_output_aliases={3 + len(turned) + len(whole) + len(waits): 0},
            compiler_params=params(),
            name=f"marginal{level}",
        )(place, supernode_sizes, diag_inverse[level], *turned, *whole, *waits, diagonals)
        diagonals = done[0]
        if not last:
            table.append([ahead, spread(done[1], level, False)])
    return crosses, diagonals


def solution(mesh):
    in_specs = (P(None, "row", "col", None), P(None, "row", "col", None), P(), P())
    out_specs = (P(None, "row", "col", None), P(None, "row", "col", None))
    return jax.shard_map(shards, mesh=mesh, in_specs=in_specs, out_specs=out_specs, check_vma=False)
```

time: 316 us -> 289 us (0.915)
  waiting for transfers between devices: 119 us -> 51.9 us
  starting transfers between devices: 43.8 us -> 67.2 us
  local copies, waits for them, and re-layouts: 18.2 us -> 4.2 us
  other arithmetic: 42.5 us -> 53.8 us
  blocking collectives: 0 us -> 9.39 us
  Pallas kernels: 76.8 us -> 84.6 us
    ppermute x21, waiting for transfers between devices: 102 us -> 18.6 us  [spread(): found.append(lax.ppermute(half, 'row', route).astype(F32))]
    all_to_all x5 -> x8, waiting for transfers between devices: 12.3 us -> 26.4 us  [turn_over(): lax.all_to_all(message.astype(F16), 'col', 0, 0, tiled=True).astype(F32)]
    all_to_all x5 -> x8, starting transfers between devices: 19.5 us -> 32.1 us  [turn_over(): lax.all_to_all(message.astype(F16), 'col', 0, 0, tiled=True).astype(F32)]
    all_to_all x0 -> x1, blocking collectives: none -> 9.39 us  [turn_over(): lax.all_to_all(message.astype(F16), 'col', 0, 0, tiled=True).astype(F32)]
    convert_element_type x19 -> x27, other arithmetic: 22.2 us -> 30.3 us  [the longest x9 13.2 us: turn_over(): message.astype(F16)]
    ppermute x0 -> x7, starting transfers between devices: none -> 8.03 us  [the longest x3 7.01 us: pieces(): lax.ppermute(mine, 'col', [(i, (i + 2 * back) % n_col) for i in range(n_c...]
    pallas_call x14 -> x16, Pallas kernels: 74.9 us -> 81.4 us  [the longest x5 30.6 us: shards(): pl.pallas_call(functools.partial(cross_kernel, level, last, len(whole), o...]
    slice x5 -> x1, local copies, waits for them, and re-layouts: 6.95 us -> 1.05 us  [shards(): whole_panel[1] = (pieces(panel[0:1]), 0)]
  transfers between devices with their start and end apart: 31 -> 40, of which waited for: 18 -> 12; matrix products, arithmetic and copies ran while one was open for 16% -> 18% of each run, Pallas kernels for 19% -> 25%
where the time goes in v5:
time: 289 us; the launch traced here: 286 us
  Pallas kernels  84.6 us (29%)
  starting transfers between devices  67.2 us (23%)
  other arithmetic  53.8 us (19%)
  waiting for transfers between devices  51.9 us (18%)
  between operations  15.5 us (5%)
  blocking collectives  9.39 us (3%)
  local copies, waits for them, and re-layouts  4.2 us (1%)
    all_to_all x8, starting transfers between devices, turn_over(): lax.all_to_all(message.astype(F16), 'col', 0, 0, tiled=True).astype(F32)  32.1 us
    pallas_call x5, Pallas kernels, shards(): pl.pallas_call(functools.partial(cross_kernel, level, last, len(whole), o...  30.6 us
    ppermute x21, starting transfers between devices, spread(): found.append(lax.ppermute(half, 'row', route).astype(F32))  26.9 us
    all_to_all x8, waiting for transfers between devices, turn_over(): lax.all_to_all(message.astype(F16), 'col', 0, 0, tiled=True).astype(F32)  26.4 us
    pallas_call x5, Pallas kernels, shards(): pl.pallas_call(functools.partial(marginal_kernel, level, last, len(whole)...  25 us
    pallas_call x4, Pallas kernels, shards(): pl.pallas_call(functools.partial(upper_kernel, level, len(whole), off, 1,...  24.8 us
    convert_element_type x21, other arithmetic, spread(): found.append(lax.ppermute(half, 'row', route).astype(F32))  19.6 us
    ppermute x21, waiting for transfers between devices, spread(): found.append(lax.ppermute(half, 'row', route).astype(F32))  18.6 us
  transfers between devices with their start and end apart: 40, of which 12 were waited for; matrix products, arithmetic and copies ran while one was open for 18% of the time, Pallas kernels for 25%

profile of v5, /device:TPU:0, one launch (start us, length us, event | category | flops | bytes accessed | tf_op | source)
XLA Modules:
  0.0 286.5 jit_solution(1819821826977269639)
XLA Ops:
  8.3 3.1 %collective-permute-start = (bf16[1,2,64,512]{3,2,1,0:T(8,128)(2,1)S(1)}, bf16[1,2,64,512]{3,2,1,0:T(8,128)(2,1)S(1)}, u32[]{:S(2)}, u32[]{:S(2)}) collective-permute-start(bf16[1,2,64,512]{3,2,1,0:T(8,128)(2,1)S(1)} %slice.30.refs_0_.refs_3_.refs_4_), channel_id=1, source_target_pairs={{0,2},{1,3},{2,4},{3,5},{4,6},{5,7},{6,0},{7,1},{8,10},{9,11},{10,... | collective-permute-start | bytes 393224 | tf_op jit(solution)/shard_map/ppermute | solution.py:406
  11.4 2.6 collective-permute-start.1
  15.8 3.2 %base.1 = (f32[6,2,64,512]{3,2,1,0:T(8,128)}, f32[2,72,512]{2,1,0:T(8,128)}) custom-call(s32[2]{0:T(128)} %pad_add_fusion.place.refs_0_, s32[6,8]{1,0:T(8,128)} %refs_1_.27, f32[6,2,64,512]{3,2,1,0:T(8,128)} %whole_diag.1), custom_call_target="tpu_custom_call" | custom-call | tf_op jit(solution)/shard_map/base/pallas_call | solution.py:412
  19.1 3.5 %collective-permute-done.1.refs_2_.refs_7_.refs_8_ = bf16[1,2,64,512]{3,2,1,0:T(8,128)(2,1)S(1)} collective-permute-done((bf16[1,2,64,512]{3,2,1,0:T(8,128)(2,1)S(1)}, bf16[1,2,64,512]{3,2,1,0:T(8,128)(2,1)S(1)}, u32[]{:S(2)}, u32[]{:S(2)}) %collective-permute-start.1) | collective-permute-done | bytes 131104 | tf_op jit(solution)/shard_map/ppermute | solution.py:406
  30.7 4.1 %collective-permute-done.3 = f16[2,72,512]{2,1,0:T(8,128)(2,1)S(1)} collective-permute-done((f16[2,72,512]{2,1,0:T(8,128)(2,1)S(1)}, f16[2,72,512]{2,1,0:T(8,128)(2,1)S(1)}, u32[]{:S(2)}, u32[]{:S(2)}) %collective-permute-start.3) | collective-permute-done | bytes 147488 | tf_op jit(solution)/shard_map/ppermute | solution.py:388
  38.9 4.3 %cross1.1 = (f32[15,2,64,512]{3,2,1,0:T(8,128)}, f32[8,72,128]{2,1,0:T(8,128)}, f32[2,72,512]{2,1,0:T(8,128)}) custom-call(s32[2]{0:T(128)} %pad_add_fusion.place.refs_0_, s32[5,8]{1,0:T(8,128)} %refs_1_.26, s32[6,8]{1,0:T(8,128)} %refs_1_.27, bf16[1,2,64,512]{3,2,1,0:T(8,128)(2,1)} %copy-done.2, bf16[1,2,64,512]{3,2,1,0:T(8,128)(2,1)} %copy-done.11, ...), custom_call_target="tpu_custom_call" | custom-call | tf_op jit(solution)/shard_map/cross1/pallas_call | solution.py:480
  46.2 2.4 collective-permute-start.12
  50.3 5.1 %all-to-all-start = ((f16[8,72,128]{2,1,0:T(8,128)(2,1)}), f16[8,72,128]{2,1,0:T(8,128)(2,1)S(1)}, u32[]{:S(2)}, u32[]{:S(2)}) async-start(f16[8,72,128]{2,1,0:T(8,128)(2,1)} %convert_element_type.167), calls=%async_computation | async-start | bytes 294912 | tf_op jit(solution)/shard_map/all_to_all | solution.py:394
  60.2 2.1 all-to-all-done
  63.1 4.3 %marginal1.1 = (f32[6,2,64,512]{3,2,1,0:T(8,128)}, f32[2,136,512]{2,1,0:T(8,128)}) custom-call(s32[2]{0:T(128)} %pad_add_fusion.place.refs_0_, s32[6,8]{1,0:T(8,128)} %refs_1_.27, f32[2,64,512]{2,1,0:T(8,128)} %get-tuple-element.68.refs_2_, f32[8,72,128]{2,1,0:T(8,128)} %convert_element_type.168.refs_3_, ...), custom_call_target="tpu_custom_call", output_to_operand_aliasing={{0}: (18, {})} | custom-call | tf_op jit(solution)/shard_map/marginal1/pallas_call | solution.py:511
  68.5 3.9 %upper2.1 = (f32[2,64,512]{2,1,0:T(8,128)}, f32[8,72,128]{2,1,0:T(8,128)}) custom-call(s32[2]{0:T(128)} %pad_add_fusion.place.refs_0_, s32[5,8]{1,0:T(8,128)} %refs_1_.26, s32[6,8]{1,0:T(8,128)} %refs_1_.27, bf16[8,2,2,64,512]{4,3,2,1,0:T(8,128)(2,1)} %bitcast.31, f32[2,72,512]{2,1,0:T(8,128)} %get-tuple-element.34.refs_4_.refs_11_, ...), custom_call_target="tpu_custom_call" | custom-call | tf_op jit(solution)/shard_map/upper2/pallas_call | solution.py:453
  72.5 1.7 convert_element_type.176
  74.2 3.4 %all-to-all-start.1 = ((f16[8,72,128]{2,1,0:T(8,128)(2,1)}), f16[8,72,128]{2,1,0:T(8,128)(2,1)S(1)}, u32[]{:S(2)}, u32[]{:S(2)}) async-start(f16[8,72,128]{2,1,0:T(8,128)(2,1)} %convert_element_type.176), calls=%async_computation.1 | async-start | bytes 294912 | tf_op jit(solution)/shard_map/all_to_all | solution.py:394
  78.6 2.4 collective-permute-start.15
  81.9 5.2 %cross2.1 = (f32[15,2,64,512]{3,2,1,0:T(8,128)}, f32[8,72,128]{2,1,0:T(8,128)}, f32[2,136,512]{2,1,0:T(8,128)}) custom-call(s32[2]{0:T(128)} %pad_add_fusion.place.refs_0_, s32[5,8]{1,0:T(8,128)} %refs_1_.26, s32[6,8]{1,0:T(8,128)} %refs_1_.27, bf16[8,2,2,64,512]{4,3,2,1,0:T(8,128)(2,1)} %bitcast.32, ...), custom_call_target="tpu_custom_call", output_to_operand_aliasing={{0}: (7, {})} | custom-call | tf_op jit(solution)/shard_map/cross2/pallas_call | solution.py:480
  91.5 5.0 %all-to-all-start.2 = ((f16[8,72,128]{2,1,0:T(8,128)(2,1)}), f16[8,72,128]{2,1,0:T(8,128)(2,1)S(1)}, u32[]{:S(2)}, u32[]{:S(2)}) async-start(f16[8,72,128]{2,1,0:T(8,128)(2,1)} %convert_element_type.178), calls=%async_computation.2 | async-start | bytes 294912 | tf_op jit(solution)/shard_map/all_to_all | solution.py:394
  99.1 4.4 %all-to-all-done.2 = f16[8,72,128]{2,1,0:T(8,128)(2,1)S(1)} async-done(((f16[8,72,128]{2,1,0:T(8,128)(2,1)}), f16[8,72,128]{2,1,0:T(8,128)(2,1)S(1)}, u32[]{:S(2)}, u32[]{:S(2)}) %all-to-all-start.2) | async-done | bytes 147488 | tf_op jit(solution)/shard_map/all_to_all | solution.py:394
  106.0 5.0 %marginal2.1 = (f32[6,2,64,512]{3,2,1,0:T(8,128)}, f32[2,200,512]{2,1,0:T(8,128)}) custom-call(s32[2]{0:T(128)} %pad_add_fusion.place.refs_0_, s32[6,8]{1,0:T(8,128)} %refs_1_.27, f32[2,64,512]{2,1,0:T(8,128)} %get-tuple-element.67.refs_2_, f32[8,72,128]{2,1,0:T(8,128)} %convert_element_type.177.refs_3_, ...), custom_call_target="tpu_custom_call", output_to_operand_aliasing={{0}: (11, {})} | custom-call | tf_op jit(solution)/shard_map/marginal2/pallas_call | solution.py:511
  112.2 1.9 collective-permute-start.18
  114.1 5.3 %upper3.1 = (f32[2,128,512]{2,1,0:T(8,128)}, f32[8,136,128]{2,1,0:T(8,128)}) custom-call(s32[2]{0:T(128)} %pad_add_fusion.place.refs_0_, s32[5,8]{1,0:T(8,128)} %refs_1_.26, s32[6,8]{1,0:T(8,128)} %refs_1_.27, bf16[8,3,2,64,512]{4,3,2,1,0:T(8,128)(2,1)} %bitcast.23, f32[2,72,512]{2,1,0:T(8,128)} %get-tuple-element.34.refs_4_.refs_11_, ...), custom_call_target="tpu_custom_call" | custom-call | tf_op jit(solution)/shard_map/upper3/pallas_call | solution.py:453
  119.4 1.8 convert_element_type.185
  121.2 3.4 %all-to-all-start.3 = ((f16[8,136,128]{2,1,0:T(8,128)(2,1)}), f16[8,136,128]{2,1,0:T(8,128)(2,1)S(1)}, u32[]{:S(2)}, u32[]{:S(2)}) async-start(f16[8,136,128]{2,1,0:T(8,128)(2,1)} %convert_element_type.185), calls=%async_computation.3 | async-start | bytes 557056 | tf_op jit(solution)/shard_map/all_to_all | solution.py:394
  124.6 1.6 collective-permute-start.19
  127.3 6.3 %cross3.1 = (f32[15,2,64,512]{3,2,1,0:T(8,128)}, f32[8,72,128]{2,1,0:T(8,128)}, f32[2,200,512]{2,1,0:T(8,128)}) custom-call(s32[2]{0:T(128)} %pad_add_fusion.place.refs_0_, s32[5,8]{1,0:T(8,128)} %refs_1_.26, s32[6,8]{1,0:T(8,128)} %refs_1_.27, bf16[8,3,2,64,512]{4,3,2,1,0:T(8,128)(2,1)} %bitcast.24, ...), custom_call_target="tpu_custom_call", output_to_operand_aliasing={{0}: (7, {})} | custom-call | tf_op jit(solution)/shard_map/cross3/pallas_call | solution.py:480
  135.3 2.8 collective-permute-start.21
  139.8 3.4 %all-to-all-done.3 = f16[8,136,128]{2,1,0:T(8,128)(2,1)S(1)} async-done(((f16[8,136,128]{2,1,0:T(8,128)(2,1)}), f16[8,136,128]{2,1,0:T(8,128)(2,1)S(1)}, u32[]{:S(2)}, u32[]{:S(2)}) %all-to-all-start.3) | async-done | bytes 278560 | tf_op jit(solution)/shard_map/all_to_all | solution.py:394
  143.2 3.6 %all-to-all-start.4 = ((f16[8,72,128]{2,1,0:T(8,128)(2,1)}), f16[8,72,128]{2,1,0:T(8,128)(2,1)S(1)}, u32[]{:S(2)}, u32[]{:S(2)}) async-start(f16[8,72,128]{2,1,0:T(8,128)(2,1)} %convert_element_type.187), calls=%async_computation.4 | async-start | bytes 294912 | tf_op jit(solution)/shard_map/all_to_all | solution.py:394
  146.7 5.4 %collective-permute-done.21 = f16[2,136,512]{2,1,0:T(8,128)(2,1)S(1)} collective-permute-done((f16[2,136,512]{2,1,0:T(8,128)(2,1)S(1)}, f16[2,136,512]{2,1,0:T(8,128)(2,1)S(1)}, u32[]{:S(2)}, u32[]{:S(2)}) %collective-permute-start.21) | collective-permute-done | bytes 278560 | tf_op jit(solution)/shard_map/ppermute | solution.py:388
  157.7 5.1 %marginal3.1 = (f32[6,2,64,512]{3,2,1,0:T(8,128)}, f32[2,264,512]{2,1,0:T(8,128)}) custom-call(s32[2]{0:T(128)} %pad_add_fusion.place.refs_0_, s32[6,8]{1,0:T(8,128)} %refs_1_.27, f32[2,64,512]{2,1,0:T(8,128)} %get-tuple-element.70.refs_2_, f32[8,136,128]{2,1,0:T(8,128)} %convert_element_type.186.refs_3_, ...), custom_call_target="tpu_custom_call", output_to_operand_aliasing={{0}: (11, {})} | custom-call | tf_op jit(solution)/shard_map/marginal3/pallas_call | solution.py:511
  164.7 6.9 %upper4.1 = (f32[2,192,512]{2,1,0:T(8,128)}, f32[8,200,128]{2,1,0:T(8,128)}) custom-call(s32[2]{0:T(128)} %pad_add_fusion.place.refs_0_, s32[5,8]{1,0:T(8,128)} %refs_1_.26, s32[6,8]{1,0:T(8,128)} %refs_1_.27, bf16[8,4,2,64,512]{4,3,2,1,0:T(8,128)(2,1)} %bitcast.19, f32[2,72,512]{2,1,0:T(8,128)} %get-tuple-element.34.refs_4_.refs_11_, ...), custom_call_target="tpu_custom_call" | custom-call | tf_op jit(solution)/shard_map/upper4/pallas_call | solution.py:453
  171.6 2.0 convert_element_type.191
  173.5 4.8 %all-to-all-start.5 = ((f16[8,200,128]{2,1,0:T(8,128)(2,1)}), f16[8,200,128]{2,1,0:T(8,128)(2,1)S(1)}, u32[]{:S(2)}, u32[]{:S(2)}) async-start(f16[8,200,128]{2,1,0:T(8,128)(2,1)} %convert_element_type.191), calls=%async_computation.5 | async-start | bytes 819200 | tf_op jit(solution)/shard_map/all_to_all | solution.py:394
  181.1 7.3 %cross4.1 = (f32[15,2,64,512]{3,2,1,0:T(8,128)}, f32[8,72,128]{2,1,0:T(8,128)}, f32[2,264,512]{2,1,0:T(8,128)}) custom-call(s32[2]{0:T(128)} %pad_add_fusion.place.refs_0_, s32[5,8]{1,0:T(8,128)} %refs_1_.26, s32[6,8]{1,0:T(8,128)} %refs_1_.27, bf16[8,4,2,64,512]{4,3,2,1,0:T(8,128)(2,1)} %bitcast.20, ...), custom_call_target="tpu_custom_call", output_to_operand_aliasing={{0}: (7, {})} | custom-call | tf_op jit(solution)/shard_map/cross4/pallas_call | solution.py:480
  193.4 9.4 %all-to-all-done.5 = f16[8,200,128]{2,1,0:T(8,128)(2,1)S(1)} async-done(((f16[8,200,128]{2,1,0:T(8,128)(2,1)}), f16[8,200,128]{2,1,0:T(8,128)(2,1)S(1)}, u32[]{:S(2)}, u32[]{:S(2)}) %all-to-all-start.5) | async-done | bytes 409632 | tf_op jit(solution)/shard_map/all_to_all | solution.py:394
  202.8 3.4 %all-to-all-start.6 = ((f16[8,72,128]{2,1,0:T(8,128)(2,1)}), f16[8,72,128]{2,1,0:T(8,128)(2,1)S(1)}, u32[]{:S(2)}, u32[]{:S(2)}) async-start(f16[8,72,128]{2,1,0:T(8,128)(2,1)} %convert_element_type.195), calls=%async_computation.6 | async-start | bytes 294912 | tf_op jit(solution)/shard_map/all_to_all | solution.py:394
  206.2 6.8 %collective-permute-done.24 = f16[2,200,512]{2,1,0:T(8,128)(2,1)S(1)} collective-permute-done((f16[2,200,512]{2,1,0:T(8,128)(2,1)S(1)}, f16[2,200,512]{2,1,0:T(8,128)(2,1)S(1)}, u32[]{:S(2)}, u32[]{:S(2)}) %collective-permute-start.24) | collective-permute-done | bytes 409632 | tf_op jit(solution)/shard_map/ppermute | solution.py:388
  216.1 2.5 all-to-all-done.6
  220.5 3.3 %all-gather.9.cloned.1.call-done = bf16[40,2,64,512]{3,2,1,0:T(8,128)(2,1)} async-done(((bf16[5,2,64,512]{3,2,1,0:T(8,128)(2,1)}), bf16[40,2,64,512]{3,2,1,0:T(8,128)(2,1)}) %all-gather.9.cloned.1.call-update) | async-done | bytes 5242896 | tf_op jit(solution)/shard_map/all_gather | solution.py:398
  223.8 5.6 %marginal4.1 = (f32[6,2,64,512]{3,2,1,0:T(8,128)}, f32[2,328,512]{2,1,0:T(8,128)}) custom-call(s32[2]{0:T(128)} %pad_add_fusion.place.refs_0_, s32[6,8]{1,0:T(8,128)} %refs_1_.27, f32[2,64,512]{2,1,0:T(8,128)} %get-tuple-element.69.refs_2_, f32[8,200,128]{2,1,0:T(8,128)} %convert_element_type.192.refs_3_, ...), custom_call_target="tpu_custom_call", output_to_operand_aliasing={{0}: (10, {})} | custom-call | tf_op jit(solution)/shard_map/marginal4/pallas_call | solution.py:511
  230.9 1.7 collective-permute-start.27
  232.6 8.6 %upper5.1 = (f32[2,256,512]{2,1,0:T(8,128)}, f32[8,264,128]{2,1,0:T(8,128)}) custom-call(s32[2]{0:T(128)} %pad_add_fusion.place.refs_0_, s32[5,8]{1,0:T(8,128)} %refs_1_.26, s32[6,8]{1,0:T(8,128)} %refs_1_.27, bf16[8,5,2,64,512]{4,3,2,1,0:T(8,128)(2,1)} %bitcast.27, f32[2,72,512]{2,1,0:T(8,128)} %get-tuple-element.34.refs_4_.refs_11_, ...), custom_call_target="tpu_custom_call" | custom-call | tf_op jit(solution)/shard_map/upper5/pallas_call | solution.py:453
  241.3 2.2 convert_element_type.203
  243.4 3.5 %all-to-all-start.7 = ((f16[8,264,128]{2,1,0:T(8,128)(2,1)}), f16[8,264,128]{2,1,0:T(8,128)(2,1)S(1)}, u32[]{:S(2)}, u32[]{:S(2)}) async-start(f16[8,264,128]{2,1,0:T(8,128)(2,1)} %convert_element_type.203), calls=%async_computation.7 | async-start | bytes 1081344 | tf_op jit(solution)/shard_map/all_to_all | solution.py:394
  247.0 2.3 collective-permute-done.27
  250.5 7.5 %cross5.1 = (f32[15,2,64,512]{3,2,1,0:T(8,128)}, f32[8,72,128]{2,1,0:T(8,128)}) custom-call(s32[2]{0:T(128)} %pad_add_fusion.place.refs_0_, s32[5,8]{1,0:T(8,128)} %refs_1_.26, s32[6,8]{1,0:T(8,128)} %refs_1_.27, bf16[8,5,2,64,512]{4,3,2,1,0:T(8,128)(2,1)} %bitcast.28, ...), custom_call_target="tpu_custom_call", output_to_operand_aliasing={{0}: (7, {})} | custom-call | flops 40000000000 | bytes 1048576 | tf_op jit(solution)/shard_map/cross5/pallas_call | solution.py:480
  258.0 4.6 %all-to-all-done.7 = f16[8,264,128]{2,1,0:T(8,128)(2,1)S(1)} async-done(((f16[8,264,128]{2,1,0:T(8,128)(2,1)}), f16[8,264,128]{2,1,0:T(8,128)(2,1)S(1)}, u32[]{:S(2)}, u32[]{:S(2)}) %all-to-all-start.7) | async-done | bytes 540704 | tf_op jit(solution)/shard_map/all_to_all | solution.py:394
  264.8 9.4 %all_to_all.45 = f16[8,72,128]{2,1,0:T(8,128)(2,1)S(1)} all-to-all(f16[8,72,128]{2,1,0:T(8,128)(2,1)S(1)} %select_convert_fusion), channel_id=1, replica_groups=mesh['row'=4,'col'=8] {'col'}, dimensions={0} | all-to-all | bytes 294912 | tf_op jit(solution)/shard_map/all_to_all | solution.py:394
  275.0 5.0 %marginal5.1 = f32[6,2,64,512]{3,2,1,0:T(8,128)} custom-call(s32[2]{0:T(128)} %pad_add_fusion.place.refs_0_, s32[6,8]{1,0:T(8,128)} %refs_1_.27, f32[2,64,512]{2,1,0:T(8,128)} %get-tuple-element.66.refs_2_, f32[8,264,128]{2,1,0:T(8,128)} %convert_element_type.204.refs_0_.refs_3_, ...), custom_call_target="tpu_custom_call", output_to_operand_aliasing={{}: (6, {})} | custom-call | tf_op jit(solution)/shard_map/marginal5/pallas_call | solution.py:511
  (143 shorter events, 68.1 us)
Async XLA Ops:
  7.2 17.3 %copy-start.4 = (bf16[15,2,64,512]{3,2,1,0:T(8,128)(2,1)S(1)}, bf16[15,2,64,512]{3,2,1,0:T(8,128)(2,1)}, u32[]{:S(2)}) copy-start(bf16[15,2,64,512]{3,2,1,0:T(8,128)(2,1)} %param.4) | copy-start | bytes 5898244
  7.2 55.9 %all-gather.13.cloned.1.call-start = ((), (), s32[]{:S(2)}) async-start(), calls=%async_computation.11 | async-start | bytes 2359296 | tf_op jit(solution)/shard_map/all_gather | solution.py:398
  8.3 14.3 %copy-start.2 = (bf16[1,2,64,512]{3,2,1,0:T(8,128)(2,1)}, bf16[1,2,64,512]{3,2,1,0:T(8,128)(2,1)S(1)}, u32[]{:S(2)}) copy-start(bf16[1,2,64,512]{3,2,1,0:T(8,128)(2,1)S(1)} %slice.30.refs_0_.refs_3_.refs_4_) | copy-start | bytes 393220
  8.3 10.8 %collective-permute-start = (bf16[1,2,64,512]{3,2,1,0:T(8,128)(2,1)S(1)}, bf16[1,2,64,512]{3,2,1,0:T(8,128)(2,1)S(1)}, u32[]{:S(2)}, u32[]{:S(2)}) collective-permute-start(bf16[1,2,64,512]{3,2,1,0:T(8,128)(2,1)S(1)} %slice.30.refs_0_.refs_3_.refs_4_), channel_id=1, source_target_pairs={{0,2},{1,3},{2,4},{3,5},{4,6},{5,7},{6,0},{7,1},{8,10},{9,11},{10,... | collective-permute-start | bytes 393224 | tf_op jit(solution)/shard_map/ppermute | solution.py:406
  11.4 11.2 %collective-permute-start.1 = (bf16[1,2,64,512]{3,2,1,0:T(8,128)(2,1)S(1)}, bf16[1,2,64,512]{3,2,1,0:T(8,128)(2,1)S(1)}, u32[]{:S(2)}, u32[]{:S(2)}) collective-permute-start(bf16[1,2,64,512]{3,2,1,0:T(8,128)(2,1)S(1)} %slice.30.refs_0_.refs_3_.refs_4_), channel_id=1, source_target_pairs={{0,4},{1,5},{2,6},{3,7},{4,0},{5,1},{6,2},{7,3},{8,12},{9,13},{10,... | collective-permute-start | bytes 393224 | tf_op jit(solution)/shard_map/ppermute | solution.py:406
  13.9 8.6 %collective-permute-start.2 = (bf16[1,2,64,512]{3,2,1,0:T(8,128)(2,1)S(1)}, bf16[1,2,64,512]{3,2,1,0:T(8,128)(2,1)S(1)}, u32[]{:S(2)}, u32[]{:S(2)}) collective-permute-start(bf16[1,2,64,512]{3,2,1,0:T(8,128)(2,1)S(1)} %slice.30.refs_0_.refs_3_.refs_4_), channel_id=1, source_target_pairs={{0,6},{1,7},{2,0},{3,1},{4,2},{5,3},{6,4},{7,5},{8,14},{9,15},{10,... | collective-permute-start | bytes 393224 | tf_op jit(solution)/shard_map/ppermute | solution.py:406
  19.1 3.5 %copy-start.5 = (bf16[1,2,64,512]{3,2,1,0:T(8,128)(2,1)}, bf16[1,2,64,512]{3,2,1,0:T(8,128)(2,1)S(1)}, u32[]{:S(2)}) copy-start(bf16[1,2,64,512]{3,2,1,0:T(8,128)(2,1)S(1)} %collective-permute-done.refs_1_.refs_5_.refs_6_) | copy-start | bytes 393220
  25.2 80.8 %all-gather.15.cloned.1.call-start = ((), (), s32[]{:S(2)}) async-start(), calls=%async_computation.12 | async-start | bytes 3538944 | tf_op jit(solution)/shard_map/all_gather | solution.py:398
  26.1 131.6 %all-gather.11.cloned.1.call-start = ((), (), s32[]{:S(2)}) async-start(), calls=%async_computation.10 | async-start | bytes 4718592 | tf_op jit(solution)/shard_map/all_gather | solution.py:398
  27.0 3.2 %copy-start.8 = (bf16[1,2,64,512]{3,2,1,0:T(8,128)(2,1)S(1)}, bf16[1,2,64,512]{3,2,1,0:T(8,128)(2,1)}, u32[]{:S(2)}) copy-start(bf16[1,2,64,512]{3,2,1,0:T(8,128)(2,1)} %copy-done.7) | copy-start | bytes 393220
  27.0 3.2 %copy-start.10 = (bf16[1,2,64,512]{3,2,1,0:T(8,128)(2,1)S(1)}, bf16[1,2,64,512]{3,2,1,0:T(8,128)(2,1)}, u32[]{:S(2)}) copy-start(bf16[1,2,64,512]{3,2,1,0:T(8,128)(2,1)} %copy-done.9) | copy-start | bytes 393220
  27.0 196.8 %all-gather.9.cloned.1.call-start = ((), (), s32[]{:S(2)}) async-start(), calls=%async_computation.9 | async-start | bytes 5898240 | tf_op jit(solution)/shard_map/all_gather | solution.py:398
  28.1 27.3 %copy-start.1 = (f32[6,2,64,512]{3,2,1,0:T(8,128)S(1)}, f32[6,2,64,512]{3,2,1,0:T(8,128)}, u32[]{:S(2)}) copy-start(f32[6,2,64,512]{3,2,1,0:T(8,128)} %whole_diag.1) | copy-start | bytes 4718596
  28.1 6.6 %collective-permute-start.3 = (f16[2,72,512]{2,1,0:T(8,128)(2,1)S(1)}, f16[2,72,512]{2,1,0:T(8,128)(2,1)S(1)}, u32[]{:S(2)}, u32[]{:S(2)}) collective-permute-start(f16[2,72,512]{2,1,0:T(8,128)(2,1)S(1)} %convert_element_type.159), channel_id=1, source_target_pairs={{0,8},{8,16},{16,24},{24,0},{1,9},{9,17},{17,25},{25,1},{2,10},{10... | collective-permute-start | bytes 442376 | tf_op jit(solution)/shard_map/ppermute | solution.py:388
  29.6 7.3 %collective-permute-start.6 = (bf16[1,2,64,512]{3,2,1,0:T(8,128)(2,1)S(1)}, bf16[1,2,64,512]{3,2,1,0:T(8,128)(2,1)S(1)}, u32[]{:S(2)}, u32[]{:S(2)}) collective-permute-start(bf16[1,2,64,512]{3,2,1,0:T(8,128)(2,1)S(1)} %copy-done.3), channel_id=1, source_target_pairs={{0,1},{1,0},{2,3},{3,2},{4,5},{5,4},{6,7},{7,6},{8,9},{9,8},{10,11... | collective-permute-start | bytes 393224 | tf_op jit(solution)/shard_map/ppermute | solution.py:407
  29.6 7.9 %collective-permute-start.7 = (bf16[1,2,64,512]{3,2,1,0:T(8,128)(2,1)S(1)}, bf16[1,2,64,512]{3,2,1,0:T(8,128)(2,1)S(1)}, u32[]{:S(2)}, u32[]{:S(2)}) collective-permute-start(bf16[1,2,64,512]{3,2,1,0:T(8,128)(2,1)S(1)} %copy-done.6), channel_id=1, source_target_pairs={{0,1},{1,0},{2,3},{3,2},{4,5},{5,4},{6,7},{7,6},{8,9},{9,8},{10,11... | collective-permute-start | bytes 393224 | tf_op jit(solution)/shard_map/ppermute | solution.py:407
  30.1 7.4 %collective-permute-start.8 = (bf16[1,2,64,512]{3,2,1,0:T(8,128)(2,1)S(1)}, bf16[1,2,64,512]{3,2,1,0:T(8,128)(2,1)S(1)}, u32[]{:S(2)}, u32[]{:S(2)}) collective-permute-start(bf16[1,2,64,512]{3,2,1,0:T(8,128)(2,1)S(1)} %copy-done.8), channel_id=1, source_target_pairs={{0,1},{1,0},{2,3},{3,2},{4,5},{5,4},{6,7},{7,6},{8,9},{9,8},{10,11... | collective-permute-start | bytes 393224 | tf_op jit(solution)/shard_map/ppermute | solution.py:407
  30.2 7.3 %collective-permute-start.9 = (bf16[1,2,64,512]{3,2,1,0:T(8,128)(2,1)S(1)}, bf16[1,2,64,512]{3,2,1,0:T(8,128)(2,1)S(1)}, u32[]{:S(2)}, u32[]{:S(2)}) collective-permute-start(bf16[1,2,64,512]{3,2,1,0:T(8,128)(2,1)S(1)} %copy-done.10), channel_id=1, source_target_pairs={{0,1},{1,0},{2,3},{3,2},{4,5},{5,4},{6,7},{7,6},{8,9},{9,8},{10,11... | collective-permute-start | bytes 393224 | tf_op jit(solution)/shard_map/ppermute | solution.py:407
  34.7 21.8 %collective-permute-start.4 = (f16[2,72,512]{2,1,0:T(8,128)(2,1)S(1)}, f16[2,72,512]{2,1,0:T(8,128)(2,1)S(1)}, u32[]{:S(2)}, u32[]{:S(2)}) collective-permute-start(f16[2,72,512]{2,1,0:T(8,128)(2,1)S(1)} %convert_element_type.159), channel_id=1, source_target_pairs={{0,16},{8,24},{16,0},{24,8},{1,17},{9,25},{17,1},{25,9},{2,18},{10... | collective-permute-start | bytes 442376 | tf_op jit(solution)/shard_map/ppermute | solution.py:388
  37.0 20.3 %collective-permute-start.5 = (f16[2,72,512]{2,1,0:T(8,128)(2,1)S(1)}, f16[2,72,512]{2,1,0:T(8,128)(2,1)S(1)}, u32[]{:S(2)}, u32[]{:S(2)}) collective-permute-start(f16[2,72,512]{2,1,0:T(8,128)(2,1)S(1)} %convert_element_type.159), channel_id=1, source_target_pairs={{0,24},{8,0},{16,8},{24,16},{1,25},{9,1},{17,9},{25,17},{2,26},{10... | collective-permute-start | bytes 442376 | tf_op jit(solution)/shard_map/ppermute | solution.py:388
  44.1 13.9 %collective-permute-start.10 = (f16[2,72,512]{2,1,0:T(8,128)(2,1)S(1)}, f16[2,72,512]{2,1,0:T(8,128)(2,1)S(1)}, u32[]{:S(2)}, u32[]{:S(2)}) collective-permute-start(f16[2,72,512]{2,1,0:T(8,128)(2,1)S(1)} %convert_element_type.163), channel_id=1, source_target_pairs={{0,8},{8,16},{16,24},{24,0},{1,9},{9,17},{17,25},{25,1},{2,10},{10... | collective-permute-start | bytes 442376 | tf_op jit(solution)/shard_map/ppermute | solution.py:388
  45.7 13.1 %collective-permute-start.11 = (f16[2,72,512]{2,1,0:T(8,128)(2,1)S(1)}, f16[2,72,512]{2,1,0:T(8,128)(2,1)S(1)}, u32[]{:S(2)}, u32[]{:S(2)}) collective-permute-start(f16[2,72,512]{2,1,0:T(8,128)(2,1)S(1)} %convert_element_type.163), channel_id=1, source_target_pairs={{0,16},{8,24},{16,0},{24,8},{1,17},{9,25},{17,1},{25,9},{2,18},{10... | collective-permute-start | bytes 442376 | tf_op jit(solution)/shard_map/ppermute | solution.py:388
  46.2 13.3 %collective-permute-start.12 = (f16[2,72,512]{2,1,0:T(8,128)(2,1)S(1)}, f16[2,72,512]{2,1,0:T(8,128)(2,1)S(1)}, u32[]{:S(2)}, u32[]{:S(2)}) collective-permute-start(f16[2,72,512]{2,1,0:T(8,128)(2,1)S(1)} %convert_element_type.163), channel_id=1, source_target_pairs={{0,24},{8,0},{16,8},{24,16},{1,25},{9,1},{17,9},{25,17},{2,26},{10... | collective-permute-start | bytes 442376 | tf_op jit(solution)/shard_map/ppermute | solution.py:388
  50.3 12.1 %all-to-all-start = ((f16[8,72,128]{2,1,0:T(8,128)(2,1)}), f16[8,72,128]{2,1,0:T(8,128)(2,1)S(1)}, u32[]{:S(2)}, u32[]{:S(2)}) async-start(f16[8,72,128]{2,1,0:T(8,128)(2,1)} %convert_element_type.167), calls=%async_computation | async-start | bytes 294912 | tf_op jit(solution)/shard_map/all_to_all | solution.py:394
  68.5 12.5 %collective-permute-start.13 = (f16[2,136,512]{2,1,0:T(8,128)(2,1)S(1)}, f16[2,136,512]{2,1,0:T(8,128)(2,1)S(1)}, u32[]{:S(2)}, u32[]{:S(2)}) collective-permute-start(f16[2,136,512]{2,1,0:T(8,128)(2,1)S(1)} %convert_element_type.169), channel_id=1, source_target_pairs={{0,8},{8,16},{16,24},{24,0},{1,9},{9,17},{17,25},{25,1},{2,10},{10... | collective-permute-start | bytes 835592 | tf_op jit(solution)/shard_map/ppermute | solution.py:388
  74.2 17.4 %all-to-all-start.1 = ((f16[8,72,128]{2,1,0:T(8,128)(2,1)}), f16[8,72,128]{2,1,0:T(8,128)(2,1)S(1)}, u32[]{:S(2)}, u32[]{:S(2)}) async-start(f16[8,72,128]{2,1,0:T(8,128)(2,1)} %convert_element_type.176), calls=%async_computation.1 | async-start | bytes 294912 | tf_op jit(solution)/shard_map/all_to_all | solution.py:394
  77.5 19.7 %collective-permute-start.14 = (f16[2,136,512]{2,1,0:T(8,128)(2,1)S(1)}, f16[2,136,512]{2,1,0:T(8,128)(2,1)S(1)}, u32[]{:S(2)}, u32[]{:S(2)}) collective-permute-start(f16[2,136,512]{2,1,0:T(8,128)(2,1)S(1)} %convert_element_type.169), channel_id=1, source_target_pairs={{0,16},{8,24},{16,0},{24,8},{1,17},{9,25},{17,1},{25,9},{2,18},{10... | collective-permute-start | bytes 835592 | tf_op jit(solution)/shard_map/ppermute | solution.py:388
  78.6 19.6 %collective-permute-start.15 = (f16[2,136,512]{2,1,0:T(8,128)(2,1)S(1)}, f16[2,136,512]{2,1,0:T(8,128)(2,1)S(1)}, u32[]{:S(2)}, u32[]{:S(2)}) collective-permute-start(f16[2,136,512]{2,1,0:T(8,128)(2,1)S(1)} %convert_element_type.169), channel_id=1, source_target_pairs={{0,24},{8,0},{16,8},{24,16},{1,25},{9,1},{17,9},{25,17},{2,26},{10... | collective-permute-start | bytes 835592 | tf_op jit(solution)/shard_map/ppermute | solution.py:388
  88.2 16.0 %collective-permute-start.16 = (f16[2,136,512]{2,1,0:T(8,128)(2,1)S(1)}, f16[2,136,512]{2,1,0:T(8,128)(2,1)S(1)}, u32[]{:S(2)}, u32[]{:S(2)}) collective-permute-start(f16[2,136,512]{2,1,0:T(8,128)(2,1)S(1)} %convert_element_type.173), channel_id=1, source_target_pairs={{0,8},{8,16},{16,24},{24,0},{1,9},{9,17},{17,25},{25,1},{2,10},{10... | collective-permute-start | bytes 835592 | tf_op jit(solution)/shard_map/ppermute | solution.py:388
  88.3 16.8 %collective-permute-start.17 = (f16[2,136,512]{2,1,0:T(8,128)(2,1)S(1)}, f16[2,136,512]{2,1,0:T(8,128)(2,1)S(1)}, u32[]{:S(2)}, u32[]{:S(2)}) collective-permute-start(f16[2,136,512]{2,1,0:T(8,128)(2,1)S(1)} %convert_element_type.173), channel_id=1, source_target_pairs={{0,16},{8,24},{16,0},{24,8},{1,17},{9,25},{17,1},{25,9},{2,18},{10... | collective-permute-start | bytes 835592 | tf_op jit(solution)/shard_map/ppermute | solution.py:388
  91.5 12.0 %all-to-all-start.2 = ((f16[8,72,128]{2,1,0:T(8,128)(2,1)}), f16[8,72,128]{2,1,0:T(8,128)(2,1)S(1)}, u32[]{:S(2)}, u32[]{:S(2)}) async-start(f16[8,72,128]{2,1,0:T(8,128)(2,1)} %convert_element_type.178), calls=%async_computation.2 | async-start | bytes 294912 | tf_op jit(solution)/shard_map/all_to_all | solution.py:394
  112.2 14.1 %collective-permute-start.18 = (f16[2,200,512]{2,1,0:T(8,128)(2,1)S(1)}, f16[2,200,512]{2,1,0:T(8,128)(2,1)S(1)}, u32[]{:S(2)}, u32[]{:S(2)}) collective-permute-start(f16[2,200,512]{2,1,0:T(8,128)(2,1)S(1)} %convert_element_type.180), channel_id=1, source_target_pairs={{0,8},{8,16},{16,24},{24,0},{1,9},{9,17},{17,25},{25,1},{2,10},{10... | collective-permute-start | bytes 1228808 | tf_op jit(solution)/shard_map/ppermute | solution.py:388
  121.2 22.0 %all-to-all-start.3 = ((f16[8,136,128]{2,1,0:T(8,128)(2,1)}), f16[8,136,128]{2,1,0:T(8,128)(2,1)S(1)}, u32[]{:S(2)}, u32[]{:S(2)}) async-start(f16[8,136,128]{2,1,0:T(8,128)(2,1)} %convert_element_type.185), calls=%async_computation.3 | async-start | bytes 557056 | tf_op jit(solution)/shard_map/all_to_all | solution.py:394
  124.6 28.4 %collective-permute-start.19 = (f16[2,200,512]{2,1,0:T(8,128)(2,1)S(1)}, f16[2,200,512]{2,1,0:T(8,128)(2,1)S(1)}, u32[]{:S(2)}, u32[]{:S(2)}) collective-permute-start(f16[2,200,512]{2,1,0:T(8,128)(2,1)S(1)} %convert_element_type.180), channel_id=1, source_target_pairs={{0,16},{8,24},{16,0},{24,8},{1,17},{9,25},{17,1},{25,9},{2,18},{10... | collective-permute-start | bytes 1228808 | tf_op jit(solution)/shard_map/ppermute | solution.py:388
  134.8 20.9 %collective-permute-start.20 = (f16[2,200,512]{2,1,0:T(8,128)(2,1)S(1)}, f16[2,200,512]{2,1,0:T(8,128)(2,1)S(1)}, u32[]{:S(2)}, u32[]{:S(2)}) collective-permute-start(f16[2,200,512]{2,1,0:T(8,128)(2,1)S(1)} %convert_element_type.183), channel_id=1, source_target_pairs={{0,8},{8,16},{16,24},{24,0},{1,9},{9,17},{17,25},{25,1},{2,10},{10... | collective-permute-start | bytes 1228808 | tf_op jit(solution)/shard_map/ppermute | solution.py:388
  134.8 21.9 %collective-permute-start.22 = (f16[2,200,512]{2,1,0:T(8,128)(2,1)S(1)}, f16[2,200,512]{2,1,0:T(8,128)(2,1)S(1)}, u32[]{:S(2)}, u32[]{:S(2)}) collective-permute-start(f16[2,200,512]{2,1,0:T(8,128)(2,1)S(1)} %convert_element_type.183), channel_id=1, source_target_pairs={{0,16},{8,24},{16,0},{24,8},{1,17},{9,25},{17,1},{25,9},{2,18},{10... | collective-permute-start | bytes 1228808 | tf_op jit(solution)/shard_map/ppermute | solution.py:388
  135.3 16.8 %collective-permute-start.21 = (f16[2,136,512]{2,1,0:T(8,128)(2,1)S(1)}, f16[2,136,512]{2,1,0:T(8,128)(2,1)S(1)}, u32[]{:S(2)}, u32[]{:S(2)}) collective-permute-start(f16[2,136,512]{2,1,0:T(8,128)(2,1)S(1)} %convert_element_type.173), channel_id=1, source_target_pairs={{0,24},{8,0},{16,8},{24,16},{1,25},{9,1},{17,9},{25,17},{2,26},{10... | collective-permute-start | bytes 835592 | tf_op jit(solution)/shard_map/ppermute | solution.py:388
  143.2 11.8 %all-to-all-start.4 = ((f16[8,72,128]{2,1,0:T(8,128)(2,1)}), f16[8,72,128]{2,1,0:T(8,128)(2,1)S(1)}, u32[]{:S(2)}, u32[]{:S(2)}) async-start(f16[8,72,128]{2,1,0:T(8,128)(2,1)} %convert_element_type.187), calls=%async_computation.4 | async-start | bytes 294912 | tf_op jit(solution)/shard_map/all_to_all | solution.py:394
  164.3 15.6 %collective-permute-start.23 = (f16[2,264,512]{2,1,0:T(8,128)(2,1)S(1)}, f16[2,264,512]{2,1,0:T(8,128)(2,1)S(1)}, u32[]{:S(2)}, u32[]{:S(2)}) collective-permute-start(f16[2,264,512]{2,1,0:T(8,128)(2,1)S(1)} %convert_element_type.193), channel_id=1, source_target_pairs={{0,8},{8,16},{16,24},{24,0},{1,9},{9,17},{17,25},{25,1},{2,10},{10... | collective-permute-start | bytes 1622024 | tf_op jit(solution)/shard_map/ppermute | solution.py:388
  173.5 29.3 %all-to-all-start.5 = ((f16[8,200,128]{2,1,0:T(8,128)(2,1)}), f16[8,200,128]{2,1,0:T(8,128)(2,1)S(1)}, u32[]{:S(2)}, u32[]{:S(2)}) async-start(f16[8,200,128]{2,1,0:T(8,128)(2,1)} %convert_element_type.191), calls=%async_computation.5 | async-start | bytes 819200 | tf_op jit(solution)/shard_map/all_to_all | solution.py:394
  178.3 35.7 %collective-permute-start.25 = (f16[2,264,512]{2,1,0:T(8,128)(2,1)S(1)}, f16[2,264,512]{2,1,0:T(8,128)(2,1)S(1)}, u32[]{:S(2)}, u32[]{:S(2)}) collective-permute-start(f16[2,264,512]{2,1,0:T(8,128)(2,1)S(1)} %convert_element_type.193), channel_id=1, source_target_pairs={{0,16},{8,24},{16,0},{24,8},{1,17},{9,25},{17,1},{25,9},{2,18},{10... | collective-permute-start | bytes 1622024 | tf_op jit(solution)/shard_map/ppermute | solution.py:388
  188.4 4.4 %copy-start.16 = (f32[8,72,128]{2,1,0:T(8,128)S(1)}, f32[8,72,128]{2,1,0:T(8,128)}, u32[]{:S(2)}) copy-start(f32[8,72,128]{2,1,0:T(8,128)} %get-tuple-element.56) | copy-start | bytes 884740
  189.8 29.6 %collective-permute-start.26 = (f16[2,264,512]{2,1,0:T(8,128)(2,1)S(1)}, f16[2,264,512]{2,1,0:T(8,128)(2,1)S(1)}, u32[]{:S(2)}, u32[]{:S(2)}) collective-permute-start(f16[2,264,512]{2,1,0:T(8,128)(2,1)S(1)} %convert_element_type.199), channel_id=1, source_target_pairs={{0,8},{8,16},{16,24},{24,0},{1,9},{9,17},{17,25},{25,1},{2,10},{10... | collective-permute-start | bytes 1622024 | tf_op jit(solution)/shard_map/ppermute | solution.py:388
  191.4 21.6 %collective-permute-start.24 = (f16[2,200,512]{2,1,0:T(8,128)(2,1)S(1)}, f16[2,200,512]{2,1,0:T(8,128)(2,1)S(1)}, u32[]{:S(2)}, u32[]{:S(2)}) collective-permute-start(f16[2,200,512]{2,1,0:T(8,128)(2,1)S(1)} %convert_element_type.180), channel_id=1, source_target_pairs={{0,24},{8,0},{16,8},{24,16},{1,25},{9,1},{17,9},{25,17},{2,26},{10... | collective-permute-start | bytes 1228808 | tf_op jit(solution)/shard_map/ppermute | solution.py:388
  202.8 15.8 %all-to-all-start.6 = ((f16[8,72,128]{2,1,0:T(8,128)(2,1)}), f16[8,72,128]{2,1,0:T(8,128)(2,1)S(1)}, u32[]{:S(2)}, u32[]{:S(2)}) async-start(f16[8,72,128]{2,1,0:T(8,128)(2,1)} %convert_element_type.195), calls=%async_computation.6 | async-start | bytes 294912 | tf_op jit(solution)/shard_map/all_to_all | solution.py:394
  230.9 18.4 %collective-permute-start.27 = (f16[2,328,512]{2,1,0:T(8,128)(2,1)S(1)}, f16[2,328,512]{2,1,0:T(8,128)(2,1)S(1)}, u32[]{:S(2)}, u32[]{:S(2)}) collective-permute-start(f16[2,328,512]{2,1,0:T(8,128)(2,1)S(1)} %convert_element_type.201), channel_id=1, source_target_pairs={{0,8},{8,16},{16,24},{24,0},{1,9},{9,17},{17,25},{25,1},{2,10},{10... | collective-permute-start | bytes 2015240 | tf_op jit(solution)/shard_map/ppermute | solution.py:388
  243.4 19.2 %all-to-all-start.7 = ((f16[8,264,128]{2,1,0:T(8,128)(2,1)}), f16[8,264,128]{2,1,0:T(8,128)(2,1)S(1)}, u32[]{:S(2)}, u32[]{:S(2)}) async-start(f16[8,264,128]{2,1,0:T(8,128)(2,1)} %convert_element_type.203), calls=%async_computation.7 | async-start | bytes 1081344 | tf_op jit(solution)/shard_map/all_to_all | solution.py:394
  258.0 6.8 %copy-start.15 = (f32[8,72,128]{2,1,0:T(8,128)S(1)}, f32[8,72,128]{2,1,0:T(8,128)}, u32[]{:S(2)}) copy-start(f32[8,72,128]{2,1,0:T(8,128)} %get-tuple-element.64) | copy-start | bytes 884740
  (9 other events, 11.3 us)
Sparse Core Ops, SparseCore 0:
  25.4 31.0 all-gather.12
  58.1 40.9 all-gather.14
  100.7 52.1 all-gather.10
  154.4 69.3 all-gather.8

commit v6 on v5

--- a/solution.py
+++ b/solution.py
@@ -10,7 +10,7 @@
 F32 = jnp.float32
 BF16 = jnp.bfloat16
 F16 = jnp.float16
-TOP = 2.0**14
+TOP = 2.0**8
 TAIL = 8
 VMEM = pl.BlockSpec(memory_space=pltpu.VMEM)
 SMEM = pl.BlockSpec(memory_space=pltpu.SMEM)
@@ -19,15 +19,17 @@
 
 def factors(peak):
     rows = lax.broadcasted_iota(jnp.int32, (TAIL, peak.shape[1]), 0)
-    rest = jnp.maximum(peak, 2.0**-100)
+    rest = peak
     table = jnp.ones((TAIL, peak.shape[1]), F32)
-    whole = jnp.ones_like(rest)
+    scale = jnp.full_like(peak, TOP)
     for i in range(TAIL):
-        one = jnp.clip(rest, 2.0**-14, TOP).astype(BF16).astype(F32)
-        rest = rest / one
-        table = jnp.where(rows == i, jnp.broadcast_to(one, table.shape), table)
-        whole = whole * one
-    return table, whole
+        large, small = rest > 2.0**7, rest < 2.0**-7
+        up = jnp.where(large, 2.0**14, jnp.where(small, 2.0**-14, 1.0))
+        down = jnp.where(large, 2.0**-14, jnp.where(small, 2.0**14, 1.0))
+        rest = rest * down
+        scale = scale * down
+        table = jnp.where(rows == i, jnp.broadcast_to(up, table.shape), table)
+    return table, scale
 
 
 def product(table):
@@ -62,8 +64,8 @@
     for n in range(npr):
         value = diag_base(diag[n], sizes[0, row * npr + n], col * rows, rows, width)
         marginal[n] = value
-        table, whole = factors(peak_of(value))
-        message[n, :rows] = value * (TOP / whole)
+        table, scale = factors(peak_of(value))
+        message[n, :rows] = value * scale
         message[n, rows:] = table
     keep = pltpu.make_async_copy(marginal, out.at[0], out_sem)
     keep.start()
@@ -81,8 +83,8 @@
     high = values[0].shape[0]
     parts = []
     for value in values:
-        table, whole = factors(peak_of(value))
-        parts.append((value * (TOP / whole), table))
+        table, scale = factors(peak_of(value))
+        parts.append((value * scale, table))
     for c in range(turn.shape[0]):
         piece = slice(c * rows, (c + 1) * rows)
         turn[c, :high] = jnp.concatenate([v[:, piece] for v, _ in parts], axis=1)
@@ -264,8 +266,8 @@
         if level > 1:
             value = jnp.concatenate([upper[n], value], axis=0)
         if not last:
-            table, whole = factors(peak_of(value))
-            passed[n, :high] = value * (TOP / whole)
+            table, scale = factors(peak_of(value))
+            passed[n, :high] = value * scale
             passed[n, high:] = table
     keep.wait()
 
@@ -326,8 +328,7 @@
             peak = peak_of(value)
             for side in sides[n]:
                 peak = jnp.maximum(peak, peak_of(side))
-            table, whole = factors(peak)
-            scale = TOP / whole
+            table, scale = factors(peak)
             for l in range(level):
                 message[n, l * rows : (l + 1) * rows] = sides[n][l] * scale
             message[n, high : high + rows] = value * scale
@@ -345,7 +346,7 @@
     if rows_only:
         if back == 1:
             return "due", level
-        return "due", (level if back < 3 or level < 2 else level + back - 2)
+        return "due", (2 if level == 1 else level + max(back - 2, 0))
     return "due", (level + 1 if level == 1 else level + back - 1)
 
 

time: 289 us -> 288 us (level)
  waiting for transfers between devices: 51.9 us -> 47.1 us
  starting transfers between devices: 67.2 us -> 71.2 us
    all_gather x4, waiting for transfers between devices: 3.27 us -> 0.01 us  [gathered(): return lax.all_gather(mine, 'col', axis=0)]
  transfers between devices with their start and end apart: 40 -> 40, of which waited for: 12 -> 10; matrix products, arithmetic and copies ran while one was open for 18% -> 18% of each run, Pallas kernels for 25% -> 25%
where the time goes in v6:
time: 288 us; the launch traced here: 285 us
  Pallas kernels  84.3 us (29%)
  starting transfers between devices  71.2 us (25%)
  other arithmetic  53.7 us (19%)
  waiting for transfers between devices  47.1 us (16%)
  between operations  15.5 us (5%)
  blocking collectives  9.39 us (3%)
  local copies, waits for them, and re-layouts  4.2 us (1%)
    all_to_all x8, starting transfers between devices, turn_over(): lax.all_to_all(message.astype(F16), 'col', 0, 0, tiled=True).astype(F32)  34.4 us
    pallas_call x5, Pallas kernels, shards(): pl.pallas_call(functools.partial(cross_kernel, level, last, len(whole), o...  30.6 us
    ppermute x21, starting transfers between devices, spread(): found.append(lax.ppermute(half, 'row', route).astype(F32))  28.6 us
    pallas_call x5, Pallas kernels, shards(): pl.pallas_call(functools.partial(marginal_kernel, level, last, len(whole)...  24.8 us
    pallas_call x4, Pallas kernels, shards(): pl.pallas_call(functools.partial(upper_kernel, level, len(whole), off, 1,...  24.7 us
    all_to_all x8, waiting for transfers between devices, turn_over(): lax.all_to_all(message.astype(F16), 'col', 0, 0, tiled=True).astype(F32)  23.7 us
    ppermute x21, waiting for transfers between devices, spread(): found.append(lax.ppermute(half, 'row', route).astype(F32))  19.8 us
    convert_element_type x21, other arithmetic, spread(): found.append(lax.ppermute(half, 'row', route).astype(F32))  19.6 us
  transfers between devices with their start and end apart: 40, of which 10 were waited for; matrix products, arithmetic and copies ran while one was open for 18% of the time, Pallas kernels for 25%

profile of v6, /device:TPU:0, one launch (start us, length us, event | category | flops | bytes accessed | tf_op | source)
XLA Modules:
  0.0 285.5 jit_solution(1990079810617240313)
XLA Ops:
  8.3 3.1 %collective-permute-start = (bf16[1,2,64,512]{3,2,1,0:T(8,128)(2,1)S(1)}, bf16[1,2,64,512]{3,2,1,0:T(8,128)(2,1)S(1)}, u32[]{:S(2)}, u32[]{:S(2)}) collective-permute-start(bf16[1,2,64,512]{3,2,1,0:T(8,128)(2,1)S(1)} %slice.30.refs_0_.refs_3_.refs_4_), channel_id=1, source_target_pairs={{0,2},{1,3},{2,4},{3,5},{4,6},{5,7},{6,0},{7,1},{8,10},{9,11},{10,... | collective-permute-start | bytes 393224 | tf_op jit(solution)/shard_map/ppermute | solution.py:407
  11.4 2.6 collective-permute-start.1
  15.8 3.2 %base.1 = (f32[6,2,64,512]{3,2,1,0:T(8,128)}, f32[2,72,512]{2,1,0:T(8,128)}) custom-call(s32[2]{0:T(128)} %pad_add_fusion.place.refs_0_, s32[6,8]{1,0:T(8,128)} %refs_1_.27, f32[6,2,64,512]{3,2,1,0:T(8,128)} %whole_diag.1), custom_call_target="tpu_custom_call" | custom-call | tf_op jit(solution)/shard_map/base/pallas_call | solution.py:413
  19.1 3.5 %collective-permute-done.1.refs_2_.refs_7_.refs_8_ = bf16[1,2,64,512]{3,2,1,0:T(8,128)(2,1)S(1)} collective-permute-done((bf16[1,2,64,512]{3,2,1,0:T(8,128)(2,1)S(1)}, bf16[1,2,64,512]{3,2,1,0:T(8,128)(2,1)S(1)}, u32[]{:S(2)}, u32[]{:S(2)}) %collective-permute-start.1) | collective-permute-done | bytes 131104 | tf_op jit(solution)/shard_map/ppermute | solution.py:407
  30.7 4.1 %collective-permute-done.3 = f16[2,72,512]{2,1,0:T(8,128)(2,1)S(1)} collective-permute-done((f16[2,72,512]{2,1,0:T(8,128)(2,1)S(1)}, f16[2,72,512]{2,1,0:T(8,128)(2,1)S(1)}, u32[]{:S(2)}, u32[]{:S(2)}) %collective-permute-start.3) | collective-permute-done | bytes 147488 | tf_op jit(solution)/shard_map/ppermute | solution.py:389
  38.9 4.3 %cross1.1 = (f32[15,2,64,512]{3,2,1,0:T(8,128)}, f32[8,72,128]{2,1,0:T(8,128)}, f32[2,72,512]{2,1,0:T(8,128)}) custom-call(s32[2]{0:T(128)} %pad_add_fusion.place.refs_0_, s32[5,8]{1,0:T(8,128)} %refs_1_.26, s32[6,8]{1,0:T(8,128)} %refs_1_.27, bf16[1,2,64,512]{3,2,1,0:T(8,128)(2,1)} %copy-done.2, bf16[1,2,64,512]{3,2,1,0:T(8,128)(2,1)} %copy-done.11, ...), custom_call_target="tpu_custom_call" | custom-call | tf_op jit(solution)/shard_map/cross1/pallas_call | solution.py:481
  44.1 1.5 collective-permute-start.10
  45.7 1.6 convert_element_type.167
  47.3 5.1 %all-to-all-start = ((f16[8,72,128]{2,1,0:T(8,128)(2,1)}), f16[8,72,128]{2,1,0:T(8,128)(2,1)S(1)}, u32[]{:S(2)}, u32[]{:S(2)}) async-start(f16[8,72,128]{2,1,0:T(8,128)(2,1)} %convert_element_type.167), calls=%async_computation | async-start | bytes 294912 | tf_op jit(solution)/shard_map/all_to_all | solution.py:395
  55.8 3.6 %all-to-all-done = f16[8,72,128]{2,1,0:T(8,128)(2,1)S(1)} async-done(((f16[8,72,128]{2,1,0:T(8,128)(2,1)}), f16[8,72,128]{2,1,0:T(8,128)(2,1)S(1)}, u32[]{:S(2)}, u32[]{:S(2)}) %all-to-all-start) | async-done | bytes 147488 | tf_op jit(solution)/shard_map/all_to_all | solution.py:395
  60.2 4.2 %marginal1.1 = (f32[6,2,64,512]{3,2,1,0:T(8,128)}, f32[2,136,512]{2,1,0:T(8,128)}) custom-call(s32[2]{0:T(128)} %pad_add_fusion.place.refs_0_, s32[6,8]{1,0:T(8,128)} %refs_1_.27, f32[2,64,512]{2,1,0:T(8,128)} %get-tuple-element.68.refs_2_, f32[8,72,128]{2,1,0:T(8,128)} %convert_element_type.168.refs_3_, ...), custom_call_target="tpu_custom_call", output_to_operand_aliasing={{0}: (16, {})} | custom-call | tf_op jit(solution)/shard_map/marginal1/pallas_call | solution.py:512
  67.0 3.9 %upper2.1 = (f32[2,64,512]{2,1,0:T(8,128)}, f32[8,72,128]{2,1,0:T(8,128)}) custom-call(s32[2]{0:T(128)} %pad_add_fusion.place.refs_0_, s32[5,8]{1,0:T(8,128)} %refs_1_.26, s32[6,8]{1,0:T(8,128)} %refs_1_.27, bf16[8,2,2,64,512]{4,3,2,1,0:T(8,128)(2,1)} %bitcast.31, f32[2,72,512]{2,1,0:T(8,128)} %get-tuple-element.34.refs_4_.refs_11_, ...), custom_call_target="tpu_custom_call" | custom-call | tf_op jit(solution)/shard_map/upper2/pallas_call | solution.py:454
  70.9 1.6 convert_element_type.176
  72.6 3.4 %all-to-all-start.1 = ((f16[8,72,128]{2,1,0:T(8,128)(2,1)}), f16[8,72,128]{2,1,0:T(8,128)(2,1)S(1)}, u32[]{:S(2)}, u32[]{:S(2)}) async-start(f16[8,72,128]{2,1,0:T(8,128)(2,1)} %convert_element_type.176), calls=%async_computation.1 | async-start | bytes 294912 | tf_op jit(solution)/shard_map/all_to_all | solution.py:395
  80.4 5.2 %cross2.1 = (f32[15,2,64,512]{3,2,1,0:T(8,128)}, f32[8,72,128]{2,1,0:T(8,128)}, f32[2,136,512]{2,1,0:T(8,128)}) custom-call(s32[2]{0:T(128)} %pad_add_fusion.place.refs_0_, s32[5,8]{1,0:T(8,128)} %refs_1_.26, s32[6,8]{1,0:T(8,128)} %refs_1_.27, bf16[8,2,2,64,512]{4,3,2,1,0:T(8,128)(2,1)} %bitcast.32, ...), custom_call_target="tpu_custom_call", output_to_operand_aliasing={{0}: (7, {})} | custom-call | tf_op jit(solution)/shard_map/cross2/pallas_call | solution.py:481
  87.8 1.6 convert_element_type.178
  89.4 5.0 %all-to-all-start.2 = ((f16[8,72,128]{2,1,0:T(8,128)(2,1)}), f16[8,72,128]{2,1,0:T(8,128)(2,1)S(1)}, u32[]{:S(2)}, u32[]{:S(2)}) async-start(f16[8,72,128]{2,1,0:T(8,128)(2,1)} %convert_element_type.178), calls=%async_computation.2 | async-start | bytes 294912 | tf_op jit(solution)/shard_map/all_to_all | solution.py:395
  94.4 2.8 collective-permute-start.12
  97.9 3.4 %collective-permute-done.12 = f16[2,72,512]{2,1,0:T(8,128)(2,1)S(1)} collective-permute-done((f16[2,72,512]{2,1,0:T(8,128)(2,1)S(1)}, f16[2,72,512]{2,1,0:T(8,128)(2,1)S(1)}, u32[]{:S(2)}, u32[]{:S(2)}) %collective-permute-start.12) | collective-permute-done | bytes 147488 | tf_op jit(solution)/shard_map/ppermute | solution.py:389
  107.1 4.7 %marginal2.1 = (f32[6,2,64,512]{3,2,1,0:T(8,128)}, f32[2,200,512]{2,1,0:T(8,128)}) custom-call(s32[2]{0:T(128)} %pad_add_fusion.place.refs_0_, s32[6,8]{1,0:T(8,128)} %refs_1_.27, f32[2,64,512]{2,1,0:T(8,128)} %get-tuple-element.67.refs_2_, f32[8,72,128]{2,1,0:T(8,128)} %convert_element_type.177.refs_3_, ...), custom_call_target="tpu_custom_call", output_to_operand_aliasing={{0}: (13, {})} | custom-call | tf_op jit(solution)/shard_map/marginal2/pallas_call | solution.py:512
  113.0 2.8 collective-permute-start.18
  115.8 5.2 %upper3.1 = (f32[2,128,512]{2,1,0:T(8,128)}, f32[8,136,128]{2,1,0:T(8,128)}) custom-call(s32[2]{0:T(128)} %pad_add_fusion.place.refs_0_, s32[5,8]{1,0:T(8,128)} %refs_1_.26, s32[6,8]{1,0:T(8,128)} %refs_1_.27, bf16[8,3,2,64,512]{4,3,2,1,0:T(8,128)(2,1)} %bitcast.23, f32[2,72,512]{2,1,0:T(8,128)} %get-tuple-element.34.refs_4_.refs_11_, ...), custom_call_target="tpu_custom_call" | custom-call | tf_op jit(solution)/shard_map/upper3/pallas_call | solution.py:454
  121.0 1.8 convert_element_type.185
  122.8 4.7 %all-to-all-start.3 = ((f16[8,136,128]{2,1,0:T(8,128)(2,1)}), f16[8,136,128]{2,1,0:T(8,128)(2,1)S(1)}, u32[]{:S(2)}, u32[]{:S(2)}) async-start(f16[8,136,128]{2,1,0:T(8,128)(2,1)} %convert_element_type.185), calls=%async_computation.3 | async-start | bytes 557056 | tf_op jit(solution)/shard_map/all_to_all | solution.py:395
  129.5 6.3 %cross3.1 = (f32[15,2,64,512]{3,2,1,0:T(8,128)}, f32[8,72,128]{2,1,0:T(8,128)}, f32[2,200,512]{2,1,0:T(8,128)}) custom-call(s32[2]{0:T(128)} %pad_add_fusion.place.refs_0_, s32[5,8]{1,0:T(8,128)} %refs_1_.26, s32[6,8]{1,0:T(8,128)} %refs_1_.27, bf16[8,3,2,64,512]{4,3,2,1,0:T(8,128)(2,1)} %bitcast.24, ...), custom_call_target="tpu_custom_call", output_to_operand_aliasing={{0}: (7, {})} | custom-call | tf_op jit(solution)/shard_map/cross3/pallas_call | solution.py:481
  138.1 2.8 collective-permute-start.21
  140.9 1.6 convert_element_type.187
  142.6 3.4 %all-to-all-done.3 = f16[8,136,128]{2,1,0:T(8,128)(2,1)S(1)} async-done(((f16[8,136,128]{2,1,0:T(8,128)(2,1)}), f16[8,136,128]{2,1,0:T(8,128)(2,1)S(1)}, u32[]{:S(2)}, u32[]{:S(2)}) %all-to-all-start.3) | async-done | bytes 278560 | tf_op jit(solution)/shard_map/all_to_all | solution.py:395
  146.0 3.6 %all-to-all-start.4 = ((f16[8,72,128]{2,1,0:T(8,128)(2,1)}), f16[8,72,128]{2,1,0:T(8,128)(2,1)S(1)}, u32[]{:S(2)}, u32[]{:S(2)}) async-start(f16[8,72,128]{2,1,0:T(8,128)(2,1)} %convert_element_type.187), calls=%async_computation.4 | async-start | bytes 294912 | tf_op jit(solution)/shard_map/all_to_all | solution.py:395
  149.5 5.6 %collective-permute-done.21 = f16[2,136,512]{2,1,0:T(8,128)(2,1)S(1)} collective-permute-done((f16[2,136,512]{2,1,0:T(8,128)(2,1)S(1)}, f16[2,136,512]{2,1,0:T(8,128)(2,1)S(1)}, u32[]{:S(2)}, u32[]{:S(2)}) %collective-permute-start.21) | collective-permute-done | bytes 278560 | tf_op jit(solution)/shard_map/ppermute | solution.py:389
  160.7 5.4 %marginal3.1 = (f32[6,2,64,512]{3,2,1,0:T(8,128)}, f32[2,264,512]{2,1,0:T(8,128)}) custom-call(s32[2]{0:T(128)} %pad_add_fusion.place.refs_0_, s32[6,8]{1,0:T(8,128)} %refs_1_.27, f32[2,64,512]{2,1,0:T(8,128)} %get-tuple-element.70.refs_2_, f32[8,136,128]{2,1,0:T(8,128)} %convert_element_type.186.refs_3_, ...), custom_call_target="tpu_custom_call", output_to_operand_aliasing={{0}: (11, {})} | custom-call | tf_op jit(solution)/shard_map/marginal3/pallas_call | solution.py:512
  168.1 6.9 %upper4.1 = (f32[2,192,512]{2,1,0:T(8,128)}, f32[8,200,128]{2,1,0:T(8,128)}) custom-call(s32[2]{0:T(128)} %pad_add_fusion.place.refs_0_, s32[5,8]{1,0:T(8,128)} %refs_1_.26, s32[6,8]{1,0:T(8,128)} %refs_1_.27, bf16[8,4,2,64,512]{4,3,2,1,0:T(8,128)(2,1)} %bitcast.19, f32[2,72,512]{2,1,0:T(8,128)} %get-tuple-element.34.refs_4_.refs_11_, ...), custom_call_target="tpu_custom_call" | custom-call | tf_op jit(solution)/shard_map/upper4/pallas_call | solution.py:454
  175.0 2.0 convert_element_type.191
  177.0 4.6 %all-to-all-start.5 = ((f16[8,200,128]{2,1,0:T(8,128)(2,1)}), f16[8,200,128]{2,1,0:T(8,128)(2,1)S(1)}, u32[]{:S(2)}, u32[]{:S(2)}) async-start(f16[8,200,128]{2,1,0:T(8,128)(2,1)} %convert_element_type.191), calls=%async_computation.5 | async-start | bytes 819200 | tf_op jit(solution)/shard_map/all_to_all | solution.py:395
  183.8 7.2 %cross4.1 = (f32[15,2,64,512]{3,2,1,0:T(8,128)}, f32[8,72,128]{2,1,0:T(8,128)}, f32[2,264,512]{2,1,0:T(8,128)}) custom-call(s32[2]{0:T(128)} %pad_add_fusion.place.refs_0_, s32[5,8]{1,0:T(8,128)} %refs_1_.26, s32[6,8]{1,0:T(8,128)} %refs_1_.27, bf16[8,4,2,64,512]{4,3,2,1,0:T(8,128)(2,1)} %bitcast.20, ...), custom_call_target="tpu_custom_call", output_to_operand_aliasing={{0}: (7, {})} | custom-call | tf_op jit(solution)/shard_map/cross4/pallas_call | solution.py:481
  192.3 1.8 collective-permute-start.26
  196.0 10.2 %all-to-all-done.5 = f16[8,200,128]{2,1,0:T(8,128)(2,1)S(1)} async-done(((f16[8,200,128]{2,1,0:T(8,128)(2,1)}), f16[8,200,128]{2,1,0:T(8,128)(2,1)S(1)}, u32[]{:S(2)}, u32[]{:S(2)}) %all-to-all-start.5) | async-done | bytes 409632 | tf_op jit(solution)/shard_map/all_to_all | solution.py:395
  206.2 3.4 %all-to-all-start.6 = ((f16[8,72,128]{2,1,0:T(8,128)(2,1)}), f16[8,72,128]{2,1,0:T(8,128)(2,1)S(1)}, u32[]{:S(2)}, u32[]{:S(2)}) async-start(f16[8,72,128]{2,1,0:T(8,128)(2,1)} %convert_element_type.195), calls=%async_computation.6 | async-start | bytes 294912 | tf_op jit(solution)/shard_map/all_to_all | solution.py:395
  209.6 6.4 %collective-permute-done.24 = f16[2,200,512]{2,1,0:T(8,128)(2,1)S(1)} collective-permute-done((f16[2,200,512]{2,1,0:T(8,128)(2,1)S(1)}, f16[2,200,512]{2,1,0:T(8,128)(2,1)S(1)}, u32[]{:S(2)}, u32[]{:S(2)}) %collective-permute-start.24) | collective-permute-done | bytes 409632 | tf_op jit(solution)/shard_map/ppermute | solution.py:389
  221.0 5.6 %marginal4.1 = (f32[6,2,64,512]{3,2,1,0:T(8,128)}, f32[2,328,512]{2,1,0:T(8,128)}) custom-call(s32[2]{0:T(128)} %pad_add_fusion.place.refs_0_, s32[6,8]{1,0:T(8,128)} %refs_1_.27, f32[2,64,512]{2,1,0:T(8,128)} %get-tuple-element.69.refs_2_, f32[8,200,128]{2,1,0:T(8,128)} %convert_element_type.192.refs_3_, ...), custom_call_target="tpu_custom_call", output_to_operand_aliasing={{0}: (10, {})} | custom-call | tf_op jit(solution)/shard_map/marginal4/pallas_call | solution.py:512
  228.1 2.2 collective-permute-start.27
  230.3 8.6 %upper5.1 = (f32[2,256,512]{2,1,0:T(8,128)}, f32[8,264,128]{2,1,0:T(8,128)}) custom-call(s32[2]{0:T(128)} %pad_add_fusion.place.refs_0_, s32[5,8]{1,0:T(8,128)} %refs_1_.26, s32[6,8]{1,0:T(8,128)} %refs_1_.27, bf16[8,5,2,64,512]{4,3,2,1,0:T(8,128)(2,1)} %bitcast.27, f32[2,72,512]{2,1,0:T(8,128)} %get-tuple-element.34.refs_4_.refs_11_, ...), custom_call_target="tpu_custom_call" | custom-call | tf_op jit(solution)/shard_map/upper5/pallas_call | solution.py:454
  239.0 2.2 convert_element_type.203
  241.1 4.7 %all-to-all-start.7 = ((f16[8,264,128]{2,1,0:T(8,128)(2,1)}), f16[8,264,128]{2,1,0:T(8,128)(2,1)S(1)}, u32[]{:S(2)}, u32[]{:S(2)}) async-start(f16[8,264,128]{2,1,0:T(8,128)(2,1)} %convert_element_type.203), calls=%async_computation.7 | async-start | bytes 1081344 | tf_op jit(solution)/shard_map/all_to_all | solution.py:395
  247.4 7.7 %cross5.1 = (f32[15,2,64,512]{3,2,1,0:T(8,128)}, f32[8,72,128]{2,1,0:T(8,128)}) custom-call(s32[2]{0:T(128)} %pad_add_fusion.place.refs_0_, s32[5,8]{1,0:T(8,128)} %refs_1_.26, s32[6,8]{1,0:T(8,128)} %refs_1_.27, bf16[8,5,2,64,512]{4,3,2,1,0:T(8,128)(2,1)} %bitcast.28, ...), custom_call_target="tpu_custom_call", output_to_operand_aliasing={{0}: (7, {})} | custom-call | flops 40000000000 | bytes 1048576 | tf_op jit(solution)/shard_map/cross5/pallas_call | solution.py:481
  255.1 6.4 %all-to-all-done.7 = f16[8,264,128]{2,1,0:T(8,128)(2,1)S(1)} async-done(((f16[8,264,128]{2,1,0:T(8,128)(2,1)}), f16[8,264,128]{2,1,0:T(8,128)(2,1)S(1)}, u32[]{:S(2)}, u32[]{:S(2)}) %all-to-all-start.7) | async-done | bytes 540704 | tf_op jit(solution)/shard_map/all_to_all | solution.py:395
  263.8 9.4 %all_to_all.45 = f16[8,72,128]{2,1,0:T(8,128)(2,1)S(1)} all-to-all(f16[8,72,128]{2,1,0:T(8,128)(2,1)S(1)} %select_convert_fusion), channel_id=1, replica_groups=mesh['row'=4,'col'=8] {'col'}, dimensions={0} | all-to-all | bytes 294912 | tf_op jit(solution)/shard_map/all_to_all | solution.py:395
  274.0 5.0 %marginal5.1 = f32[6,2,64,512]{3,2,1,0:T(8,128)} custom-call(s32[2]{0:T(128)} %pad_add_fusion.place.refs_0_, s32[6,8]{1,0:T(8,128)} %refs_1_.27, f32[2,64,512]{2,1,0:T(8,128)} %get-tuple-element.66.refs_2_, f32[8,264,128]{2,1,0:T(8,128)} %convert_element_type.204.refs_0_.refs_3_, ...), custom_call_target="tpu_custom_call", output_to_operand_aliasing={{}: (6, {})} | custom-call | tf_op jit(solution)/shard_map/marginal5/pallas_call | solution.py:512
  (143 shorter events, 64.2 us)
Async XLA Ops:
  7.2 17.3 %copy-start.4 = (bf16[15,2,64,512]{3,2,1,0:T(8,128)(2,1)S(1)}, bf16[15,2,64,512]{3,2,1,0:T(8,128)(2,1)}, u32[]{:S(2)}) copy-start(bf16[15,2,64,512]{3,2,1,0:T(8,128)(2,1)} %param.4) | copy-start | bytes 5898244
  7.2 53.0 %all-gather.13.cloned.1.call-start = ((), (), s32[]{:S(2)}) async-start(), calls=%async_computation.11 | async-start | bytes 2359296 | tf_op jit(solution)/shard_map/all_gather | solution.py:399
  8.3 14.3 %copy-start.2 = (bf16[1,2,64,512]{3,2,1,0:T(8,128)(2,1)}, bf16[1,2,64,512]{3,2,1,0:T(8,128)(2,1)S(1)}, u32[]{:S(2)}) copy-start(bf16[1,2,64,512]{3,2,1,0:T(8,128)(2,1)S(1)} %slice.30.refs_0_.refs_3_.refs_4_) | copy-start | bytes 393220
  8.3 10.8 %collective-permute-start = (bf16[1,2,64,512]{3,2,1,0:T(8,128)(2,1)S(1)}, bf16[1,2,64,512]{3,2,1,0:T(8,128)(2,1)S(1)}, u32[]{:S(2)}, u32[]{:S(2)}) collective-permute-start(bf16[1,2,64,512]{3,2,1,0:T(8,128)(2,1)S(1)} %slice.30.refs_0_.refs_3_.refs_4_), channel_id=1, source_target_pairs={{0,2},{1,3},{2,4},{3,5},{4,6},{5,7},{6,0},{7,1},{8,10},{9,11},{10,... | collective-permute-start | bytes 393224 | tf_op jit(solution)/shard_map/ppermute | solution.py:407
  11.4 11.2 %collective-permute-start.1 = (bf16[1,2,64,512]{3,2,1,0:T(8,128)(2,1)S(1)}, bf16[1,2,64,512]{3,2,1,0:T(8,128)(2,1)S(1)}, u32[]{:S(2)}, u32[]{:S(2)}) collective-permute-start(bf16[1,2,64,512]{3,2,1,0:T(8,128)(2,1)S(1)} %slice.30.refs_0_.refs_3_.refs_4_), channel_id=1, source_target_pairs={{0,4},{1,5},{2,6},{3,7},{4,0},{5,1},{6,2},{7,3},{8,12},{9,13},{10,... | collective-permute-start | bytes 393224 | tf_op jit(solution)/shard_map/ppermute | solution.py:407
  13.9 8.6 %collective-permute-start.2 = (bf16[1,2,64,512]{3,2,1,0:T(8,128)(2,1)S(1)}, bf16[1,2,64,512]{3,2,1,0:T(8,128)(2,1)S(1)}, u32[]{:S(2)}, u32[]{:S(2)}) collective-permute-start(bf16[1,2,64,512]{3,2,1,0:T(8,128)(2,1)S(1)} %slice.30.refs_0_.refs_3_.refs_4_), channel_id=1, source_target_pairs={{0,6},{1,7},{2,0},{3,1},{4,2},{5,3},{6,4},{7,5},{8,14},{9,15},{10,... | collective-permute-start | bytes 393224 | tf_op jit(solution)/shard_map/ppermute | solution.py:407
  19.1 3.5 %copy-start.5 = (bf16[1,2,64,512]{3,2,1,0:T(8,128)(2,1)}, bf16[1,2,64,512]{3,2,1,0:T(8,128)(2,1)S(1)}, u32[]{:S(2)}) copy-start(bf16[1,2,64,512]{3,2,1,0:T(8,128)(2,1)S(1)} %collective-permute-done.refs_1_.refs_5_.refs_6_) | copy-start | bytes 393220
  25.2 81.9 %all-gather.15.cloned.1.call-start = ((), (), s32[]{:S(2)}) async-start(), calls=%async_computation.12 | async-start | bytes 3538944 | tf_op jit(solution)/shard_map/all_gather | solution.py:399
  26.1 134.6 %all-gather.11.cloned.1.call-start = ((), (), s32[]{:S(2)}) async-start(), calls=%async_computation.10 | async-start | bytes 4718592 | tf_op jit(solution)/shard_map/all_gather | solution.py:399
  27.0 3.2 %copy-start.8 = (bf16[1,2,64,512]{3,2,1,0:T(8,128)(2,1)S(1)}, bf16[1,2,64,512]{3,2,1,0:T(8,128)(2,1)}, u32[]{:S(2)}) copy-start(bf16[1,2,64,512]{3,2,1,0:T(8,128)(2,1)} %copy-done.7) | copy-start | bytes 393220
  27.0 3.2 %copy-start.10 = (bf16[1,2,64,512]{3,2,1,0:T(8,128)(2,1)S(1)}, bf16[1,2,64,512]{3,2,1,0:T(8,128)(2,1)}, u32[]{:S(2)}) copy-start(bf16[1,2,64,512]{3,2,1,0:T(8,128)(2,1)} %copy-done.9) | copy-start | bytes 393220
  27.0 194.0 %all-gather.9.cloned.1.call-start = ((), (), s32[]{:S(2)}) async-start(), calls=%async_computation.9 | async-start | bytes 5898240 | tf_op jit(solution)/shard_map/all_gather | solution.py:399
  28.1 24.3 %copy-start.1 = (f32[6,2,64,512]{3,2,1,0:T(8,128)S(1)}, f32[6,2,64,512]{3,2,1,0:T(8,128)}, u32[]{:S(2)}) copy-start(f32[6,2,64,512]{3,2,1,0:T(8,128)} %whole_diag.1) | copy-start | bytes 4718596
  28.1 6.6 %collective-permute-start.3 = (f16[2,72,512]{2,1,0:T(8,128)(2,1)S(1)}, f16[2,72,512]{2,1,0:T(8,128)(2,1)S(1)}, u32[]{:S(2)}, u32[]{:S(2)}) collective-permute-start(f16[2,72,512]{2,1,0:T(8,128)(2,1)S(1)} %convert_element_type.159), channel_id=1, source_target_pairs={{0,8},{8,16},{16,24},{24,0},{1,9},{9,17},{17,25},{25,1},{2,10},{10... | collective-permute-start | bytes 442376 | tf_op jit(solution)/shard_map/ppermute | solution.py:389
  29.6 7.3 %collective-permute-start.6 = (bf16[1,2,64,512]{3,2,1,0:T(8,128)(2,1)S(1)}, bf16[1,2,64,512]{3,2,1,0:T(8,128)(2,1)S(1)}, u32[]{:S(2)}, u32[]{:S(2)}) collective-permute-start(bf16[1,2,64,512]{3,2,1,0:T(8,128)(2,1)S(1)} %copy-done.3), channel_id=1, source_target_pairs={{0,1},{1,0},{2,3},{3,2},{4,5},{5,4},{6,7},{7,6},{8,9},{9,8},{10,11... | collective-permute-start | bytes 393224 | tf_op jit(solution)/shard_map/ppermute | solution.py:408
  29.6 7.9 %collective-permute-start.7 = (bf16[1,2,64,512]{3,2,1,0:T(8,128)(2,1)S(1)}, bf16[1,2,64,512]{3,2,1,0:T(8,128)(2,1)S(1)}, u32[]{:S(2)}, u32[]{:S(2)}) collective-permute-start(bf16[1,2,64,512]{3,2,1,0:T(8,128)(2,1)S(1)} %copy-done.6), channel_id=1, source_target_pairs={{0,1},{1,0},{2,3},{3,2},{4,5},{5,4},{6,7},{7,6},{8,9},{9,8},{10,11... | collective-permute-start | bytes 393224 | tf_op jit(solution)/shard_map/ppermute | solution.py:408
  30.1 7.4 %collective-permute-start.8 = (bf16[1,2,64,512]{3,2,1,0:T(8,128)(2,1)S(1)}, bf16[1,2,64,512]{3,2,1,0:T(8,128)(2,1)S(1)}, u32[]{:S(2)}, u32[]{:S(2)}) collective-permute-start(bf16[1,2,64,512]{3,2,1,0:T(8,128)(2,1)S(1)} %copy-done.8), channel_id=1, source_target_pairs={{0,1},{1,0},{2,3},{3,2},{4,5},{5,4},{6,7},{7,6},{8,9},{9,8},{10,11... | collective-permute-start | bytes 393224 | tf_op jit(solution)/shard_map/ppermute | solution.py:408
  30.2 7.3 %collective-permute-start.9 = (bf16[1,2,64,512]{3,2,1,0:T(8,128)(2,1)S(1)}, bf16[1,2,64,512]{3,2,1,0:T(8,128)(2,1)S(1)}, u32[]{:S(2)}, u32[]{:S(2)}) collective-permute-start(bf16[1,2,64,512]{3,2,1,0:T(8,128)(2,1)S(1)} %copy-done.10), channel_id=1, source_target_pairs={{0,1},{1,0},{2,3},{3,2},{4,5},{5,4},{6,7},{7,6},{8,9},{9,8},{10,11... | collective-permute-start | bytes 393224 | tf_op jit(solution)/shard_map/ppermute | solution.py:408
  34.7 18.8 %collective-permute-start.4 = (f16[2,72,512]{2,1,0:T(8,128)(2,1)S(1)}, f16[2,72,512]{2,1,0:T(8,128)(2,1)S(1)}, u32[]{:S(2)}, u32[]{:S(2)}) collective-permute-start(f16[2,72,512]{2,1,0:T(8,128)(2,1)S(1)} %convert_element_type.159), channel_id=1, source_target_pairs={{0,16},{8,24},{16,0},{24,8},{1,17},{9,25},{17,1},{25,9},{2,18},{10... | collective-permute-start | bytes 442376 | tf_op jit(solution)/shard_map/ppermute | solution.py:389
  37.0 17.3 %collective-permute-start.5 = (f16[2,72,512]{2,1,0:T(8,128)(2,1)S(1)}, f16[2,72,512]{2,1,0:T(8,128)(2,1)S(1)}, u32[]{:S(2)}, u32[]{:S(2)}) collective-permute-start(f16[2,72,512]{2,1,0:T(8,128)(2,1)S(1)} %convert_element_type.159), channel_id=1, source_target_pairs={{0,24},{8,0},{16,8},{24,16},{1,25},{9,1},{17,9},{25,17},{2,26},{10... | collective-permute-start | bytes 442376 | tf_op jit(solution)/shard_map/ppermute | solution.py:389
  44.1 10.9 %collective-permute-start.10 = (f16[2,72,512]{2,1,0:T(8,128)(2,1)S(1)}, f16[2,72,512]{2,1,0:T(8,128)(2,1)S(1)}, u32[]{:S(2)}, u32[]{:S(2)}) collective-permute-start(f16[2,72,512]{2,1,0:T(8,128)(2,1)S(1)} %convert_element_type.163), channel_id=1, source_target_pairs={{0,8},{8,16},{16,24},{24,0},{1,9},{9,17},{17,25},{25,1},{2,10},{10... | collective-permute-start | bytes 442376 | tf_op jit(solution)/shard_map/ppermute | solution.py:389
  47.3 12.1 %all-to-all-start = ((f16[8,72,128]{2,1,0:T(8,128)(2,1)}), f16[8,72,128]{2,1,0:T(8,128)(2,1)S(1)}, u32[]{:S(2)}, u32[]{:S(2)}) async-start(f16[8,72,128]{2,1,0:T(8,128)(2,1)} %convert_element_type.167), calls=%async_computation | async-start | bytes 294912 | tf_op jit(solution)/shard_map/all_to_all | solution.py:395
  65.5 14.0 %collective-permute-start.13 = (f16[2,136,512]{2,1,0:T(8,128)(2,1)S(1)}, f16[2,136,512]{2,1,0:T(8,128)(2,1)S(1)}, u32[]{:S(2)}, u32[]{:S(2)}) collective-permute-start(f16[2,136,512]{2,1,0:T(8,128)(2,1)S(1)} %convert_element_type.169), channel_id=1, source_target_pairs={{0,8},{8,16},{16,24},{24,0},{1,9},{9,17},{17,25},{25,1},{2,10},{10... | collective-permute-start | bytes 835592 | tf_op jit(solution)/shard_map/ppermute | solution.py:389
  72.6 16.8 %all-to-all-start.1 = ((f16[8,72,128]{2,1,0:T(8,128)(2,1)}), f16[8,72,128]{2,1,0:T(8,128)(2,1)S(1)}, u32[]{:S(2)}, u32[]{:S(2)}) async-start(f16[8,72,128]{2,1,0:T(8,128)(2,1)} %convert_element_type.176), calls=%async_computation.1 | async-start | bytes 294912 | tf_op jit(solution)/shard_map/all_to_all | solution.py:395
  75.9 18.4 %collective-permute-start.11 = (f16[2,72,512]{2,1,0:T(8,128)(2,1)S(1)}, f16[2,72,512]{2,1,0:T(8,128)(2,1)S(1)}, u32[]{:S(2)}, u32[]{:S(2)}) collective-permute-start(f16[2,72,512]{2,1,0:T(8,128)(2,1)S(1)} %convert_element_type.163), channel_id=1, source_target_pairs={{0,16},{8,24},{16,0},{24,8},{1,17},{9,25},{17,1},{25,9},{2,18},{10... | collective-permute-start | bytes 442376 | tf_op jit(solution)/shard_map/ppermute | solution.py:389
  76.5 26.3 %collective-permute-start.14 = (f16[2,136,512]{2,1,0:T(8,128)(2,1)S(1)}, f16[2,136,512]{2,1,0:T(8,128)(2,1)S(1)}, u32[]{:S(2)}, u32[]{:S(2)}) collective-permute-start(f16[2,136,512]{2,1,0:T(8,128)(2,1)S(1)} %convert_element_type.169), channel_id=1, source_target_pairs={{0,16},{8,24},{16,0},{24,8},{1,17},{9,25},{17,1},{25,9},{2,18},{10... | collective-permute-start | bytes 835592 | tf_op jit(solution)/shard_map/ppermute | solution.py:389
  78.0 25.7 %collective-permute-start.15 = (f16[2,136,512]{2,1,0:T(8,128)(2,1)S(1)}, f16[2,136,512]{2,1,0:T(8,128)(2,1)S(1)}, u32[]{:S(2)}, u32[]{:S(2)}) collective-permute-start(f16[2,136,512]{2,1,0:T(8,128)(2,1)S(1)} %convert_element_type.169), channel_id=1, source_target_pairs={{0,24},{8,0},{16,8},{24,16},{1,25},{9,1},{17,9},{25,17},{2,26},{10... | collective-permute-start | bytes 835592 | tf_op jit(solution)/shard_map/ppermute | solution.py:389
  86.7 18.7 %collective-permute-start.16 = (f16[2,136,512]{2,1,0:T(8,128)(2,1)S(1)}, f16[2,136,512]{2,1,0:T(8,128)(2,1)S(1)}, u32[]{:S(2)}, u32[]{:S(2)}) collective-permute-start(f16[2,136,512]{2,1,0:T(8,128)(2,1)S(1)} %convert_element_type.173), channel_id=1, source_target_pairs={{0,8},{8,16},{16,24},{24,0},{1,9},{9,17},{17,25},{25,1},{2,10},{10... | collective-permute-start | bytes 835592 | tf_op jit(solution)/shard_map/ppermute | solution.py:389
  87.3 18.9 %collective-permute-start.17 = (f16[2,136,512]{2,1,0:T(8,128)(2,1)S(1)}, f16[2,136,512]{2,1,0:T(8,128)(2,1)S(1)}, u32[]{:S(2)}, u32[]{:S(2)}) collective-permute-start(f16[2,136,512]{2,1,0:T(8,128)(2,1)S(1)} %convert_element_type.173), channel_id=1, source_target_pairs={{0,16},{8,24},{16,0},{24,8},{1,17},{9,25},{17,1},{25,9},{2,18},{10... | collective-permute-start | bytes 835592 | tf_op jit(solution)/shard_map/ppermute | solution.py:389
  89.4 15.2 %all-to-all-start.2 = ((f16[8,72,128]{2,1,0:T(8,128)(2,1)}), f16[8,72,128]{2,1,0:T(8,128)(2,1)S(1)}, u32[]{:S(2)}, u32[]{:S(2)}) async-start(f16[8,72,128]{2,1,0:T(8,128)(2,1)} %convert_element_type.178), calls=%async_computation.2 | async-start | bytes 294912 | tf_op jit(solution)/shard_map/all_to_all | solution.py:395
  94.4 6.9 %collective-permute-start.12 = (f16[2,72,512]{2,1,0:T(8,128)(2,1)S(1)}, f16[2,72,512]{2,1,0:T(8,128)(2,1)S(1)}, u32[]{:S(2)}, u32[]{:S(2)}) collective-permute-start(f16[2,72,512]{2,1,0:T(8,128)(2,1)S(1)} %convert_element_type.163), channel_id=1, source_target_pairs={{0,24},{8,0},{16,8},{24,16},{1,25},{9,1},{17,9},{25,17},{2,26},{10... | collective-permute-start | bytes 442376 | tf_op jit(solution)/shard_map/ppermute | solution.py:389
  113.0 15.5 %collective-permute-start.18 = (f16[2,200,512]{2,1,0:T(8,128)(2,1)S(1)}, f16[2,200,512]{2,1,0:T(8,128)(2,1)S(1)}, u32[]{:S(2)}, u32[]{:S(2)}) collective-permute-start(f16[2,200,512]{2,1,0:T(8,128)(2,1)S(1)} %convert_element_type.180), channel_id=1, source_target_pairs={{0,8},{8,16},{16,24},{24,0},{1,9},{9,17},{17,25},{25,1},{2,10},{10... | collective-permute-start | bytes 1228808 | tf_op jit(solution)/shard_map/ppermute | solution.py:389
  122.8 23.1 %all-to-all-start.3 = ((f16[8,136,128]{2,1,0:T(8,128)(2,1)}), f16[8,136,128]{2,1,0:T(8,128)(2,1)S(1)}, u32[]{:S(2)}, u32[]{:S(2)}) async-start(f16[8,136,128]{2,1,0:T(8,128)(2,1)} %convert_element_type.185), calls=%async_computation.3 | async-start | bytes 557056 | tf_op jit(solution)/shard_map/all_to_all | solution.py:395
  127.5 28.5 %collective-permute-start.19 = (f16[2,200,512]{2,1,0:T(8,128)(2,1)S(1)}, f16[2,200,512]{2,1,0:T(8,128)(2,1)S(1)}, u32[]{:S(2)}, u32[]{:S(2)}) collective-permute-start(f16[2,200,512]{2,1,0:T(8,128)(2,1)S(1)} %convert_element_type.180), channel_id=1, source_target_pairs={{0,16},{8,24},{16,0},{24,8},{1,17},{9,25},{17,1},{25,9},{2,18},{10... | collective-permute-start | bytes 1228808 | tf_op jit(solution)/shard_map/ppermute | solution.py:389
  137.0 21.7 %collective-permute-start.20 = (f16[2,200,512]{2,1,0:T(8,128)(2,1)S(1)}, f16[2,200,512]{2,1,0:T(8,128)(2,1)S(1)}, u32[]{:S(2)}, u32[]{:S(2)}) collective-permute-start(f16[2,200,512]{2,1,0:T(8,128)(2,1)S(1)} %convert_element_type.183), channel_id=1, source_target_pairs={{0,8},{8,16},{16,24},{24,0},{1,9},{9,17},{17,25},{25,1},{2,10},{10... | collective-permute-start | bytes 1228808 | tf_op jit(solution)/shard_map/ppermute | solution.py:389
  137.0 22.6 %collective-permute-start.22 = (f16[2,200,512]{2,1,0:T(8,128)(2,1)S(1)}, f16[2,200,512]{2,1,0:T(8,128)(2,1)S(1)}, u32[]{:S(2)}, u32[]{:S(2)}) collective-permute-start(f16[2,200,512]{2,1,0:T(8,128)(2,1)S(1)} %convert_element_type.183), channel_id=1, source_target_pairs={{0,16},{8,24},{16,0},{24,8},{1,17},{9,25},{17,1},{25,9},{2,18},{10... | collective-permute-start | bytes 1228808 | tf_op jit(solution)/shard_map/ppermute | solution.py:389
  138.1 17.0 %collective-permute-start.21 = (f16[2,136,512]{2,1,0:T(8,128)(2,1)S(1)}, f16[2,136,512]{2,1,0:T(8,128)(2,1)S(1)}, u32[]{:S(2)}, u32[]{:S(2)}) collective-permute-start(f16[2,136,512]{2,1,0:T(8,128)(2,1)S(1)} %convert_element_type.173), channel_id=1, source_target_pairs={{0,24},{8,0},{16,8},{24,16},{1,25},{9,1},{17,9},{25,17},{2,26},{10... | collective-permute-start | bytes 835592 | tf_op jit(solution)/shard_map/ppermute | solution.py:389
  146.0 11.9 %all-to-all-start.4 = ((f16[8,72,128]{2,1,0:T(8,128)(2,1)}), f16[8,72,128]{2,1,0:T(8,128)(2,1)S(1)}, u32[]{:S(2)}, u32[]{:S(2)}) async-start(f16[8,72,128]{2,1,0:T(8,128)(2,1)} %convert_element_type.187), calls=%async_computation.4 | async-start | bytes 294912 | tf_op jit(solution)/shard_map/all_to_all | solution.py:395
  167.4 15.2 %collective-permute-start.23 = (f16[2,264,512]{2,1,0:T(8,128)(2,1)S(1)}, f16[2,264,512]{2,1,0:T(8,128)(2,1)S(1)}, u32[]{:S(2)}, u32[]{:S(2)}) collective-permute-start(f16[2,264,512]{2,1,0:T(8,128)(2,1)S(1)} %convert_element_type.193), channel_id=1, source_target_pairs={{0,8},{8,16},{16,24},{24,0},{1,9},{9,17},{17,25},{25,1},{2,10},{10... | collective-permute-start | bytes 1622024 | tf_op jit(solution)/shard_map/ppermute | solution.py:389
  177.0 29.3 %all-to-all-start.5 = ((f16[8,200,128]{2,1,0:T(8,128)(2,1)}), f16[8,200,128]{2,1,0:T(8,128)(2,1)S(1)}, u32[]{:S(2)}, u32[]{:S(2)}) async-start(f16[8,200,128]{2,1,0:T(8,128)(2,1)} %convert_element_type.191), calls=%async_computation.5 | async-start | bytes 819200 | tf_op jit(solution)/shard_map/all_to_all | solution.py:395
  181.6 35.5 %collective-permute-start.25 = (f16[2,264,512]{2,1,0:T(8,128)(2,1)S(1)}, f16[2,264,512]{2,1,0:T(8,128)(2,1)S(1)}, u32[]{:S(2)}, u32[]{:S(2)}) collective-permute-start(f16[2,264,512]{2,1,0:T(8,128)(2,1)S(1)} %convert_element_type.193), channel_id=1, source_target_pairs={{0,16},{8,24},{16,0},{24,8},{1,17},{9,25},{17,1},{25,9},{2,18},{10... | collective-permute-start | bytes 1622024 | tf_op jit(solution)/shard_map/ppermute | solution.py:389
  190.9 4.4 %copy-start.16 = (f32[8,72,128]{2,1,0:T(8,128)S(1)}, f32[8,72,128]{2,1,0:T(8,128)}, u32[]{:S(2)}) copy-start(f32[8,72,128]{2,1,0:T(8,128)} %get-tuple-element.56) | copy-start | bytes 884740
  192.3 27.6 %collective-permute-start.26 = (f16[2,264,512]{2,1,0:T(8,128)(2,1)S(1)}, f16[2,264,512]{2,1,0:T(8,128)(2,1)S(1)}, u32[]{:S(2)}, u32[]{:S(2)}) collective-permute-start(f16[2,264,512]{2,1,0:T(8,128)(2,1)S(1)} %convert_element_type.199), channel_id=1, source_target_pairs={{0,8},{8,16},{16,24},{24,0},{1,9},{9,17},{17,25},{25,1},{2,10},{10... | collective-permute-start | bytes 1622024 | tf_op jit(solution)/shard_map/ppermute | solution.py:389
  194.2 21.9 %collective-permute-start.24 = (f16[2,200,512]{2,1,0:T(8,128)(2,1)S(1)}, f16[2,200,512]{2,1,0:T(8,128)(2,1)S(1)}, u32[]{:S(2)}, u32[]{:S(2)}) collective-permute-start(f16[2,200,512]{2,1,0:T(8,128)(2,1)S(1)} %convert_element_type.180), channel_id=1, source_target_pairs={{0,24},{8,0},{16,8},{24,16},{1,25},{9,1},{17,9},{25,17},{2,26},{10... | collective-permute-start | bytes 1228808 | tf_op jit(solution)/shard_map/ppermute | solution.py:389
  206.2 12.9 %all-to-all-start.6 = ((f16[8,72,128]{2,1,0:T(8,128)(2,1)}), f16[8,72,128]{2,1,0:T(8,128)(2,1)S(1)}, u32[]{:S(2)}, u32[]{:S(2)}) async-start(f16[8,72,128]{2,1,0:T(8,128)(2,1)} %convert_element_type.195), calls=%async_computation.6 | async-start | bytes 294912 | tf_op jit(solution)/shard_map/all_to_all | solution.py:395
  228.1 18.0 %collective-permute-start.27 = (f16[2,328,512]{2,1,0:T(8,128)(2,1)S(1)}, f16[2,328,512]{2,1,0:T(8,128)(2,1)S(1)}, u32[]{:S(2)}, u32[]{:S(2)}) collective-permute-start(f16[2,328,512]{2,1,0:T(8,128)(2,1)S(1)} %convert_element_type.201), channel_id=1, source_target_pairs={{0,8},{8,16},{16,24},{24,0},{1,9},{9,17},{17,25},{25,1},{2,10},{10... | collective-permute-start | bytes 2015240 | tf_op jit(solution)/shard_map/ppermute | solution.py:389
  241.1 20.4 %all-to-all-start.7 = ((f16[8,264,128]{2,1,0:T(8,128)(2,1)}), f16[8,264,128]{2,1,0:T(8,128)(2,1)S(1)}, u32[]{:S(2)}, u32[]{:S(2)}) async-start(f16[8,264,128]{2,1,0:T(8,128)(2,1)} %convert_element_type.203), calls=%async_computation.7 | async-start | bytes 1081344 | tf_op jit(solution)/shard_map/all_to_all | solution.py:395
  255.1 8.6 %copy-start.15 = (f32[8,72,128]{2,1,0:T(8,128)S(1)}, f32[8,72,128]{2,1,0:T(8,128)}, u32[]{:S(2)}) copy-start(f32[8,72,128]{2,1,0:T(8,128)} %get-tuple-element.64) | copy-start | bytes 884740
  (9 other events, 11.2 us)
Sparse Core Ops, SparseCore 0:
  25.4 31.0 all-gather.12
  58.1 40.9 all-gather.14
  100.7 51.7 all-gather.10
  154.0 66.5 all-gather.8

commit v7 on v6

--- a/solution.py
+++ b/solution.py
@@ -272,6 +272,43 @@
     keep.wait()
 
 
+def scales_of(part, rows):
+    lines = part.shape[1] - TAIL
+    return jnp.concatenate(
+        [jnp.broadcast_to(product(part[c, lines:]), (rows, part.shape[2])) for c in range(part.shape[0])], axis=0
+    )
+
+
+def flat_terms(part, at_row, scale, rows, width):
+    flat = (part[:, at_row : at_row + rows].reshape(width, part.shape[2]) * scale).T
+    top = flat.astype(BF16)
+    return flat, top, (flat - top.astype(F32)).astype(BF16)
+
+
+def against(top, low, mine, block, rows):
+    pair = jnp.concatenate([top[mine], low[mine]], axis=0)
+    term = jnp.dot(pair, block, preferred_element_type=F32)
+    return term[:rows] + term[rows:]
+
+
+def partial_kernel(level, off, npr, rows, width, place, turned, panel, out, lower, panel_sem):
+    start, wait = panel_moves([panel], off, lower, panel_sem, place[1], lower.shape[2])
+    for m in range(level - 1):
+        for n in range(npr):
+            start(n, m)
+    scale = scales_of(turned, rows)
+    totals = [None] * npr
+    for l in range(level - 1):
+        _, top, low = flat_terms(turned, l * rows, scale, rows, width)
+        for n in range(npr):
+            wait(n, l)
+            mine = slice(n * rows, (n + 1) * rows)
+            term = against(top, low, mine, lower[n, l].reshape(width, width), rows)
+            totals[n] = term if totals[n] is None else totals[n] + term
+    for n in range(npr):
+        out[n] = totals[n]
+
+
 def marginal_kernel(level, last, n_panel, off, n_wait, n_row, npr, rows, width, *refs):
     place, sizes, diag = refs[:3]
     n_turned = min(level, 2)
@@ -288,32 +325,24 @@
 
     start, wait = panel_moves(panel, off, lower, panel_sem, place[1], lower.shape[2])
 
-    for m in range(level):
+    todo = range(level)
+    totals = [None] * npr
+    if last and level > 1:
+        todo = range(level - 1, level)
+        totals = [turned[0][n] for n in range(npr)]
+    for m in todo:
         for n in range(npr):
             start(n, m)
 
-    def scales_of(part):
-        lines = part.shape[1] - TAIL
-        return jnp.concatenate(
-            [jnp.broadcast_to(product(part[c, lines:]), (rows, npr * rows)) for c in range(n_col)], axis=0
-        )
-
-    scales = [scales_of(part) for part in turned]
-    totals = [None] * npr
+    scales = [None if len(todo) < level and i == 0 else scales_of(part, rows) for i, part in enumerate(turned)]
     sides = [[] for _ in range(npr)]
-    for l in range(level):
+    for l in todo:
         i, at_row = (n_turned - 1, 0) if l == level - 1 else (0, l * rows)
-        upright = turned[i][:, at_row : at_row + rows].reshape(width, npr * rows) * scales[i]
-        flat = upright.T
-        top = flat.astype(BF16)
-        low = (flat - top.astype(F32)).astype(BF16)
+        flat, top, low = flat_terms(turned[i], at_row, scales[i], rows, width)
         for n in range(npr):
             mine = slice(n * rows, (n + 1) * rows)
             wait(n, l)
-            block = lower[n, l].reshape(width, width)
-            pair = jnp.concatenate([top[mine], low[mine]], axis=0)
-            term = jnp.dot(pair, block, preferred_element_type=F32)
-            term = term[:rows] + term[rows:]
+            term = against(top, low, mine, lower[n, l].reshape(width, width), rows)
             totals[n] = term if totals[n] is None else totals[n] + term
             sides[n].append(flat[mine])
     for n in range(npr):
@@ -504,6 +533,18 @@
         newer = made[1]
         if last and turned:
             newer = jnp.where(gate(f"turn{level}", turned) > 0, newer, 0.0)
+        if last and turned:
+            turned = [
+                pl.pallas_call(
+                    functools.partial(partial_kernel, level, off, npr, rows, width),
+                    out_shape=shape(npr, rows, width),
+                    in_specs=[SMEM, VMEM, ANY],
+                    out_specs=VMEM,
+                    scratch_shapes=panel_scratch + [pltpu.SemaphoreType.DMA((npr, level))],
+                    compiler_params=params(),
+                    name=f"partial{level}",
+                )(place, turned[0], *whole)
+            ]
         turned.append(turn_over(newer))
         waits = [] if last else due[level] + whole_panel[level + 1][0]
         out_shape = [shape(levels, npr, rows, width)]

time: 288 us -> 288 us (level)
  blocking collectives: 9.39 us -> 0 us
  starting transfers between devices: 71.2 us -> 74.2 us
    all_to_all x1 -> x0, blocking collectives: 9.39 us -> none  [turn_over(): lax.all_to_all(message.astype(F16), 'col', 0, 0, tiled=True).astype(F32)]
    pallas_call x0 -> x1, Pallas kernels: none -> 4.5 us  [shards(): pl.pallas_call(functools.partial(partial_kernel, level, off, npr, rows, w...]
    all_to_all x8 -> x9, starting transfers between devices: 34.4 us -> 38.8 us  [turn_over(): lax.all_to_all(message.astype(F16), 'col', 0, 0, tiled=True).astype(F32)]
    all_to_all x8 -> x9, waiting for transfers between devices: 23.7 us -> 23.7 us  [turn_over(): lax.all_to_all(message.astype(F16), 'col', 0, 0, tiled=True).astype(F32)]
  transfers between devices with their start and end apart: 40 -> 41, of which waited for: 10 -> 13; matrix products, arithmetic and copies ran while one was open for 18% -> 18% of each run, Pallas kernels for 25% -> 27%
where the time goes in v7:
time: 288 us; the launch traced here: 285 us
  Pallas kernels  87.1 us (30%)
  starting transfers between devices  74.2 us (26%)
  other arithmetic  54.4 us (19%)
  waiting for transfers between devices  49.8 us (17%)
  between operations  15.4 us (5%)
  local copies, waits for them, and re-layouts  4.2 us (1%)
    all_to_all x9, starting transfers between devices, turn_over(): lax.all_to_all(message.astype(F16), 'col', 0, 0, tiled=True).astype(F32)  38.8 us
    pallas_call x5, Pallas kernels, shards(): pl.pallas_call(functools.partial(cross_kernel, level, last, len(whole), o...  30.6 us
    ppermute x21, starting transfers between devices, spread(): found.append(lax.ppermute(half, 'row', route).astype(F32))  27.3 us
    pallas_call x4, Pallas kernels, shards(): pl.pallas_call(functools.partial(upper_kernel, level, len(whole), off, 1,...  24.5 us
    all_to_all x9, waiting for transfers between devices, turn_over(): lax.all_to_all(message.astype(F16), 'col', 0, 0, tiled=True).astype(F32)  23.7 us
    pallas_call x5, Pallas kernels, shards(): pl.pallas_call(functools.partial(marginal_kernel, level, last, len(whole)...  23.4 us
    ppermute x21, waiting for transfers between devices, spread(): found.append(lax.ppermute(half, 'row', route).astype(F32))  22.1 us
    convert_element_type x21, other arithmetic, spread(): found.append(lax.ppermute(half, 'row', route).astype(F32))  19.6 us
  transfers between devices with their start and end apart: 41, of which 13 were waited for; matrix products, arithmetic and copies ran while one was open for 18% of the time, Pallas kernels for 27%

profile of v7, /device:TPU:0, one launch (start us, length us, event | category | flops | bytes accessed | tf_op | source)
XLA Modules:
  0.0 285.2 jit_solution(17042608565604875250)
XLA Ops:
  8.3 3.1 %collective-permute-start = (bf16[1,2,64,512]{3,2,1,0:T(8,128)(2,1)S(1)}, bf16[1,2,64,512]{3,2,1,0:T(8,128)(2,1)S(1)}, u32[]{:S(2)}, u32[]{:S(2)}) collective-permute-start(bf16[1,2,64,512]{3,2,1,0:T(8,128)(2,1)S(1)} %slice.30.refs_0_.refs_3_.refs_4_), channel_id=1, source_target_pairs={{0,2},{1,3},{2,4},{3,5},{4,6},{5,7},{6,0},{7,1},{8,10},{9,11},{10,... | collective-permute-start | bytes 393224 | tf_op jit(solution)/shard_map/ppermute | solution.py:436
  11.4 2.6 collective-permute-start.1
  15.9 3.2 %base.1 = (f32[6,2,64,512]{3,2,1,0:T(8,128)}, f32[2,72,512]{2,1,0:T(8,128)}) custom-call(s32[2]{0:T(128)} %pad_add_fusion.place.refs_0_, s32[6,8]{1,0:T(8,128)} %refs_1_.27, f32[6,2,64,512]{3,2,1,0:T(8,128)} %whole_diag.1), custom_call_target="tpu_custom_call" | custom-call | tf_op jit(solution)/shard_map/base/pallas_call | solution.py:442
  19.1 3.5 %collective-permute-done.1.refs_2_.refs_7_.refs_8_ = bf16[1,2,64,512]{3,2,1,0:T(8,128)(2,1)S(1)} collective-permute-done((bf16[1,2,64,512]{3,2,1,0:T(8,128)(2,1)S(1)}, bf16[1,2,64,512]{3,2,1,0:T(8,128)(2,1)S(1)}, u32[]{:S(2)}, u32[]{:S(2)}) %collective-permute-start.1) | collective-permute-done | bytes 131104 | tf_op jit(solution)/shard_map/ppermute | solution.py:436
  30.7 4.1 %collective-permute-done.3 = f16[2,72,512]{2,1,0:T(8,128)(2,1)S(1)} collective-permute-done((f16[2,72,512]{2,1,0:T(8,128)(2,1)S(1)}, f16[2,72,512]{2,1,0:T(8,128)(2,1)S(1)}, u32[]{:S(2)}, u32[]{:S(2)}) %collective-permute-start.3) | collective-permute-done | bytes 147488 | tf_op jit(solution)/shard_map/ppermute | solution.py:418
  38.9 4.3 %cross1.1 = (f32[15,2,64,512]{3,2,1,0:T(8,128)}, f32[8,72,128]{2,1,0:T(8,128)}, f32[2,72,512]{2,1,0:T(8,128)}) custom-call(s32[2]{0:T(128)} %pad_add_fusion.place.refs_0_, s32[5,8]{1,0:T(8,128)} %refs_1_.26, s32[6,8]{1,0:T(8,128)} %refs_1_.27, bf16[1,2,64,512]{3,2,1,0:T(8,128)(2,1)} %copy-done.2, bf16[1,2,64,512]{3,2,1,0:T(8,128)(2,1)} %copy-done.11, ...), custom_call_target="tpu_custom_call" | custom-call | tf_op jit(solution)/shard_map/cross1/pallas_call | solution.py:510
  45.7 1.6 convert_element_type.167
  47.3 5.1 %all-to-all-start = ((f16[8,72,128]{2,1,0:T(8,128)(2,1)}), f16[8,72,128]{2,1,0:T(8,128)(2,1)S(1)}, u32[]{:S(2)}, u32[]{:S(2)}) async-start(f16[8,72,128]{2,1,0:T(8,128)(2,1)} %convert_element_type.167), calls=%async_computation | async-start | bytes 294912 | tf_op jit(solution)/shard_map/all_to_all | solution.py:424
  55.8 3.6 %all-to-all-done = f16[8,72,128]{2,1,0:T(8,128)(2,1)S(1)} async-done(((f16[8,72,128]{2,1,0:T(8,128)(2,1)}), f16[8,72,128]{2,1,0:T(8,128)(2,1)S(1)}, u32[]{:S(2)}, u32[]{:S(2)}) %all-to-all-start) | async-done | bytes 147488 | tf_op jit(solution)/shard_map/all_to_all | solution.py:424
  60.2 4.2 %marginal1.1 = (f32[6,2,64,512]{3,2,1,0:T(8,128)}, f32[2,136,512]{2,1,0:T(8,128)}) custom-call(s32[2]{0:T(128)} %pad_add_fusion.place.refs_0_, s32[6,8]{1,0:T(8,128)} %refs_1_.27, f32[2,64,512]{2,1,0:T(8,128)} %get-tuple-element.68.refs_2_, f32[8,72,128]{2,1,0:T(8,128)} %convert_element_type.168.refs_3_, ...), custom_call_target="tpu_custom_call", output_to_operand_aliasing={{0}: (16, {})} | custom-call | tf_op jit(solution)/shard_map/marginal1/pallas_call | solution.py:553
  67.1 3.9 %upper2.1 = (f32[2,64,512]{2,1,0:T(8,128)}, f32[8,72,128]{2,1,0:T(8,128)}) custom-call(s32[2]{0:T(128)} %pad_add_fusion.place.refs_0_, s32[5,8]{1,0:T(8,128)} %refs_1_.26, s32[6,8]{1,0:T(8,128)} %refs_1_.27, bf16[8,2,2,64,512]{4,3,2,1,0:T(8,128)(2,1)} %bitcast.32, f32[2,72,512]{2,1,0:T(8,128)} %get-tuple-element.34.refs_4_.refs_11_, ...), custom_call_target="tpu_custom_call" | custom-call | tf_op jit(solution)/shard_map/upper2/pallas_call | solution.py:483
  71.0 1.6 convert_element_type.176
  72.6 3.4 %all-to-all-start.1 = ((f16[8,72,128]{2,1,0:T(8,128)(2,1)}), f16[8,72,128]{2,1,0:T(8,128)(2,1)S(1)}, u32[]{:S(2)}, u32[]{:S(2)}) async-start(f16[8,72,128]{2,1,0:T(8,128)(2,1)} %convert_element_type.176), calls=%async_computation.1 | async-start | bytes 294912 | tf_op jit(solution)/shard_map/all_to_all | solution.py:424
  80.4 5.2 %cross2.1 = (f32[15,2,64,512]{3,2,1,0:T(8,128)}, f32[8,72,128]{2,1,0:T(8,128)}, f32[2,136,512]{2,1,0:T(8,128)}) custom-call(s32[2]{0:T(128)} %pad_add_fusion.place.refs_0_, s32[5,8]{1,0:T(8,128)} %refs_1_.26, s32[6,8]{1,0:T(8,128)} %refs_1_.27, bf16[8,2,2,64,512]{4,3,2,1,0:T(8,128)(2,1)} %bitcast.33, ...), custom_call_target="tpu_custom_call", output_to_operand_aliasing={{0}: (7, {})} | custom-call | tf_op jit(solution)/shard_map/cross2/pallas_call | solution.py:510
  89.5 5.0 %all-to-all-start.2 = ((f16[8,72,128]{2,1,0:T(8,128)(2,1)}), f16[8,72,128]{2,1,0:T(8,128)(2,1)S(1)}, u32[]{:S(2)}, u32[]{:S(2)}) async-start(f16[8,72,128]{2,1,0:T(8,128)(2,1)} %convert_element_type.178), calls=%async_computation.2 | async-start | bytes 294912 | tf_op jit(solution)/shard_map/all_to_all | solution.py:424
  94.5 2.3 collective-permute-start.12
  97.6 3.8 %collective-permute-done.12 = f16[2,72,512]{2,1,0:T(8,128)(2,1)S(1)} collective-permute-done((f16[2,72,512]{2,1,0:T(8,128)(2,1)S(1)}, f16[2,72,512]{2,1,0:T(8,128)(2,1)S(1)}, u32[]{:S(2)}, u32[]{:S(2)}) %collective-permute-start.12) | collective-permute-done | bytes 147488 | tf_op jit(solution)/shard_map/ppermute | solution.py:418
  107.2 4.8 %marginal2.1 = (f32[6,2,64,512]{3,2,1,0:T(8,128)}, f32[2,200,512]{2,1,0:T(8,128)}) custom-call(s32[2]{0:T(128)} %pad_add_fusion.place.refs_0_, s32[6,8]{1,0:T(8,128)} %refs_1_.27, f32[2,64,512]{2,1,0:T(8,128)} %get-tuple-element.67.refs_2_, f32[8,72,128]{2,1,0:T(8,128)} %convert_element_type.177.refs_3_, ...), custom_call_target="tpu_custom_call", output_to_operand_aliasing={{0}: (13, {})} | custom-call | tf_op jit(solution)/shard_map/marginal2/pallas_call | solution.py:553
  113.2 2.6 collective-permute-start.18
  115.8 5.2 %upper3.1 = (f32[2,128,512]{2,1,0:T(8,128)}, f32[8,136,128]{2,1,0:T(8,128)}) custom-call(s32[2]{0:T(128)} %pad_add_fusion.place.refs_0_, s32[5,8]{1,0:T(8,128)} %refs_1_.26, s32[6,8]{1,0:T(8,128)} %refs_1_.27, bf16[8,3,2,64,512]{4,3,2,1,0:T(8,128)(2,1)} %bitcast.28, f32[2,72,512]{2,1,0:T(8,128)} %get-tuple-element.34.refs_4_.refs_11_, ...), custom_call_target="tpu_custom_call" | custom-call | tf_op jit(solution)/shard_map/upper3/pallas_call | solution.py:483
  121.0 1.8 convert_element_type.185
  122.8 4.7 %all-to-all-start.3 = ((f16[8,136,128]{2,1,0:T(8,128)(2,1)}), f16[8,136,128]{2,1,0:T(8,128)(2,1)S(1)}, u32[]{:S(2)}, u32[]{:S(2)}) async-start(f16[8,136,128]{2,1,0:T(8,128)(2,1)} %convert_element_type.185), calls=%async_computation.3 | async-start | bytes 557056 | tf_op jit(solution)/shard_map/all_to_all | solution.py:424
  129.3 6.2 %cross3.1 = (f32[15,2,64,512]{3,2,1,0:T(8,128)}, f32[8,72,128]{2,1,0:T(8,128)}, f32[2,200,512]{2,1,0:T(8,128)}) custom-call(s32[2]{0:T(128)} %pad_add_fusion.place.refs_0_, s32[5,8]{1,0:T(8,128)} %refs_1_.26, s32[6,8]{1,0:T(8,128)} %refs_1_.27, bf16[8,3,2,64,512]{4,3,2,1,0:T(8,128)(2,1)} %bitcast.29, ...), custom_call_target="tpu_custom_call", output_to_operand_aliasing={{0}: (7, {})} | custom-call | tf_op jit(solution)/shard_map/cross3/pallas_call | solution.py:510
  138.1 2.8 collective-permute-start.21
  140.9 1.6 convert_element_type.187
  142.6 3.4 %all-to-all-done.3 = f16[8,136,128]{2,1,0:T(8,128)(2,1)S(1)} async-done(((f16[8,136,128]{2,1,0:T(8,128)(2,1)}), f16[8,136,128]{2,1,0:T(8,128)(2,1)S(1)}, u32[]{:S(2)}, u32[]{:S(2)}) %all-to-all-start.3) | async-done | bytes 278560 | tf_op jit(solution)/shard_map/all_to_all | solution.py:424
  146.0 3.6 %all-to-all-start.4 = ((f16[8,72,128]{2,1,0:T(8,128)(2,1)}), f16[8,72,128]{2,1,0:T(8,128)(2,1)S(1)}, u32[]{:S(2)}, u32[]{:S(2)}) async-start(f16[8,72,128]{2,1,0:T(8,128)(2,1)} %convert_element_type.187), calls=%async_computation.4 | async-start | bytes 294912 | tf_op jit(solution)/shard_map/all_to_all | solution.py:424
  149.5 5.6 %collective-permute-done.21 = f16[2,136,512]{2,1,0:T(8,128)(2,1)S(1)} collective-permute-done((f16[2,136,512]{2,1,0:T(8,128)(2,1)S(1)}, f16[2,136,512]{2,1,0:T(8,128)(2,1)S(1)}, u32[]{:S(2)}, u32[]{:S(2)}) %collective-permute-start.21) | collective-permute-done | bytes 278560 | tf_op jit(solution)/shard_map/ppermute | solution.py:418
  160.6 5.3 %marginal3.1 = (f32[6,2,64,512]{3,2,1,0:T(8,128)}, f32[2,264,512]{2,1,0:T(8,128)}) custom-call(s32[2]{0:T(128)} %pad_add_fusion.place.refs_0_, s32[6,8]{1,0:T(8,128)} %refs_1_.27, f32[2,64,512]{2,1,0:T(8,128)} %get-tuple-element.70.refs_2_, f32[8,136,128]{2,1,0:T(8,128)} %convert_element_type.186.refs_3_, ...), custom_call_target="tpu_custom_call", output_to_operand_aliasing={{0}: (11, {})} | custom-call | tf_op jit(solution)/shard_map/marginal3/pallas_call | solution.py:553
  167.7 6.8 %upper4.1 = (f32[2,192,512]{2,1,0:T(8,128)}, f32[8,200,128]{2,1,0:T(8,128)}) custom-call(s32[2]{0:T(128)} %pad_add_fusion.place.refs_0_, s32[5,8]{1,0:T(8,128)} %refs_1_.26, s32[6,8]{1,0:T(8,128)} %refs_1_.27, bf16[8,4,2,64,512]{4,3,2,1,0:T(8,128)(2,1)} %bitcast.24, f32[2,72,512]{2,1,0:T(8,128)} %get-tuple-element.34.refs_4_.refs_11_, ...), custom_call_target="tpu_custom_call" | custom-call | tf_op jit(solution)/shard_map/upper4/pallas_call | solution.py:483
  174.6 2.0 convert_element_type.191
  176.5 4.7 %all-to-all-start.5 = ((f16[8,200,128]{2,1,0:T(8,128)(2,1)}), f16[8,200,128]{2,1,0:T(8,128)(2,1)S(1)}, u32[]{:S(2)}, u32[]{:S(2)}) async-start(f16[8,200,128]{2,1,0:T(8,128)(2,1)} %convert_element_type.191), calls=%async_computation.5 | async-start | bytes 819200 | tf_op jit(solution)/shard_map/all_to_all | solution.py:424
  183.4 7.3 %cross4.1 = (f32[15,2,64,512]{3,2,1,0:T(8,128)}, f32[8,72,128]{2,1,0:T(8,128)}, f32[2,264,512]{2,1,0:T(8,128)}) custom-call(s32[2]{0:T(128)} %pad_add_fusion.place.refs_0_, s32[5,8]{1,0:T(8,128)} %refs_1_.26, s32[6,8]{1,0:T(8,128)} %refs_1_.27, bf16[8,4,2,64,512]{4,3,2,1,0:T(8,128)(2,1)} %bitcast.25, ...), custom_call_target="tpu_custom_call", output_to_operand_aliasing={{0}: (7, {})} | custom-call | tf_op jit(solution)/shard_map/cross4/pallas_call | solution.py:510
  192.1 2.4 collective-permute-start.26
  195.7 8.5 %all-to-all-done.5 = f16[8,200,128]{2,1,0:T(8,128)(2,1)S(1)} async-done(((f16[8,200,128]{2,1,0:T(8,128)(2,1)}), f16[8,200,128]{2,1,0:T(8,128)(2,1)S(1)}, u32[]{:S(2)}, u32[]{:S(2)}) %all-to-all-start.5) | async-done | bytes 409632 | tf_op jit(solution)/shard_map/all_to_all | solution.py:424
  204.3 4.2 %all-to-all-start.6 = ((f16[8,72,128]{2,1,0:T(8,128)(2,1)}), f16[8,72,128]{2,1,0:T(8,128)(2,1)S(1)}, u32[]{:S(2)}, u32[]{:S(2)}) async-start(f16[8,72,128]{2,1,0:T(8,128)(2,1)} %convert_element_type.195), calls=%async_computation.6 | async-start | bytes 294912 | tf_op jit(solution)/shard_map/all_to_all | solution.py:424
  208.5 7.4 %collective-permute-done.24 = f16[2,200,512]{2,1,0:T(8,128)(2,1)S(1)} collective-permute-done((f16[2,200,512]{2,1,0:T(8,128)(2,1)S(1)}, f16[2,200,512]{2,1,0:T(8,128)(2,1)S(1)}, u32[]{:S(2)}, u32[]{:S(2)}) %collective-permute-start.24) | collective-permute-done | bytes 409632 | tf_op jit(solution)/shard_map/ppermute | solution.py:418
  221.3 5.6 %marginal4.1 = (f32[6,2,64,512]{3,2,1,0:T(8,128)}, f32[2,328,512]{2,1,0:T(8,128)}) custom-call(s32[2]{0:T(128)} %pad_add_fusion.place.refs_0_, s32[6,8]{1,0:T(8,128)} %refs_1_.27, f32[2,64,512]{2,1,0:T(8,128)} %get-tuple-element.69.refs_2_, f32[8,200,128]{2,1,0:T(8,128)} %convert_element_type.192.refs_3_, ...), custom_call_target="tpu_custom_call", output_to_operand_aliasing={{0}: (10, {})} | custom-call | tf_op jit(solution)/shard_map/marginal4/pallas_call | solution.py:553
  228.4 1.8 collective-permute-start.27
  230.2 8.6 %upper5.1 = (f32[2,256,512]{2,1,0:T(8,128)}, f32[8,264,128]{2,1,0:T(8,128)}) custom-call(s32[2]{0:T(128)} %pad_add_fusion.place.refs_0_, s32[5,8]{1,0:T(8,128)} %refs_1_.26, s32[6,8]{1,0:T(8,128)} %refs_1_.27, bf16[8,5,2,64,512]{4,3,2,1,0:T(8,128)(2,1)} %bitcast.19, f32[2,72,512]{2,1,0:T(8,128)} %get-tuple-element.34.refs_4_.refs_11_, ...), custom_call_target="tpu_custom_call" | custom-call | tf_op jit(solution)/shard_map/upper5/pallas_call | solution.py:483
  238.8 2.1 convert_element_type.203
  240.9 4.7 %all-to-all-start.7 = ((f16[8,264,128]{2,1,0:T(8,128)(2,1)}), f16[8,264,128]{2,1,0:T(8,128)(2,1)S(1)}, u32[]{:S(2)}, u32[]{:S(2)}) async-start(f16[8,264,128]{2,1,0:T(8,128)(2,1)} %convert_element_type.203), calls=%async_computation.7 | async-start | bytes 1081344 | tf_op jit(solution)/shard_map/all_to_all | solution.py:424
  248.0 7.6 %cross5.1 = (f32[15,2,64,512]{3,2,1,0:T(8,128)}, f32[8,72,128]{2,1,0:T(8,128)}) custom-call(s32[2]{0:T(128)} %pad_add_fusion.place.refs_0_, s32[5,8]{1,0:T(8,128)} %refs_1_.26, s32[6,8]{1,0:T(8,128)} %refs_1_.27, bf16[8,5,2,64,512]{4,3,2,1,0:T(8,128)(2,1)} %bitcast.20, ...), custom_call_target="tpu_custom_call", output_to_operand_aliasing={{0}: (7, {})} | custom-call | flops 40000000000 | bytes 1048576 | tf_op jit(solution)/shard_map/cross5/pallas_call | solution.py:510
  255.6 5.7 %all-to-all-done.7 = f16[8,264,128]{2,1,0:T(8,128)(2,1)S(1)} async-done(((f16[8,264,128]{2,1,0:T(8,128)(2,1)}), f16[8,264,128]{2,1,0:T(8,128)(2,1)S(1)}, u32[]{:S(2)}, u32[]{:S(2)}) %all-to-all-start.7) | async-done | bytes 540704 | tf_op jit(solution)/shard_map/all_to_all | solution.py:424
  264.1 3.4 %all-to-all-start.8 = ((f16[8,72,128]{2,1,0:T(8,128)(2,1)}), f16[8,72,128]{2,1,0:T(8,128)(2,1)S(1)}, u32[]{:S(2)}, u32[]{:S(2)}) async-start(f16[8,72,128]{2,1,0:T(8,128)(2,1)} %select_convert_fusion), calls=%async_computation.8 | async-start | bytes 294912 | tf_op jit(solution)/shard_map/all_to_all | solution.py:424
  267.5 4.5 %partial5.1.refs_3_ = f32[2,64,512]{2,1,0:T(8,128)} custom-call(s32[2]{0:T(128)} %pad_add_fusion.place.refs_0_, f32[8,264,128]{2,1,0:T(8,128)} %convert_element_type.204.turned.refs_0_, bf16[8,5,2,64,512]{4,3,2,1,0:T(8,128)(2,1)} %bitcast.21), custom_call_target="tpu_custom_call" | custom-call | tf_op jit(solution)/shard_map/partial5/pallas_call | solution.py:538
  272.0 2.4 all-to-all-done.8
  275.2 3.4 %marginal5.1 = f32[6,2,64,512]{3,2,1,0:T(8,128)} custom-call(s32[2]{0:T(128)} %pad_add_fusion.place.refs_0_, s32[6,8]{1,0:T(8,128)} %refs_1_.27, f32[2,64,512]{2,1,0:T(8,128)} %get-tuple-element.66.refs_2_, f32[2,64,512]{2,1,0:T(8,128)} %partial5.1.refs_3_, f32[8,72,128]{2,1,0:T(8,128)} %convert_element_type.206.refs_4_, ...), custom_call_target="tpu_custom_call", output_to_operand_aliasing={{}: (6, {})} | custom-call | tf_op jit(solution)/shard_map/marginal5/pallas_call | solution.py:553
  (145 shorter events, 68.5 us)
Async XLA Ops:
  7.2 17.3 %copy-start.4 = (bf16[15,2,64,512]{3,2,1,0:T(8,128)(2,1)S(1)}, bf16[15,2,64,512]{3,2,1,0:T(8,128)(2,1)}, u32[]{:S(2)}) copy-start(bf16[15,2,64,512]{3,2,1,0:T(8,128)(2,1)} %param.4) | copy-start | bytes 5898244
  7.2 53.0 %all-gather.13.cloned.1.call-start = ((), (), s32[]{:S(2)}) async-start(), calls=%async_computation.11 | async-start | bytes 2359296 | tf_op jit(solution)/shard_map/all_gather | solution.py:428
  8.3 14.3 %copy-start.2 = (bf16[1,2,64,512]{3,2,1,0:T(8,128)(2,1)}, bf16[1,2,64,512]{3,2,1,0:T(8,128)(2,1)S(1)}, u32[]{:S(2)}) copy-start(bf16[1,2,64,512]{3,2,1,0:T(8,128)(2,1)S(1)} %slice.30.refs_0_.refs_3_.refs_4_) | copy-start | bytes 393220
  8.3 10.8 %collective-permute-start = (bf16[1,2,64,512]{3,2,1,0:T(8,128)(2,1)S(1)}, bf16[1,2,64,512]{3,2,1,0:T(8,128)(2,1)S(1)}, u32[]{:S(2)}, u32[]{:S(2)}) collective-permute-start(bf16[1,2,64,512]{3,2,1,0:T(8,128)(2,1)S(1)} %slice.30.refs_0_.refs_3_.refs_4_), channel_id=1, source_target_pairs={{0,2},{1,3},{2,4},{3,5},{4,6},{5,7},{6,0},{7,1},{8,10},{9,11},{10,... | collective-permute-start | bytes 393224 | tf_op jit(solution)/shard_map/ppermute | solution.py:436
  11.4 11.2 %collective-permute-start.1 = (bf16[1,2,64,512]{3,2,1,0:T(8,128)(2,1)S(1)}, bf16[1,2,64,512]{3,2,1,0:T(8,128)(2,1)S(1)}, u32[]{:S(2)}, u32[]{:S(2)}) collective-permute-start(bf16[1,2,64,512]{3,2,1,0:T(8,128)(2,1)S(1)} %slice.30.refs_0_.refs_3_.refs_4_), channel_id=1, source_target_pairs={{0,4},{1,5},{2,6},{3,7},{4,0},{5,1},{6,2},{7,3},{8,12},{9,13},{10,... | collective-permute-start | bytes 393224 | tf_op jit(solution)/shard_map/ppermute | solution.py:436
  13.9 8.6 %collective-permute-start.2 = (bf16[1,2,64,512]{3,2,1,0:T(8,128)(2,1)S(1)}, bf16[1,2,64,512]{3,2,1,0:T(8,128)(2,1)S(1)}, u32[]{:S(2)}, u32[]{:S(2)}) collective-permute-start(bf16[1,2,64,512]{3,2,1,0:T(8,128)(2,1)S(1)} %slice.30.refs_0_.refs_3_.refs_4_), channel_id=1, source_target_pairs={{0,6},{1,7},{2,0},{3,1},{4,2},{5,3},{6,4},{7,5},{8,14},{9,15},{10,... | collective-permute-start | bytes 393224 | tf_op jit(solution)/shard_map/ppermute | solution.py:436
  19.1 3.5 %copy-start.5 = (bf16[1,2,64,512]{3,2,1,0:T(8,128)(2,1)}, bf16[1,2,64,512]{3,2,1,0:T(8,128)(2,1)S(1)}, u32[]{:S(2)}) copy-start(bf16[1,2,64,512]{3,2,1,0:T(8,128)(2,1)S(1)} %collective-permute-done.refs_1_.refs_5_.refs_6_) | copy-start | bytes 393220
  25.2 81.9 %all-gather.15.cloned.1.call-start = ((), (), s32[]{:S(2)}) async-start(), calls=%async_computation.12 | async-start | bytes 3538944 | tf_op jit(solution)/shard_map/all_gather | solution.py:428
  26.1 134.5 %all-gather.11.cloned.1.call-start = ((), (), s32[]{:S(2)}) async-start(), calls=%async_computation.10 | async-start | bytes 4718592 | tf_op jit(solution)/shard_map/all_gather | solution.py:428
  27.0 3.2 %copy-start.10 = (bf16[1,2,64,512]{3,2,1,0:T(8,128)(2,1)S(1)}, bf16[1,2,64,512]{3,2,1,0:T(8,128)(2,1)}, u32[]{:S(2)}) copy-start(bf16[1,2,64,512]{3,2,1,0:T(8,128)(2,1)} %copy-done.9) | copy-start | bytes 393220
  27.0 194.3 %all-gather.9.cloned.1.call-start = ((), (), s32[]{:S(2)}) async-start(), calls=%async_computation.9 | async-start | bytes 5898240 | tf_op jit(solution)/shard_map/all_gather | solution.py:428
  28.1 24.4 %copy-start.1 = (f32[6,2,64,512]{3,2,1,0:T(8,128)S(1)}, f32[6,2,64,512]{3,2,1,0:T(8,128)}, u32[]{:S(2)}) copy-start(f32[6,2,64,512]{3,2,1,0:T(8,128)} %whole_diag.1) | copy-start | bytes 4718596
  28.1 6.6 %collective-permute-start.3 = (f16[2,72,512]{2,1,0:T(8,128)(2,1)S(1)}, f16[2,72,512]{2,1,0:T(8,128)(2,1)S(1)}, u32[]{:S(2)}, u32[]{:S(2)}) collective-permute-start(f16[2,72,512]{2,1,0:T(8,128)(2,1)S(1)} %convert_element_type.159), channel_id=1, source_target_pairs={{0,8},{8,16},{16,24},{24,0},{1,9},{9,17},{17,25},{25,1},{2,10},{10... | collective-permute-start | bytes 442376 | tf_op jit(solution)/shard_map/ppermute | solution.py:418
  29.6 7.3 %collective-permute-start.6 = (bf16[1,2,64,512]{3,2,1,0:T(8,128)(2,1)S(1)}, bf16[1,2,64,512]{3,2,1,0:T(8,128)(2,1)S(1)}, u32[]{:S(2)}, u32[]{:S(2)}) collective-permute-start(bf16[1,2,64,512]{3,2,1,0:T(8,128)(2,1)S(1)} %copy-done.3), channel_id=1, source_target_pairs={{0,1},{1,0},{2,3},{3,2},{4,5},{5,4},{6,7},{7,6},{8,9},{9,8},{10,11... | collective-permute-start | bytes 393224 | tf_op jit(solution)/shard_map/ppermute | solution.py:437
  29.6 7.9 %collective-permute-start.7 = (bf16[1,2,64,512]{3,2,1,0:T(8,128)(2,1)S(1)}, bf16[1,2,64,512]{3,2,1,0:T(8,128)(2,1)S(1)}, u32[]{:S(2)}, u32[]{:S(2)}) collective-permute-start(bf16[1,2,64,512]{3,2,1,0:T(8,128)(2,1)S(1)} %copy-done.6), channel_id=1, source_target_pairs={{0,1},{1,0},{2,3},{3,2},{4,5},{5,4},{6,7},{7,6},{8,9},{9,8},{10,11... | collective-permute-start | bytes 393224 | tf_op jit(solution)/shard_map/ppermute | solution.py:437
  30.2 7.4 %collective-permute-start.8 = (bf16[1,2,64,512]{3,2,1,0:T(8,128)(2,1)S(1)}, bf16[1,2,64,512]{3,2,1,0:T(8,128)(2,1)S(1)}, u32[]{:S(2)}, u32[]{:S(2)}) collective-permute-start(bf16[1,2,64,512]{3,2,1,0:T(8,128)(2,1)S(1)} %copy-done.8), channel_id=1, source_target_pairs={{0,1},{1,0},{2,3},{3,2},{4,5},{5,4},{6,7},{7,6},{8,9},{9,8},{10,11... | collective-permute-start | bytes 393224 | tf_op jit(solution)/shard_map/ppermute | solution.py:437
  30.2 7.3 %collective-permute-start.9 = (bf16[1,2,64,512]{3,2,1,0:T(8,128)(2,1)S(1)}, bf16[1,2,64,512]{3,2,1,0:T(8,128)(2,1)S(1)}, u32[]{:S(2)}, u32[]{:S(2)}) collective-permute-start(bf16[1,2,64,512]{3,2,1,0:T(8,128)(2,1)S(1)} %copy-done.10), channel_id=1, source_target_pairs={{0,1},{1,0},{2,3},{3,2},{4,5},{5,4},{6,7},{7,6},{8,9},{9,8},{10,11... | collective-permute-start | bytes 393224 | tf_op jit(solution)/shard_map/ppermute | solution.py:437
  34.7 18.8 %collective-permute-start.4 = (f16[2,72,512]{2,1,0:T(8,128)(2,1)S(1)}, f16[2,72,512]{2,1,0:T(8,128)(2,1)S(1)}, u32[]{:S(2)}, u32[]{:S(2)}) collective-permute-start(f16[2,72,512]{2,1,0:T(8,128)(2,1)S(1)} %convert_element_type.159), channel_id=1, source_target_pairs={{0,16},{8,24},{16,0},{24,8},{1,17},{9,25},{17,1},{25,9},{2,18},{10... | collective-permute-start | bytes 442376 | tf_op jit(solution)/shard_map/ppermute | solution.py:418
  37.0 17.3 %collective-permute-start.5 = (f16[2,72,512]{2,1,0:T(8,128)(2,1)S(1)}, f16[2,72,512]{2,1,0:T(8,128)(2,1)S(1)}, u32[]{:S(2)}, u32[]{:S(2)}) collective-permute-start(f16[2,72,512]{2,1,0:T(8,128)(2,1)S(1)} %convert_element_type.159), channel_id=1, source_target_pairs={{0,24},{8,0},{16,8},{24,16},{1,25},{9,1},{17,9},{25,17},{2,26},{10... | collective-permute-start | bytes 442376 | tf_op jit(solution)/shard_map/ppermute | solution.py:418
  44.2 10.9 %collective-permute-start.10 = (f16[2,72,512]{2,1,0:T(8,128)(2,1)S(1)}, f16[2,72,512]{2,1,0:T(8,128)(2,1)S(1)}, u32[]{:S(2)}, u32[]{:S(2)}) collective-permute-start(f16[2,72,512]{2,1,0:T(8,128)(2,1)S(1)} %convert_element_type.163), channel_id=1, source_target_pairs={{0,8},{8,16},{16,24},{24,0},{1,9},{9,17},{17,25},{25,1},{2,10},{10... | collective-permute-start | bytes 442376 | tf_op jit(solution)/shard_map/ppermute | solution.py:418
  47.3 12.1 %all-to-all-start = ((f16[8,72,128]{2,1,0:T(8,128)(2,1)}), f16[8,72,128]{2,1,0:T(8,128)(2,1)S(1)}, u32[]{:S(2)}, u32[]{:S(2)}) async-start(f16[8,72,128]{2,1,0:T(8,128)(2,1)} %convert_element_type.167), calls=%async_computation | async-start | bytes 294912 | tf_op jit(solution)/shard_map/all_to_all | solution.py:424
  65.5 14.0 %collective-permute-start.13 = (f16[2,136,512]{2,1,0:T(8,128)(2,1)S(1)}, f16[2,136,512]{2,1,0:T(8,128)(2,1)S(1)}, u32[]{:S(2)}, u32[]{:S(2)}) collective-permute-start(f16[2,136,512]{2,1,0:T(8,128)(2,1)S(1)} %convert_element_type.169), channel_id=1, source_target_pairs={{0,8},{8,16},{16,24},{24,0},{1,9},{9,17},{17,25},{25,1},{2,10},{10... | collective-permute-start | bytes 835592 | tf_op jit(solution)/shard_map/ppermute | solution.py:418
  72.6 16.9 %all-to-all-start.1 = ((f16[8,72,128]{2,1,0:T(8,128)(2,1)}), f16[8,72,128]{2,1,0:T(8,128)(2,1)S(1)}, u32[]{:S(2)}, u32[]{:S(2)}) async-start(f16[8,72,128]{2,1,0:T(8,128)(2,1)} %convert_element_type.176), calls=%async_computation.1 | async-start | bytes 294912 | tf_op jit(solution)/shard_map/all_to_all | solution.py:424
  76.0 18.5 %collective-permute-start.11 = (f16[2,72,512]{2,1,0:T(8,128)(2,1)S(1)}, f16[2,72,512]{2,1,0:T(8,128)(2,1)S(1)}, u32[]{:S(2)}, u32[]{:S(2)}) collective-permute-start(f16[2,72,512]{2,1,0:T(8,128)(2,1)S(1)} %convert_element_type.163), channel_id=1, source_target_pairs={{0,16},{8,24},{16,0},{24,8},{1,17},{9,25},{17,1},{25,9},{2,18},{10... | collective-permute-start | bytes 442376 | tf_op jit(solution)/shard_map/ppermute | solution.py:418
  76.6 26.3 %collective-permute-start.14 = (f16[2,136,512]{2,1,0:T(8,128)(2,1)S(1)}, f16[2,136,512]{2,1,0:T(8,128)(2,1)S(1)}, u32[]{:S(2)}, u32[]{:S(2)}) collective-permute-start(f16[2,136,512]{2,1,0:T(8,128)(2,1)S(1)} %convert_element_type.169), channel_id=1, source_target_pairs={{0,16},{8,24},{16,0},{24,8},{1,17},{9,25},{17,1},{25,9},{2,18},{10... | collective-permute-start | bytes 835592 | tf_op jit(solution)/shard_map/ppermute | solution.py:418
  78.1 25.7 %collective-permute-start.15 = (f16[2,136,512]{2,1,0:T(8,128)(2,1)S(1)}, f16[2,136,512]{2,1,0:T(8,128)(2,1)S(1)}, u32[]{:S(2)}, u32[]{:S(2)}) collective-permute-start(f16[2,136,512]{2,1,0:T(8,128)(2,1)S(1)} %convert_element_type.169), channel_id=1, source_target_pairs={{0,24},{8,0},{16,8},{24,16},{1,25},{9,1},{17,9},{25,17},{2,26},{10... | collective-permute-start | bytes 835592 | tf_op jit(solution)/shard_map/ppermute | solution.py:418
  86.7 18.7 %collective-permute-start.16 = (f16[2,136,512]{2,1,0:T(8,128)(2,1)S(1)}, f16[2,136,512]{2,1,0:T(8,128)(2,1)S(1)}, u32[]{:S(2)}, u32[]{:S(2)}) collective-permute-start(f16[2,136,512]{2,1,0:T(8,128)(2,1)S(1)} %convert_element_type.173), channel_id=1, source_target_pairs={{0,8},{8,16},{16,24},{24,0},{1,9},{9,17},{17,25},{25,1},{2,10},{10... | collective-permute-start | bytes 835592 | tf_op jit(solution)/shard_map/ppermute | solution.py:418
  87.3 19.0 %collective-permute-start.17 = (f16[2,136,512]{2,1,0:T(8,128)(2,1)S(1)}, f16[2,136,512]{2,1,0:T(8,128)(2,1)S(1)}, u32[]{:S(2)}, u32[]{:S(2)}) collective-permute-start(f16[2,136,512]{2,1,0:T(8,128)(2,1)S(1)} %convert_element_type.173), channel_id=1, source_target_pairs={{0,16},{8,24},{16,0},{24,8},{1,17},{9,25},{17,1},{25,9},{2,18},{10... | collective-permute-start | bytes 835592 | tf_op jit(solution)/shard_map/ppermute | solution.py:418
  89.5 15.1 %all-to-all-start.2 = ((f16[8,72,128]{2,1,0:T(8,128)(2,1)}), f16[8,72,128]{2,1,0:T(8,128)(2,1)S(1)}, u32[]{:S(2)}, u32[]{:S(2)}) async-start(f16[8,72,128]{2,1,0:T(8,128)(2,1)} %convert_element_type.178), calls=%async_computation.2 | async-start | bytes 294912 | tf_op jit(solution)/shard_map/all_to_all | solution.py:424
  94.5 6.8 %collective-permute-start.12 = (f16[2,72,512]{2,1,0:T(8,128)(2,1)S(1)}, f16[2,72,512]{2,1,0:T(8,128)(2,1)S(1)}, u32[]{:S(2)}, u32[]{:S(2)}) collective-permute-start(f16[2,72,512]{2,1,0:T(8,128)(2,1)S(1)} %convert_element_type.163), channel_id=1, source_target_pairs={{0,24},{8,0},{16,8},{24,16},{1,25},{9,1},{17,9},{25,17},{2,26},{10... | collective-permute-start | bytes 442376 | tf_op jit(solution)/shard_map/ppermute | solution.py:418
  113.2 15.2 %collective-permute-start.18 = (f16[2,200,512]{2,1,0:T(8,128)(2,1)S(1)}, f16[2,200,512]{2,1,0:T(8,128)(2,1)S(1)}, u32[]{:S(2)}, u32[]{:S(2)}) collective-permute-start(f16[2,200,512]{2,1,0:T(8,128)(2,1)S(1)} %convert_element_type.180), channel_id=1, source_target_pairs={{0,8},{8,16},{16,24},{24,0},{1,9},{9,17},{17,25},{25,1},{2,10},{10... | collective-permute-start | bytes 1228808 | tf_op jit(solution)/shard_map/ppermute | solution.py:418
  122.8 23.1 %all-to-all-start.3 = ((f16[8,136,128]{2,1,0:T(8,128)(2,1)}), f16[8,136,128]{2,1,0:T(8,128)(2,1)S(1)}, u32[]{:S(2)}, u32[]{:S(2)}) async-start(f16[8,136,128]{2,1,0:T(8,128)(2,1)} %convert_element_type.185), calls=%async_computation.3 | async-start | bytes 557056 | tf_op jit(solution)/shard_map/all_to_all | solution.py:424
  127.5 28.5 %collective-permute-start.19 = (f16[2,200,512]{2,1,0:T(8,128)(2,1)S(1)}, f16[2,200,512]{2,1,0:T(8,128)(2,1)S(1)}, u32[]{:S(2)}, u32[]{:S(2)}) collective-permute-start(f16[2,200,512]{2,1,0:T(8,128)(2,1)S(1)} %convert_element_type.180), channel_id=1, source_target_pairs={{0,16},{8,24},{16,0},{24,8},{1,17},{9,25},{17,1},{25,9},{2,18},{10... | collective-permute-start | bytes 1228808 | tf_op jit(solution)/shard_map/ppermute | solution.py:418
  136.8 21.8 %collective-permute-start.20 = (f16[2,200,512]{2,1,0:T(8,128)(2,1)S(1)}, f16[2,200,512]{2,1,0:T(8,128)(2,1)S(1)}, u32[]{:S(2)}, u32[]{:S(2)}) collective-permute-start(f16[2,200,512]{2,1,0:T(8,128)(2,1)S(1)} %convert_element_type.183), channel_id=1, source_target_pairs={{0,8},{8,16},{16,24},{24,0},{1,9},{9,17},{17,25},{25,1},{2,10},{10... | collective-permute-start | bytes 1228808 | tf_op jit(solution)/shard_map/ppermute | solution.py:418
  136.9 22.7 %collective-permute-start.22 = (f16[2,200,512]{2,1,0:T(8,128)(2,1)S(1)}, f16[2,200,512]{2,1,0:T(8,128)(2,1)S(1)}, u32[]{:S(2)}, u32[]{:S(2)}) collective-permute-start(f16[2,200,512]{2,1,0:T(8,128)(2,1)S(1)} %convert_element_type.183), channel_id=1, source_target_pairs={{0,16},{8,24},{16,0},{24,8},{1,17},{9,25},{17,1},{25,9},{2,18},{10... | collective-permute-start | bytes 1228808 | tf_op jit(solution)/shard_map/ppermute | solution.py:418
  138.1 17.0 %collective-permute-start.21 = (f16[2,136,512]{2,1,0:T(8,128)(2,1)S(1)}, f16[2,136,512]{2,1,0:T(8,128)(2,1)S(1)}, u32[]{:S(2)}, u32[]{:S(2)}) collective-permute-start(f16[2,136,512]{2,1,0:T(8,128)(2,1)S(1)} %convert_element_type.173), channel_id=1, source_target_pairs={{0,24},{8,0},{16,8},{24,16},{1,25},{9,1},{17,9},{25,17},{2,26},{10... | collective-permute-start | bytes 835592 | tf_op jit(solution)/shard_map/ppermute | solution.py:418
  146.0 11.9 %all-to-all-start.4 = ((f16[8,72,128]{2,1,0:T(8,128)(2,1)}), f16[8,72,128]{2,1,0:T(8,128)(2,1)S(1)}, u32[]{:S(2)}, u32[]{:S(2)}) async-start(f16[8,72,128]{2,1,0:T(8,128)(2,1)} %convert_element_type.187), calls=%async_computation.4 | async-start | bytes 294912 | tf_op jit(solution)/shard_map/all_to_all | solution.py:424
  167.3 14.9 %collective-permute-start.23 = (f16[2,264,512]{2,1,0:T(8,128)(2,1)S(1)}, f16[2,264,512]{2,1,0:T(8,128)(2,1)S(1)}, u32[]{:S(2)}, u32[]{:S(2)}) collective-permute-start(f16[2,264,512]{2,1,0:T(8,128)(2,1)S(1)} %convert_element_type.193), channel_id=1, source_target_pairs={{0,8},{8,16},{16,24},{24,0},{1,9},{9,17},{17,25},{25,1},{2,10},{10... | collective-permute-start | bytes 1622024 | tf_op jit(solution)/shard_map/ppermute | solution.py:418
  176.5 27.8 %all-to-all-start.5 = ((f16[8,200,128]{2,1,0:T(8,128)(2,1)}), f16[8,200,128]{2,1,0:T(8,128)(2,1)S(1)}, u32[]{:S(2)}, u32[]{:S(2)}) async-start(f16[8,200,128]{2,1,0:T(8,128)(2,1)} %convert_element_type.191), calls=%async_computation.5 | async-start | bytes 819200 | tf_op jit(solution)/shard_map/all_to_all | solution.py:424
  181.2 35.7 %collective-permute-start.25 = (f16[2,264,512]{2,1,0:T(8,128)(2,1)S(1)}, f16[2,264,512]{2,1,0:T(8,128)(2,1)S(1)}, u32[]{:S(2)}, u32[]{:S(2)}) collective-permute-start(f16[2,264,512]{2,1,0:T(8,128)(2,1)S(1)} %convert_element_type.193), channel_id=1, source_target_pairs={{0,16},{8,24},{16,0},{24,8},{1,17},{9,25},{17,1},{25,9},{2,18},{10... | collective-permute-start | bytes 1622024 | tf_op jit(solution)/shard_map/ppermute | solution.py:418
  190.7 4.4 %copy-start.16 = (f32[8,72,128]{2,1,0:T(8,128)S(1)}, f32[8,72,128]{2,1,0:T(8,128)}, u32[]{:S(2)}) copy-start(f32[8,72,128]{2,1,0:T(8,128)} %get-tuple-element.56) | copy-start | bytes 884740
  192.1 27.7 %collective-permute-start.26 = (f16[2,264,512]{2,1,0:T(8,128)(2,1)S(1)}, f16[2,264,512]{2,1,0:T(8,128)(2,1)S(1)}, u32[]{:S(2)}, u32[]{:S(2)}) collective-permute-start(f16[2,264,512]{2,1,0:T(8,128)(2,1)S(1)} %convert_element_type.199), channel_id=1, source_target_pairs={{0,8},{8,16},{16,24},{24,0},{1,9},{9,17},{17,25},{25,1},{2,10},{10... | collective-permute-start | bytes 1622024 | tf_op jit(solution)/shard_map/ppermute | solution.py:418
  194.5 21.4 %collective-permute-start.24 = (f16[2,200,512]{2,1,0:T(8,128)(2,1)S(1)}, f16[2,200,512]{2,1,0:T(8,128)(2,1)S(1)}, u32[]{:S(2)}, u32[]{:S(2)}) collective-permute-start(f16[2,200,512]{2,1,0:T(8,128)(2,1)S(1)} %convert_element_type.180), channel_id=1, source_target_pairs={{0,24},{8,0},{16,8},{24,16},{1,25},{9,1},{17,9},{25,17},{2,26},{10... | collective-permute-start | bytes 1228808 | tf_op jit(solution)/shard_map/ppermute | solution.py:418
  204.3 14.7 %all-to-all-start.6 = ((f16[8,72,128]{2,1,0:T(8,128)(2,1)}), f16[8,72,128]{2,1,0:T(8,128)(2,1)S(1)}, u32[]{:S(2)}, u32[]{:S(2)}) async-start(f16[8,72,128]{2,1,0:T(8,128)(2,1)} %convert_element_type.195), calls=%async_computation.6 | async-start | bytes 294912 | tf_op jit(solution)/shard_map/all_to_all | solution.py:424
  228.4 18.4 %collective-permute-start.27 = (f16[2,328,512]{2,1,0:T(8,128)(2,1)S(1)}, f16[2,328,512]{2,1,0:T(8,128)(2,1)S(1)}, u32[]{:S(2)}, u32[]{:S(2)}) collective-permute-start(f16[2,328,512]{2,1,0:T(8,128)(2,1)S(1)} %convert_element_type.201), channel_id=1, source_target_pairs={{0,8},{8,16},{16,24},{24,0},{1,9},{9,17},{17,25},{25,1},{2,10},{10... | collective-permute-start | bytes 2015240 | tf_op jit(solution)/shard_map/ppermute | solution.py:418
  240.9 20.5 %all-to-all-start.7 = ((f16[8,264,128]{2,1,0:T(8,128)(2,1)}), f16[8,264,128]{2,1,0:T(8,128)(2,1)S(1)}, u32[]{:S(2)}, u32[]{:S(2)}) async-start(f16[8,264,128]{2,1,0:T(8,128)(2,1)} %convert_element_type.203), calls=%async_computation.7 | async-start | bytes 1081344 | tf_op jit(solution)/shard_map/all_to_all | solution.py:424
  255.6 7.8 %copy-start.15 = (f32[8,72,128]{2,1,0:T(8,128)S(1)}, f32[8,72,128]{2,1,0:T(8,128)}, u32[]{:S(2)}) copy-start(f32[8,72,128]{2,1,0:T(8,128)} %get-tuple-element.64) | copy-start | bytes 884740
  264.1 10.3 %all-to-all-start.8 = ((f16[8,72,128]{2,1,0:T(8,128)(2,1)}), f16[8,72,128]{2,1,0:T(8,128)(2,1)S(1)}, u32[]{:S(2)}, u32[]{:S(2)}) async-start(f16[8,72,128]{2,1,0:T(8,128)(2,1)} %select_convert_fusion), calls=%async_computation.8 | async-start | bytes 294912 | tf_op jit(solution)/shard_map/all_to_all | solution.py:424
  (10 other events, 14.4 us)
Sparse Core Ops, SparseCore 0:
  25.4 31.0 all-gather.12
  58.1 40.9 all-gather.14
  100.7 51.7 all-gather.10
  154.0 67.2 all-gather.8
